TPU v7x, 32 devices: a whole 2x2x4 slice. The times are simulated.
32 devices in a mesh: dp: 2 (over core), tx: 4 (over y, x), ty: 4 (over z).
Axes of the slice: x: 2, y: 2, z: 4, core: 2. Of those that a mesh axis runs over, the one named last changes fastest.
Arguments:
- x_given: bfloat16 [4, 2048, 1536], P('tx', 'dp', 'ty'), may hold values from -6 to 6
- cotangent: bfloat16 [4, 2048, 1536], P('tx', 'dp', 'ty'), may hold values from -6 to 6
- seq_lengths: int32 [4, 4], replicated, may hold values from 128 to 896, as said below
- seq_deal: int32 [4, 4], replicated, may hold values from 0 to 3, as said below
- attn_gain: float32 [1536], P('ty'), may hold values from 0.5 to 1.5
- w_query: bfloat16 [1536, 1536], P('ty', 'tx'), may hold values from -0.15625 to 0.15625
- w_key: bfloat16 [1536, 1536], P('ty', 'tx'), may hold values from -0.15625 to 0.15625
- w_value: bfloat16 [1536, 1536], P('ty', 'tx'), may hold values from -0.15625 to 0.15625
- w_ogate: bfloat16 [1536, 1536], P('ty', 'tx'), may hold values from -0.15625 to 0.15625
- w_forget: bfloat16 [1536, 24], P('ty', 'tx'), may hold values from -0.21875 to 0.21875
- b_forget: float32 [24], P('tx'), may hold values from 2.5 to 9
- w_out: bfloat16 [1536, 1536], P('tx', 'ty'), may hold values from -0.625 to 0.625
- mlp_gain: float32 [1536], P('ty'), may hold values from 0.5 to 1.5
- w_gate: bfloat16 [1536, 4096], P('ty', 'tx'), may hold values from -0.15625 to 0.15625
- w_up: bfloat16 [1536, 4096], P('ty', 'tx'), may hold values from -0.15625 to 0.15625
- w_down: bfloat16 [4096, 1536], P('tx', 'ty'), may hold values from -0.09375 to 0.09375
Outputs:
- output: bfloat16 [4, 2048, 1536], P('tx', 'dp', 'ty')
- grad_input: bfloat16 [4, 2048, 1536], P('tx', 'dp', 'ty')
- grad_attn_gain: float32 [1536], P('ty')
- grad_w_query: float32 [1536, 1536], P('ty', 'tx')
- grad_w_key: float32 [1536, 1536], P('ty', 'tx')
- grad_w_value: float32 [1536, 1536], P('ty', 'tx')
- grad_w_ogate: float32 [1536, 1536], P('ty', 'tx')
- grad_w_forget: float32 [1536, 24], P('ty', 'tx')
- grad_b_forget: float32 [24], P('tx')
- grad_w_out: float32 [1536, 1536], P('tx', 'ty')
- grad_mlp_gain: float32 [1536], P('ty')
- grad_w_gate: float32 [1536, 4096], P('ty', 'tx')
- grad_w_up: float32 [1536, 4096], P('ty', 'tx')
- grad_w_down: float32 [4096, 1536], P('tx', 'ty')
Inputs may be any that keep to these rules, and one draw needn't show every extreme that they name: `seq_lengths`: in every stream, dealt slots 2r and 2r + 1 hold block r's two sequences, whose lengths sum to 1024; in every stream some block holds a sequence of 128 tokens. `seq_deal`: each row is a permutation of 0 to 3.
All inputs are finite; a program needn't handle non-finite values.
Results may differ from a plain program's by a relative error of at most 0.017.
Values may be sent and summed in bfloat16 or wider, within the bound.
No kernel may reach another device: no remote copies, remote signals or barrier semaphores. Data moves between devices by JAX's collectives and lax.ppermute only.
A program may use at most 256 MiB of HBM per device.

v0:
```python
import jax
import jax.numpy as jnp
from jax import lax
from jax.sharding import PartitionSpec as P

EPSILON = 1e-06


def as_sent(shard):
    return jax.tree.map(lambda a: a.astype(jnp.bfloat16) if a.dtype == jnp.float32 else a, shard)


def product(left, right):
    return jnp.dot(left, right, preferred_element_type=jnp.float32)


def rows_product(left, right):
    return lax.dot_general(
        left, right, (((0,), (0,)), ((), ())), preferred_element_type=jnp.float32
    )


def cols_product(left, right):
    return lax.dot_general(
        left, right, (((1,), (1,)), ((), ())), preferred_element_type=jnp.float32
    )


def pick_small(lookup, indices):
    width = lookup.shape[0]
    matches = indices[:, None] == jnp.arange(width, dtype=jnp.int32)[None, :]
    return jnp.sum(jnp.where(matches, lookup[None, :], 0), axis=1)


def stream_tables(lengths, dealing):
    width = lengths.shape[0]
    numbers = jnp.arange(width, dtype=jnp.int32)
    given_start = jnp.cumsum(lengths) - lengths
    owners = jnp.sum(jnp.where(dealing[None, :] == numbers[:, None], numbers[None, :], 0), axis=1)
    dealt_length = pick_small(lengths, owners)
    dealt_start = jnp.cumsum(dealt_length) - dealt_length
    return (given_start, owners, dealt_start)


def dealt_sources(lengths, dealing, first_place, row_total):
    given_start, owners, dealt_start = stream_tables(lengths, dealing)
    places = first_place + jnp.arange(row_total, dtype=jnp.int32)
    slot_ids = jnp.sum((dealt_start[None, :] <= places[:, None]).astype(jnp.int32), axis=1) - 1
    source = (
        pick_small(given_start, pick_small(owners, slot_ids))
        + places
        - pick_small(dealt_start, slot_ids)
    )
    return (source, slot_ids)


def given_targets(lengths, dealing, first_place, row_total):
    given_start, owners, dealt_start = stream_tables(lengths, dealing)
    places = first_place + jnp.arange(row_total, dtype=jnp.int32)
    member = jnp.sum((given_start[None, :] <= places[:, None]).astype(jnp.int32), axis=1) - 1
    target = (
        pick_small(dealt_start, pick_small(dealing, member))
        + places
        - pick_small(given_start, member)
    )
    return target


def rows_tx(values):
    return lax.all_gather(values, "tx", axis=0, tiled=True)


def parts_ty(values):
    return lax.psum_scatter(values, "ty", scatter_dimension=0, tiled=True)


def rows_ty(values):
    return jax.tree.map(
        lambda part, own: part.astype(own.dtype),
        lax.all_gather(as_sent(values), "ty", axis=0, tiled=True),
        values,
    )


def parts_tx(values):
    return lax.psum_scatter(values, "tx", scatter_dimension=0, tiled=True)


def row_sum(values):
    return lax.psum(values, "ty")


def norm_forward(resid, gain):
    width = resid.shape[1] * lax.axis_size("ty")
    scale = lax.rsqrt(row_sum(jnp.sum(resid * resid, axis=1)) / width + EPSILON)
    normed = resid * scale[:, None]
    return ((normed * gain).astype(jnp.bfloat16), normed, scale)


def norm_backward(grad_in, normed, scale, gain):
    width = normed.shape[1] * lax.axis_size("ty")
    grad_normed = grad_in * gain
    inner = row_sum(jnp.sum(grad_normed * normed, axis=1)) / width
    grad_resid = scale[:, None] * (grad_normed - normed * inner[:, None])
    grad_gain = jnp.sum(grad_in * normed, axis=0)
    return (grad_resid, grad_gain)


def block_scores(queries, keys_in, decays, slot_ids, begin_row, end_row, score_scale):
    places = jnp.arange(end_row, dtype=jnp.int32)
    raw_scores = (
        jnp.einsum(
            "qhd,khd->hqk",
            queries[begin_row:end_row],
            keys_in[:end_row],
            preferred_element_type=jnp.float32,
        )
        * score_scale
    )
    raw_scores = (
        raw_scores + decays[begin_row:end_row].T[:, :, None] - decays[:end_row].T[:, None, :]
    )
    allowed = (slot_ids[begin_row:end_row, None] == slot_ids[None, :end_row]) & (
        places[begin_row:end_row, None] >= places[None, :]
    )
    return jnp.where(allowed[None], raw_scores, -1e30)


def attend_forward(queries, keys_in, values, decays, slot_ids, block_rows):
    row_total, head_count, head_size = queries.shape
    score_scale = head_size ** (-0.5)
    outputs = []
    lse_parts = []
    for begin_row in range(0, row_total, block_rows):
        end_row = begin_row + block_rows
        raw_scores = block_scores(
            queries, keys_in, decays, slot_ids, begin_row, end_row, score_scale
        )
        row_top = jnp.max(raw_scores, axis=-1, keepdims=True)
        weights = jnp.exp(raw_scores - row_top)
        weight_total = jnp.sum(weights, axis=-1, keepdims=True)
        probabilities = (weights / weight_total).astype(jnp.bfloat16)
        outputs.append(
            jnp.einsum(
                "hqk,khd->qhd", probabilities, values[:end_row], preferred_element_type=jnp.float32
            )
        )
        lse_parts.append(row_top + jnp.log(weight_total))
    return (jnp.concatenate(outputs, axis=0), jnp.concatenate(lse_parts, axis=1))


def attend_backward(queries, keys_in, values, decays, slot_ids, block_rows, log_totals, grad_att):
    row_total, head_count, head_size = queries.shape
    score_scale = head_size ** (-0.5)
    grad_keys = jnp.zeros((row_total, head_count, head_size), jnp.float32)
    grad_values = jnp.zeros((row_total, head_count, head_size), jnp.float32)
    grad_decays = jnp.zeros((row_total, head_count), jnp.float32)
    query_parts = []
    for begin_row in range(0, row_total, block_rows):
        end_row = begin_row + block_rows
        raw_scores = block_scores(
            queries, keys_in, decays, slot_ids, begin_row, end_row, score_scale
        )
        probabilities = jnp.exp(raw_scores - log_totals[:, begin_row:end_row])
        grad_probs = jnp.einsum(
            "qhd,khd->hqk",
            grad_att[begin_row:end_row],
            values[:end_row],
            preferred_element_type=jnp.float32,
        )
        delta = jnp.sum(probabilities * grad_probs, axis=-1, keepdims=True)
        grad_scores = (probabilities * (grad_probs - delta)).astype(jnp.bfloat16)
        grad_values = grad_values.at[:end_row].add(
            jnp.einsum(
                "hqk,qhd->khd",
                probabilities.astype(jnp.bfloat16),
                grad_att[begin_row:end_row],
                preferred_element_type=jnp.float32,
            )
        )
        query_parts.append(
            jnp.einsum(
                "hqk,khd->qhd", grad_scores, keys_in[:end_row], preferred_element_type=jnp.float32
            )
            * score_scale
        )
        grad_keys = grad_keys.at[:end_row].add(
            jnp.einsum(
                "hqk,qhd->khd",
                grad_scores,
                queries[begin_row:end_row],
                preferred_element_type=jnp.float32,
            )
            * score_scale
        )
        grad_decays = grad_decays.at[begin_row:end_row].add(
            jnp.sum(grad_scores, axis=2, dtype=jnp.float32).T
        )
        grad_decays = grad_decays.at[:end_row].add(
            -jnp.sum(grad_scores, axis=1, dtype=jnp.float32).T
        )
    return (jnp.concatenate(query_parts, axis=0), grad_keys, grad_values, grad_decays)


def on_device(
    x_given,
    cotangent,
    seq_lengths,
    seq_deal,
    attn_gain,
    w_query,
    w_key,
    w_value,
    w_ogate,
    w_forget,
    b_forget,
    w_out,
    mlp_gain,
    w_gate,
    w_up,
    w_down,
):
    quarter = x_given.shape[1]
    block_rows = min(512, quarter)
    row_index = lax.axis_index("dp")
    column_index = lax.axis_index("tx")
    lane_index = lax.axis_index("ty")
    first_place = row_index * quarter
    own_lengths = lax.dynamic_index_in_dim(seq_lengths, column_index, 0, keepdims=False)
    own_dealing = lax.dynamic_index_in_dim(seq_deal, column_index, 0, keepdims=False)
    sources, unused_ids = dealt_sources(own_lengths, own_dealing, first_place, quarter)
    targets = given_targets(own_lengths, own_dealing, first_place, quarter)
    block_lengths = lax.dynamic_index_in_dim(seq_lengths, lane_index, 0, keepdims=False)
    block_dealing = lax.dynamic_index_in_dim(seq_deal, lane_index, 0, keepdims=False)
    unused_rows, slot_ids = dealt_sources(block_lengths, block_dealing, first_place, quarter)
    blank = jnp.zeros(x_given.shape[1:], jnp.bfloat16)
    pieces = (
        lax.all_gather(x_given[0], "dp", axis=0, tiled=True),
        lax.all_gather(cotangent[0], "dp", axis=0, tiled=True),
    )
    span_rows = pieces[0].shape[0]
    inside = ((sources >= 0) & (sources < span_rows))[:, None]
    picked = jnp.clip(sources, 0, span_rows - 1)
    resid_in = jnp.where(inside, pieces[0][picked], blank)
    grad_out = jnp.where(inside, pieces[1][picked], blank)

    def send_back(values):
        pieces = lax.all_gather(values, "dp", axis=0, tiled=True)
        span_rows = pieces.shape[0]
        inside = ((targets >= 0) & (targets < span_rows))[:, None]
        picked = jnp.clip(targets, 0, span_rows - 1)
        return jnp.where(inside, pieces[picked], jnp.zeros_like(values))

    head_count = w_forget.shape[1]
    head_size = w_query.shape[1] // head_count
    resid_first = resid_in.astype(jnp.float32)
    first_normed, normed_one, scale_one = norm_forward(resid_first, attn_gain)
    first_rows = rows_tx(first_normed)
    query_pre, key_pre, value_pre, ogate_pre, forget_part = parts_ty(
        (
            product(first_rows, w_query),
            product(first_rows, w_key),
            product(first_rows, w_value),
            product(first_rows, w_ogate),
            product(first_rows, w_forget),
        )
    )
    forget_pre = forget_part + b_forget
    decays = jnp.cumsum(jax.nn.log_sigmoid(forget_pre), axis=0)
    queries = query_pre.astype(jnp.bfloat16).reshape(quarter, head_count, head_size)
    keys_in = key_pre.astype(jnp.bfloat16).reshape(quarter, head_count, head_size)
    values = value_pre.astype(jnp.bfloat16).reshape(quarter, head_count, head_size)
    out_gate = jax.nn.sigmoid(ogate_pre)
    attended, log_totals = attend_forward(queries, keys_in, values, decays, slot_ids, block_rows)
    attended_flat = attended.reshape(quarter, head_count * head_size)
    mixed = (attended_flat * out_gate).astype(jnp.bfloat16)
    mixed_rows = rows_ty(mixed)
    second_resid = resid_first + parts_tx(product(mixed_rows, w_out))
    second_normed, normed_two, scale_two = norm_forward(second_resid, mlp_gain)
    second_rows = rows_tx(second_normed)
    gate_pre, up_pre = parts_ty((product(second_rows, w_gate), product(second_rows, w_up)))
    gate_sigmoid = jax.nn.sigmoid(gate_pre)
    gate_silu = gate_pre * gate_sigmoid
    hidden = (gate_silu * up_pre).astype(jnp.bfloat16)
    hidden_rows = rows_ty(hidden)
    result = second_resid + parts_tx(product(hidden_rows, w_down))
    output_given = send_back(result.astype(jnp.bfloat16))
    grad_out_rows = rows_tx(grad_out)
    grad_w_down = rows_product(hidden_rows, grad_out_rows)
    grad_hidden = parts_ty(cols_product(grad_out_rows, w_down))
    grad_gate = (
        grad_hidden * up_pre * gate_sigmoid * (1.0 + gate_pre * (1.0 - gate_sigmoid))
    ).astype(jnp.bfloat16)
    grad_up = (grad_hidden * gate_silu).astype(jnp.bfloat16)
    gate_grad_rows, up_grad_rows = rows_ty((grad_gate, grad_up))
    grad_w_gate = rows_product(second_rows, gate_grad_rows)
    grad_w_up = rows_product(second_rows, up_grad_rows)
    grad_second_normed = parts_tx(
        cols_product(gate_grad_rows, w_gate) + cols_product(up_grad_rows, w_up)
    )
    grad_from_norm, grad_mlp_gain = norm_backward(
        grad_second_normed, normed_two, scale_two, mlp_gain
    )
    grad_second = grad_out.astype(jnp.float32) + grad_from_norm
    grad_branch_rows = rows_tx(grad_second.astype(jnp.bfloat16))
    grad_w_out = rows_product(mixed_rows, grad_branch_rows)
    grad_mixed = parts_ty(cols_product(grad_branch_rows, w_out))
    grad_att = (grad_mixed * out_gate).astype(jnp.bfloat16).reshape(quarter, head_count, head_size)
    grad_ogate = (grad_mixed * attended_flat * out_gate * (1.0 - out_gate)).astype(jnp.bfloat16)
    grad_queries, grad_keys, grad_values, grad_decays = attend_backward(
        queries, keys_in, values, decays, slot_ids, block_rows, log_totals, grad_att
    )
    grad_keep = jnp.flip(jnp.cumsum(jnp.flip(grad_decays, 0), axis=0), 0)
    grad_forget = (grad_keep * jax.nn.sigmoid(-forget_pre)).astype(jnp.bfloat16)
    query_flat = grad_queries.reshape(quarter, -1).astype(jnp.bfloat16)
    key_flat = grad_keys.reshape(quarter, -1).astype(jnp.bfloat16)
    value_flat = grad_values.reshape(quarter, -1).astype(jnp.bfloat16)
    query_rows, key_rows, value_rows, ogate_rows, forget_rows = rows_ty(
        (query_flat, key_flat, value_flat, grad_ogate, grad_forget)
    )
    grad_w_query = rows_product(first_rows, query_rows)
    grad_w_key = rows_product(first_rows, key_rows)
    grad_w_value = rows_product(first_rows, value_rows)
    grad_w_ogate = rows_product(first_rows, ogate_rows)
    grad_w_forget = rows_product(first_rows, forget_rows)
    grad_b_forget = jnp.sum(forget_rows, axis=0, dtype=jnp.float32)
    grad_first_normed = parts_tx(
        cols_product(query_rows, w_query)
        + cols_product(key_rows, w_key)
        + cols_product(value_rows, w_value)
        + cols_product(ogate_rows, w_ogate)
        + cols_product(forget_rows, w_forget)
    )
    grad_from_first, grad_attn_gain = norm_backward(
        grad_first_normed, normed_one, scale_one, attn_gain
    )
    grad_input_given = send_back((grad_second + grad_from_first).astype(jnp.bfloat16))
    summed = lax.psum(
        (
            grad_w_query,
            grad_w_key,
            grad_w_value,
            grad_w_ogate,
            grad_w_forget,
            grad_b_forget,
            grad_w_out,
            grad_w_gate,
            grad_w_up,
            grad_w_down,
        ),
        "dp",
    )
    gains = lax.psum((grad_attn_gain, grad_mlp_gain), ("dp", "tx"))
    return (
        output_given[None],
        grad_input_given[None],
        gains[0],
        summed[0],
        summed[1],
        summed[2],
        summed[3],
        summed[4],
        summed[5],
        summed[6],
        gains[1],
        summed[7],
        summed[8],
        summed[9],
    )


def solution(mesh):
    return jax.shard_map(
        on_device,
        mesh=mesh,
        in_specs=(
            P("tx", "dp", "ty"),
            P("tx", "dp", "ty"),
            P(),
            P(),
            P("ty"),
            P("ty", "tx"),
            P("ty", "tx"),
            P("ty", "tx"),
            P("ty", "tx"),
            P("ty", "tx"),
            P("tx"),
            P("tx", "ty"),
            P("ty"),
            P("ty", "tx"),
            P("ty", "tx"),
            P("tx", "ty"),
        ),
        out_specs=(
            P("tx", "dp", "ty"),
            P("tx", "dp", "ty"),
            P("ty"),
            P("ty", "tx"),
            P("ty", "tx"),
            P("ty", "tx"),
            P("ty", "tx"),
            P("ty", "tx"),
            P("tx"),
            P("tx", "ty"),
            P("ty"),
            P("ty", "tx"),
            P("ty", "tx"),
            P("tx", "ty"),
        ),
        check_vma=False,
    )
```

profile of v0, /device:TPU:9, one launch (start us, length us, event | category | flops | bytes accessed | tf_op | source)
XLA Modules:
  0.0 2873.9 jit_solution(10479496229082389157)
XLA Ops:
  12.2 9.2 all-gather.47.cloned.1.call-done
  27.2 6.9 psum.112
  36.0 46.6 %all-gather.19.cloned.1.call-done = bf16[4096,384]{1,0:T(8,128)(2,1)} async-done(((bf16[1024,384]{1,0:T(8,128)(2,1)}), bf16[4096,384]{1,0:T(8,128)(2,1)}) %all-gather.19.cloned.1.call-update) | async-done | bytes 3145744 | tf_op jit(solution)/shard_map/all_gather | solution.py:70
  122.1 94.5 %reduce-scatter.18.cloned.1.call-done = f32[1024,384]{1,0:T(8,128)} async-done(((f32[4096,384]{1,0:T(8,128)}), f32[1024,384]{1,0:T(8,128)}) %reduce-scatter.18.cloned.1.call-update) | async-done | bytes 1572880 | tf_op jit(solution)/shard_map/reduce_scatter | solution.py:74
  219.4 110.8 %reduce-scatter.14.cloned.1.call-done = f32[1024,384]{1,0:T(8,128)} async-done(((f32[4096,384]{1,0:T(8,128)}), f32[1024,384]{1,0:T(8,128)}) %reduce-scatter.14.cloned.1.call-update) | async-done | bytes 1572880 | tf_op jit(solution)/shard_map/reduce_scatter | solution.py:74
  333.8 110.0 %reduce-scatter.16.cloned.1.call-done = f32[1024,384]{1,0:T(8,128)} async-done(((f32[4096,384]{1,0:T(8,128)}), f32[1024,384]{1,0:T(8,128)}) %reduce-scatter.16.cloned.1.call-update) | async-done | bytes 1572880 | tf_op jit(solution)/shard_map/reduce_scatter | solution.py:74
  467.7 89.8 %reduce-scatter.22.cloned.1.call-done = f32[1024,384]{1,0:T(8,128)} async-done(((f32[4096,384]{1,0:T(8,128)}), f32[1024,384]{1,0:T(8,128)}) %reduce-scatter.22.cloned.1.call-update) | async-done | bytes 1572880 | tf_op jit(solution)/shard_map/reduce_scatter | solution.py:74
  561.4 60.5 %all-gather.21.cloned.1.call-done = bf16[4096,384]{1,0:T(8,128)(2,1)} async-done(((bf16[1024,384]{1,0:T(8,128)(2,1)}), bf16[4096,384]{1,0:T(8,128)(2,1)}) %all-gather.21.cloned.1.call-update) | async-done | bytes 3145744 | tf_op jit(solution)/shard_map/all_gather | solution.py:80
  621.9 6.6 fusion.60
  641.8 67.2 %reduce-scatter.24.cloned.1.call-done = f32[1024,384]{1,0:T(8,128)} async-done(((f32[4096,384]{1,0:T(8,128)}), f32[1024,384]{1,0:T(8,128)}) %reduce-scatter.24.cloned.1.call-update) | async-done | bytes 1572880 | tf_op jit(solution)/shard_map/reduce_scatter | solution.py:86
  710.9 7.1 psum.113
  719.2 36.4 %all-gather.29.cloned.1.call-done = bf16[4096,384]{1,0:T(8,128)(2,1)} async-done(((bf16[1024,384]{1,0:T(8,128)(2,1)}), bf16[4096,384]{1,0:T(8,128)(2,1)}) %all-gather.29.cloned.1.call-update) | async-done | bytes 3145744 | tf_op jit(solution)/shard_map/all_gather | solution.py:70
  755.6 13.0 fusion.64
  768.6 33.4 %all-gather.23.cloned.1.call-done = bf16[4096,384]{1,0:T(8,128)(2,1)} async-done(((bf16[1024,384]{1,0:T(8,128)(2,1)}), bf16[4096,384]{1,0:T(8,128)(2,1)}) %all-gather.23.cloned.1.call-update) | async-done | bytes 3145744 | tf_op jit(solution)/shard_map/all_gather | solution.py:70
  802.0 10.3 fusion.62
  812.6 10.1 fusion.61
  822.7 259.0 %reduce-scatter.32.cloned.1.call-done = f32[1024,1024]{1,0:T(8,128)} async-done(((f32[4096,1024]{1,0:T(8,128)}), f32[1024,1024]{1,0:T(8,128)}) %reduce-scatter.32.cloned.1.call-update) | async-done | bytes 4194320 | tf_op jit(solution)/shard_map/reduce_scatter | solution.py:74
  1081.8 283.3 %reduce-scatter.28.cloned.1.call-done = f32[1024,1024]{1,0:T(8,128)} async-done(((f32[4096,1024]{1,0:T(8,128)}), f32[1024,1024]{1,0:T(8,128)}) %reduce-scatter.28.cloned.1.call-update) | async-done | bytes 4194320 | tf_op jit(solution)/shard_map/reduce_scatter | solution.py:74
  1365.0 283.4 %reduce-scatter.26.cloned.1.call-done = f32[1024,1024]{1,0:T(8,128)} async-done(((f32[4096,1024]{1,0:T(8,128)}), f32[1024,1024]{1,0:T(8,128)}) %reduce-scatter.26.cloned.1.call-update) | async-done | bytes 4194320 | tf_op jit(solution)/shard_map/reduce_scatter | solution.py:74
  1648.4 8.4 multiply_convert_fusion.2
  1657.5 150.1 %all-gather.31.cloned.1.call-done = bf16[4096,1024]{1,0:T(8,128)(2,1)} async-done(((bf16[1024,1024]{1,0:T(8,128)(2,1)}), bf16[4096,1024]{1,0:T(8,128)(2,1)}) %all-gather.31.cloned.1.call-update) | async-done | bytes 8388624 | tf_op jit(solution)/shard_map/all_gather | solution.py:80
  1807.6 9.6 fusion.65
  1817.2 139.7 %all-gather.33.cloned.1.call-done = bf16[4096,1024]{1,0:T(8,128)(2,1)} async-done(((bf16[1024,1024]{1,0:T(8,128)(2,1)}), bf16[4096,1024]{1,0:T(8,128)(2,1)}) %all-gather.33.cloned.1.call-update) | async-done | bytes 8388624 | tf_op jit(solution)/shard_map/all_gather | solution.py:80
  1956.9 12.4 convolution_add_fusion
  1969.6 71.2 %reduce-scatter.34.cloned.1.call-done = f32[1024,384]{1,0:T(8,128)} async-done(((f32[4096,384]{1,0:T(8,128)}), f32[1024,384]{1,0:T(8,128)}) %reduce-scatter.34.cloned.1.call-update) | async-done | bytes 1572880 | tf_op jit(solution)/shard_map/reduce_scatter | solution.py:86
  2043.3 7.1 psum.114
  2053.3 46.0 %all-gather.35.cloned.1.call-done = bf16[4096,384]{1,0:T(8,128)(2,1)} async-done(((bf16[1024,384]{1,0:T(8,128)(2,1)}), bf16[4096,384]{1,0:T(8,128)(2,1)}) %all-gather.35.cloned.1.call-update) | async-done | bytes 3145744 | tf_op jit(solution)/shard_map/all_gather | solution.py:70
  2099.3 6.6 fusion.66
  2107.3 109.6 %reduce-scatter.36.cloned.1.call-done = f32[1024,384]{1,0:T(8,128)} async-done(((f32[4096,384]{1,0:T(8,128)}), f32[1024,384]{1,0:T(8,128)}) %reduce-scatter.36.cloned.1.call-update) | async-done | bytes 1572880 | tf_op jit(solution)/shard_map/reduce_scatter | solution.py:74
  2227.9 6.8 fusion.26
  2254.2 8.0 convert_reduce_fusion
  2278.1 10.8 all_gather.66
  2288.8 8.6 all-gather.41.cloned.1.call-done
  2297.4 6.7 fusion.69
  2304.1 57.6 %all-gather.43.cloned.1.call-done = bf16[4096,384]{1,0:T(8,128)(2,1)} async-done(((bf16[1024,384]{1,0:T(8,128)(2,1)}), bf16[4096,384]{1,0:T(8,128)(2,1)}) %all-gather.43.cloned.1.call-update) | async-done | bytes 3145744 | tf_op jit(solution)/shard_map/all_gather | solution.py:80
  2368.3 57.7 %all-gather.39.cloned.1.call-done = bf16[4096,384]{0,1:T(8,128)(2,1)} async-done(((bf16[1024,384]{0,1:T(8,128)(2,1)}), bf16[4096,384]{0,1:T(8,128)(2,1)}) %all-gather.39.cloned.1.call-update) | async-done | bytes 3145744 | tf_op jit(solution)/shard_map/all_gather | solution.py:80
  2426.1 6.7 fusion.68
  2432.8 57.4 %all-gather.37.cloned.1.call-done = bf16[4096,384]{0,1:T(8,128)(2,1)} async-done(((bf16[1024,384]{0,1:T(8,128)(2,1)}), bf16[4096,384]{0,1:T(8,128)(2,1)}) %all-gather.37.cloned.1.call-update) | async-done | bytes 3145744 | tf_op jit(solution)/shard_map/all_gather | solution.py:80
  2494.5 9.2 add_add_fusion
  2503.9 135.9 %all-gather.25.cloned.1.call-done = bf16[4096,1024]{1,0:T(8,128)(2,1)} async-done(((bf16[1024,1024]{1,0:T(8,128)(2,1)}), bf16[4096,1024]{1,0:T(8,128)(2,1)}) %all-gather.25.cloned.1.call-update) | async-done | bytes 8388624 | tf_op jit(solution)/shard_map/all_gather | solution.py:80
  2639.8 9.5 fusion.63
  2649.4 10.1 fusion.77
  2659.6 8.1 fusion.79
  2667.7 46.2 %reduce-scatter.38.cloned.1.call-done = f32[1024,384]{1,0:T(8,128)} async-done(((f32[4096,384]{1,0:T(8,128)}), f32[1024,384]{1,0:T(8,128)}) %reduce-scatter.38.cloned.1.call-update) | async-done | bytes 1572880 | tf_op jit(solution)/shard_map/reduce_scatter | solution.py:86
  2716.0 7.1 psum.115
  2723.1 63.9 %reduce-scatter.30.cloned.1.call-done = f32[1024,384]{1,0:T(8,128)} async-done(((f32[4096,384]{1,0:T(8,128)}), f32[1024,384]{1,0:T(8,128)}) %reduce-scatter.30.cloned.1.call-update) | async-done | bytes 1572880 | tf_op jit(solution)/shard_map/reduce_scatter | solution.py:86
  2790.9 9.0 fusion.78
  2824.1 14.9 all-reduce.3
  (358 shorter events, 224.8 us)
Async XLA Ops:
  7.2 805.4 %copy-start = (bf16[384,1024]{1,0:T(8,128)(2,1)S(1)}, bf16[384,1024]{1,0:T(8,128)(2,1)}, u32[]{:S(2)}) copy-start(bf16[384,1024]{1,0:T(8,128)(2,1)} %param.51) | copy-start | bytes 2359300
  7.2 14.1 all-gather.47.cloned.1.call-start
  7.9 74.6 %all-gather.19.cloned.1.call-start = ((), (), s32[]{:S(2)}) async-start(), calls=%async_computation.13 | async-start | bytes 3932160 | tf_op jit(solution)/shard_map/all_gather | solution.py:70
  12.1 2038.3 %copy-start.62 = (pred[1024]{0:T(1024)(128)(4,1)}, pred[1024]{0:T(1024)(128)(4,1)S(1)}, u32[]{:S(2)}) copy-start(pred[1024]{0:T(1024)(128)(4,1)S(1)} %compare_and_fusion) | copy-start | bytes 3076
  26.7 682.3 %copy-start.7 = (bf16[1024,384]{1,0:T(8,128)(2,1)}, bf16[1024,384]{1,0:T(8,128)(2,1)S(1)}, u32[]{:S(2)}) copy-start(bf16[1024,384]{1,0:T(8,128)(2,1)S(1)} %gather_fusion) | copy-start | bytes 2359300
  26.7 55.8 %copy-start.71 = (bf16[384,6]{0,1:T(8,128)(2,1)S(1)}, bf16[384,6]{0,1:T(8,128)(2,1)}, u32[]{:S(2)}) copy-start(bf16[384,6]{0,1:T(8,128)(2,1)} %param.47) | copy-start | bytes 13828
  35.9 82.0 %reduce-scatter.20.cloned.1.call-start = ((), (), s32[]{:S(2)}) async-start(), calls=%async_computation.17 | async-start | bytes 163840 | tf_op jit(solution)/shard_map/reduce_scatter | solution.py:74
  86.1 130.6 %reduce-scatter.18.cloned.1.call-start = ((), (), s32[]{:S(2)}) async-start(), calls=%async_computation.16 | async-start | bytes 7864320 | tf_op jit(solution)/shard_map/reduce_scatter | solution.py:74
  92.7 237.5 %reduce-scatter.14.cloned.1.call-start = ((), (), s32[]{:S(2)}) async-start(), calls=%async_computation.14 | async-start | bytes 7864320 | tf_op jit(solution)/shard_map/reduce_scatter | solution.py:74
  100.2 343.6 %reduce-scatter.16.cloned.1.call-start = ((), (), s32[]{:S(2)}) async-start(), calls=%async_computation.15 | async-start | bytes 7864320 | tf_op jit(solution)/shard_map/reduce_scatter | solution.py:74
  107.8 449.8 %reduce-scatter.22.cloned.1.call-start = ((), (), s32[]{:S(2)}) async-start(), calls=%async_computation.18 | async-start | bytes 7864320 | tf_op jit(solution)/shard_map/reduce_scatter | solution.py:74
  115.3 506.6 %all-gather.21.cloned.1.call-start = ((), (), s32[]{:S(2)}) async-start(), calls=%async_computation.19 | async-start | bytes 3932160 | tf_op jit(solution)/shard_map/all_gather | solution.py:80
  332.8 127.5 %copy-start.19 = (bf16[1024,384]{0,1:T(8,128)(2,1)}, bf16[1024,384]{0,1:T(8,128)(2,1)S(1)}, u32[]{:S(2)}) copy-start(bf16[1024,384]{0,1:T(8,128)(2,1)S(1)} %copy.70) | copy-start | bytes 2359300
  467.7 160.9 %copy-start.10 = (f32[1024,384]{1,0:T(8,128)}, f32[1024,384]{1,0:T(8,128)S(1)}, u32[]{:S(2)}) copy-start(f32[1024,384]{1,0:T(8,128)S(1)} %copy.73) | copy-start | bytes 4718596
  560.2 75.0 %all-gather.49.cloned.1.call-start = ((), (), s32[]{:S(2)}) async-start(), calls=%async_computation.41 | async-start | bytes 2359296 | tf_op jit(solution)/shard_map/all_gather | solution.py:239
  561.0 148.0 %reduce-scatter.24.cloned.1.call-start = ((), (), s32[]{:S(2)}) async-start(), calls=%async_computation.20 | async-start | bytes 7864320 | tf_op jit(solution)/shard_map/reduce_scatter | solution.py:86
  628.6 127.0 %all-gather.29.cloned.1.call-start = ((), (), s32[]{:S(2)}) async-start(), calls=%async_computation.27 | async-start | bytes 3932160 | tf_op jit(solution)/shard_map/all_gather | solution.py:70
  640.6 77.4 %copy-start.69 = (f32[384]{0:T(512)S(1)}, f32[384]{0:T(512)}, u32[]{:S(2)}) copy-start(f32[384]{0:T(512)} %param.50) | copy-start | bytes 4612
  641.8 160.2 %all-gather.23.cloned.1.call-start = ((), (), s32[]{:S(2)}) async-start(), calls=%async_computation.21 | async-start | bytes 3932160 | tf_op jit(solution)/shard_map/all_gather | solution.py:70
  718.0 1332.5 %copy-start.49 = (f32[1024]{0:T(1024)}, f32[1024]{0:T(1024)S(1)}, u32[]{:S(2)}) copy-start(f32[1024]{0:T(1024)S(1)} %add_rsqrt_fusion) | copy-start | bytes 12292
  719.1 362.7 %reduce-scatter.32.cloned.1.call-start = ((), (), s32[]{:S(2)}) async-start(), calls=%async_computation.28 | async-start | bytes 20971520 | tf_op jit(solution)/shard_map/reduce_scatter | solution.py:74
  768.6 596.5 %reduce-scatter.28.cloned.1.call-start = ((), (), s32[]{:S(2)}) async-start(), calls=%async_computation.23 | async-start | bytes 20971520 | tf_op jit(solution)/shard_map/reduce_scatter | solution.py:74
  812.3 836.1 %reduce-scatter.26.cloned.1.call-start = ((), (), s32[]{:S(2)}) async-start(), calls=%async_computation.22 | async-start | bytes 20971520 | tf_op jit(solution)/shard_map/reduce_scatter | solution.py:74
  822.7 984.9 %all-gather.31.cloned.1.call-start = ((), (), s32[]{:S(2)}) async-start(), calls=%async_computation.29 | async-start | bytes 10485760 | tf_op jit(solution)/shard_map/all_gather | solution.py:80
  1656.9 300.0 %all-gather.33.cloned.1.call-start = ((), (), s32[]{:S(2)}) async-start(), calls=%async_computation.30 | async-start | bytes 10485760 | tf_op jit(solution)/shard_map/all_gather | solution.py:80
  1657.5 383.3 %reduce-scatter.34.cloned.1.call-start = ((), (), s32[]{:S(2)}) async-start(), calls=%async_computation.31 | async-start | bytes 7864320 | tf_op jit(solution)/shard_map/reduce_scatter | solution.py:86
  1969.3 81.1 %copy-start.12 = (bf16[1024,384]{1,0:T(8,128)(2,1)S(1)}, bf16[1024,384]{1,0:T(8,128)(2,1)}, u32[]{:S(2)}) copy-start(bf16[1024,384]{1,0:T(8,128)(2,1)} %copy-done.11) | copy-start | bytes 2359300
  1969.4 129.9 %all-gather.35.cloned.1.call-start = ((), (), s32[]{:S(2)}) async-start(), calls=%async_computation.32 | async-start | bytes 3932160 | tf_op jit(solution)/shard_map/all_gather | solution.py:70
  2043.3 56.0 %copy-start.29 = (bf16[384,384]{1,0:T(8,128)(2,1)S(1)}, bf16[384,384]{1,0:T(8,128)(2,1)}, u32[]{:S(2)}) copy-start(bf16[384,384]{1,0:T(8,128)(2,1)} %param.49) | copy-start | bytes 884740
  2053.3 163.6 %reduce-scatter.36.cloned.1.call-start = ((), (), s32[]{:S(2)}) async-start(), calls=%async_computation.33 | async-start | bytes 7864320 | tf_op jit(solution)/shard_map/reduce_scatter | solution.py:74
  2106.0 191.5 %all-gather.41.cloned.1.call-start = ((), (), s32[]{:S(2)}) async-start(), calls=%async_computation.36 | async-start | bytes 3932160 | tf_op jit(solution)/shard_map/all_gather | solution.py:80
  2234.8 127.0 %all-gather.43.cloned.1.call-start = ((), (), s32[]{:S(2)}) async-start(), calls=%async_computation.37 | async-start | bytes 3932160 | tf_op jit(solution)/shard_map/all_gather | solution.py:80
  2235.5 190.6 %all-gather.39.cloned.1.call-start = ((), (), s32[]{:S(2)}) async-start(), calls=%async_computation.35 | async-start | bytes 3932160 | tf_op jit(solution)/shard_map/all_gather | solution.py:80
  2265.1 225.1 %all-gather.37.cloned.1.call-start = ((), (), s32[]{:S(2)}) async-start(), calls=%async_computation.34 | async-start | bytes 3932160 | tf_op jit(solution)/shard_map/all_gather | solution.py:80
  2273.8 366.0 %all-gather.25.cloned.1.call-start = ((), (), s32[]{:S(2)}) async-start(), calls=%async_computation.24 | async-start | bytes 10485760 | tf_op jit(solution)/shard_map/all_gather | solution.py:80
  2274.5 439.4 %reduce-scatter.38.cloned.1.call-start = ((), (), s32[]{:S(2)}) async-start(), calls=%async_computation.38 | async-start | bytes 7864320 | tf_op jit(solution)/shard_map/reduce_scatter | solution.py:86
  2288.8 72.9 %copy-start.33 = (bf16[384,384]{1,0:T(8,128)(2,1)S(1)}, bf16[384,384]{1,0:T(8,128)(2,1)}, u32[]{:S(2)}) copy-start(bf16[384,384]{1,0:T(8,128)(2,1)} %param.46) | copy-start | bytes 884740
  2304.1 122.0 %copy-start.35 = (bf16[384,384]{1,0:T(8,128)(2,1)S(1)}, bf16[384,384]{1,0:T(8,128)(2,1)}, u32[]{:S(2)}) copy-start(bf16[384,384]{1,0:T(8,128)(2,1)} %param.44) | copy-start | bytes 884740
  2368.3 121.9 %copy-start.37 = (bf16[384,384]{1,0:T(8,128)(2,1)S(1)}, bf16[384,384]{1,0:T(8,128)(2,1)}, u32[]{:S(2)}) copy-start(bf16[384,384]{1,0:T(8,128)(2,1)} %param.43) | copy-start | bytes 884740
  2432.8 61.6 %copy-start.72 = (bf16[384,6]{0,1:T(8,128)(2,1)S(1)}, bf16[384,6]{0,1:T(8,128)(2,1)}, u32[]{:S(2)}) copy-start(bf16[384,6]{0,1:T(8,128)(2,1)} %param.47) | copy-start | bytes 13828
  2503.6 136.1 %copy-start.38 = (bf16[1024,384]{1,0:T(8,128)(2,1)S(1)}, bf16[1024,384]{1,0:T(8,128)(2,1)}, u32[]{:S(2)}) copy-start(bf16[1024,384]{1,0:T(8,128)(2,1)} %param.53) | copy-start | bytes 2359300
  2503.7 283.3 %reduce-scatter.30.cloned.1.call-start = ((), (), s32[]{:S(2)}) async-start(), calls=%async_computation.25 | async-start | bytes 7864320 | tf_op jit(solution)/shard_map/reduce_scatter | solution.py:86
  2649.3 189.7 %all-gather.45.cloned.1.call-start = ((), (), s32[]{:S(2)}) async-start(), calls=%async_computation.39 | async-start | bytes 2359296 | tf_op jit(solution)/shard_map/all_gather | solution.py:248
  2659.5 127.5 %copy-start.50 = (f32[1024]{0:T(1024)S(1)}, f32[1024]{0:T(1024)}, u32[]{:S(2)}) copy-start(f32[1024]{0:T(1024)} %copy-done.49) | copy-start | bytes 12292
  2659.5 127.5 %copy-start.66 = (f32[1024]{0:T(1024)S(1)}, f32[1024]{0:T(1024)}, u32[]{:S(2)}) copy-start(f32[1024]{0:T(1024)} %copy-done.65) | copy-start | bytes 12292
  2659.5 127.4 %copy-start.70 = (f32[384]{0:T(512)S(1)}, f32[384]{0:T(512)}, u32[]{:S(2)}) copy-start(f32[384]{0:T(512)} %param.50) | copy-start | bytes 4612
  2790.8 53.7 %all-gather.27.cloned.1.call-start = ((), (), s32[]{:S(2)}) async-start(), calls=%async_computation.26 | async-start | bytes 2359296 | tf_op jit(solution)/shard_map/all_gather | solution.py:248
  2802.6 52.9 %all-reduce.8.cloned.1.call-start = ((), (), s32[]{:S(2)}) async-start(), calls=%async_computation.42 | async-start | bytes 15335424 | tf_op jit(solution)/shard_map/psum | solution.py:338
  (64 other events, 627.9 us)
Sparse Core Ops, SparseCore 0:
  9.6 11.6 all-gather.46
  36.1 46.4 all-gather.18
  86.2 14.6 reduce-scatter.19
  103.1 113.5 reduce-scatter.17
  218.9 111.2 reduce-scatter.13
  332.5 111.2 reduce-scatter.15
  446.2 111.2 reduce-scatter.21
  560.4 61.5 all-gather.20
  623.5 11.6 all-gather.48
  638.3 70.6 reduce-scatter.23
  711.6 43.9 all-gather.28
  758.0 43.9 all-gather.22
  804.5 277.2 reduce-scatter.31
  1084.0 281.0 reduce-scatter.27
  1367.4 281.0 reduce-scatter.25
  1657.0 150.5 all-gather.30
  1809.0 147.8 all-gather.32
  1969.5 71.2 reduce-scatter.33
  2053.4 45.8 all-gather.34
  2106.1 110.7 reduce-scatter.35
  2234.9 62.4 all-gather.40
  2299.6 62.1 all-gather.42
  2363.9 62.1 all-gather.38
  2428.1 62.1 all-gather.36
  2491.8 147.8 all-gather.24
  2642.6 71.2 reduce-scatter.37
  2716.8 70.1 reduce-scatter.29
  2790.9 10.5 all-gather.44
  2803.6 10.9 all-gather.26
  2819.0 36.4 all-reduce.7
where the time goes:
time: 2880 us; the launch traced here: 2870 us
  waiting for transfers between devices  2440 us (85%)
  matrix products  232 us (8%)
  other arithmetic  67 us (2%)
  blocking collectives  58.2 us (2%)
  local copies, waits for them, and re-layouts  55.8 us (2%)
    reduce_scatter x9, waiting for transfers between devices, parts_ty(): return lax.psum_scatter(values, 'ty', scatter_dimension=0, tiled=True)  1340 us
    all_gather x8, waiting for transfers between devices, rows_ty(): lax.all_gather(as_sent(values), 'ty', axis=0, tiled=True)  668 us
    reduce_scatter x4, waiting for transfers between devices, parts_tx(): return lax.psum_scatter(values, 'tx', scatter_dimension=0, tiled=True)  249 us
    all_gather x4, waiting for transfers between devices, rows_tx(): return lax.all_gather(values, 'tx', axis=0, tiled=True)  162 us
    dot_general x9, matrix products, cols_product(): lax.dot_general(left, right, (((1,), (1,)), ((), ())), preferred_element_...  74.9 us
    dot_general x9, matrix products, product(): return jnp.dot(left, right, preferred_element_type=jnp.float32)  66.3 us
  transfers between devices with their start and end apart: 30, of which 27 were waited for; matrix products, arithmetic and copies ran while one was open for 9% of the time, Pallas kernels for 0%

commit v1 on v0

v1 whole, which is shorter than its diff:
```python
import jax
import jax.numpy as jnp
from jax import lax
from jax.experimental import pallas as pl
from jax.experimental.pallas import tpu as pltpu
from jax.sharding import PartitionSpec as P

EPSILON = 1e-06
FAR = 1e30
LANES = 128
BF = jnp.bfloat16
F32 = jnp.float32


def dot(left, right, dims=((1,), (0,))):
    return lax.dot_general(left, right, (dims, ((), ())), preferred_element_type=F32)


NT = ((1,), (1,))
TN = ((0,), (0,))


def three_parts(values):
    one = lax.reduce_precision(values, 8, 7)
    two = lax.reduce_precision(values - one, 8, 7)
    three = lax.reduce_precision(values - one - two, 8, 7)
    return one, two, three


def pick_small(lookup, indices):
    width = lookup.shape[0]
    matches = indices[:, None] == jnp.arange(width, dtype=jnp.int32)[None, :]
    return jnp.sum(jnp.where(matches, lookup[None, :], 0), axis=1)


def stream_tables(lengths, dealing):
    width = lengths.shape[0]
    numbers = jnp.arange(width, dtype=jnp.int32)
    given_start = jnp.cumsum(lengths) - lengths
    owners = jnp.sum(jnp.where(dealing[None, :] == numbers[:, None], numbers[None, :], 0), axis=1)
    dealt_length = pick_small(lengths, owners)
    dealt_start = jnp.cumsum(dealt_length) - dealt_length
    return (given_start, owners, dealt_start, dealt_length)


def dealt_sources(lengths, dealing, places):
    given_start, owners, dealt_start, unused = stream_tables(lengths, dealing)
    slot_ids = jnp.sum((dealt_start[None, :] <= places[:, None]).astype(jnp.int32), axis=1) - 1
    return (
        pick_small(given_start, pick_small(owners, slot_ids))
        + places
        - pick_small(dealt_start, slot_ids)
    )


def given_targets(lengths, dealing, places):
    given_start, unused, dealt_start, unused = stream_tables(lengths, dealing)
    member = jnp.sum((given_start[None, :] <= places[:, None]).astype(jnp.int32), axis=1) - 1
    return (
        pick_small(dealt_start, pick_small(dealing, member))
        + places
        - pick_small(given_start, member)
    )


def swap(values, axis, step):
    return lax.ppermute(values, axis, [(at, at ^ step) for at in range(lax.axis_size(axis))])


def spread_plane(pieces):
    return [pieces[0]] + [swap(pieces[k], "tx", k) for k in (1, 2, 3)]


def spread_line(pieces):
    return [pieces[0]] + [swap(pieces[k], "ty", k) for k in (1, 2, 3)]


def mixed(pieces, start):
    stacked = jnp.stack(pieces)
    return [lax.dynamic_index_in_dim(stacked, start ^ k, 0, keepdims=False) for k in range(4)]


def to_plane(pieces, column, lane):
    pieces = spread_plane(pieces)
    pieces = spread_line(mixed(pieces, column ^ lane))
    return jnp.concatenate(mixed(pieces, lane), axis=1)


def from_plane(rows, column, lane):
    width = rows.shape[1] // 4
    pieces = [
        lax.dynamic_slice_in_dim(rows, (lane ^ k) * width, width, axis=1) for k in range(4)
    ]
    pieces = spread_line(pieces)
    return jnp.concatenate(spread_plane(mixed(pieces, column ^ lane)), axis=0)


def gather_rows(rows):
    half = rows.shape[0] // 2
    top, low = rows[:half], rows[half:]
    top_x, low_y = swap(top, "tx", 1), swap(low, "tx", 2)
    low_x, top_y = swap(low, "tx", 1), swap(top, "tx", 2)
    top_d, low_d = swap(top_x, "tx", 2), swap(low_y, "tx", 1)
    return jnp.concatenate([top, low, top_x, low_x, top_y, low_y, top_d, low_d], axis=0)


def scatter_product(rows, weights):
    piece = rows.shape[0] // 4
    half = weights.shape[0] // 2

    def part(k, w):
        return dot(rows[k * piece : (k + 1) * piece], w, NT)

    wa, wb = weights[:half], weights[half:]
    a3 = swap(part(3, wa).astype(BF), "tx", 1)
    b3 = swap(part(3, wb).astype(BF), "tx", 2)
    a1 = swap(part(1, wa).astype(BF), "tx", 1)
    b2 = swap(part(2, wb).astype(BF), "tx", 2)
    a2 = swap((part(2, wa) + a3.astype(F32)).astype(BF), "tx", 2)
    b1 = swap((part(1, wb) + b3.astype(F32)).astype(BF), "tx", 1)
    a0 = part(0, wa) + a1.astype(F32) + a2.astype(F32)
    b0 = part(0, wb) + b2.astype(F32) + b1.astype(F32)
    return jnp.concatenate([a0, b0], axis=1)


def pair_rows(piece):
    if lax.axis_size("dp") != 2:
        return lax.all_gather(piece, "dp", axis=0, tiled=True)
    other = swap(piece, "dp", 1)
    mine = lax.axis_index("dp") == 0
    return jnp.concatenate([jnp.where(mine, piece, other), jnp.where(mine, other, piece)], axis=0)


def pick_kernel(index_ref, *refs):
    count = len(refs) // 3
    row_total = refs[0].shape[0]
    places = lax.broadcasted_iota(jnp.int32, (index_ref.shape[0], 2 * row_total), 1)
    chosen = jnp.where(places == index_ref[...], 1.0, 0.0).astype(BF)
    for at in range(count):
        own, other, out = refs[2 * at], refs[2 * at + 1], refs[2 * count + at]
        picked = dot(chosen[:, :row_total], own[...]) + dot(chosen[:, row_total:], other[...])
        out[...] = picked.astype(BF)


def pick_rows(indices, pairs):
    row_total, width = pairs[0][0].shape
    block = row_total // 4
    whole = pl.BlockSpec((row_total, width), lambda i: (0, 0))
    return pl.pallas_call(
        pick_kernel,
        grid=(4,),
        in_specs=[pl.BlockSpec((block, 1), lambda i: (i, 0))] + [whole] * (2 * len(pairs)),
        out_specs=[pl.BlockSpec((block, width), lambda i: (i, 0))] * len(pairs),
        out_shape=[jax.ShapeDtypeStruct((row_total, width), BF)] * len(pairs),
        compiler_params=pltpu.CompilerParams(vmem_limit_bytes=32 * 2**20),
        cost_estimate=pl.CostEstimate(
            flops=4 * row_total * row_total * width * len(pairs),
            bytes_accessed=6 * row_total * width * len(pairs),
            transcendentals=0,
        ),
    )(indices[:, None], *[half for pair in pairs for half in pair])


def moved_rows(indices, arrays, first_place):
    row_total = arrays[0].shape[0]
    if lax.axis_size("dp") != 2:
        return [jnp.take(lax.all_gather(a, "dp", axis=0, tiled=True), indices, axis=0) for a in arrays]
    span = 2 * row_total
    near = lax.rem(indices - first_place + span, span)
    return pick_rows(near, [(a, swap(a, "dp", 1)) for a in arrays])


def lanes_of(rows):
    return lax.broadcasted_iota(jnp.int32, (rows, LANES), 1)


def split_column(column):
    one = column.astype(BF).astype(F32)
    two = (column - one).astype(BF).astype(F32)
    return one, two, column - one - two


def fill(lanes, base, columns, rest):
    for at, column in reversed(list(enumerate(columns))):
        rest = jnp.where(lanes == base + at, column, rest)
    return rest


def forward_kernel(
    meta, q_ref, k_ref, v_ref, gate_ref, keep_ref, y_ref, att_ref, qa_ref, ka_ref, c_ref, va_ref
):
    pair = pl.program_id(0)
    column, first_length = meta[0], meta[1]
    row_total = q_ref.shape[0]
    block = row_total // 4
    lanes = lanes_of(block)

    def rows_of(at):
        return pl.ds(pl.multiple_of((column ^ at) * block, block), block)

    @pl.when(pair == 0)
    def sum_keeps():
        below = lax.broadcasted_iota(jnp.int32, (block, block), 0)
        across = lax.broadcasted_iota(jnp.int32, (block, block), 1)
        ones = jnp.where(below >= across, 1.0, 0.0)
        running = jnp.zeros((1, LANES), F32)
        for at in range(4):
            sums = running + lax.dot_general(
                ones,
                keep_ref[rows_of(at), :],
                (((1,), (0,)), ((), ())),
                precision=lax.Precision.HIGHEST,
                preferred_element_type=F32,
            )
            c_ref[pl.ds(at * block, block), :] = sums
            running = sums[block - 1 :, :]

    for head in range(2):
        mine = (lanes < 64) if head == 0 else (lanes >= 64)
        base = 64 if head == 0 else 0
        for at in range(4):
            rows, own = rows_of(at), pl.ds(at * block, block)
            decay = jnp.sum(
                jnp.where(lanes == 2 * pair + head, c_ref[own, :], 0.0), axis=1, keepdims=True
            )
            one, two, three = split_column(decay)
            places = at * block + lax.broadcasted_iota(jnp.int32, (block, 1), 0)
            second = jnp.where(places >= first_length, 1.0, 0.0)
            q_side = fill(lanes, base, (1.0, 1.0, 1.0, second), 0.0)
            k_side = fill(
                lanes, base, (-one, -two, -three, (second - 1.0) * FAR, 1.0, 1.0, 1.0), 0.0
            )
            qa_ref[head, own, :] = jnp.where(
                mine, q_ref[rows, :].astype(F32) * 0.125, q_side
            ).astype(BF)
            ka_ref[head, own, :] = jnp.where(mine, k_ref[rows, :].astype(F32), k_side).astype(BF)
            va_ref[head, own, :] = jnp.where(mine, v_ref[rows, :].astype(F32), 1.0).astype(BF)

    below = lax.broadcasted_iota(jnp.int32, (block, block), 0)
    across = lax.broadcasted_iota(jnp.int32, (block, block), 1)
    for at in range(4):
        own = pl.ds(at * block, block)
        width = (at + 1) * block
        results = []
        for head in range(2):
            base = 64 if head == 0 else 0
            queries = qa_ref[head, own, :]
            last = jnp.where(
                below >= across, dot(queries, ka_ref[head, at * block : width, :], NT), -FAR
            )
            top = jnp.max(last, axis=1, keepdims=True)
            if at > 0:
                early = dot(queries, ka_ref[head, : at * block, :], NT)
                top = jnp.maximum(top, jnp.max(early, axis=1, keepdims=True))
            total = dot(jnp.exp(last - top).astype(BF), va_ref[head, at * block : width, :])
            if at > 0:
                total += dot(jnp.exp(early - top).astype(BF), va_ref[head, : at * block, :])
            weight = pltpu.roll(total, 64, 1)
            results.append(total / weight)
            log_total = top + jnp.log(total[:, base : base + 1])
            one, two, three = split_column(log_total)
            qa_ref[head, own, :] = fill(
                lanes, base + 4, (-one, -two, -three), queries.astype(F32)
            ).astype(BF)
        attended = jnp.where(lanes < 64, results[0], results[1])
        rows = rows_of(at)
        att_ref[rows, :] = attended
        y_ref[rows, :] = (attended * gate_ref[rows, :]).astype(BF)


def attend_forward(meta, qkv, out_gate, keep):
    row_total, width = out_gate.shape
    pairs = width // LANES
    heads = 2 * pairs

    def columns(first):
        return pl.BlockSpec((row_total, LANES), lambda p, m: (0, first + p))

    sided = pl.BlockSpec((2, row_total, LANES), lambda p, m: (p, 0, 0))
    return pl.pallas_call(
        forward_kernel,
        grid_spec=pltpu.PrefetchScalarGridSpec(
            num_scalar_prefetch=1,
            grid=(pairs,),
            in_specs=[
                columns(0),
                columns(pairs),
                columns(2 * pairs),
                columns(0),
                pl.BlockSpec((row_total, LANES), lambda p, m: (0, 0)),
            ],
            out_specs=[columns(0), columns(0), sided, sided],
            scratch_shapes=[
                pltpu.VMEM((row_total, LANES), F32),
                pltpu.VMEM((2, row_total, LANES), BF),
            ],
        ),
        out_shape=[
            jax.ShapeDtypeStruct((row_total, width), BF),
            jax.ShapeDtypeStruct((row_total, width), F32),
            jax.ShapeDtypeStruct((heads, row_total, LANES), BF),
            jax.ShapeDtypeStruct((heads, row_total, LANES), BF),
        ],
        compiler_params=pltpu.CompilerParams(vmem_limit_bytes=48 * 2**20),
        cost_estimate=pl.CostEstimate(
            flops=heads * row_total * row_total * 256,
            bytes_accessed=row_total * width * 16,
            transcendentals=heads * row_total * row_total // 2,
        ),
    )(meta, qkv, qkv, qkv, out_gate, keep)


def backward_kernel(
    meta,
    qa_ref,
    ka_ref,
    v_ref,
    dy_ref,
    gate_ref,
    att_ref,
    slope_ref,
    out_ref,
    va_ref,
    da_ref,
    kt_ref,
    dk_ref,
    dv_ref,
    dq_ref,
    dc_ref,
):
    pair = pl.program_id(0)
    pairs = pl.num_programs(0)
    column = meta[0]
    row_total = v_ref.shape[0]
    block = row_total // 4
    lanes = lanes_of(block)
    width = gate_ref.shape[1] * pairs

    def rows_of(at):
        return pl.ds(pl.multiple_of((column ^ at) * block, block), block)

    def lanes_at(group):
        return pl.ds(pl.multiple_of((group * pairs + pair) * LANES, LANES), LANES)

    @pl.when(pair == 0)
    def clear():
        dc_ref[...] = jnp.zeros_like(dc_ref)

    for at in range(4):
        rows, own = rows_of(at), pl.ds(at * block, block)
        gate, grad_y, attended = gate_ref[rows, :], dy_ref[rows, :], att_ref[rows, :]
        grad_att = (grad_y * gate).astype(BF).astype(F32)
        out_ref[rows, lanes_at(3)] = (grad_y * attended * gate * (1.0 - gate)).astype(BF)
        inner = grad_att * attended
        values = v_ref[rows, :].astype(F32)
        for head in range(2):
            mine = (lanes < 64) if head == 0 else (lanes >= 64)
            base = 64 if head == 0 else 0
            delta = jnp.sum(jnp.where(mine, inner, 0.0), axis=1, keepdims=True)
            one, two, three = split_column(delta)
            da_ref[head, own, :] = jnp.where(
                mine, grad_att, fill(lanes, base, (-one, -two, -three), 0.0)
            ).astype(BF)
            va_ref[head, own, :] = jnp.where(
                mine, values, fill(lanes, base, (1.0, 1.0, 1.0), 0.0)
            ).astype(BF)

    below = lax.broadcasted_iota(jnp.int32, (block, block), 0)
    across = lax.broadcasted_iota(jnp.int32, (block, block), 1)
    for head in range(2):
        for at in range(4):
            own = pl.ds(at * block, block)
            kt_ref[:, own] = ka_ref[head, own, :].astype(F32).T.astype(BF)
        for at in range(4):
            own = pl.ds(at * block, block)
            queries, grads = qa_ref[head, own, :], da_ref[head, own, :]
            dq_t = jnp.zeros((LANES, block), F32)
            for past in range(at + 1):
                keys = pl.ds(past * block, block)
                probs = jnp.exp(dot(ka_ref[head, keys, :], queries, NT))
                if past == at:
                    probs = jnp.where(below <= across, probs, 0.0)
                grad_scores = (probs * dot(va_ref[head, keys, :], grads, NT)).astype(BF)
                dv = dot(probs.astype(BF), grads)
                dk = dot(grad_scores, queries)
                dq_t += dot(kt_ref[:, keys], grad_scores)
                if past == at:
                    dv_ref[head, keys, :] = dv
                    dk_ref[head, keys, :] = dk
                else:
                    dv_ref[head, keys, :] += dv
                    dk_ref[head, keys, :] += dk
            dq_ref[head, own, :] = dq_t.T

    for at in range(4):
        rows, own = rows_of(at), pl.ds(at * block, block)
        for head in range(2):
            base = 64 if head == 0 else 0
            change = (
                dq_ref[head, own, base + 4 : base + 5] - dk_ref[head, own, base : base + 1]
            )
            dc_ref[own, :] += jnp.where(lanes == 2 * pair + head, change, 0.0)
        left = lanes < 64
        for group, ref, scale in ((0, dq_ref, 0.125), (1, dk_ref, 1.0), (2, dv_ref, 1.0)):
            both = jnp.where(left, ref[0, own, :], ref[1, own, :])
            out_ref[rows, lanes_at(group)] = (both * scale).astype(BF)

    @pl.when(pair == pairs - 1)
    def finish():
        ones = jnp.where(below <= across, 1.0, 0.0)
        running = jnp.zeros((1, LANES), F32)
        for at in reversed(range(4)):
            sums = running + lax.dot_general(
                ones,
                dc_ref[pl.ds(at * block, block), :],
                (((1,), (0,)), ((), ())),
                precision=lax.Precision.HIGHEST,
                preferred_element_type=F32,
            )
            running = sums[:1, :]
            rows = rows_of(at)
            out_ref[rows, 4 * width :] = (sums * slope_ref[rows, :]).astype(BF)


def attend_backward(meta, qa, ka, qkv, grad_y, out_gate, attended, slope):
    row_total, width = out_gate.shape
    pairs = width // LANES
    heads = 2 * pairs
    total = 4 * width + LANES

    def columns(first):
        return pl.BlockSpec((row_total, LANES), lambda p, m: (0, first + p))

    sided = pl.BlockSpec((2, row_total, LANES), lambda p, m: (p, 0, 0))
    both = (2, row_total, LANES)
    return pl.pallas_call(
        backward_kernel,
        grid_spec=pltpu.PrefetchScalarGridSpec(
            num_scalar_prefetch=1,
            grid=(pairs,),
            in_specs=[
                sided,
                sided,
                columns(2 * pairs),
                columns(0),
                columns(0),
                columns(0),
                pl.BlockSpec((row_total, LANES), lambda p, m: (0, 0)),
            ],
            out_specs=pl.BlockSpec((row_total, total), lambda p, m: (0, 0)),
            scratch_shapes=[
                pltpu.VMEM(both, BF),
                pltpu.VMEM(both, BF),
                pltpu.VMEM((LANES, row_total), BF),
                pltpu.VMEM(both, F32),
                pltpu.VMEM(both, F32),
                pltpu.VMEM(both, F32),
                pltpu.VMEM((row_total, LANES), F32),
            ],
        ),
        out_shape=jax.ShapeDtypeStruct((row_total, total), BF),
        compiler_params=pltpu.CompilerParams(vmem_limit_bytes=48 * 2**20),
        cost_estimate=pl.CostEstimate(
            flops=heads * row_total * row_total * 640,
            bytes_accessed=row_total * width * 20,
            transcendentals=heads * row_total * row_total // 2,
        ),
    )(meta, qa, ka, qkv, grad_y, out_gate, attended, slope)


def mean_scale(rows):
    return lax.rsqrt(jnp.mean(rows * rows, axis=1, keepdims=True) + EPSILON)


def norm_backward(grad, normed, scale, gain):
    grad_normed = grad * gain
    inner = jnp.mean(grad_normed * normed, axis=1, keepdims=True)
    return scale * (grad_normed - normed * inner), jnp.sum(grad * normed, axis=0)


def on_device(
    x_given,
    cotangent,
    seq_lengths,
    seq_deal,
    attn_gain,
    w_query,
    w_key,
    w_value,
    w_ogate,
    w_forget,
    b_forget,
    w_out,
    mlp_gain,
    w_gate,
    w_up,
    w_down,
):
    quarter = x_given.shape[1]
    piece = quarter // 4
    row, column, lane = lax.axis_index("dp"), lax.axis_index("tx"), lax.axis_index("ty")
    first_place = row * quarter
    heads = w_forget.shape[1]
    width = w_query.shape[1]
    hidden = w_gate.shape[1]
    share = w_query.shape[0] // lax.axis_size("dp")

    def own_share(weights):
        return lax.dynamic_slice_in_dim(weights, row * share, share, axis=0)

    def whole(weights):
        return lax.all_gather(weights, ("ty", "dp"), axis=0, tiled=True)

    gains = jnp.stack(three_parts(attn_gain) + three_parts(mlp_gain), axis=1).astype(BF)
    spare = jnp.zeros((w_query.shape[0], LANES - heads - 6), BF)
    w_first = whole(
        jnp.concatenate(
            [own_share(w) for w in (w_query, w_key, w_value, w_ogate, w_forget, gains, spare)],
            axis=1,
        )
    )
    w_out_t = whole(own_share(w_out.T))
    w_gate_up = whole(jnp.concatenate([own_share(w_gate), own_share(w_up)], axis=1))
    w_down_t = whole(own_share(w_down.T))

    local = jnp.arange(quarter, dtype=jnp.int32)
    swapped = (((local // piece) ^ column) * piece) + local % piece
    own_lengths = lax.dynamic_index_in_dim(seq_lengths, column, 0, keepdims=False)
    own_dealing = lax.dynamic_index_in_dim(seq_deal, column, 0, keepdims=False)
    sources = dealt_sources(own_lengths, own_dealing, first_place + swapped)
    x_dealt, grad_dealt = moved_rows(sources, (x_given[0], cotangent[0]), first_place)

    def cut(rows):
        return [rows[k * piece : (k + 1) * piece] for k in range(4)]

    x_rows = to_plane(cut(x_dealt), column, lane)
    x_full = gather_rows(x_rows)
    grad_rows = to_plane(cut(grad_dealt), column, lane)
    grad_full = gather_rows(grad_rows)

    gain_parts = w_first[:, 4 * width + heads : 4 * width + heads + 6].astype(F32).T
    gain_one = (gain_parts[0] + gain_parts[1] + gain_parts[2])[None]
    gain_two = (gain_parts[3] + gain_parts[4] + gain_parts[5])[None]

    x_wide = x_full.astype(F32)
    first_normed = (x_wide * mean_scale(x_wide) * gain_one).astype(BF)
    pre = dot(first_normed, w_first)
    qkv = pre[:, : 3 * width].astype(BF)
    out_gate = jax.nn.sigmoid(pre[:, 3 * width : 4 * width])
    real = jnp.arange(LANES) < heads
    forget_pre = jnp.where(
        real[None], pre[:, 4 * width :] + jnp.pad(b_forget, (0, LANES - heads))[None], 0.0
    )
    keep = jax.nn.log_sigmoid(forget_pre)
    slope = jnp.where(real[None], jax.nn.sigmoid(-forget_pre), 0.0)

    block_lengths = lax.dynamic_index_in_dim(seq_lengths, lane, 0, keepdims=False)
    block_dealing = lax.dynamic_index_in_dim(seq_deal, lane, 0, keepdims=False)
    slot_lengths = stream_tables(block_lengths, block_dealing)[3]
    first_length = lax.dynamic_index_in_dim(slot_lengths, 2 * row, 0, keepdims=False)
    meta = jnp.stack([column, first_length]).astype(jnp.int32)
    gated, attended, qa, ka = attend_forward(meta, qkv, out_gate, keep)

    x_own = x_rows.astype(F32)
    second = x_own + scatter_product(gated, w_out_t)

    scale_two = mean_scale(second)
    normed_two = second * scale_two
    h2_full = gather_rows((normed_two * gain_two).astype(BF))
    up_gate = dot(h2_full, w_gate_up)
    gate_pre, up_pre = up_gate[:, :hidden], up_gate[:, hidden:]
    grad_mid = dot(grad_full, w_down_t)
    gate_sig = jax.nn.sigmoid(gate_pre)
    gate_silu = gate_pre * gate_sig
    mid = (gate_silu * up_pre).astype(BF)
    grad_gate = (grad_mid * up_pre * gate_sig * (1.0 + gate_pre * (1.0 - gate_sig))).astype(BF)
    grad_up = (grad_mid * gate_silu).astype(BF)
    grad_gate_up = jnp.concatenate([grad_gate, grad_up], axis=1)
    grad_h2 = scatter_product(grad_gate_up, w_gate_up)
    result = second + scatter_product(mid, w_down_t)

    def summed(grads):
        return lax.psum_scatter(grads, ("ty", "dp"), scatter_dimension=0, tiled=True)

    grads_mlp = summed(
        jnp.concatenate(
            [dot(h2_full, grad_gate_up, TN).astype(BF), dot(grad_full, mid, TN).astype(BF)], axis=1
        )
    )

    grad_norm, gain_two_part = norm_backward(grad_h2, normed_two, scale_two, gain_two)
    grad_second = grad_rows.astype(F32) + grad_norm
    grad_z = gather_rows(grad_second.astype(BF))
    grad_y = dot(grad_z, w_out_t)
    grad_first = attend_backward(meta, qa, ka, qkv, grad_y, out_gate, attended, slope)
    grad_h1 = scatter_product(grad_first, w_first)
    grads_attn = summed(
        jnp.concatenate(
            [dot(first_normed, grad_first, TN).astype(BF), dot(grad_z, gated, TN).astype(BF)],
            axis=1,
        )
    )
    scale_one = mean_scale(x_own)
    grad_norm, gain_one_part = norm_backward(grad_h1, x_own * scale_one, scale_one, gain_one)
    grad_x = grad_second + grad_norm

    targets = given_targets(own_lengths, own_dealing, first_place + local)
    at = targets % quarter
    dealt_at = targets - at + ((at // piece) ^ column) * piece + at % piece
    output = moved_rows(
        dealt_at, (from_plane(result.astype(BF), column, lane),), first_place
    )[0]
    grad_input = moved_rows(
        dealt_at, (from_plane(grad_x.astype(BF), column, lane),), first_place
    )[0]

    bias_part = jnp.sum(grad_first[:, 4 * width :].astype(F32), axis=0)
    bias_slots = jnp.where(jnp.arange(4)[:, None] == column, bias_part[None], 0.0).reshape(-1)
    small = lax.psum(
        jnp.concatenate([gain_one_part, gain_two_part, bias_slots]), ("dp", "tx", "ty")
    )
    total = w_query.shape[0]
    full = total * 4
    grad_attn_gain = lax.dynamic_slice_in_dim(small, lane * total, total)
    grad_mlp_gain = lax.dynamic_slice_in_dim(small, full + lane * total, total)
    grad_b_forget = lax.dynamic_slice_in_dim(small, 2 * full + column * LANES, heads)

    mlp = pair_rows(grads_mlp).astype(F32)
    attn = pair_rows(grads_attn).astype(F32)
    last = 4 * width + LANES
    return (
        output[None],
        grad_input[None],
        grad_attn_gain,
        attn[:, :width],
        attn[:, width : 2 * width],
        attn[:, 2 * width : 3 * width],
        attn[:, 3 * width : 4 * width],
        attn[:, 4 * width : 4 * width + heads],
        grad_b_forget,
        attn[:, last:].T,
        grad_mlp_gain,
        mlp[:, :hidden],
        mlp[:, hidden : 2 * hidden],
        mlp[:, 2 * hidden :].T,
    )


def solution(mesh):
    tokens, feature, grid, flipped = P("tx", "dp", "ty"), P("ty"), P("ty", "tx"), P("tx", "ty")
    return jax.shard_map(
        on_device,
        mesh=mesh,
        in_specs=(
            tokens,
            tokens,
            P(),
            P(),
            feature,
            grid,
            grid,
            grid,
            grid,
            grid,
            P("tx"),
            flipped,
            feature,
            grid,
            grid,
            flipped,
        ),
        out_specs=(
            tokens,
            tokens,
            feature,
            grid,
            grid,
            grid,
            grid,
            grid,
            P("tx"),
            flipped,
            feature,
            grid,
            grid,
            flipped,
        ),
        check_vma=False,
    )
```

time: 2880 us -> 601 us (0.21)
  waiting for transfers between devices: 2440 us -> 232 us
  matrix products: 232 us -> 91.1 us
  starting transfers between devices: 3.1 us -> 87.1 us
  Pallas kernels: 0 us -> 53.6 us
  other arithmetic: 67 us -> 34.4 us
    reduce_scatter x13 -> x2, waiting for transfers between devices: 1590 us -> 28 us  [summed(): lax.psum_scatter(grads, ('ty', 'dp'), scatter_dimension=0, tiled=True)]
    all_gather x16 -> x4, waiting for transfers between devices: 846 us -> 0.05 us  [whole(): return lax.all_gather(weights, ('ty', 'dp'), axis=0, tiled=True)]
    ppermute x0 -> x78, waiting for transfers between devices: none -> 204 us  [swap(): lax.ppermute(values, axis, [(at, at ^ step) for at in range(lax.axis_size...]
    dot_general x39 -> x40, matrix products: 232 us -> 91.1 us  [dot(): lax.dot_general(left, right, (dims, ((), ())), preferred_element_type=F32)]
    ppermute x0 -> x78, starting transfers between devices: none -> 86.8 us  [swap(): lax.ppermute(values, axis, [(at, at ^ step) for at in range(lax.axis_size...]
    pallas_call x0 -> x5, Pallas kernels: none -> 53.6 us  [the longest x1 20.7 us: attend_backward(): pl.pallas_call(backward_kernel, grid_spec=pltpu.PrefetchScalarGridSpec(nu...]
  transfers between devices with their start and end apart: 30 -> 84, of which waited for: 27 -> 40; matrix products, arithmetic and copies ran while one was open for 9% -> 19% of each run, Pallas kernels for 0% -> 6%
where the time goes in v1:
time: 601 us; the launch traced here: 593 us
  waiting for transfers between devices  232 us (39%)
  matrix products  91.1 us (15%)
  starting transfers between devices  87.1 us (14%)
  Pallas kernels  53.6 us (9%)
  blocking collectives  41.1 us (7%)
  local copies, waits for them, and re-layouts  38.4 us (6%)
  other arithmetic  34.4 us (6%)
  between operations  15.9 us (3%)
    ppermute x78, waiting for transfers between devices, swap(): lax.ppermute(values, axis, [(at, at ^ step) for at in range(lax.axis_size...  204 us
    dot_general x40, matrix products, dot(): lax.dot_general(left, right, (dims, ((), ())), preferred_element_type=F32)  91.1 us
    ppermute x78, starting transfers between devices, swap(): lax.ppermute(values, axis, [(at, at ^ step) for at in range(lax.axis_size...  86.8 us
    psum x1, blocking collectives, on_device(): lax.psum(jnp.concatenate([gain_one_part, gain_two_part, bias_slots]), ('d...  41.1 us
    reduce_scatter x2, waiting for transfers between devices, summed(): lax.psum_scatter(grads, ('ty', 'dp'), scatter_dimension=0, tiled=True)  28 us
    unnamed x120, local copies, waits for them, and re-layouts  21 us
    pallas_call x1, Pallas kernels, attend_backward(): pl.pallas_call(backward_kernel, grid_spec=pltpu.PrefetchScalarGridSpec(nu...  20.7 us
    pallas_call x1, Pallas kernels, attend_forward(): pl.pallas_call(forward_kernel, grid_spec=pltpu.PrefetchScalarGridSpec(num...  17.3 us
  transfers between devices with their start and end apart: 84, of which 40 were waited for; matrix products, arithmetic and copies ran while one was open for 19% of the time, Pallas kernels for 6%

profile of v1, /device:TPU:9, one launch (start us, length us, event | category | flops | bytes accessed | tf_op | source)
XLA Modules:
  0.0 593.5 jit_solution(12659848484238202980)
XLA Ops:
  22.5 7.0 %shard_map.263 = (bf16[1024,384]{1,0:T(8,128)(2,1)S(1)}, bf16[1024,384]{1,0:T(8,128)(2,1)S(1)}) custom-call(s32[1024,1]{1,0:T(8,128)S(1)} %negate_select_fusion.index_ref, bf16[1024,384]{1,0:T(8,128)(2,1)S(1)} %bitcast.115, bf16[1024,384]{1,0:T(8,128)(2,1)} %collective-permute-done.refs_1_, bf16[1024,384]{1,0:T(8,128)(2,1)S(1)} %bitcast.117, ...), custom_call_target="tpu_custom_call" | custom-call | flops 3221225472 | bytes 4718592 | tf_op jit(solution)/shard_map/pallas_call | solution.py:149
  37.8 4.6 collective-permute-done.3
  46.4 3.7 collective-permute-done.40
  52.9 14.5 %collective-permute-done.7 = bf16[256,384]{1,0:T(8,128)(2,1)S(1)} collective-permute-done((bf16[256,384]{1,0:T(8,128)(2,1)S(1)}, bf16[256,384]{1,0:T(8,128)(2,1)S(1)}, u32[]{:S(2)}, u32[]{:S(2)}) %collective-permute-start.7) | collective-permute-done | bytes 196640 | tf_op jit(solution)/shard_map/ppermute | solution.py:67
  67.4 20.3 %collective-permute-done.6 = bf16[256,384]{1,0:T(8,128)(2,1)S(1)} collective-permute-done((bf16[256,384]{1,0:T(8,128)(2,1)S(1)}, bf16[256,384]{1,0:T(8,128)(2,1)S(1)}, u32[]{:S(2)}, u32[]{:S(2)}) %collective-permute-start.6) | collective-permute-done | bytes 196640 | tf_op jit(solution)/shard_map/ppermute | solution.py:67
  89.8 6.1 %collective-permute-done.44 = bf16[256,384]{1,0:T(8,128)(2,1)S(1)} collective-permute-done((bf16[256,384]{1,0:T(8,128)(2,1)S(1)}, bf16[256,384]{1,0:T(8,128)(2,1)S(1)}, u32[]{:S(2)}, u32[]{:S(2)}) %collective-permute-start.44) | collective-permute-done | bytes 196640 | tf_op jit(solution)/shard_map/ppermute | solution.py:67
  101.5 5.4 collective-permute-done.9
  110.0 5.4 collective-permute-done.45
  117.9 5.9 collective-permute-done.46
  125.3 8.4 %collective-permute-done.12 = bf16[128,1536]{1,0:T(8,128)(2,1)S(1)} collective-permute-done((bf16[128,1536]{1,0:T(8,128)(2,1)S(1)}, bf16[128,1536]{1,0:T(8,128)(2,1)S(1)}, u32[]{:S(2)}, u32[]{:S(2)}) %collective-permute-start.12) | collective-permute-done | bytes 393248 | tf_op jit(solution)/shard_map/ppermute | solution.py:67
  139.1 8.4 %fusion.95 = f32[1024,1664]{1,0:T(8,128)S(1)} fusion(bf16[1536,1664]{1,0:T(8,128)(2,1)} %all-gather.5.cloned.1.call-done, bf16[1024,1536]{1,0:T(8,128)(2,1)S(1)} %copy-done.14, f32[1536]{0:T(1024)S(1)} %get-tuple-element.87, f32[1024]{0:T(1024)S(1)} %add_rsqrt_fusion), kind=kOutput, calls=%fused_computation.129 | convolution fusion | flops 5240782848 | bytes 15083520 | tf_op jit(solution)/shard_map/dot_general | solution.py:16
  151.1 17.3 %shard_map.264 = (bf16[1024,384]{1,0:T(8,128)(2,1)S(1)}, f32[1024,384]{1,0:T(8,128)S(1)}, bf16[6,1024,128]{2,1,0:T(8,128)(2,1)S(1)}, bf16[6,1024,128]{2,1,0:T(8,128)(2,1)S(1)}) custom-call(s32[2]{0:T(128)S(1)} %pad_add_fusion.meta, bf16[1024,1152]{1,0:T(8,128)(2,1)} %slice.563.q_ref.k_ref.v_ref, bf16[1024,1152]{1,0:T(8,128)(2,1)} %slice.563.q_ref.k_ref.v_ref, ...), custom_call_target="tpu_custom_call" | custom-call | flops 1610612736 | bytes 6291456 | tf_op jit(solution)/shard_map/pallas_call | solution.py:280
  186.7 2.5 collective-permute-done.17
  190.3 11.4 %collective-permute-done.19 = bf16[256,768]{1,0:T(8,128)(2,1)S(1)} collective-permute-done((bf16[256,768]{1,0:T(8,128)(2,1)S(1)}, bf16[256,768]{1,0:T(8,128)(2,1)S(1)}, u32[]{:S(2)}, u32[]{:S(2)}) %collective-permute-start.19) | collective-permute-done | bytes 393248 | tf_op jit(solution)/shard_map/ppermute | solution.py:67
  212.0 6.5 %collective-permute-done.20 = bf16[128,1536]{1,0:T(8,128)(2,1)S(1)} collective-permute-done((bf16[128,1536]{1,0:T(8,128)(2,1)S(1)}, bf16[128,1536]{1,0:T(8,128)(2,1)S(1)}, u32[]{:S(2)}, u32[]{:S(2)}) %collective-permute-start.20) | collective-permute-done | bytes 393248 | tf_op jit(solution)/shard_map/ppermute | solution.py:67
  220.5 6.3 %collective-permute-done.21 = bf16[128,1536]{1,0:T(8,128)(2,1)S(1)} collective-permute-done((bf16[128,1536]{1,0:T(8,128)(2,1)S(1)}, bf16[128,1536]{1,0:T(8,128)(2,1)S(1)}, u32[]{:S(2)}, u32[]{:S(2)}) %collective-permute-start.21) | collective-permute-done | bytes 393248 | tf_op jit(solution)/shard_map/ppermute | solution.py:67
  230.5 4.8 collective-permute-done.25
  236.1 12.1 %fusion.223 = f32[1024,2048]{1,0:T(8,128)} fusion(bf16[1024,1536]{1,0:T(8,128)(2,1)} %constant_dynamic-update-slice_fusion.7, bf16[1536,2048]{1,0:T(8,128)(2,1)} %all-gather.9.cloned.1.call-done), kind=kOutput, calls=%fused_computation.397 | convolution fusion | flops 6442450944 | bytes 17825792 | tf_op jit(solution)/shard_map/dot_general | solution.py:16
  248.2 10.2 %multiply_convert_fusion = (bf16[1024,1024]{1,0:T(8,128)(2,1)S(1)}, bf16[1024,1024]{1,0:T(8,128)(2,1)S(1)}, bf16[1024,1024]{1,0:T(8,128)(2,1)S(1)}) fusion(f32[1024,2048]{1,0:T(8,128)} %fusion.223, bf16[1024,1536]{1,0:T(8,128)(2,1)} %constant_dynamic-update-slice_fusion.14, bf16[1536,1024]{1,0:T(8,128)(2,1)} %all-gather.11.cloned.1.call-done), kind=kOutput, calls=%fused_computation.19 | convolution fusion | flops 3236954112 | bytes 20971520 | tf_op jit(solution)/shard_map/dot_general | solution.py:16
  276.9 6.4 %collective-permute-done.30 = bf16[256,768]{1,0:T(8,128)(2,1)S(1)} collective-permute-done((bf16[256,768]{1,0:T(8,128)(2,1)S(1)}, bf16[256,768]{1,0:T(8,128)(2,1)S(1)}, u32[]{:S(2)}, u32[]{:S(2)}) %collective-permute-start.30) | collective-permute-done | bytes 393248 | tf_op jit(solution)/shard_map/ppermute | solution.py:67
  288.3 6.6 %collective-permute-done.56 = bf16[256,768]{1,0:T(8,128)(2,1)S(1)} collective-permute-done((bf16[256,768]{1,0:T(8,128)(2,1)S(1)}, bf16[256,768]{1,0:T(8,128)(2,1)S(1)}, u32[]{:S(2)}, u32[]{:S(2)}) %collective-permute-start.56) | collective-permute-done | bytes 393248 | tf_op jit(solution)/shard_map/ppermute | solution.py:67
  296.1 4.0 collective-permute-done.53
  300.3 11.4 %collective-permute-done.31 = bf16[256,768]{1,0:T(8,128)(2,1)S(1)} collective-permute-done((bf16[256,768]{1,0:T(8,128)(2,1)S(1)}, bf16[256,768]{1,0:T(8,128)(2,1)S(1)}, u32[]{:S(2)}, u32[]{:S(2)}) %collective-permute-start.31) | collective-permute-done | bytes 393248 | tf_op jit(solution)/shard_map/ppermute | solution.py:67
  318.1 3.7 collective-permute-done.57
  323.2 5.7 collective-permute-done.58
  329.8 8.4 %collective-permute-done.61 = bf16[128,1536]{1,0:T(8,128)(2,1)S(1)} collective-permute-done((bf16[128,1536]{1,0:T(8,128)(2,1)S(1)}, bf16[128,1536]{1,0:T(8,128)(2,1)S(1)}, u32[]{:S(2)}, u32[]{:S(2)}) %collective-permute-start.61) | collective-permute-done | bytes 393248 | tf_op jit(solution)/shard_map/ppermute | solution.py:67
  338.2 2.9 convolution_convert_fusion.3
  342.9 20.7 %shard_map.266 = bf16[1024,1664]{1,0:T(8,128)(2,1)} custom-call(s32[2]{0:T(128)S(1)} %pad_add_fusion.meta, bf16[6,1024,128]{2,1,0:T(8,128)(2,1)S(1)} %get-tuple-element.23.qa_ref, bf16[6,1024,128]{2,1,0:T(8,128)(2,1)S(1)} %copy-done.4, bf16[1024,1152]{1,0:T(8,128)(2,1)} %slice.563.q_ref.k_ref.v_ref, f32[1024,384]{1,0:T(8,128)S(1)} %fusion.224.dy_ref, ...), custom_call_target="tpu_custom_call" | custom-call | flops 4026531840 | bytes 7864320 | tf_op jit(solution)/shard_map/pallas_call | solution.py:436
  363.6 8.5 %convolution_convert_fusion = bf16[1536,1664]{1,0:T(8,128)(2,1)S(1)} fusion(bf16[1024,1664]{1,0:T(8,128)(2,1)} %shard_map.266, bf16[1024,1536]{1,0:T(8,128)(2,1)S(1)} %copy-done.15, f32[1536]{0:T(1024)S(1)} %get-tuple-element.87, f32[1024]{0:T(1024)S(1)} %add_rsqrt_fusion), kind=kOutput, calls=%fused_computation.3 | convolution fusion | flops 5243338752 | bytes 11675648 | tf_op jit(solution)/shard_map/dot_general | solution.py:16
  372.2 3.6 pad_maximum_fusion.2
  377.6 5.5 convolution_convert_fusion.2
  383.1 9.1 %convolution_convert_fusion.1 = bf16[1536,2048]{1,0:T(8,128)(2,1)S(1)} fusion(bf16[1024,1536]{1,0:T(8,128)(2,1)} %constant_dynamic-update-slice_fusion.7, bf16[1024,1024]{1,0:T(8,128)(2,1)S(1)} %copy-done.41, bf16[1024,1024]{1,0:T(8,128)(2,1)S(1)} %copy-done.43), kind=kOutput, calls=%fused_computation.4 | convolution fusion | flops 6453985280 | bytes 13631488 | tf_op jit(solution)/shard_map/dot_general | solution.py:16
  392.2 5.1 pad_maximum_fusion
  398.6 4.8 collective-permute-start.33
  404.5 10.8 %collective-permute-done.34 = bf16[256,384]{1,0:T(8,128)(2,1)S(1)} collective-permute-done((bf16[256,384]{1,0:T(8,128)(2,1)S(1)}, bf16[256,384]{1,0:T(8,128)(2,1)S(1)}, u32[]{:S(2)}, u32[]{:S(2)}) %collective-permute-start.34) | collective-permute-done | bytes 196640 | tf_op jit(solution)/shard_map/ppermute | solution.py:67
  415.3 11.3 %collective-permute-done.33 = bf16[256,384]{1,0:T(8,128)(2,1)S(1)} collective-permute-done((bf16[256,384]{1,0:T(8,128)(2,1)S(1)}, bf16[256,384]{1,0:T(8,128)(2,1)S(1)}, u32[]{:S(2)}, u32[]{:S(2)}) %collective-permute-start.33) | collective-permute-done | bytes 196640 | tf_op jit(solution)/shard_map/ppermute | solution.py:67
  426.7 2.6 collective-permute-done.32
  430.0 2.8 fusion.59
  434.7 2.7 fusion.56
  437.5 2.6 fusion.53
  451.3 9.1 %collective-permute-done.68 = bf16[256,768]{1,0:T(8,128)(2,1)S(1)} collective-permute-done((bf16[256,768]{1,0:T(8,128)(2,1)S(1)}, bf16[256,768]{1,0:T(8,128)(2,1)S(1)}, u32[]{:S(2)}, u32[]{:S(2)}) %collective-permute-start.68) | collective-permute-done | bytes 393248 | tf_op jit(solution)/shard_map/ppermute | solution.py:67
  462.7 5.3 collective-permute-start.70
  471.0 9.3 %collective-permute-start.38 = (bf16[1024,384]{1,0:T(8,128)(2,1)S(1)}, bf16[1024,384]{1,0:T(8,128)(2,1)S(1)}, u32[]{:S(2)}, u32[]{:S(2)}) collective-permute-start(bf16[1024,384]{1,0:T(8,128)(2,1)S(1)} %pad_maximum_fusion.11.refs_0_), channel_id=1, source_target_pairs={{0,16},{16,0},{1,17},{17,1},{2,18},{18,2},{3,19},{19,3},{4,20},{20... | collective-permute-start | bytes 2359304 | tf_op jit(solution)/shard_map/ppermute | solution.py:67
  490.7 5.1 collective-permute-start.75
  497.2 3.7 shard_map.265
  500.9 41.1 %psum.7 = f32[3584]{0:T(1024)S(1)} all-reduce(f32[3584]{0:T(1024)S(1)} %pad_maximum_fusion.17), channel_id=1, replica_groups=mesh['dp'=2,'tx'=4,'ty'=4] {'dp','tx','ty'}, use_global_device_ids=true, to_apply=%region_22.23 | all-reduce | flops 3584 | bytes 28672 | tf_op jit(solution)/shard_map/psum | solution.py:619
  543.2 4.9 shard_map.267
  548.1 28.0 %reduce-scatter.5.cloned.1.call-done = bf16[192,3072]{1,0:T(8,128)(2,1)} async-done(((bf16[1536,3072]{1,0:T(8,128)(2,1)}), bf16[192,3072]{1,0:T(8,128)(2,1)}) %reduce-scatter.5.cloned.1.call-update) | async-done | bytes 1179664 | tf_op jit(solution)/shard_map/reduce_scatter | solution.py:583
  (409 shorter events, 171.2 us)
Async XLA Ops:
  7.2 129.0 %all-gather.5.cloned.1.call-start = ((), (), s32[]{:S(2)}) async-start(), calls=%async_computation.2 | async-start | bytes 5750784 | tf_op jit(solution)/shard_map/all_gather | solution.py:512
  13.0 157.7 %all-gather.7.cloned.1.call-start = ((), (), s32[]{:S(2)}) async-start(), calls=%async_computation.3 | async-start | bytes 1327104 | tf_op jit(solution)/shard_map/all_gather | solution.py:512
  14.1 222.0 %all-gather.9.cloned.1.call-start = ((), (), s32[]{:S(2)}) async-start(), calls=%async_computation.4 | async-start | bytes 7077888 | tf_op jit(solution)/shard_map/all_gather | solution.py:512
  16.3 231.9 %all-gather.11.cloned.1.call-start = ((), (), s32[]{:S(2)}) async-start(), calls=%async_computation.5 | async-start | bytes 3538944 | tf_op jit(solution)/shard_map/all_gather | solution.py:512
  18.4 477.5 %reduce-scatter.3.cloned.1.call-start = ((), (), s32[]{:S(2)}) async-start(), calls=%async_computation.6 | async-start | bytes 7077888 | tf_op jit(solution)/shard_map/reduce_scatter | solution.py:583
  34.7 15.5 %collective-permute-start.40 = (bf16[256,384]{1,0:T(8,128)(2,1)S(1)}, bf16[256,384]{1,0:T(8,128)(2,1)S(1)}, u32[]{:S(2)}, u32[]{:S(2)}) collective-permute-start(bf16[256,384]{1,0:T(8,128)(2,1)S(1)} %get-tuple-element.143), channel_id=1, source_target_pairs={{0,8},{4,12},{8,0},{12,4},{1,9},{5,13},{9,1},{13,5},{2,10},{6,14},... | collective-permute-start | bytes 589832 | tf_op jit(solution)/shard_map/ppermute | solution.py:67
  42.6 24.8 %collective-permute-start.7 = (bf16[256,384]{1,0:T(8,128)(2,1)S(1)}, bf16[256,384]{1,0:T(8,128)(2,1)S(1)}, u32[]{:S(2)}, u32[]{:S(2)}) collective-permute-start(bf16[256,384]{1,0:T(8,128)(2,1)S(1)} %get-tuple-element.162), channel_id=1, source_target_pairs={{0,3},{1,2},{2,1},{3,0},{4,7},{5,6},{6,5},{7,4},{8,11},{9,10},{10,... | collective-permute-start | bytes 589832 | tf_op jit(solution)/shard_map/ppermute | solution.py:67
  44.2 43.5 %collective-permute-start.6 = (bf16[256,384]{1,0:T(8,128)(2,1)S(1)}, bf16[256,384]{1,0:T(8,128)(2,1)S(1)}, u32[]{:S(2)}, u32[]{:S(2)}) collective-permute-start(bf16[256,384]{1,0:T(8,128)(2,1)S(1)} %get-tuple-element.163), channel_id=1, source_target_pairs={{0,2},{1,3},{2,0},{3,1},{4,6},{5,7},{6,4},{7,5},{8,10},{9,11},{10,... | collective-permute-start | bytes 589832 | tf_op jit(solution)/shard_map/ppermute | solution.py:67
  45.3 42.4 %collective-permute-start.5 = (bf16[256,384]{1,0:T(8,128)(2,1)S(1)}, bf16[256,384]{1,0:T(8,128)(2,1)S(1)}, u32[]{:S(2)}, u32[]{:S(2)}) collective-permute-start(bf16[256,384]{1,0:T(8,128)(2,1)S(1)} %get-tuple-element.164), channel_id=1, source_target_pairs={{0,1},{1,0},{2,3},{3,2},{4,5},{5,4},{6,7},{7,6},{8,9},{9,8},{10,11... | collective-permute-start | bytes 589832 | tf_op jit(solution)/shard_map/ppermute | solution.py:67
  50.4 45.6 %collective-permute-start.44 = (bf16[256,384]{1,0:T(8,128)(2,1)S(1)}, bf16[256,384]{1,0:T(8,128)(2,1)S(1)}, u32[]{:S(2)}, u32[]{:S(2)}) collective-permute-start(bf16[256,384]{1,0:T(8,128)(2,1)S(1)} %get-tuple-element.138), channel_id=1, source_target_pairs={{0,3},{1,2},{2,1},{3,0},{4,7},{5,6},{6,5},{7,4},{8,11},{9,10},{10,... | collective-permute-start | bytes 589832 | tf_op jit(solution)/shard_map/ppermute | solution.py:67
  51.8 46.1 %collective-permute-start.43 = (bf16[256,384]{1,0:T(8,128)(2,1)S(1)}, bf16[256,384]{1,0:T(8,128)(2,1)S(1)}, u32[]{:S(2)}, u32[]{:S(2)}) collective-permute-start(bf16[256,384]{1,0:T(8,128)(2,1)S(1)} %get-tuple-element.139), channel_id=1, source_target_pairs={{0,2},{1,3},{2,0},{3,1},{4,6},{5,7},{6,4},{7,5},{8,10},{9,11},{10,... | collective-permute-start | bytes 589832 | tf_op jit(solution)/shard_map/ppermute | solution.py:67
  67.4 32.0 %collective-permute-start.42 = (bf16[256,384]{1,0:T(8,128)(2,1)S(1)}, bf16[256,384]{1,0:T(8,128)(2,1)S(1)}, u32[]{:S(2)}, u32[]{:S(2)}) collective-permute-start(bf16[256,384]{1,0:T(8,128)(2,1)S(1)} %get-tuple-element.140), channel_id=1, source_target_pairs={{0,1},{1,0},{2,3},{3,2},{4,5},{5,4},{6,7},{7,6},{8,9},{9,8},{10,11... | collective-permute-start | bytes 589832 | tf_op jit(solution)/shard_map/ppermute | solution.py:67
  89.8 18.6 %collective-permute-start.10 = (bf16[128,1536]{1,0:T(8,128)(2,1)S(1)}, bf16[128,1536]{1,0:T(8,128)(2,1)S(1)}, u32[]{:S(2)}, u32[]{:S(2)}) collective-permute-start(bf16[128,1536]{1,0:T(8,128)(2,1)S(1)} %get-tuple-element.156), channel_id=1, source_target_pairs={{0,8},{4,12},{8,0},{12,4},{1,9},{5,13},{9,1},{13,5},{2,10},{6,14},... | collective-permute-start | bytes 1179656 | tf_op jit(solution)/shard_map/ppermute | solution.py:67
  99.8 15.7 %collective-permute-start.45 = (bf16[128,1536]{1,0:T(8,128)(2,1)S(1)}, bf16[128,1536]{1,0:T(8,128)(2,1)}, u32[]{:S(2)}, u32[]{:S(2)}) collective-permute-start(bf16[128,1536]{1,0:T(8,128)(2,1)S(1)} %get-tuple-element.130), channel_id=1, source_target_pairs={{0,4},{4,0},{8,12},{12,8},{1,5},{5,1},{9,13},{13,9},{2,6},{6,2},{1... | collective-permute-start | bytes 1179656 | tf_op jit(solution)/shard_map/ppermute | solution.py:67
  100.6 24.6 %collective-permute-start.47 = (bf16[128,1536]{1,0:T(8,128)(2,1)S(1)}, bf16[128,1536]{1,0:T(8,128)(2,1)S(1)}, u32[]{:S(2)}, u32[]{:S(2)}) collective-permute-start(bf16[128,1536]{1,0:T(8,128)(2,1)S(1)} %get-tuple-element.130), channel_id=1, source_target_pairs={{0,8},{4,12},{8,0},{12,4},{1,9},{5,13},{9,1},{13,5},{2,10},{6,14},... | collective-permute-start | bytes 1179656 | tf_op jit(solution)/shard_map/ppermute | solution.py:67
  106.9 16.9 %collective-permute-start.46 = (bf16[128,1536]{1,0:T(8,128)(2,1)S(1)}, bf16[128,1536]{1,0:T(8,128)(2,1)S(1)}, u32[]{:S(2)}, u32[]{:S(2)}) collective-permute-start(bf16[128,1536]{1,0:T(8,128)(2,1)S(1)} %get-tuple-element.129), channel_id=1, source_target_pairs={{0,4},{4,0},{8,12},{12,8},{1,5},{5,1},{9,13},{13,9},{2,6},{6,2},{1... | collective-permute-start | bytes 1179656 | tf_op jit(solution)/shard_map/ppermute | solution.py:67
  108.4 16.9 %collective-permute-start.48 = (bf16[128,1536]{1,0:T(8,128)(2,1)S(1)}, bf16[128,1536]{1,0:T(8,128)(2,1)S(1)}, u32[]{:S(2)}, u32[]{:S(2)}) collective-permute-start(bf16[128,1536]{1,0:T(8,128)(2,1)S(1)} %get-tuple-element.129), channel_id=1, source_target_pairs={{0,8},{4,12},{8,0},{12,4},{1,9},{5,13},{9,1},{13,5},{2,10},{6,14},... | collective-permute-start | bytes 1179656 | tf_op jit(solution)/shard_map/ppermute | solution.py:67
  108.5 25.2 %collective-permute-start.12 = (bf16[128,1536]{1,0:T(8,128)(2,1)S(1)}, bf16[128,1536]{1,0:T(8,128)(2,1)S(1)}, u32[]{:S(2)}, u32[]{:S(2)}) collective-permute-start(bf16[128,1536]{1,0:T(8,128)(2,1)S(1)} %collective-permute-done.8), channel_id=1, source_target_pairs={{0,8},{4,12},{8,0},{12,4},{1,9},{5,13},{9,1},{13,5},{2,10},{6,14},... | collective-permute-start | bytes 1179656 | tf_op jit(solution)/shard_map/ppermute | solution.py:67
  115.5 18.3 %collective-permute-start.13 = (bf16[128,1536]{1,0:T(8,128)(2,1)S(1)}, bf16[128,1536]{1,0:T(8,128)(2,1)S(1)}, u32[]{:S(2)}, u32[]{:S(2)}) collective-permute-start(bf16[128,1536]{1,0:T(8,128)(2,1)S(1)} %collective-permute-done.11), channel_id=1, source_target_pairs={{0,4},{4,0},{8,12},{12,8},{1,5},{5,1},{9,13},{13,9},{2,6},{6,2},{1... | collective-permute-start | bytes 1179656 | tf_op jit(solution)/shard_map/ppermute | solution.py:67
  123.8 81.2 %collective-permute-start.49 = (bf16[128,1536]{1,0:T(8,128)(2,1)}, bf16[128,1536]{1,0:T(8,128)(2,1)}, u32[]{:S(2)}, u32[]{:S(2)}) collective-permute-start(bf16[128,1536]{1,0:T(8,128)(2,1)} %collective-permute-done.45), channel_id=1, source_target_pairs={{0,8},{4,12},{8,0},{12,4},{1,9},{5,13},{9,1},{13,5},{2,10},{6,14},... | collective-permute-start | bytes 1179656 | tf_op jit(solution)/shard_map/ppermute | solution.py:67
  178.5 23.3 %collective-permute-start.14 = (bf16[256,768]{1,0:T(8,128)(2,1)S(1)}, bf16[256,768]{1,0:T(8,128)(2,1)S(1)}, u32[]{:S(2)}, u32[]{:S(2)}) collective-permute-start(bf16[256,768]{1,0:T(8,128)(2,1)S(1)} %convolution_convert_fusion.11), channel_id=1, source_target_pairs={{0,4},{4,0},{8,12},{12,8},{1,5},{5,1},{9,13},{13,9},{2,6},{6,2},{1... | collective-permute-start | bytes 1179656 | tf_op jit(solution)/shard_map/ppermute | solution.py:67
  181.2 20.5 %collective-permute-start.19 = (bf16[256,768]{1,0:T(8,128)(2,1)S(1)}, bf16[256,768]{1,0:T(8,128)(2,1)S(1)}, u32[]{:S(2)}, u32[]{:S(2)}) collective-permute-start(bf16[256,768]{1,0:T(8,128)(2,1)S(1)} %add_convert_fusion.6), channel_id=1, source_target_pairs={{0,4},{4,0},{8,12},{12,8},{1,5},{5,1},{9,13},{13,9},{2,6},{6,2},{1... | collective-permute-start | bytes 1179656 | tf_op jit(solution)/shard_map/ppermute | solution.py:67
  185.1 16.7 %collective-permute-start.16 = (bf16[256,768]{1,0:T(8,128)(2,1)S(1)}, bf16[256,768]{1,0:T(8,128)(2,1)S(1)}, u32[]{:S(2)}, u32[]{:S(2)}) collective-permute-start(bf16[256,768]{1,0:T(8,128)(2,1)S(1)} %add_convert_fusion.7), channel_id=1, source_target_pairs={{0,8},{4,12},{8,0},{12,4},{1,9},{5,13},{9,1},{13,5},{2,10},{6,14},... | collective-permute-start | bytes 1179656 | tf_op jit(solution)/shard_map/ppermute | solution.py:67
  189.2 20.9 %collective-permute-start.50 = (bf16[128,1536]{1,0:T(8,128)(2,1)S(1)}, bf16[128,1536]{1,0:T(8,128)(2,1)S(1)}, u32[]{:S(2)}, u32[]{:S(2)}) collective-permute-start(bf16[128,1536]{1,0:T(8,128)(2,1)S(1)} %copy-done.25), channel_id=1, source_target_pairs={{0,4},{4,0},{8,12},{12,8},{1,5},{5,1},{9,13},{13,9},{2,6},{6,2},{1... | collective-permute-start | bytes 1179656 | tf_op jit(solution)/shard_map/ppermute | solution.py:67
  206.8 20.1 %collective-permute-start.21 = (bf16[128,1536]{1,0:T(8,128)(2,1)S(1)}, bf16[128,1536]{1,0:T(8,128)(2,1)S(1)}, u32[]{:S(2)}, u32[]{:S(2)}) collective-permute-start(bf16[128,1536]{1,0:T(8,128)(2,1)S(1)} %get-tuple-element.153), channel_id=1, source_target_pairs={{0,4},{4,0},{8,12},{12,8},{1,5},{5,1},{9,13},{13,9},{2,6},{6,2},{1... | collective-permute-start | bytes 1179656 | tf_op jit(solution)/shard_map/ppermute | solution.py:67
  210.9 16.8 %collective-permute-start.22 = (bf16[128,1536]{1,0:T(8,128)(2,1)S(1)}, bf16[128,1536]{1,0:T(8,128)(2,1)S(1)}, u32[]{:S(2)}, u32[]{:S(2)}) collective-permute-start(bf16[128,1536]{1,0:T(8,128)(2,1)S(1)} %get-tuple-element.154), channel_id=1, source_target_pairs={{0,8},{4,12},{8,0},{12,4},{1,9},{5,13},{9,1},{13,5},{2,10},{6,14},... | collective-permute-start | bytes 1179656 | tf_op jit(solution)/shard_map/ppermute | solution.py:67
  219.7 15.6 %collective-permute-start.25 = (bf16[128,1536]{1,0:T(8,128)(2,1)S(1)}, bf16[128,1536]{1,0:T(8,128)(2,1)S(1)}, u32[]{:S(2)}, u32[]{:S(2)}) collective-permute-start(bf16[128,1536]{1,0:T(8,128)(2,1)S(1)} %collective-permute-done.23), channel_id=1, source_target_pairs={{0,4},{4,0},{8,12},{12,8},{1,5},{5,1},{9,13},{13,9},{2,6},{6,2},{1... | collective-permute-start | bytes 1179656 | tf_op jit(solution)/shard_map/ppermute | solution.py:67
  261.7 26.4 %collective-permute-start.54 = (bf16[256,768]{1,0:T(8,128)(2,1)S(1)}, bf16[256,768]{1,0:T(8,128)(2,1)S(1)}, u32[]{:S(2)}, u32[]{:S(2)}) collective-permute-start(bf16[256,768]{1,0:T(8,128)(2,1)S(1)} %fusion.68), channel_id=1, source_target_pairs={{0,8},{4,12},{8,0},{12,4},{1,9},{5,13},{9,1},{13,5},{2,10},{6,14},... | collective-permute-start | bytes 1179656 | tf_op jit(solution)/shard_map/ppermute | solution.py:67
  265.4 30.6 %collective-permute-start.51 = (bf16[256,768]{1,0:T(8,128)(2,1)S(1)}, bf16[256,768]{1,0:T(8,128)(2,1)S(1)}, u32[]{:S(2)}, u32[]{:S(2)}) collective-permute-start(bf16[256,768]{1,0:T(8,128)(2,1)S(1)} %fusion.62), channel_id=1, source_target_pairs={{0,4},{4,0},{8,12},{12,8},{1,5},{5,1},{9,13},{13,9},{2,6},{6,2},{1... | collective-permute-start | bytes 1179656 | tf_op jit(solution)/shard_map/ppermute | solution.py:67
  266.4 16.9 %collective-permute-start.30 = (bf16[256,768]{1,0:T(8,128)(2,1)S(1)}, bf16[256,768]{1,0:T(8,128)(2,1)S(1)}, u32[]{:S(2)}, u32[]{:S(2)}) collective-permute-start(bf16[256,768]{1,0:T(8,128)(2,1)S(1)} %convolution_convert_fusion.4), channel_id=1, source_target_pairs={{0,8},{4,12},{8,0},{12,4},{1,9},{5,13},{9,1},{13,5},{2,10},{6,14},... | collective-permute-start | bytes 1179656 | tf_op jit(solution)/shard_map/ppermute | solution.py:67
  273.1 27.1 %collective-permute-start.29 = (bf16[256,768]{1,0:T(8,128)(2,1)S(1)}, bf16[256,768]{1,0:T(8,128)(2,1)S(1)}, u32[]{:S(2)}, u32[]{:S(2)}) collective-permute-start(bf16[256,768]{1,0:T(8,128)(2,1)S(1)} %convolution_convert_fusion.5), channel_id=1, source_target_pairs={{0,8},{4,12},{8,0},{12,4},{1,9},{5,13},{9,1},{13,5},{2,10},{6,14},... | collective-permute-start | bytes 1179656 | tf_op jit(solution)/shard_map/ppermute | solution.py:67
  288.1 23.7 %collective-permute-start.26 = (bf16[256,768]{1,0:T(8,128)(2,1)S(1)}, bf16[256,768]{1,0:T(8,128)(2,1)S(1)}, u32[]{:S(2)}, u32[]{:S(2)}) collective-permute-start(bf16[256,768]{1,0:T(8,128)(2,1)S(1)} %convolution_convert_fusion.7), channel_id=1, source_target_pairs={{0,4},{4,0},{8,12},{12,8},{1,5},{5,1},{9,13},{13,9},{2,6},{6,2},{1... | collective-permute-start | bytes 1179656 | tf_op jit(solution)/shard_map/ppermute | solution.py:67
  294.8 16.9 %collective-permute-start.31 = (bf16[256,768]{1,0:T(8,128)(2,1)S(1)}, bf16[256,768]{1,0:T(8,128)(2,1)S(1)}, u32[]{:S(2)}, u32[]{:S(2)}) collective-permute-start(bf16[256,768]{1,0:T(8,128)(2,1)S(1)} %add_convert_fusion.4), channel_id=1, source_target_pairs={{0,4},{4,0},{8,12},{12,8},{1,5},{5,1},{9,13},{13,9},{2,6},{6,2},{1... | collective-permute-start | bytes 1179656 | tf_op jit(solution)/shard_map/ppermute | solution.py:67
  296.1 15.8 %collective-permute-start.28 = (bf16[256,768]{1,0:T(8,128)(2,1)S(1)}, bf16[256,768]{1,0:T(8,128)(2,1)S(1)}, u32[]{:S(2)}, u32[]{:S(2)}) collective-permute-start(bf16[256,768]{1,0:T(8,128)(2,1)S(1)} %add_convert_fusion.5), channel_id=1, source_target_pairs={{0,8},{4,12},{8,0},{12,4},{1,9},{5,13},{9,1},{13,5},{2,10},{6,14},... | collective-permute-start | bytes 1179656 | tf_op jit(solution)/shard_map/ppermute | solution.py:67
  321.7 16.4 %collective-permute-start.61 = (bf16[128,1536]{1,0:T(8,128)(2,1)S(1)}, bf16[128,1536]{1,0:T(8,128)(2,1)S(1)}, u32[]{:S(2)}, u32[]{:S(2)}) collective-permute-start(bf16[128,1536]{1,0:T(8,128)(2,1)S(1)} %collective-permute-done.57), channel_id=1, source_target_pairs={{0,8},{4,12},{8,0},{12,4},{1,9},{5,13},{9,1},{13,5},{2,10},{6,14},... | collective-permute-start | bytes 1179656 | tf_op jit(solution)/shard_map/ppermute | solution.py:67
  375.8 200.4 %reduce-scatter.5.cloned.1.call-start = ((), (), s32[]{:S(2)}) async-start(), calls=%async_computation.7 | async-start | bytes 10616832 | tf_op jit(solution)/shard_map/reduce_scatter | solution.py:583
  398.5 16.8 %collective-permute-start.34 = (bf16[256,384]{1,0:T(8,128)(2,1)S(1)}, bf16[256,384]{1,0:T(8,128)(2,1)S(1)}, u32[]{:S(2)}, u32[]{:S(2)}) collective-permute-start(bf16[256,384]{1,0:T(8,128)(2,1)S(1)} %get-tuple-element.150), channel_id=1, source_target_pairs={{0,3},{1,2},{2,1},{3,0},{4,7},{5,6},{6,5},{7,4},{8,11},{9,10},{10,... | collective-permute-start | bytes 589832 | tf_op jit(solution)/shard_map/ppermute | solution.py:67
  398.6 28.1 %collective-permute-start.33 = (bf16[256,384]{1,0:T(8,128)(2,1)S(1)}, bf16[256,384]{1,0:T(8,128)(2,1)S(1)}, u32[]{:S(2)}, u32[]{:S(2)}) collective-permute-start(bf16[256,384]{1,0:T(8,128)(2,1)S(1)} %get-tuple-element.151), channel_id=1, source_target_pairs={{0,2},{1,3},{2,0},{3,1},{4,6},{5,7},{6,4},{7,5},{8,10},{9,11},{10,... | collective-permute-start | bytes 589832 | tf_op jit(solution)/shard_map/ppermute | solution.py:67
  403.4 25.9 %collective-permute-start.32 = (bf16[256,384]{1,0:T(8,128)(2,1)S(1)}, bf16[256,384]{1,0:T(8,128)(2,1)S(1)}, u32[]{:S(2)}, u32[]{:S(2)}) collective-permute-start(bf16[256,384]{1,0:T(8,128)(2,1)S(1)} %get-tuple-element.152), channel_id=1, source_target_pairs={{0,1},{1,0},{2,3},{3,2},{4,5},{5,4},{6,7},{7,6},{8,9},{9,8},{10,11... | collective-permute-start | bytes 589832 | tf_op jit(solution)/shard_map/ppermute | solution.py:67
  429.4 38.5 %collective-permute-start.37 = (bf16[256,384]{1,0:T(8,128)(2,1)S(1)}, bf16[256,384]{1,0:T(8,128)(2,1)}, u32[]{:S(2)}, u32[]{:S(2)}) collective-permute-start(bf16[256,384]{1,0:T(8,128)(2,1)S(1)} %get-tuple-element.146), channel_id=1, source_target_pairs={{0,12},{4,8},{8,4},{12,0},{1,13},{5,9},{9,5},{13,1},{2,14},{6,10},... | collective-permute-start | bytes 589832 | tf_op jit(solution)/shard_map/ppermute | solution.py:67
  441.7 19.6 %collective-permute-start.63 = (bf16[256,768]{1,0:T(8,128)(2,1)S(1)}, bf16[256,768]{1,0:T(8,128)(2,1)S(1)}, u32[]{:S(2)}, u32[]{:S(2)}) collective-permute-start(bf16[256,768]{1,0:T(8,128)(2,1)S(1)} %fusion.50), channel_id=1, source_target_pairs={{0,4},{4,0},{8,12},{12,8},{1,5},{5,1},{9,13},{13,9},{2,6},{6,2},{1... | collective-permute-start | bytes 1179656 | tf_op jit(solution)/shard_map/ppermute | solution.py:67
  444.6 15.8 %collective-permute-start.68 = (bf16[256,768]{1,0:T(8,128)(2,1)S(1)}, bf16[256,768]{1,0:T(8,128)(2,1)S(1)}, u32[]{:S(2)}, u32[]{:S(2)}) collective-permute-start(bf16[256,768]{1,0:T(8,128)(2,1)S(1)} %add_convert_fusion), channel_id=1, source_target_pairs={{0,4},{4,0},{8,12},{12,8},{1,5},{5,1},{9,13},{13,9},{2,6},{6,2},{1... | collective-permute-start | bytes 1179656 | tf_op jit(solution)/shard_map/ppermute | solution.py:67
  450.7 18.4 %collective-permute-start.36 = (bf16[256,384]{1,0:T(8,128)(2,1)S(1)}, bf16[256,384]{1,0:T(8,128)(2,1)}, u32[]{:S(2)}, u32[]{:S(2)}) collective-permute-start(bf16[256,384]{1,0:T(8,128)(2,1)S(1)} %get-tuple-element.147), channel_id=1, source_target_pairs={{0,8},{4,12},{8,0},{12,4},{1,9},{5,13},{9,1},{13,5},{2,10},{6,14},... | collective-permute-start | bytes 589832 | tf_op jit(solution)/shard_map/ppermute | solution.py:67
  462.6 17.7 %collective-permute-start.71 = (bf16[256,384]{1,0:T(8,128)(2,1)S(1)}, bf16[256,384]{1,0:T(8,128)(2,1)S(1)}, u32[]{:S(2)}, u32[]{:S(2)}) collective-permute-start(bf16[256,384]{1,0:T(8,128)(2,1)S(1)} %get-tuple-element.124), channel_id=1, source_target_pairs={{0,3},{1,2},{2,1},{3,0},{4,7},{5,6},{6,5},{7,4},{8,11},{9,10},{10,... | collective-permute-start | bytes 589832 | tf_op jit(solution)/shard_map/ppermute | solution.py:67
  462.7 17.6 %collective-permute-start.70 = (bf16[256,384]{1,0:T(8,128)(2,1)S(1)}, bf16[256,384]{1,0:T(8,128)(2,1)}, u32[]{:S(2)}, u32[]{:S(2)}) collective-permute-start(bf16[256,384]{1,0:T(8,128)(2,1)S(1)} %get-tuple-element.125), channel_id=1, source_target_pairs={{0,2},{1,3},{2,0},{3,1},{4,6},{5,7},{6,4},{7,5},{8,10},{9,11},{10,... | collective-permute-start | bytes 589832 | tf_op jit(solution)/shard_map/ppermute | solution.py:67
  471.0 26.2 %collective-permute-start.38 = (bf16[1024,384]{1,0:T(8,128)(2,1)S(1)}, bf16[1024,384]{1,0:T(8,128)(2,1)S(1)}, u32[]{:S(2)}, u32[]{:S(2)}) collective-permute-start(bf16[1024,384]{1,0:T(8,128)(2,1)S(1)} %pad_maximum_fusion.11.refs_0_), channel_id=1, source_target_pairs={{0,16},{16,0},{1,17},{17,1},{2,18},{18,2},{3,19},{19,3},{4,20},{20... | collective-permute-start | bytes 2359304 | tf_op jit(solution)/shard_map/ppermute | solution.py:67
  490.7 52.5 %collective-permute-start.75 = (bf16[1024,384]{1,0:T(8,128)(2,1)S(1)}, bf16[1024,384]{1,0:T(8,128)(2,1)}, u32[]{:S(2)}, u32[]{:S(2)}) collective-permute-start(bf16[1024,384]{1,0:T(8,128)(2,1)S(1)} %pad_maximum_fusion.16.refs_0_), channel_id=1, source_target_pairs={{0,16},{16,0},{1,17},{17,1},{2,18},{18,2},{3,19},{19,3},{4,20},{20... | collective-permute-start | bytes 2359304 | tf_op jit(solution)/shard_map/ppermute | solution.py:67
  495.9 80.3 %collective-permute-start.76 = (bf16[192,2048]{1,0:T(8,128)(2,1)}, bf16[192,2048]{1,0:T(8,128)(2,1)}, u32[]{:S(2)}, u32[]{:S(2)}) collective-permute-start(bf16[192,2048]{1,0:T(8,128)(2,1)} %reduce-scatter.3.cloned.1.call-done), channel_id=1, source_target_pairs={{0,16},{16,0},{1,17},{17,1},{2,18},{18,2},{3,19},{19,3},{4,20},{20... | collective-permute-start | bytes 2359304 | tf_op jit(solution)/shard_map/ppermute | solution.py:67
  (83 other events, 744.3 us)
Sparse Core Ops, SparseCore 0:
  13.1 78.2 all-gather.4
  93.6 27.5 all-gather.6
  123.4 62.1 all-gather.8
  187.7 38.1 all-gather.10
  375.9 100.2 reduce-scatter.2
  478.3 97.7 reduce-scatter.4

commit v2 on v1

v2 whole, which is shorter than its diff:
```python
import jax
import jax.numpy as jnp
from jax import lax
from jax.experimental import pallas as pl
from jax.experimental.pallas import tpu as pltpu
from jax.sharding import PartitionSpec as P

EPSILON = 1e-06
FAR = 1e30
LANES = 128
BF = jnp.bfloat16
F32 = jnp.float32


def dot(left, right, dims=((1,), (0,))):
    return lax.dot_general(left, right, (dims, ((), ())), preferred_element_type=F32)


NT = ((1,), (1,))
TN = ((0,), (0,))


def three_parts(values):
    one = lax.reduce_precision(values, 8, 7)
    two = lax.reduce_precision(values - one, 8, 7)
    three = lax.reduce_precision(values - one - two, 8, 7)
    return one, two, three


def pick_small(lookup, indices):
    width = lookup.shape[0]
    matches = indices[:, None] == jnp.arange(width, dtype=jnp.int32)[None, :]
    return jnp.sum(jnp.where(matches, lookup[None, :], 0), axis=1)


def stream_tables(lengths, dealing):
    width = lengths.shape[0]
    numbers = jnp.arange(width, dtype=jnp.int32)
    given_start = jnp.cumsum(lengths) - lengths
    owners = jnp.sum(jnp.where(dealing[None, :] == numbers[:, None], numbers[None, :], 0), axis=1)
    dealt_length = pick_small(lengths, owners)
    dealt_start = jnp.cumsum(dealt_length) - dealt_length
    return (given_start, owners, dealt_start, dealt_length)


def dealt_sources(lengths, dealing, places):
    given_start, owners, dealt_start, unused = stream_tables(lengths, dealing)
    slot_ids = jnp.sum((dealt_start[None, :] <= places[:, None]).astype(jnp.int32), axis=1) - 1
    return (
        pick_small(given_start, pick_small(owners, slot_ids))
        + places
        - pick_small(dealt_start, slot_ids)
    )


def given_targets(lengths, dealing, places):
    given_start, unused, dealt_start, unused = stream_tables(lengths, dealing)
    member = jnp.sum((given_start[None, :] <= places[:, None]).astype(jnp.int32), axis=1) - 1
    return (
        pick_small(dealt_start, pick_small(dealing, member))
        + places
        - pick_small(given_start, member)
    )


def swap(values, axis, step):
    return lax.ppermute(values, axis, [(at, at ^ step) for at in range(lax.axis_size(axis))])


def spread_plane(pieces):
    return [pieces[0]] + [swap(pieces[k], "tx", k) for k in (1, 2, 3)]


def spread_line(pieces):
    return [pieces[0]] + [swap(pieces[k], "ty", k) for k in (1, 2, 3)]


def pairs_sum(parts):
    return (parts[0] + parts[1]) + (parts[2] + parts[3])


def tie(*groups):
    return lax.optimization_barrier(groups)


def gather_rows(top, low, beside=None, ahead=None):
    top_x, low_y = swap(top, "tx", 1), swap(low, "tx", 2)
    low_x, top_y = swap(low, "tx", 1), swap(top, "tx", 2)
    top_x, low_y, ahead = tie(top_x, low_y, ahead)
    top_d, low_d = swap(top_x, "tx", 2), swap(low_y, "tx", 1)
    done = None if beside is None else beside((top_x, ahead))
    return [top, low, top_x, low_x, top_y, low_y, top_d, low_d], done


def scatter_products(lefts, weights, beside=None):
    a3, a1, a2, a0 = half_products(0, (3, 1, 2, 0), lefts, weights)
    arrays, a3, a1 = tie([array for array, unused in lefts], a3, a1)
    lefts = [(array, lead) for array, (unused, lead) in zip(arrays, lefts)]
    a3, a1 = swap(a3, "tx", 1), swap(a1, "tx", 1)
    b3, b2, b1, b0 = half_products(1, (3, 2, 1, 0), lefts, weights)
    a3, b3, b2 = tie(a3, b3, b2)
    b3, b2 = swap(b3, "tx", 2), swap(b2, "tx", 2)
    send_a2 = (a2 + a3.astype(F32)).astype(BF)
    send_b1 = (b1 + b3.astype(F32)).astype(BF)
    done = None if beside is None else beside(send_b1)
    a2, b1 = swap(send_a2, "tx", 2), swap(send_b1, "tx", 1)
    a1, a2, b1, b2, done = tie(a1, a2, b1, b2, done)
    return [a0, a1, a2, b0, b1, b2], done


def summed(part):
    return lax.psum_scatter(part, ("ty", "dp"), scatter_dimension=0, tiled=True)


def reduce_end(piece):
    if lax.axis_size("dp") != 2:
        return lax.all_gather(piece, "dp", axis=0, tiled=True).astype(F32)
    other = swap(piece, "dp", 1)
    lower = lax.axis_index("dp") == 0
    return jnp.concatenate(
        [jnp.where(lower, piece, other), jnp.where(lower, other, piece)], axis=0
    ).astype(F32)


def cost(flops, bytes_accessed):
    return pl.CostEstimate(flops=flops, bytes_accessed=bytes_accessed, transcendentals=0)


LIMIT = pltpu.CompilerParams(vmem_limit_bytes=50 * 2**20)
ALONE = pltpu.CompilerParams(vmem_limit_bytes=60 * 2**20)


def part_kernel(order, count, *refs):
    lefts, rights, outs = refs[:count], refs[count : 2 * count], refs[2 * count :]
    total = 0.0
    for left, right in zip(lefts, rights):
        rows = left[...]
        total += dot(rows.reshape(rows.shape[-2:]), right[...], NT)
    piece = outs[0].shape[0]
    for at, out in zip(order, outs):
        out[...] = total[at * piece : (at + 1) * piece].astype(out.dtype)


def half_products(half_at, order, lefts, weights):
    row_total, feature = lefts[0][0].shape[-2], weights[0][0].shape[0]
    piece, half, block = row_total // 4, feature // 2, 256
    first = half_at * half // block
    left_specs, right_specs = [], []
    flops = 0
    for (array, lead), (weight, width, at) in zip(lefts, weights):
        if lead is None:
            left_specs.append(pl.BlockSpec((row_total, width), lambda i: (0, 0)))
        else:
            left_specs.append(
                pl.BlockSpec((1, row_total, width), lambda i, lead=lead: (lead, 0, 0))
            )
        right_specs.append(pl.BlockSpec((block, width), lambda i, at=at: (first + i, at)))
        flops += 2 * row_total * half * width
    return pl.pallas_call(
        lambda *refs: part_kernel(order, len(lefts), *refs),
        grid=(half // block,),
        in_specs=left_specs + right_specs,
        out_specs=[pl.BlockSpec((piece, block), lambda i: (0, i))] * 4,
        out_shape=[jax.ShapeDtypeStruct((piece, half), BF)] * 2
        + [jax.ShapeDtypeStruct((piece, half), F32)] * 2,
        compiler_params=LIMIT,
        cost_estimate=cost(flops, flops // 500),
    )(*[a for a, unused in lefts], *[w for w, *unused in weights])


def row_kernel(left, right, out):
    width = right.shape[2]
    for n in range(2):
        out[:, n * width : (n + 1) * width] = dot(left[...], right[n], TN).astype(BF)


def row_products(left, right):
    row_total, feature = left.shape
    width, block = right.shape[2], 256
    flops = 4 * row_total * feature * width
    return pl.pallas_call(
        row_kernel,
        grid=(feature // block,),
        in_specs=[
            pl.BlockSpec((row_total, block), lambda i: (0, i)),
            pl.BlockSpec(right.shape, lambda i: (0, 0, 0)),
        ],
        out_specs=pl.BlockSpec((block, 2 * width), lambda i: (i, 0)),
        out_shape=jax.ShapeDtypeStruct((feature, 2 * width), BF),
        compiler_params=LIMIT,
        cost_estimate=cost(flops, flops // 500),
    )(left, right)


def join_kernel(*refs):
    join(refs[:8], refs[8])


def joined(pieces):
    rows, feature = pieces[0].shape
    block = feature // 4
    return pl.pallas_call(
        join_kernel,
        grid=(4,),
        in_specs=[pl.BlockSpec((rows, block), lambda i: (0, i))] * 8,
        out_specs=pl.BlockSpec((8 * rows, block), lambda i: (0, i)),
        out_shape=jax.ShapeDtypeStruct((8 * rows, feature), BF),
        compiler_params=ALONE,
        cost_estimate=cost(1, 6 * 2**20),
    )(*pieces)


def turned_kernel(left, right, out):
    out[...] = dot(left[...], right[...], TN).astype(BF)


def turned_products(left, right):
    row_total, feature = right.shape
    width, block = left.shape[1], feature // 4
    flops = 2 * row_total * feature * width
    return pl.pallas_call(
        turned_kernel,
        grid=(4,),
        in_specs=[
            pl.BlockSpec((row_total, width), lambda i: (0, 0)),
            pl.BlockSpec((row_total, block), lambda i: (0, i)),
        ],
        out_specs=pl.BlockSpec((width, block), lambda i: (i, 0)),
        out_shape=jax.ShapeDtypeStruct((4 * width, block), BF),
        compiler_params=LIMIT,
        cost_estimate=cost(flops, flops // 500),
    )(left, right)


def attn_kernel(h_ref, z_ref, d_ref, g_ref, y_ref, out):
    total, width = d_ref.shape[1], y_ref.shape[1]
    normed = h_ref[...]
    out[:, :total] = dot(normed, d_ref[...], TN).astype(BF)
    out[:, total : total + width] = dot(normed, g_ref[...], TN).astype(BF)
    out[:, total + width :] = dot(y_ref[...], z_ref[...], TN).astype(BF)


def attn_products(first_normed, grad_first, grad_gate, grad_z, gated):
    row_total, feature = first_normed.shape
    total, width = grad_first.shape[1], gated.shape[1]
    block = feature // 4
    column = pl.BlockSpec((row_total, block), lambda i: (0, i))

    def whole(columns):
        return pl.BlockSpec((row_total, columns), lambda i: (0, 0))

    return pl.pallas_call(
        attn_kernel,
        grid=(4,),
        in_specs=[column, column, whole(total), whole(width), whole(width)],
        out_specs=pl.BlockSpec((block, total + 2 * width), lambda i: (i, 0)),
        out_shape=jax.ShapeDtypeStruct((feature, total + 2 * width), BF),
        compiler_params=LIMIT,
        cost_estimate=cost(2 * row_total * feature * (total + 2 * width), 16 * 2**20),
    )(first_normed, grad_z, grad_first, grad_gate, gated)


def place_kernel(at, *refs):
    ins, outs = refs[:4], refs[4:]
    width, half = ins[0].shape[1], outs[0].shape[0]
    for k in range(4):
        columns = pl.ds(pl.multiple_of((at[0] ^ k) * width, LANES), width)
        for n, out in enumerate(outs):
            out[:, columns] = ins[k][n * half : (n + 1) * half, :]


def placed(pieces, start):
    rows, width = pieces[0].shape
    return pl.pallas_call(
        place_kernel,
        grid_spec=pltpu.PrefetchScalarGridSpec(
            num_scalar_prefetch=1,
            grid=(1,),
            in_specs=[pl.BlockSpec((rows, width), lambda i, at: (0, 0))] * 4,
            out_specs=[pl.BlockSpec((rows // 2, 4 * width), lambda i, at: (0, 0))] * 2,
        ),
        out_shape=[jax.ShapeDtypeStruct((rows // 2, 4 * width), BF)] * 2,
        compiler_params=ALONE,
        cost_estimate=cost(1, 4 * 2**20),
    )(start.astype(jnp.int32)[None], *pieces)


def reorder_kernel(at, *refs):
    count = len(refs) // 4 - 1
    rows = refs[0].shape[0]
    for k in range(4):
        for n in range(4):

            @pl.when((at[0] ^ k) == n)
            def copy(k=k, n=n):
                for m in range(count):
                    refs[4 * count + k][m * rows : (m + 1) * rows, :] = refs[4 * m + n][...]


def reordered(sets, start):
    rows, width = sets[0][0].shape
    total = rows * len(sets)
    return pl.pallas_call(
        reorder_kernel,
        grid_spec=pltpu.PrefetchScalarGridSpec(
            num_scalar_prefetch=1,
            grid=(1,),
            in_specs=[pl.BlockSpec((rows, width), lambda i, at: (0, 0))] * (4 * len(sets)),
            out_specs=[pl.BlockSpec((total, width), lambda i, at: (0, 0))] * 4,
        ),
        out_shape=[jax.ShapeDtypeStruct((total, width), BF)] * 4,
        compiler_params=ALONE,
        cost_estimate=cost(1, 4 * 2**20),
    )(start.astype(jnp.int32)[None], *[p for pieces in sets for p in pieces])


def half_sums(parts):
    a0, a1, a2, b0, b1, b2 = (p[...].astype(F32) for p in parts)
    return jnp.concatenate([a0 + a1 + a2, b0 + b1 + b2], axis=1)


def mean_scale(rows):
    return lax.rsqrt(jnp.mean(rows * rows, axis=1, keepdims=True) + EPSILON)


def norm_backward(grad, rows, gain):
    scale = mean_scale(rows)
    normed = rows * scale
    grad_normed = grad * gain
    inner = jnp.mean(grad_normed * normed, axis=1, keepdims=True)
    return scale * (grad_normed - normed * inner)


def put_halves(value, top, low):
    step = pl.program_id(0)

    @pl.when(step < 2)
    def first():
        top[...] = value

    @pl.when(step >= 2)
    def second():
        low[...] = value


def put_quarters(lane, value, outs, held):
    held[...] = value
    width = outs[0].shape[1]
    for k, out in enumerate(outs):
        out[...] = held[:, pl.ds(pl.multiple_of((lane ^ k) * width, LANES), width)]


def either(top, low):
    return jnp.where(pl.program_id(0) < 2, top[...].astype(F32), low[...].astype(F32))


def up_norm_kernel(where, x_top, x_low, gain_ref, *refs):
    second = either(x_top, x_low) + half_sums(refs[:6])
    refs[6][...] = second
    put_halves((second * mean_scale(second) * gain_ref[1:2, :]).astype(BF), refs[7], refs[8])


def down_norm_kernel(where, second_ref, grad_top, grad_low, gain_ref, *refs):
    grad = either(grad_top, grad_low) + norm_backward(
        half_sums(refs[:6]), second_ref[...], gain_ref[1:2, :]
    )
    refs[6][...] = grad
    put_halves(grad.astype(BF), refs[7], refs[8])


def result_kernel(where, second_ref, *refs):
    result = second_ref[...] + half_sums(refs[:6])
    put_quarters(where[2], result.astype(BF), refs[6:10], refs[10])


def input_norm_kernel(where, x_top, x_low, grad_ref, gain_ref, *refs):
    grad = grad_ref[...] + norm_backward(
        half_sums(refs[:6]), either(x_top, x_low), gain_ref[0:1, :]
    )
    put_quarters(where[2], grad.astype(BF), refs[6:10], refs[10])


def on_rows(kernel, where, rows, gains, parts, quarters):
    feature = gains.shape[1] if gains is not None else rows[0].shape[1]
    row_total = parts[0].shape[0]
    block = row_total // 4

    def spec(width):
        return pl.BlockSpec((block, width), lambda i, *_: (i, 0))

    top = pl.BlockSpec((block, feature), lambda i, *_: (jnp.minimum(i, 1), 0))
    low = pl.BlockSpec((block, feature), lambda i, *_: (jnp.maximum(i - 2, 0), 0))
    ins, args = [], []
    for r in rows:
        if isinstance(r, (list, tuple)):
            ins += [top, low]
            args += list(r)
        else:
            ins.append(spec(feature))
            args.append(r)
    if gains is not None:
        ins.append(pl.BlockSpec(gains.shape, lambda i, *_: (0, 0)))
    ins += [spec(feature // 2)] * 6
    if quarters:
        outs = [spec(feature // 4)] * 4
        shapes = [jax.ShapeDtypeStruct((row_total, feature // 4), BF)] * 4
        scratch = [pltpu.VMEM((block, feature), BF)]
    else:
        outs = [spec(feature), top, low]
        shapes = [jax.ShapeDtypeStruct((row_total, feature), F32)]
        shapes += [jax.ShapeDtypeStruct((2 * block, feature), BF)] * 2
        scratch = []
    return pl.pallas_call(
        kernel,
        grid_spec=pltpu.PrefetchScalarGridSpec(
            num_scalar_prefetch=1,
            grid=(4,),
            in_specs=ins,
            out_specs=outs,
            scratch_shapes=scratch,
        ),
        out_shape=shapes,
        compiler_params=ALONE,
        cost_estimate=cost(1, 6 * 2**20),
    )(where, *args, *([] if gains is None else [gains]), *parts)


def first_kernel(heads, pieces, w_ref, wf_ref, b_ref, h_ref, qkv_ref, keep_ref, slope_ref, gain_ref):
    step = pl.program_id(0)

    @pl.when(step == 0)
    def norm():
        turned = wf_ref[...].astype(F32).T
        for n in range(2):
            first = heads + 3 * n
            gain_ref[n : n + 1, :] = (
                turned[first : first + 1] + turned[first + 1 : first + 2] + turned[first + 2 : first + 3]
            )
        block = pieces[0].shape[0]
        for at in range(8):
            x = pieces[at][...].astype(F32)
            h_ref[pl.ds(at * block, block), :] = (x * mean_scale(x) * gain_ref[0:1, :]).astype(BF)

    pre = dot(h_ref[...], w_ref[...])
    qkv_ref[...] = pre.astype(BF)

    @pl.when(step == 4)
    def forget():
        real = lanes_of(pre.shape[0]) < heads
        forget_pre = jnp.where(real, pre[:, LANES:] + b_ref[...], 0.0)
        less = jnp.exp(-jnp.abs(forget_pre))
        keep_ref[...] = jnp.minimum(forget_pre, 0.0) - jnp.log1p(less)
        slope_ref[...] = jnp.where(
            real, jnp.where(forget_pre >= 0, less, 1.0) / (1.0 + less), 0.0
        )


def first_products(heads, pieces, weights, bias):
    row_total, feature = 8 * pieces[0].shape[0], pieces[0].shape[1]
    block = 256

    def whole_block(shape):
        return pl.BlockSpec(shape, lambda i: (0, 0))

    def spec(shape, at):
        return pl.BlockSpec(shape, at)

    def kernel(*refs):
        first_kernel(heads, refs[:8], *refs[8:])

    return pl.pallas_call(
        kernel,
        grid=(5,),
        in_specs=[whole_block(p.shape) for p in pieces]
        + [
            spec((feature, block), lambda i: (0, i)),
            spec((feature, LANES), lambda i: (0, 9)),
            whole_block((1, LANES)),
        ],
        out_specs=[
            whole_block((row_total, feature)),
            spec((row_total, block), lambda i: (0, i)),
            whole_block((row_total, LANES)),
            whole_block((row_total, LANES)),
            whole_block((8, feature)),
        ],
        out_shape=[
            jax.ShapeDtypeStruct((row_total, feature), BF),
            jax.ShapeDtypeStruct((row_total, 5 * block), BF),
            jax.ShapeDtypeStruct((row_total, LANES), F32),
            jax.ShapeDtypeStruct((row_total, LANES), F32),
            jax.ShapeDtypeStruct((8, feature), F32),
        ],
        compiler_params=ALONE,
        cost_estimate=cost(14 * row_total * feature * block, 16 * 2**20),
    )(*pieces, weights, weights, bias)


def gate_kernel(h_ref, w_ref, att_ref, gate_ref, y_ref):
    gate = jax.nn.sigmoid(dot(h_ref[...], w_ref[...]))
    gate_ref[...] = gate
    y_ref[...] = (att_ref[...] * gate).astype(BF)


def gate_products(first_normed, weights, attended):
    row_total, feature = first_normed.shape
    width = attended.shape[1]

    def by_rows(columns):
        return pl.BlockSpec((row_total // 4, columns), lambda i: (i, 0))

    return pl.pallas_call(
        gate_kernel,
        grid=(4,),
        in_specs=[
            by_rows(feature),
            pl.BlockSpec((feature, width), lambda i: (0, 0)),
            by_rows(width),
        ],
        out_specs=[by_rows(width)] * 2,
        out_shape=[
            jax.ShapeDtypeStruct((row_total, width), F32),
            jax.ShapeDtypeStruct((row_total, width), BF),
        ],
        compiler_params=LIMIT,
        cost_estimate=cost(2 * row_total * feature * width, 10 * 2**20),
    )(first_normed, weights, attended)


def join(pieces, whole):
    block = pieces[0].shape[0]
    for at in range(8):
        whole[pl.ds(at * block, block), :] = pieces[at][...]


def up_kernel(*refs):
    pieces, (g_ref, u_ref, h_ref, m_ref, to_gate_ref, to_up_ref) = refs[:8], refs[8:]

    @pl.when(pl.program_id(0) == 0)
    def first():
        join(pieces, h_ref)

    gate = dot(h_ref[...], g_ref[...])
    up = dot(h_ref[...], u_ref[...])
    sig = jax.nn.sigmoid(gate)
    silu = gate * sig
    m_ref[...] = (silu * up).astype(BF)
    to_gate_ref[...] = (up * sig * (1.0 + gate * (1.0 - sig))).astype(to_gate_ref.dtype)
    to_up_ref[...] = silu.astype(to_up_ref.dtype)


def up_products(pieces, weights):
    row_total, feature = 8 * pieces[0].shape[0], pieces[0].shape[1]
    hidden, block = weights.shape[1] // 2, 256
    steps = hidden // block
    out = pl.BlockSpec((row_total, block), lambda i: (0, i))
    return pl.pallas_call(
        up_kernel,
        grid=(steps,),
        in_specs=[pl.BlockSpec(p.shape, lambda i: (0, 0)) for p in pieces]
        + [
            pl.BlockSpec((feature, block), lambda i: (0, i)),
            pl.BlockSpec((feature, block), lambda i: (0, steps + i)),
        ],
        out_specs=[pl.BlockSpec((row_total, feature), lambda i: (0, 0))] + [out] * 3,
        out_shape=[
            jax.ShapeDtypeStruct((row_total, feature), BF),
            jax.ShapeDtypeStruct((row_total, hidden), BF),
            jax.ShapeDtypeStruct((row_total, hidden), BF),
            jax.ShapeDtypeStruct((row_total, hidden), BF),
        ],
        compiler_params=ALONE,
        cost_estimate=cost(4 * row_total * feature * hidden, 20 * 2**20),
    )(*pieces, weights, weights)


def down_kernel(g_ref, w_ref, to_gate_ref, to_up_ref, out_ref):
    grad = dot(g_ref[...], w_ref[...])
    out_ref[0] = (grad * to_gate_ref[...]).astype(BF)
    out_ref[1] = (grad * to_up_ref[...]).astype(BF)


def down_products(grad_out, weights, to_gate, to_up):
    row_total, feature = grad_out.shape
    hidden, block = weights.shape[1], 256
    column = pl.BlockSpec((row_total, block), lambda i: (0, i))
    return pl.pallas_call(
        down_kernel,
        grid=(hidden // block,),
        in_specs=[
            pl.BlockSpec((row_total, feature), lambda i: (0, 0)),
            pl.BlockSpec((feature, block), lambda i: (0, i)),
            column,
            column,
        ],
        out_specs=pl.BlockSpec((2, row_total, block), lambda i: (0, 0, i)),
        out_shape=jax.ShapeDtypeStruct((2, row_total, hidden), BF),
        compiler_params=LIMIT,
        cost_estimate=cost(2 * row_total * feature * hidden, 16 * 2**20),
    )(grad_out, weights, to_gate, to_up)


def back_kernel(*refs):
    pieces, (w_ref, gate_ref, att_ref, z_ref, datt_ref, dgate_ref) = refs[:8], refs[8:]
    block = pieces[0].shape[0]
    for at in range(4):

        @pl.when(pl.program_id(0) == at)
        def put(at=at):
            z_ref[:block, :] = pieces[2 * at][...]
            z_ref[block:, :] = pieces[2 * at + 1][...]

    grad = dot(z_ref[...], w_ref[...])
    gate = gate_ref[...]
    datt_ref[...] = (grad * gate).astype(BF)
    dgate_ref[...] = (grad * att_ref[...] * gate * (1.0 - gate)).astype(BF)


def back_products(pieces, weights, gate, attended):
    row_total, feature = 8 * pieces[0].shape[0], pieces[0].shape[1]
    width = attended.shape[1]

    def spec(shape, at=0):
        return pl.BlockSpec(shape, lambda i: (0, at))

    def by_rows(columns):
        return pl.BlockSpec((row_total // 4, columns), lambda i: (i, 0))

    return pl.pallas_call(
        back_kernel,
        grid=(4,),
        in_specs=[spec(p.shape) for p in pieces]
        + [spec((feature, width), 1), by_rows(width), by_rows(width)],
        out_specs=[by_rows(feature), by_rows(width), by_rows(width)],
        out_shape=[
            jax.ShapeDtypeStruct((row_total, feature), BF),
            jax.ShapeDtypeStruct((row_total, width), BF),
            jax.ShapeDtypeStruct((row_total, width), BF),
        ],
        compiler_params=ALONE,
        cost_estimate=cost(2 * row_total * feature * width, 10 * 2**20),
    )(*pieces, weights, gate, attended)


def slot_tables(lengths, dealing, stream):
    width = lengths.shape[1]
    given, slot_of = [], []
    start = jnp.int32(0)
    for g in range(width):
        given.append(start)
        start = start + lengths[stream, g]
        slot_of.append(dealing[stream, g])
    dealt, given_at = [], []
    start = jnp.int32(0)
    for k in range(width):
        dealt.append(start)
        here = jnp.int32(0)
        for g in range(width):
            here = jnp.where(slot_of[g] == k, given[g], here)
            start = start + jnp.where(slot_of[g] == k, lengths[stream, g], 0)
        given_at.append(here)
    return given, slot_of, dealt, given_at


def pick_kernel(backward, where, lengths, dealing, *refs):
    count = 2
    column, row = where[0], where[1]
    row_total = refs[0].shape[0] // (2 if backward else 1)
    block = row_total // 4
    step = pl.program_id(0)
    given, slot_of, dealt, given_at = slot_tables(lengths, dealing, column)
    within = lax.broadcasted_iota(jnp.int32, (block, 1), 0)
    if backward:
        places = row * row_total + step * block + within
        moves = []
        for g in range(len(given)):
            there = jnp.int32(0)
            for k in range(len(given)):
                there = jnp.where(slot_of[g] == k, dealt[k], there)
            moves.append((given[g], there - given[g]))
    else:
        places = row * row_total + (step ^ column) * block + within
        moves = [(s, g - s) for s, g in zip(dealt, given_at)]
    move = jnp.zeros_like(places) + moves[0][1]
    for first, by in moves[1:]:
        move = jnp.where(places >= first, by, move)
    near = places + move - row * row_total
    near = jnp.where(near < 0, near + 2 * row_total, near)
    if backward:
        other = jnp.where(near >= row_total, row_total, 0)
        local = near - other
        part = sum(jnp.where(local >= k * block, 1, 0) for k in (1, 2, 3))
        near = other + local + (jnp.bitwise_xor(part, column) - part) * block
    across = lax.broadcasted_iota(jnp.int32, (block, 2 * row_total), 1)
    chosen = jnp.where(across == near, 1.0, 0.0).astype(BF)
    for at in range(count):
        if backward:
            picked = 0.0
            for n in range(2):
                for k in range(4):
                    first = (4 * n + k) * block
                    picked += dot(
                        chosen[:, first : first + block],
                        refs[n][(2 * k + at) * block : (2 * k + at + 1) * block, :],
                    )
            refs[2 + at][...] = picked.astype(BF)
        else:
            own, other = refs[2 * at][...], refs[2 * at + 1][...]
            picked = dot(chosen[:, :row_total], own) + dot(chosen[:, row_total:], other)
            picked = picked.astype(BF)
            for k in range(4):

                @pl.when(step == k)
                def put(k=k, at=at, picked=picked):
                    refs[2 * count + 4 * at + k][...] = picked


def moved_rows(backward, where, lengths, dealing, arrays):
    row_total, width = arrays[0].shape
    if backward:
        row_total = row_total // 2
    block = row_total // 4
    if lax.axis_size("dp") != 2:
        column, row = where[0], where[1]
        local = jnp.arange(row_total, dtype=jnp.int32)
        own_lengths = lax.dynamic_index_in_dim(lengths, column, 0, keepdims=False)
        own_dealing = lax.dynamic_index_in_dim(dealing, column, 0, keepdims=False)
        if backward:
            to = given_targets(own_lengths, own_dealing, row * row_total + local)
            at = to % row_total
            to = to - at + ((at // block) ^ column) * block + at % block
            both = arrays[0].reshape(4, 2, block, width).transpose(1, 0, 2, 3)
            arrays = [half.reshape(row_total, width) for half in both]
        else:
            swapped = (((local // block) ^ column) * block) + local % block
            to = dealt_sources(own_lengths, own_dealing, row * row_total + swapped)
        moved = [jnp.take(lax.all_gather(a, "dp", axis=0, tiled=True), to, axis=0) for a in arrays]
        if backward:
            return moved
        return [m[k * block : (k + 1) * block] for m in moved for k in range(4)]
    if backward:
        outs = [pl.BlockSpec((block, width), lambda i, *_: (i, 0))] * 2
        shapes = [jax.ShapeDtypeStruct((row_total, width), BF)] * 2
    else:
        outs = [pl.BlockSpec((block, width), lambda i, *_: (0, 0))] * 8
        shapes = [jax.ShapeDtypeStruct((block, width), BF)] * 8
    return pl.pallas_call(
        lambda *refs: pick_kernel(backward, *refs),
        grid_spec=pltpu.PrefetchScalarGridSpec(
            num_scalar_prefetch=3,
            grid=(4,),
            in_specs=[pl.BlockSpec(arrays[0].shape, lambda i, *_: (0, 0))] * (2 * len(arrays)),
            out_specs=outs,
        ),
        out_shape=shapes,
        compiler_params=pltpu.CompilerParams(vmem_limit_bytes=40 * 2**20),
        cost_estimate=cost(8 * row_total * row_total * width * 2, 8 * 2**20),
    )(where, lengths, dealing, *[half for a in arrays for half in (a, swap(a, "dp", 1))])


def lanes_of(rows):
    return lax.broadcasted_iota(jnp.int32, (rows, LANES), 1)


def split_column(column):
    one = column.astype(BF).astype(F32)
    two = (column - one).astype(BF).astype(F32)
    return one, two, column - one - two


def fill(lanes, base, columns, rest):
    for at, column in reversed(list(enumerate(columns))):
        rest = jnp.where(lanes == base + at, column, rest)
    return rest


def forward_kernel(
    where,
    lengths,
    dealing,
    q_ref,
    k_ref,
    v_ref,
    keep_ref,
    att_ref,
    qa_ref,
    ka_ref,
    c_ref,
    va_ref,
):
    pair = pl.program_id(0)
    column, row, lane = where[0], where[1], where[2]
    first_length = jnp.int32(0)
    for g in range(lengths.shape[1]):
        first_length += jnp.where(dealing[lane, g] == 2 * row, lengths[lane, g], 0)
    row_total = q_ref.shape[0]
    block = row_total // 4
    lanes = lanes_of(block)

    def rows_of(at):
        return pl.ds(pl.multiple_of((column ^ at) * block, block), block)

    @pl.when(pair == 0)
    def sum_keeps():
        below = lax.broadcasted_iota(jnp.int32, (block, block), 0)
        across = lax.broadcasted_iota(jnp.int32, (block, block), 1)
        ones = jnp.where(below >= across, 1.0, 0.0)
        running = jnp.zeros((1, LANES), F32)
        for at in range(4):
            sums = running + lax.dot_general(
                ones,
                keep_ref[rows_of(at), :],
                (((1,), (0,)), ((), ())),
                precision=lax.Precision.HIGHEST,
                preferred_element_type=F32,
            )
            c_ref[pl.ds(at * block, block), :] = sums
            running = sums[block - 1 :, :]

    for head in range(2):
        mine = (lanes < 64) if head == 0 else (lanes >= 64)
        base = 64 if head == 0 else 0
        for at in range(4):
            rows, own = rows_of(at), pl.ds(at * block, block)
            decay = jnp.sum(
                jnp.where(lanes == 2 * pair + head, c_ref[own, :], 0.0), axis=1, keepdims=True
            )
            one, two, three = split_column(decay)
            places = at * block + lax.broadcasted_iota(jnp.int32, (block, 1), 0)
            second = jnp.where(places >= first_length, 1.0, 0.0)
            q_side = fill(lanes, base, (1.0, 1.0, 1.0, second), 0.0)
            k_side = fill(
                lanes, base, (-one, -two, -three, (second - 1.0) * FAR, 1.0, 1.0, 1.0), 0.0
            )
            qa_ref[head, own, :] = jnp.where(
                mine, q_ref[rows, :].astype(F32) * 0.125, q_side
            ).astype(BF)
            ka_ref[head, own, :] = jnp.where(mine, k_ref[rows, :].astype(F32), k_side).astype(BF)
            va_ref[head, own, :] = jnp.where(mine, v_ref[rows, :].astype(F32), 1.0).astype(BF)

    below = lax.broadcasted_iota(jnp.int32, (block, block), 0)
    across = lax.broadcasted_iota(jnp.int32, (block, block), 1)
    for at in range(4):
        own = pl.ds(at * block, block)
        width = (at + 1) * block
        results = []
        for head in range(2):
            base = 64 if head == 0 else 0
            queries = qa_ref[head, own, :]
            last = jnp.where(
                below >= across, dot(queries, ka_ref[head, at * block : width, :], NT), -FAR
            )
            top = jnp.max(last, axis=1, keepdims=True)
            if at > 0:
                early = dot(queries, ka_ref[head, : at * block, :], NT)
                top = jnp.maximum(top, jnp.max(early, axis=1, keepdims=True))
            total = dot(jnp.exp(last - top).astype(BF), va_ref[head, at * block : width, :])
            if at > 0:
                total += dot(jnp.exp(early - top).astype(BF), va_ref[head, : at * block, :])
            weight = pltpu.roll(total, 64, 1)
            results.append(total / weight)
            log_total = top + jnp.log(total[:, base : base + 1])
            one, two, three = split_column(log_total)
            qa_ref[head, own, :] = fill(
                lanes, base + 4, (-one, -two, -three), queries.astype(F32)
            ).astype(BF)
        attended = jnp.where(lanes < 64, results[0], results[1])
        att_ref[rows_of(at), :] = attended


def attend_forward(where, lengths, dealing, qkv, keep):
    row_total, width = qkv.shape[0], qkv.shape[1] // LANES // 3 * LANES
    pairs = width // LANES
    heads = 2 * pairs

    def columns(first):
        return pl.BlockSpec((row_total, LANES), lambda p, *_: (0, first + p))

    sided = pl.BlockSpec((2, row_total, LANES), lambda p, *_: (p, 0, 0))
    return pl.pallas_call(
        forward_kernel,
        grid_spec=pltpu.PrefetchScalarGridSpec(
            num_scalar_prefetch=3,
            grid=(pairs,),
            in_specs=[
                columns(0),
                columns(pairs),
                columns(2 * pairs),
                pl.BlockSpec((row_total, LANES), lambda p, *_: (0, 0)),
            ],
            out_specs=[columns(0), sided, sided],
            scratch_shapes=[
                pltpu.VMEM((row_total, LANES), F32),
                pltpu.VMEM((2, row_total, LANES), BF),
            ],
        ),
        out_shape=[
            jax.ShapeDtypeStruct((row_total, width), F32),
            jax.ShapeDtypeStruct((heads, row_total, LANES), BF),
            jax.ShapeDtypeStruct((heads, row_total, LANES), BF),
        ],
        compiler_params=pltpu.CompilerParams(vmem_limit_bytes=60 * 2**20),
        cost_estimate=cost(10 * 10**9, 8 * 2**20),
    )(where, lengths, dealing, qkv, qkv, qkv, keep)


def backward_kernel(
    where,
    qa_ref,
    ka_ref,
    v_ref,
    datt_ref,
    att_ref,
    slope_ref,
    out_ref,
    va_ref,
    da_ref,
    kt_ref,
    dk_ref,
    dv_ref,
    dq_ref,
    dc_ref,
):
    pair = pl.program_id(0)
    pairs = pl.num_programs(0)
    column = where[0]
    row_total = v_ref.shape[0]
    block = row_total // 4
    lanes = lanes_of(block)
    width = att_ref.shape[1] * pairs

    def rows_of(at):
        return pl.ds(pl.multiple_of((column ^ at) * block, block), block)

    def lanes_at(group):
        return pl.ds(pl.multiple_of((group * pairs + pair) * LANES, LANES), LANES)

    @pl.when(pair == 0)
    def clear():
        dc_ref[...] = jnp.zeros_like(dc_ref)

    for at in range(4):
        rows, own = rows_of(at), pl.ds(at * block, block)
        grad_att = datt_ref[rows, :].astype(F32)
        inner = grad_att * att_ref[rows, :]
        values = v_ref[rows, :].astype(F32)
        for head in range(2):
            mine = (lanes < 64) if head == 0 else (lanes >= 64)
            base = 64 if head == 0 else 0
            delta = jnp.sum(jnp.where(mine, inner, 0.0), axis=1, keepdims=True)
            one, two, three = split_column(delta)
            da_ref[head, own, :] = jnp.where(
                mine, grad_att, fill(lanes, base, (-one, -two, -three), 0.0)
            ).astype(BF)
            va_ref[head, own, :] = jnp.where(
                mine, values, fill(lanes, base, (1.0, 1.0, 1.0), 0.0)
            ).astype(BF)

    below = lax.broadcasted_iota(jnp.int32, (block, block), 0)
    across = lax.broadcasted_iota(jnp.int32, (block, block), 1)
    for head in range(2):
        for at in range(4):
            own = pl.ds(at * block, block)
            kt_ref[:, own] = ka_ref[head, own, :].astype(F32).T.astype(BF)
        for at in range(4):
            own = pl.ds(at * block, block)
            queries, grads = qa_ref[head, own, :], da_ref[head, own, :]
            dq_t = jnp.zeros((LANES, block), F32)
            for past in range(at + 1):
                keys = pl.ds(past * block, block)
                probs = jnp.exp(dot(ka_ref[head, keys, :], queries, NT))
                if past == at:
                    probs = jnp.where(below <= across, probs, 0.0)
                grad_scores = (probs * dot(va_ref[head, keys, :], grads, NT)).astype(BF)
                dv = dot(probs.astype(BF), grads)
                dk = dot(grad_scores, queries)
                dq_t += dot(kt_ref[:, keys], grad_scores)
                if past == at:
                    dv_ref[head, keys, :] = dv
                    dk_ref[head, keys, :] = dk
                else:
                    dv_ref[head, keys, :] += dv
                    dk_ref[head, keys, :] += dk
            dq_ref[head, own, :] = dq_t.T

    for at in range(4):
        rows, own = rows_of(at), pl.ds(at * block, block)
        for head in range(2):
            base = 64 if head == 0 else 0
            change = (
                dq_ref[head, own, base + 4 : base + 5] - dk_ref[head, own, base : base + 1]
            )
            dc_ref[own, :] += jnp.where(lanes == 2 * pair + head, change, 0.0)
        left = lanes < 64
        for group, ref, scale in ((0, dq_ref, 0.125), (1, dk_ref, 1.0), (2, dv_ref, 1.0)):
            both = jnp.where(left, ref[0, own, :], ref[1, own, :])
            out_ref[rows, lanes_at(group)] = (both * scale).astype(BF)

    @pl.when(pair == pairs - 1)
    def finish():
        ones = jnp.where(below <= across, 1.0, 0.0)
        running = jnp.zeros((1, LANES), F32)
        for at in reversed(range(4)):
            sums = running + lax.dot_general(
                ones,
                dc_ref[pl.ds(at * block, block), :],
                (((1,), (0,)), ((), ())),
                precision=lax.Precision.HIGHEST,
                preferred_element_type=F32,
            )
            running = sums[:1, :]
            rows = rows_of(at)
            out_ref[rows, 3 * width :] = (sums * slope_ref[rows, :]).astype(BF)


def attend_backward(where, qa, ka, qkv, grad_att, attended, slope):
    row_total, width = attended.shape
    pairs = width // LANES
    heads = 2 * pairs
    total = 3 * width + LANES

    def columns(first):
        return pl.BlockSpec((row_total, LANES), lambda p, *_: (0, first + p))

    sided = pl.BlockSpec((2, row_total, LANES), lambda p, *_: (p, 0, 0))
    both = (2, row_total, LANES)
    return pl.pallas_call(
        backward_kernel,
        grid_spec=pltpu.PrefetchScalarGridSpec(
            num_scalar_prefetch=1,
            grid=(pairs,),
            in_specs=[
                sided,
                sided,
                columns(2 * pairs),
                columns(0),
                columns(0),
                pl.BlockSpec((row_total, LANES), lambda p, *_: (0, 0)),
            ],
            out_specs=pl.BlockSpec((row_total, total), lambda p, *_: (0, 0)),
            scratch_shapes=[
                pltpu.VMEM(both, BF),
                pltpu.VMEM(both, BF),
                pltpu.VMEM((LANES, row_total), BF),
                pltpu.VMEM(both, F32),
                pltpu.VMEM(both, F32),
                pltpu.VMEM(both, F32),
                pltpu.VMEM((row_total, LANES), F32),
            ],
        ),
        out_shape=jax.ShapeDtypeStruct((row_total, total), BF),
        compiler_params=pltpu.CompilerParams(vmem_limit_bytes=60 * 2**20),
        cost_estimate=cost(12 * 10**9, 8 * 2**20),
    )(where, qa, ka, qkv, grad_att, attended, slope)


def on_device(
    x_given,
    cotangent,
    seq_lengths,
    seq_deal,
    attn_gain,
    w_query,
    w_key,
    w_value,
    w_ogate,
    w_forget,
    b_forget,
    w_out,
    mlp_gain,
    w_gate,
    w_up,
    w_down,
):
    quarter = x_given.shape[1]
    piece = quarter // 4
    row, column, lane = lax.axis_index("dp"), lax.axis_index("tx"), lax.axis_index("ty")
    heads = w_forget.shape[1]
    width = w_query.shape[1]
    hidden = w_gate.shape[1]
    share = w_query.shape[0] // lax.axis_size("dp")

    def own_share(weights):
        return lax.dynamic_slice_in_dim(weights, row * share, share, axis=0)

    def whole(weights):
        return lax.all_gather(weights, ("ty", "dp"), axis=0, tiled=True)

    gains = jnp.stack(three_parts(attn_gain) + three_parts(mlp_gain), axis=1).astype(BF)
    spare = jnp.zeros((w_query.shape[0], LANES - heads - 6), BF)
    side = 3 * width
    last = side + LANES
    w_first = whole(
        jnp.concatenate(
            [own_share(w) for w in (w_query, w_key, w_value, w_forget, gains, spare)], axis=1
        )
    )

    where = jnp.stack([column, row, lane]).astype(jnp.int32)
    paired = lax.axis_size("dp") == 2

    dealt = moved_rows(False, where, seq_lengths, seq_deal, (x_given[0], cotangent[0]))
    x_parts, grad_parts = tie(spread_plane(dealt[:4]), dealt[4:])
    x_parts, grad_parts = tie(
        spread_line(reordered([x_parts], column ^ lane)), spread_plane(grad_parts)
    )
    grad_parts, x_parts = tie(reordered([grad_parts], column ^ lane), x_parts)
    grad_parts = spread_line(grad_parts)
    x_full, unused = gather_rows(*placed(x_parts, lane), ahead=grad_parts[1])
    w_second = jnp.concatenate([own_share(w_ogate), own_share(w_out.T)], axis=1)
    w_gate_up = jnp.concatenate([own_share(w_gate), own_share(w_up)], axis=1)
    x_full, grad_parts, w_second, w_gate_up = tie(x_full, grad_parts, w_second, w_gate_up)
    w_second, w_gate_up = whole(w_second), whole(w_gate_up)
    grad_rows = placed(grad_parts, lane)

    bias = jnp.pad(b_forget, (0, LANES - heads))[None]
    first_normed, qkv, keep, slope, gains = first_products(heads, x_full, w_first, bias)
    grad_full, (attended, qa, ka) = gather_rows(
        *grad_rows,
        lambda ready: attend_forward(where, seq_lengths, seq_deal, ready[1], keep),
        qkv,
    )
    grad_full, attended = tie(grad_full, attended)
    w_down_t, attended = tie(own_share(w_down.T), attended)
    w_down_t = whole(w_down_t)
    out_gate, gated = gate_products(first_normed, w_second, attended)
    parts, unused = scatter_products([(gated, None)], [(w_second, width, 1)])
    second, top, low = on_rows(up_norm_kernel, where, [x_full[:2]], gains, parts, False)

    h2_parts, grad_full = gather_rows(
        top, low, lambda ready: joined(tie(grad_full, ready)[0])
    )
    h2_parts, w_gate_up = tie(h2_parts, w_gate_up)
    h2_full, mid, to_gate, to_up = up_products(h2_parts, w_gate_up)
    part, grad_full = tie(turned_products(mid, grad_full), grad_full)
    grads_down = summed(part)
    grad_gate_up = down_products(grad_full, w_down_t, to_gate, to_up)

    def gate_up_products(ready):
        left, unused = tie(h2_full, ready)
        return row_products(left, grad_gate_up)

    parts, part = scatter_products(
        [(grad_gate_up, 0), (grad_gate_up, 1)],
        [(w_gate_up, hidden, 0), (w_gate_up, hidden, 1)],
        gate_up_products,
    )
    part, parts = tie(part, parts)
    grads_gate_up = summed(part)
    grad_second, top, low = on_rows(
        down_norm_kernel, where, [second, grad_rows], gains, parts, False
    )

    def result_products(ready):
        left, unused = tie(mid, ready)
        return [
            half_products(at, order, [(left, None)], [(w_down_t, hidden, 0)])
            for at, order in ((0, (3, 1, 2, 0)), (1, (3, 2, 1, 0)))
        ]

    z_parts, ((a3, a1, a2, a0), (b3, b2, b1, b0)) = gather_rows(top, low, result_products)

    z_parts, a3, a1, b3, b2 = tie(z_parts, a3, a1, b3, b2)
    a3, a1 = swap(a3, "tx", 1), swap(a1, "tx", 1)
    b3, b2 = swap(b3, "tx", 2), swap(b2, "tx", 2)
    z_full, grad_att, grad_ogate = back_products(z_parts, w_second, out_gate, attended)
    a3, b3, grad_att = tie(a3, b3, grad_att)
    a2 = swap((a2 + a3.astype(F32)).astype(BF), "tx", 2)
    b1 = swap((b1 + b3.astype(F32)).astype(BF), "tx", 1)
    grad_first = attend_backward(where, qa, ka, qkv, grad_att, attended, slope)
    grad_first, a1, a2, b1, b2, grads_down = tie(grad_first, a1, a2, b1, b2, grads_down)
    output = on_rows(result_kernel, where, [second], None, [a0, a1, a2, b0, b1, b2], True)
    output, grad_first = tie(output, grad_first)
    output = spread_line(output)
    part = attn_products(first_normed, grad_first, grad_ogate, z_full, gated)
    part, grad_first, output = tie(part, grad_first, output)
    grads_attn = summed(part)
    parts, unused = scatter_products(
        [(grad_first, None), (grad_ogate, None)],
        [(w_first, last, 0), (w_second, width, 0)],
    )
    bias_grad = jnp.sum(grad_first[:, side:].astype(F32), axis=0, keepdims=True)
    if paired:
        bias_grad = bias_grad + swap(bias_grad, "dp", 1)
        bias_grad = pairs_sum(spread_line([bias_grad] * 4))
    else:
        bias_grad = lax.psum(bias_grad, ("dp", "ty"))
    parts, grads_gate_up, bias_grad = tie(parts, grads_gate_up, bias_grad)
    grad_x = on_rows(input_norm_kernel, where, [x_full[:2], grad_second], gains, parts, True)

    output, grad_x = tie(output, spread_line(grad_x))
    back = spread_plane(reordered([output, grad_x], column ^ lane))

    grad_down = reduce_end(grads_down)
    grad_gate_up = reduce_end(grads_gate_up)
    grad_attn = reduce_end(grads_attn)

    def row_dots(*sides):
        return sum(jnp.sum(w.astype(F32) * g, axis=1) for w, g in sides)

    grads = [
        grad_attn[:, :width],
        grad_attn[:, width : 2 * width],
        grad_attn[:, 2 * width : side],
        grad_attn[:, last : last + width],
        grad_attn[:, side : side + heads],
    ]
    own_gains = jnp.stack(
        [
            row_dots(*zip((w_query, w_key, w_value, w_ogate, w_forget), grads)) / attn_gain,
            row_dots((w_gate, grad_gate_up[:, :hidden]), (w_up, grad_gate_up[:, hidden:]))
            / mlp_gain,
        ]
    )
    grad_gains = spread_plane([own_gains] * 4)
    back, grad_gains, grads = tie(back, grad_gains, grads)
    grad_gains = pairs_sum(grad_gains)
    output, grad_input = moved_rows(
        True, where, seq_lengths, seq_deal, [jnp.concatenate(back, axis=0)]
    )
    return (
        output[None],
        grad_input[None],
        grad_gains[0],
        *grads,
        bias_grad[0, :heads],
        grad_attn[:, last + width :],
        grad_gains[1],
        grad_gate_up[:, :hidden],
        grad_gate_up[:, hidden:],
        grad_down,
    )


def solution(mesh):
    tokens, feature, grid, flipped = P("tx", "dp", "ty"), P("ty"), P("ty", "tx"), P("tx", "ty")
    return jax.shard_map(
        on_device,
        mesh=mesh,
        in_specs=(
            tokens,
            tokens,
            P(),
            P(),
            feature,
            grid,
            grid,
            grid,
            grid,
            grid,
            P("tx"),
            flipped,
            feature,
            grid,
            grid,
            flipped,
        ),
        out_specs=(
            tokens,
            tokens,
            feature,
            grid,
            grid,
            grid,
            grid,
            grid,
            P("tx"),
            flipped,
            feature,
            grid,
            grid,
            flipped,
        ),
        check_vma=False,
    )
```

time: 601 us -> 531 us (0.88)
  Pallas kernels: 53.6 us -> 207 us
  matrix products: 91.1 us -> 0 us
  waiting for transfers between devices: 232 us -> 154 us
  blocking collectives: 41.1 us -> 0 us
  other arithmetic: 34.4 us -> 14.6 us
  starting transfers between devices: 87.1 us -> 101 us
    pallas_call x3 -> x28, Pallas kernels: 15.6 us -> 170 us  [the longest x8 40.7 us: half_products(): pl.pallas_call(lambda *refs: part_kernel(order, len(lefts), *refs), grid=...]
    dot_general x40 -> x0, matrix products: 91.1 us -> none  [dot(): lax.dot_general(left, right, (dims, ((), ())), preferred_element_type=F32)]
    ppermute x78 -> x82, waiting for transfers between devices: 204 us -> 152 us  [swap(): lax.ppermute(values, axis, [(at, at ^ step) for at in range(lax.axis_size...]
    psum x1 -> x0, blocking collectives: 41.1 us -> none  [on_device(): lax.psum(jnp.concatenate([gain_one_part, gain_two_part, bias_slots]), ('d...]
    reduce_scatter x2 -> x3, waiting for transfers between devices: 28 us -> 0.06 us  [summed(): return lax.psum_scatter(part, ('ty', 'dp'), scatter_dimension=0, tiled=True)]
    ppermute x78 -> x82, starting transfers between devices: 86.8 us -> 100 us  [swap(): lax.ppermute(values, axis, [(at, at ^ step) for at in range(lax.axis_size...]
    concatenate x7 -> x2, other arithmetic: 10.9 us -> 1.68 us  [the longest x1 0.95 us: on_device(): w_gate_up = jnp.concatenate([own_share(w_gate), own_share(w_up)], axis=1)]
    unnamed x120 -> x200, local copies, waits for them, and re-layouts: 21 us -> 26.3 us
  transfers between devices with their start and end apart: 84 -> 89, of which waited for: 40 -> 41; matrix products, arithmetic and copies ran while one was open for 19% -> 3% of each run, Pallas kernels for 6% -> 38%
where the time goes in v2:
time: 531 us; the launch traced here: 525 us
  Pallas kernels  207 us (39%)
  waiting for transfers between devices  154 us (29%)
  starting transfers between devices  101 us (19%)
  local copies, waits for them, and re-layouts  33.3 us (6%)
  between operations  15.4 us (3%)
  other arithmetic  14.6 us (3%)
    ppermute x82, waiting for transfers between devices, swap(): lax.ppermute(values, axis, [(at, at ^ step) for at in range(lax.axis_size...  152 us
    ppermute x82, starting transfers between devices, swap(): lax.ppermute(values, axis, [(at, at ^ step) for at in range(lax.axis_size...  100 us
    pallas_call x8, Pallas kernels, half_products(): pl.pallas_call(lambda *refs: part_kernel(order, len(lefts), *refs), grid=...  40.7 us
    unnamed x200, local copies, waits for them, and re-layouts  26.3 us
    pallas_call x4, Pallas kernels, on_rows(): pl.pallas_call(kernel, grid_spec=pltpu.PrefetchScalarGridSpec(num_scalar_...  22.3 us
    pallas_call x1, Pallas kernels, attend_backward(): pl.pallas_call(backward_kernel, grid_spec=pltpu.PrefetchScalarGridSpec(nu...  20.7 us
    pallas_call x2, Pallas kernels, moved_rows(): pl.pallas_call(lambda *refs: pick_kernel(backward, *refs), grid_spec=pltp...  16.9 us
    pallas_call x1, Pallas kernels, attend_forward(): pl.pallas_call(forward_kernel, grid_spec=pltpu.PrefetchScalarGridSpec(num...  16.7 us
  transfers between devices with their start and end apart: 89, of which 41 were waited for; matrix products, arithmetic and copies ran while one was open for 3% of the time, Pallas kernels for 38%

profile of v2, /device:TPU:9, one launch (start us, length us, event | category | flops | bytes accessed | tf_op | source)
XLA Modules:
  0.0 524.9 jit_solution(2783232812000346170)
XLA Ops:
  16.9 8.6 %shard_map.263 = (bf16[256,384]{1,0:T(8,128)(2,1)S(1)}, bf16[256,384]{1,0:T(8,128)(2,1)}, bf16[256,384]{1,0:T(8,128)(2,1)}, bf16[256,384]{1,0:T(8,128)(2,1)}, bf...) custom-call(s32[3]{0:T(128)S(1)} %pad_add_fusion.refs_0_.where, ...), custom_call_target="tpu_custom_call" | custom-call | flops 6442450944 | bytes 8388608 | tf_op jit(solution)/shard_map/pallas_call | solution.py:747
  30.3 3.8 collective-permute-done.2.refs_1_
  34.9 4.2 collective-permute-done.4.refs_3_
  46.2 13.1 %collective-permute-done.5.refs_1_ = bf16[256,384]{1,0:T(8,128)(2,1)S(1)} collective-permute-done((bf16[256,384]{1,0:T(8,128)(2,1)}, bf16[256,384]{1,0:T(8,128)(2,1)S(1)}, u32[]{:S(2)}, u32[]{:S(2)}) %collective-permute-start.5) | collective-permute-done | bytes 196640 | tf_op jit(solution)/shard_map/ppermute | solution.py:67
  62.2 11.0 %collective-permute-done.7.refs_3_ = bf16[256,384]{1,0:T(8,128)(2,1)S(1)} collective-permute-done((bf16[256,384]{1,0:T(8,128)(2,1)}, bf16[256,384]{1,0:T(8,128)(2,1)S(1)}, u32[]{:S(2)}, u32[]{:S(2)}) %collective-permute-start.7) | collective-permute-done | bytes 196640 | tf_op jit(solution)/shard_map/ppermute | solution.py:67
  82.5 4.1 collective-permute-done.13.refs_1_
  100.3 6.6 %collective-permute-done.16.refs_6_ = bf16[128,1536]{1,0:T(8,128)(2,1)} collective-permute-done((bf16[128,1536]{1,0:T(8,128)(2,1)}, bf16[128,1536]{1,0:T(8,128)(2,1)}, u32[]{:S(2)}, u32[]{:S(2)}) %collective-permute-start.16) | collective-permute-done | bytes 393248 | tf_op jit(solution)/shard_map/ppermute | solution.py:67
  114.8 11.9 %shard_map.267 = (bf16[1024,1536]{1,0:T(8,128)(2,1)}, bf16[1024,1280]{1,0:T(8,128)(2,1)}, f32[1024,128]{1,0:T(8,128)}, f32[1024,128]{1,0:T(8,128)}, f32[8,1536]{1,0:T(8,128)}) custom-call(bf16[128,1536]{1,0:T(8,128)(2,1)} %get-tuple-element.327.refs_0_.x_top, bf16[128,1536]{1,0:T(8,128)(2,1)} %get-tuple-element.328.refs_1_.x_low, ...), custom_call_target="tpu_custom_call" | custom-call | flops 5637144576 | bytes 16777216 | tf_op jit(solution)/shard_map/pallas_call | solution.py:471
  130.8 16.7 %shard_map.269 = (f32[1024,384]{1,0:T(8,128)}, bf16[6,1024,128]{2,1,0:T(8,128)(2,1)}, bf16[6,1024,128]{2,1,0:T(8,128)(2,1)}) custom-call(s32[3]{0:T(128)} %copy-done.16, s32[4,4]{1,0:T(4,128)} %refs_1_.3, s32[4,4]{1,0:T(4,128)} %refs_2_.3, bf16[1024,1280]{1,0:T(8,128)(2,1)} %get-tuple-element.347.q_ref.k_ref.v_ref, ...), custom_call_target="tpu_custom_call" | custom-call | flops 10000000000 | bytes 8388608 | tf_op jit(solution)/shard_map/pallas_call | solution.py:880
  149.9 4.5 shard_map.270
  163.5 3.3 collective-permute-done.27
  169.9 3.9 collective-permute-done.29
  175.0 6.7 %collective-permute-done.28.refs_2_ = bf16[256,768]{1,0:T(8,128)(2,1)S(1)} collective-permute-done((bf16[256,768]{1,0:T(8,128)(2,1)S(1)}, bf16[256,768]{1,0:T(8,128)(2,1)S(1)}, u32[]{:S(2)}, u32[]{:S(2)}) %collective-permute-start.28) | collective-permute-done | bytes 393248 | tf_op jit(solution)/shard_map/ppermute | solution.py:67
  181.7 8.4 %collective-permute-done.31.refs_5_ = bf16[256,768]{1,0:T(8,128)(2,1)S(1)} collective-permute-done((bf16[256,768]{1,0:T(8,128)(2,1)S(1)}, bf16[256,768]{1,0:T(8,128)(2,1)S(1)}, u32[]{:S(2)}, u32[]{:S(2)}) %collective-permute-start.31) | collective-permute-done | bytes 393248 | tf_op jit(solution)/shard_map/ppermute | solution.py:67
  191.0 5.6 %shard_map.273 = (f32[256,1536]{1,0:T(8,128)}, bf16[128,1536]{1,0:T(8,128)(2,1)}, bf16[128,1536]{1,0:T(8,128)(2,1)}) custom-call(s32[3]{0:T(128)} %copy-done.16, bf16[128,1536]{1,0:T(8,128)(2,1)} %get-tuple-element.327.refs_0_.x_top, bf16[128,1536]{1,0:T(8,128)(2,1)} %get-tuple-element.328.refs_1_.x_low, f32[8,1536]{1,0:T(8,128)} %get-tuple-element.336.gain_ref, ...), custom_call_target="tpu_custom_call" | custom-call | flops 1 | bytes 6291456 | tf_op jit(solution)/shard_map/pallas_call | solution.py:413
  199.6 3.9 collective-permute-done.32.refs_2_
  205.2 4.5 shard_map.275.right.g_ref
  210.8 8.0 %collective-permute-done.36.refs_6_ = bf16[128,1536]{1,0:T(8,128)(2,1)S(1)} collective-permute-done((bf16[128,1536]{1,0:T(8,128)(2,1)S(1)}, bf16[128,1536]{1,0:T(8,128)(2,1)S(1)}, u32[]{:S(2)}, u32[]{:S(2)}) %collective-permute-start.36) | collective-permute-done | bytes 393248 | tf_op jit(solution)/shard_map/ppermute | solution.py:67
  220.1 11.8 %shard_map.274 = (bf16[1024,1536]{1,0:T(8,128)(2,1)}, bf16[1024,1024]{1,0:T(8,128)(2,1)}, bf16[1024,1024]{1,0:T(8,128)(2,1)}, bf16[1024,1024]{1,0:T(8,128)(2,1)}) custom-call(bf16[128,1536]{1,0:T(8,128)(2,1)} %get-tuple-element.377.refs_0_, bf16[128,1536]{1,0:T(8,128)(2,1)} %get-tuple-element.378.refs_1_, bf16[128,1536]{1,0:T(8,128)(2,1)} %copy-done.89, ...), custom_call_target="tpu_custom_call" | custom-call | flops 6442450944 | bytes 20971520 | tf_op jit(solution)/shard_map/pallas_call | solution.py:557
  233.4 7.4 %shard_map.276 = bf16[4096,384]{1,0:T(8,128)(2,1)} custom-call(bf16[1024,1024]{1,0:T(8,128)(2,1)S(1)} %copy-done.25, bf16[1024,1536]{1,0:T(8,128)(2,1)} %shard_map.275.right.g_ref), custom_call_target="tpu_custom_call" | custom-call | flops 3221225472 | bytes 6442450 | tf_op jit(solution)/shard_map/pallas_call | solution.py:221
  243.4 8.2 %shard_map.277.refs_0_.refs_1_.right = bf16[2,1024,1024]{2,1,0:T(8,128)(2,1)} custom-call(bf16[1024,1536]{1,0:T(8,128)(2,1)} %shard_map.275.right.g_ref, bf16[1536,1024]{1,0:T(8,128)(2,1)} %all-gather.11.cloned.1.call-done.w_ref.refs_1_, bf16[1024,1024]{1,0:T(8,128)(2,1)S(1)} %copy-done.4, bf16[1024,1024]{1,0:T(8,128)(2,1)} %get-tuple-element.406.to_up_ref), custom_call_target="tpu_custom_call" | custom-call | flops 3221225472 | bytes 16777216 | tf_op jit(solution)/shard_map/pallas_call | solution.py:587
  251.5 6.8 %shard_map.278 = (bf16[256,768]{1,0:T(8,128)(2,1)S(1)}, bf16[256,768]{1,0:T(8,128)(2,1)S(1)}, f32[256,768]{1,0:T(8,128)S(1)}, f32[256,768]{1,0:T(8,128)S(1)}) custom-call(bf16[2,1024,1024]{2,1,0:T(8,128)(2,1)} %shard_map.277.refs_0_.refs_1_.right, bf16[2,1024,1024]{2,1,0:T(8,128)(2,1)} %shard_map.277.refs_0_.refs_1_.right, ...), custom_call_target="tpu_custom_call" | custom-call | flops 3221225472 | bytes 6442450 | tf_op jit(solution)/shard_map/pallas_call | solution.py:159
  260.4 6.8 %shard_map.279 = (bf16[256,768]{1,0:T(8,128)(2,1)S(1)}, bf16[256,768]{1,0:T(8,128)(2,1)S(1)}, f32[256,768]{1,0:T(8,128)S(1)}, f32[256,768]{1,0:T(8,128)S(1)}) custom-call(bf16[2,1024,1024]{2,1,0:T(8,128)(2,1)} %shard_map.277.refs_0_.refs_1_.right, bf16[2,1024,1024]{2,1,0:T(8,128)(2,1)} %shard_map.277.refs_0_.refs_1_.right, ...), custom_call_target="tpu_custom_call" | custom-call | flops 3221225472 | bytes 6442450 | tf_op jit(solution)/shard_map/pallas_call | solution.py:159
  270.4 3.9 collective-permute-done.41
  275.4 11.2 %shard_map.280 = bf16[1536,2048]{1,0:T(8,128)(2,1)} custom-call(bf16[1024,1536]{1,0:T(8,128)(2,1)S(1)} %copy-done.26, bf16[2,1024,1024]{2,1,0:T(8,128)(2,1)} %shard_map.277.refs_0_.refs_1_.right), custom_call_target="tpu_custom_call" | custom-call | flops 6442450944 | bytes 12884901 | tf_op jit(solution)/shard_map/pallas_call | solution.py:181
  289.9 6.2 %shard_map.281 = (f32[256,1536]{1,0:T(8,128)}, bf16[128,1536]{1,0:T(8,128)(2,1)}, bf16[128,1536]{1,0:T(8,128)(2,1)}) custom-call(s32[3]{0:T(128)} %copy-done.16, f32[256,1536]{1,0:T(8,128)} %get-tuple-element.371.second_ref, bf16[128,1536]{1,0:T(8,128)(2,1)} %get-tuple-element.395.refs_0_.grad_top, bf16[128,1536]{1,0:T(8,128)(2,1)} %get-tuple-element.396.refs_1_.grad_low, ...), custom_call_target="tpu_custom_call" | custom-call | flops 1 | bytes 6291456 | tf_op jit(solution)/shard_map/pallas_call | solution.py:413
  299.0 3.9 collective-permute-done.44.refs_2_
  305.8 4.4 shard_map.282
  311.2 4.5 shard_map.283
  319.6 6.9 %shard_map.284 = (bf16[1024,1536]{1,0:T(8,128)(2,1)}, bf16[1024,384]{1,0:T(8,128)(2,1)}, bf16[1024,384]{1,0:T(8,128)(2,1)}) custom-call(bf16[128,1536]{1,0:T(8,128)(2,1)} %get-tuple-element.444.refs_0_, bf16[128,1536]{1,0:T(8,128)(2,1)} %get-tuple-element.445.refs_1_, bf16[128,1536]{1,0:T(8,128)(2,1)} %copy-done.38, bf16[128,1536]{1,0:T(8,128)(2,1)} %copy-done.40, ...), custom_call_target="tpu_custom_call" | custom-call | flops 1207959552 | bytes 10485760 | tf_op jit(solution)/shard_map/pallas_call | solution.py:629
  331.8 20.7 %shard_map.285.d_ref.refs_0_ = bf16[1024,1280]{1,0:T(8,128)(2,1)} custom-call(s32[3]{0:T(128)} %copy-done.16, bf16[6,1024,128]{2,1,0:T(8,128)(2,1)} %get-tuple-element.455.qa_ref, bf16[6,1024,128]{2,1,0:T(8,128)(2,1)} %get-tuple-element.456.ka_ref, bf16[1024,1280]{1,0:T(8,128)(2,1)} %get-tuple-element.347.q_ref.k_ref.v_ref, ...), custom_call_target="tpu_custom_call" | custom-call | flops 12000000000 | bytes 8388608 | tf_op jit(solution)/shard_map/pallas_call | solution.py:1027
  353.3 5.0 shard_map.286
  358.3 13.1 %collective-permute-start.56 = (bf16[256,384]{1,0:T(8,128)(2,1)}, bf16[256,384]{1,0:T(8,128)(2,1)S(1)}, u32[]{:S(2)}, u32[]{:S(2)}) collective-permute-start(bf16[256,384]{1,0:T(8,128)(2,1)} %get-tuple-element.482), channel_id=1, source_target_pairs={{0,1},{1,0},{2,3},{3,2},{4,5},{5,4},{6,7},{7,6},{8,9},{9,8},{10,11... | collective-permute-start | bytes 589832 | tf_op jit(solution)/shard_map/ppermute | solution.py:67
  372.7 11.6 %shard_map.287 = bf16[1536,2048]{1,0:T(8,128)(2,1)} custom-call(bf16[1024,1536]{1,0:T(8,128)(2,1)} %get-tuple-element.335.h_ref, bf16[1024,1536]{1,0:T(8,128)(2,1)} %get-tuple-element.453.z_ref, bf16[1024,1280]{1,0:T(8,128)(2,1)} %shard_map.285.d_ref.refs_0_, bf16[1024,384]{1,0:T(8,128)(2,1)S(1)} %copy-done.3, ...), custom_call_target="tpu_custom_call" | custom-call | flops 6442450944 | bytes 16777216 | tf_op jit(solution)/shard_map/pallas_call | solution.py:252
  385.1 6.1 %shard_map.288 = (bf16[256,768]{1,0:T(8,128)(2,1)S(1)}, bf16[256,768]{1,0:T(8,128)(2,1)S(1)}, f32[256,768]{1,0:T(8,128)S(1)}, f32[256,768]{1,0:T(8,128)S(1)}) custom-call(bf16[1024,1280]{1,0:T(8,128)(2,1)} %shard_map.285.d_ref.refs_0_, bf16[1024,384]{1,0:T(8,128)(2,1)S(1)} %copy-done.3, ...), custom_call_target="tpu_custom_call" | custom-call | flops 2617245696 | bytes 5234491 | tf_op jit(solution)/shard_map/pallas_call | solution.py:159
  392.0 4.5 collective-permute-start.60
  396.5 6.3 %shard_map.289 = (bf16[256,768]{1,0:T(8,128)(2,1)S(1)}, bf16[256,768]{1,0:T(8,128)(2,1)S(1)}, f32[256,768]{1,0:T(8,128)S(1)}, f32[256,768]{1,0:T(8,128)S(1)}) custom-call(bf16[1024,1280]{1,0:T(8,128)(2,1)} %shard_map.285.d_ref.refs_0_, bf16[1024,384]{1,0:T(8,128)(2,1)S(1)} %copy-done.3, ...), custom_call_target="tpu_custom_call" | custom-call | flops 2617245696 | bytes 5234491 | tf_op jit(solution)/shard_map/pallas_call | solution.py:159
  405.1 6.0 %collective-permute-start.65 = (f32[1,128]{1,0:T(1,128)S(1)}, f32[1,128]{1,0:T(1,128)S(1)}, u32[]{:S(2)}, u32[]{:S(2)}) collective-permute-start(f32[1,128]{1,0:T(1,128)S(1)} %bitcast.22), channel_id=1, source_target_pairs={{0,16},{16,0},{1,17},{17,1},{2,18},{18,2},{3,19},{19,3},{4,20},{20... | collective-permute-start | bytes 1544 | tf_op jit(solution)/shard_map/ppermute | solution.py:67
  414.9 4.9 collective-permute-start.67
  423.9 4.1 collective-permute-start.66
  431.2 4.0 collective-permute-start.76
  435.2 5.6 %shard_map.290 = (bf16[256,384]{1,0:T(8,128)(2,1)}, bf16[256,384]{1,0:T(8,128)(2,1)}, bf16[256,384]{1,0:T(8,128)(2,1)}, bf16[256,384]{1,0:T(8,128)(2,1)}) custom-call(s32[3]{0:T(128)} %copy-done.16, bf16[128,1536]{1,0:T(8,128)(2,1)} %get-tuple-element.327.refs_0_.x_top, bf16[128,1536]{1,0:T(8,128)(2,1)} %get-tuple-element.328.refs_1_.x_low, ...), custom_call_target="tpu_custom_call" | custom-call | flops 1 | bytes 6291456 | tf_op jit(solution)/shard_map/pallas_call | solution.py:413
  445.1 12.5 %collective-permute-done.69.refs_5_ = bf16[256,384]{1,0:T(8,128)(2,1)S(1)} collective-permute-done((bf16[256,384]{1,0:T(8,128)(2,1)}, bf16[256,384]{1,0:T(8,128)(2,1)S(1)}, u32[]{:S(2)}, u32[]{:S(2)}) %collective-permute-start.69) | collective-permute-done | bytes 196640 | tf_op jit(solution)/shard_map/ppermute | solution.py:67
  457.6 4.5 collective-permute-done.70.refs_6_
  462.1 11.7 %collective-permute-done.71.refs_7_ = bf16[256,384]{1,0:T(8,128)(2,1)S(1)} collective-permute-done((bf16[256,384]{1,0:T(8,128)(2,1)}, bf16[256,384]{1,0:T(8,128)(2,1)S(1)}, u32[]{:S(2)}, u32[]{:S(2)}) %collective-permute-start.71) | collective-permute-done | bytes 196640 | tf_op jit(solution)/shard_map/ppermute | solution.py:67
  492.2 4.0 collective-permute-done.74
  502.1 3.5 collective-permute-done.81
  509.6 8.2 %shard_map.292 = (bf16[1024,384]{1,0:T(8,128)(2,1)}, bf16[1024,384]{1,0:T(8,128)(2,1)}) custom-call(s32[3]{0:T(128)S(1)} %copy-done.17, s32[4,4]{1,0:T(4,128)S(1)} %copy-done.22, s32[4,4]{1,0:T(4,128)S(1)} %copy-done.24, bf16[2048,384]{1,0:T(8,128)(2,1)S(1)} %constant_dynamic-update-slice_fusion.refs_3_, bf16[2048,384]{1,0:T(8,128)(2,1)} %collective-permute-done.80.refs_4_), custom_call_target="tpu_custom_call" | custom-call | flops 6442450944 | bytes 8388608 | tf_op jit(solution)/shard_map/pallas_call | solution.py:747
  (420 shorter events, 162.7 us)
Async XLA Ops:
  7.2 107.6 %all-gather.5.cloned.1.call-start = ((), (), s32[]{:S(2)}) async-start(), calls=%async_computation.3 | async-start | bytes 4423680 | tf_op jit(solution)/shard_map/all_gather | solution.py:1087
  13.0 135.1 %all-gather.7.cloned.1.call-start = ((), (), s32[]{:S(2)}) async-start(), calls=%async_computation.4 | async-start | bytes 2654208 | tf_op jit(solution)/shard_map/all_gather | solution.py:1087
  42.1 17.3 %collective-permute-start.5 = (bf16[256,384]{1,0:T(8,128)(2,1)}, bf16[256,384]{1,0:T(8,128)(2,1)S(1)}, u32[]{:S(2)}, u32[]{:S(2)}) collective-permute-start(bf16[256,384]{1,0:T(8,128)(2,1)} %get-tuple-element.296), channel_id=1, source_target_pairs={{0,1},{1,0},{2,3},{3,2},{4,5},{5,4},{6,7},{7,6},{8,9},{9,8},{10,11... | collective-permute-start | bytes 589832 | tf_op jit(solution)/shard_map/ppermute | solution.py:67
  42.4 19.8 %collective-permute-start.6 = (bf16[256,384]{1,0:T(8,128)(2,1)}, bf16[256,384]{1,0:T(8,128)(2,1)S(1)}, u32[]{:S(2)}, u32[]{:S(2)}) collective-permute-start(bf16[256,384]{1,0:T(8,128)(2,1)} %get-tuple-element.297), channel_id=1, source_target_pairs={{0,2},{1,3},{2,0},{3,1},{4,6},{5,7},{6,4},{7,5},{8,10},{9,11},{10,... | collective-permute-start | bytes 589832 | tf_op jit(solution)/shard_map/ppermute | solution.py:67
  44.6 28.6 %collective-permute-start.7 = (bf16[256,384]{1,0:T(8,128)(2,1)}, bf16[256,384]{1,0:T(8,128)(2,1)S(1)}, u32[]{:S(2)}, u32[]{:S(2)}) collective-permute-start(bf16[256,384]{1,0:T(8,128)(2,1)} %get-tuple-element.298), channel_id=1, source_target_pairs={{0,3},{1,2},{2,1},{3,0},{4,7},{5,6},{6,5},{7,4},{8,11},{9,10},{10,... | collective-permute-start | bytes 589832 | tf_op jit(solution)/shard_map/ppermute | solution.py:67
  44.8 28.4 %collective-permute-start.8 = (bf16[256,384]{1,0:T(8,128)(2,1)}, bf16[256,384]{1,0:T(8,128)(2,1)S(1)}, u32[]{:S(2)}, u32[]{:S(2)}) collective-permute-start(bf16[256,384]{1,0:T(8,128)(2,1)} %copy-done.20), channel_id=1, source_target_pairs={{0,4},{4,0},{8,12},{12,8},{1,5},{5,1},{9,13},{13,9},{2,6},{6,2},{1... | collective-permute-start | bytes 589832 | tf_op jit(solution)/shard_map/ppermute | solution.py:67
  46.0 27.2 %collective-permute-start.9 = (bf16[256,384]{1,0:T(8,128)(2,1)S(1)}, bf16[256,384]{1,0:T(8,128)(2,1)S(1)}, u32[]{:S(2)}, u32[]{:S(2)}) collective-permute-start(bf16[256,384]{1,0:T(8,128)(2,1)S(1)} %get-tuple-element.301), channel_id=1, source_target_pairs={{0,8},{4,12},{8,0},{12,4},{1,9},{5,13},{9,1},{13,5},{2,10},{6,14},... | collective-permute-start | bytes 589832 | tf_op jit(solution)/shard_map/ppermute | solution.py:67
  59.4 13.9 %collective-permute-start.10 = (bf16[256,384]{1,0:T(8,128)(2,1)S(1)}, bf16[256,384]{1,0:T(8,128)(2,1)S(1)}, u32[]{:S(2)}, u32[]{:S(2)}) collective-permute-start(bf16[256,384]{1,0:T(8,128)(2,1)S(1)} %get-tuple-element.302), channel_id=1, source_target_pairs={{0,12},{4,8},{8,4},{12,0},{1,13},{5,9},{9,5},{13,1},{2,14},{6,10},... | collective-permute-start | bytes 589832 | tf_op jit(solution)/shard_map/ppermute | solution.py:67
  81.7 18.6 %collective-permute-start.14 = (bf16[128,1536]{1,0:T(8,128)(2,1)}, bf16[128,1536]{1,0:T(8,128)(2,1)S(1)}, u32[]{:S(2)}, u32[]{:S(2)}) collective-permute-start(bf16[128,1536]{1,0:T(8,128)(2,1)} %get-tuple-element.328.refs_1_.x_low), channel_id=1, source_target_pairs={{0,4},{4,0},{8,12},{12,8},{1,5},{5,1},{9,13},{13,9},{2,6},{6,2},{1... | collective-permute-start | bytes 1179656 | tf_op jit(solution)/shard_map/ppermute | solution.py:67
  82.2 18.1 %collective-permute-start.15 = (bf16[128,1536]{1,0:T(8,128)(2,1)}, bf16[128,1536]{1,0:T(8,128)(2,1)}, u32[]{:S(2)}, u32[]{:S(2)}) collective-permute-start(bf16[128,1536]{1,0:T(8,128)(2,1)} %get-tuple-element.327.refs_0_.x_top), channel_id=1, source_target_pairs={{0,8},{4,12},{8,0},{12,4},{1,9},{5,13},{9,1},{13,5},{2,10},{6,14},... | collective-permute-start | bytes 1179656 | tf_op jit(solution)/shard_map/ppermute | solution.py:67
  90.1 16.9 %collective-permute-start.16 = (bf16[128,1536]{1,0:T(8,128)(2,1)}, bf16[128,1536]{1,0:T(8,128)(2,1)}, u32[]{:S(2)}, u32[]{:S(2)}) collective-permute-start(bf16[128,1536]{1,0:T(8,128)(2,1)} %collective-permute-done.11.refs_2_), channel_id=1, source_target_pairs={{0,8},{4,12},{8,0},{12,4},{1,9},{5,13},{9,1},{13,5},{2,10},{6,14},... | collective-permute-start | bytes 1179656 | tf_op jit(solution)/shard_map/ppermute | solution.py:67
  91.1 15.9 %collective-permute-start.17 = (bf16[128,1536]{1,0:T(8,128)(2,1)}, bf16[128,1536]{1,0:T(8,128)(2,1)}, u32[]{:S(2)}, u32[]{:S(2)}) collective-permute-start(bf16[128,1536]{1,0:T(8,128)(2,1)} %collective-permute-done.12.refs_5_), channel_id=1, source_target_pairs={{0,4},{4,0},{8,12},{12,8},{1,5},{5,1},{9,13},{13,9},{2,6},{6,2},{1... | collective-permute-start | bytes 1179656 | tf_op jit(solution)/shard_map/ppermute | solution.py:67
  107.0 112.3 %all-gather.9.cloned.1.call-start = ((), (), s32[]{:S(2)}) async-start(), calls=%async_computation.5 | async-start | bytes 7077888 | tf_op jit(solution)/shard_map/all_gather | solution.py:1087
  107.7 134.0 %all-gather.11.cloned.1.call-start = ((), (), s32[]{:S(2)}) async-start(), calls=%async_computation.6 | async-start | bytes 3538944 | tf_op jit(solution)/shard_map/all_gather | solution.py:1087
  111.9 17.9 %collective-permute-start.21 = (bf16[128,1536]{1,0:T(8,128)(2,1)}, bf16[128,1536]{1,0:T(8,128)(2,1)S(1)}, u32[]{:S(2)}, u32[]{:S(2)}) collective-permute-start(bf16[128,1536]{1,0:T(8,128)(2,1)} %get-tuple-element.396.refs_1_.grad_low), channel_id=1, source_target_pairs={{0,8},{4,12},{8,0},{12,4},{1,9},{5,13},{9,1},{13,5},{2,10},{6,14},... | collective-permute-start | bytes 1179656 | tf_op jit(solution)/shard_map/ppermute | solution.py:67
  112.9 34.6 %collective-permute-start.22 = (bf16[128,1536]{1,0:T(8,128)(2,1)}, bf16[128,1536]{1,0:T(8,128)(2,1)S(1)}, u32[]{:S(2)}, u32[]{:S(2)}) collective-permute-start(bf16[128,1536]{1,0:T(8,128)(2,1)} %get-tuple-element.396.refs_1_.grad_low), channel_id=1, source_target_pairs={{0,4},{4,0},{8,12},{12,8},{1,5},{5,1},{9,13},{13,9},{2,6},{6,2},{1... | collective-permute-start | bytes 1179656 | tf_op jit(solution)/shard_map/ppermute | solution.py:67
  113.3 16.5 %collective-permute-start.20 = (bf16[128,1536]{1,0:T(8,128)(2,1)}, bf16[128,1536]{1,0:T(8,128)(2,1)S(1)}, u32[]{:S(2)}, u32[]{:S(2)}) collective-permute-start(bf16[128,1536]{1,0:T(8,128)(2,1)} %get-tuple-element.395.refs_0_.grad_top), channel_id=1, source_target_pairs={{0,4},{4,0},{8,12},{12,8},{1,5},{5,1},{9,13},{13,9},{2,6},{6,2},{1... | collective-permute-start | bytes 1179656 | tf_op jit(solution)/shard_map/ppermute | solution.py:67
  114.3 33.1 %collective-permute-start.23 = (bf16[128,1536]{1,0:T(8,128)(2,1)}, bf16[128,1536]{1,0:T(8,128)(2,1)S(1)}, u32[]{:S(2)}, u32[]{:S(2)}) collective-permute-start(bf16[128,1536]{1,0:T(8,128)(2,1)} %get-tuple-element.395.refs_0_.grad_top), channel_id=1, source_target_pairs={{0,8},{4,12},{8,0},{12,4},{1,9},{5,13},{9,1},{13,5},{2,10},{6,14},... | collective-permute-start | bytes 1179656 | tf_op jit(solution)/shard_map/ppermute | solution.py:67
  129.8 17.7 %collective-permute-start.24 = (bf16[128,1536]{1,0:T(8,128)(2,1)S(1)}, bf16[128,1536]{1,0:T(8,128)(2,1)S(1)}, u32[]{:S(2)}, u32[]{:S(2)}) collective-permute-start(bf16[128,1536]{1,0:T(8,128)(2,1)S(1)} %collective-permute-done.20.refs_2_), channel_id=1, source_target_pairs={{0,8},{4,12},{8,0},{12,4},{1,9},{5,13},{9,1},{13,5},{2,10},{6,14},... | collective-permute-start | bytes 1179656 | tf_op jit(solution)/shard_map/ppermute | solution.py:67
  130.4 17.1 %collective-permute-start.25 = (bf16[128,1536]{1,0:T(8,128)(2,1)S(1)}, bf16[128,1536]{1,0:T(8,128)(2,1)S(1)}, u32[]{:S(2)}, u32[]{:S(2)}) collective-permute-start(bf16[128,1536]{1,0:T(8,128)(2,1)S(1)} %collective-permute-done.21.refs_5_), channel_id=1, source_target_pairs={{0,4},{4,0},{8,12},{12,8},{1,5},{5,1},{9,13},{13,9},{2,6},{6,2},{1... | collective-permute-start | bytes 1179656 | tf_op jit(solution)/shard_map/ppermute | solution.py:67
  147.6 204.9 %reduce-scatter.4.cloned.1.call-start = ((), (), s32[]{:S(2)}) async-start(), calls=%async_computation.7 | async-start | bytes 3538944 | tf_op jit(solution)/shard_map/reduce_scatter | solution.py:112
  169.4 20.7 %collective-permute-start.31 = (bf16[256,768]{1,0:T(8,128)(2,1)S(1)}, bf16[256,768]{1,0:T(8,128)(2,1)S(1)}, u32[]{:S(2)}, u32[]{:S(2)}) collective-permute-start(bf16[256,768]{1,0:T(8,128)(2,1)S(1)} %get-tuple-element.365), channel_id=1, source_target_pairs={{0,8},{4,12},{8,0},{12,4},{1,9},{5,13},{9,1},{13,5},{2,10},{6,14},... | collective-permute-start | bytes 1179656 | tf_op jit(solution)/shard_map/ppermute | solution.py:67
  173.9 16.2 %collective-permute-start.30 = (bf16[256,768]{1,0:T(8,128)(2,1)S(1)}, bf16[256,768]{1,0:T(8,128)(2,1)S(1)}, u32[]{:S(2)}, u32[]{:S(2)}) collective-permute-start(bf16[256,768]{1,0:T(8,128)(2,1)S(1)} %add_convert_fusion.6), channel_id=1, source_target_pairs={{0,4},{4,0},{8,12},{12,8},{1,5},{5,1},{9,13},{13,9},{2,6},{6,2},{1... | collective-permute-start | bytes 1179656 | tf_op jit(solution)/shard_map/ppermute | solution.py:67
  203.8 14.9 %collective-permute-start.36 = (bf16[128,1536]{1,0:T(8,128)(2,1)S(1)}, bf16[128,1536]{1,0:T(8,128)(2,1)S(1)}, u32[]{:S(2)}, u32[]{:S(2)}) collective-permute-start(bf16[128,1536]{1,0:T(8,128)(2,1)S(1)} %collective-permute-done.32.refs_2_), channel_id=1, source_target_pairs={{0,8},{4,12},{8,0},{12,4},{1,9},{5,13},{9,1},{13,5},{2,10},{6,14},... | collective-permute-start | bytes 1179656 | tf_op jit(solution)/shard_map/ppermute | solution.py:67
  204.4 14.9 %collective-permute-start.37 = (bf16[128,1536]{1,0:T(8,128)(2,1)S(1)}, bf16[128,1536]{1,0:T(8,128)(2,1)S(1)}, u32[]{:S(2)}, u32[]{:S(2)}) collective-permute-start(bf16[128,1536]{1,0:T(8,128)(2,1)S(1)} %collective-permute-done.33.refs_5_), channel_id=1, source_target_pairs={{0,4},{4,0},{8,12},{12,8},{1,5},{5,1},{9,13},{13,9},{2,6},{6,2},{1... | collective-permute-start | bytes 1179656 | tf_op jit(solution)/shard_map/ppermute | solution.py:67
  240.8 190.4 %reduce-scatter.6.cloned.1.call-start = ((), (), s32[]{:S(2)}) async-start(), calls=%async_computation.8 | async-start | bytes 7077888 | tf_op jit(solution)/shard_map/reduce_scatter | solution.py:112
  268.5 18.2 %collective-permute-start.38 = (bf16[256,768]{1,0:T(8,128)(2,1)S(1)}, bf16[256,768]{1,0:T(8,128)(2,1)S(1)}, u32[]{:S(2)}, u32[]{:S(2)}) collective-permute-start(bf16[256,768]{1,0:T(8,128)(2,1)S(1)} %get-tuple-element.409), channel_id=1, source_target_pairs={{0,4},{4,0},{8,12},{12,8},{1,5},{5,1},{9,13},{13,9},{2,6},{6,2},{1... | collective-permute-start | bytes 1179656 | tf_op jit(solution)/shard_map/ppermute | solution.py:67
  268.8 17.8 %collective-permute-start.40 = (bf16[256,768]{1,0:T(8,128)(2,1)S(1)}, bf16[256,768]{1,0:T(8,128)(2,1)S(1)}, u32[]{:S(2)}, u32[]{:S(2)}) collective-permute-start(bf16[256,768]{1,0:T(8,128)(2,1)S(1)} %add_convert_fusion.5), channel_id=1, source_target_pairs={{0,8},{4,12},{8,0},{12,4},{1,9},{5,13},{9,1},{13,5},{2,10},{6,14},... | collective-permute-start | bytes 1179656 | tf_op jit(solution)/shard_map/ppermute | solution.py:67
  269.2 19.6 %collective-permute-start.43 = (bf16[256,768]{1,0:T(8,128)(2,1)S(1)}, bf16[256,768]{1,0:T(8,128)(2,1)S(1)}, u32[]{:S(2)}, u32[]{:S(2)}) collective-permute-start(bf16[256,768]{1,0:T(8,128)(2,1)S(1)} %get-tuple-element.419), channel_id=1, source_target_pairs={{0,8},{4,12},{8,0},{12,4},{1,9},{5,13},{9,1},{13,5},{2,10},{6,14},... | collective-permute-start | bytes 1179656 | tf_op jit(solution)/shard_map/ppermute | solution.py:67
  289.7 190.4 %reduce-scatter.8.cloned.1.call-start = ((), (), s32[]{:S(2)}) async-start(), calls=%async_computation.9 | async-start | bytes 7077888 | tf_op jit(solution)/shard_map/reduce_scatter | solution.py:112
  297.6 18.9 %collective-permute-start.46 = (bf16[128,1536]{1,0:T(8,128)(2,1)}, bf16[128,1536]{1,0:T(8,128)(2,1)S(1)}, u32[]{:S(2)}, u32[]{:S(2)}) collective-permute-start(bf16[128,1536]{1,0:T(8,128)(2,1)} %get-tuple-element.445.refs_1_), channel_id=1, source_target_pairs={{0,4},{4,0},{8,12},{12,8},{1,5},{5,1},{9,13},{13,9},{2,6},{6,2},{1... | collective-permute-start | bytes 1179656 | tf_op jit(solution)/shard_map/ppermute | solution.py:67
  299.0 17.6 %collective-permute-start.47 = (bf16[128,1536]{1,0:T(8,128)(2,1)}, bf16[128,1536]{1,0:T(8,128)(2,1)S(1)}, u32[]{:S(2)}, u32[]{:S(2)}) collective-permute-start(bf16[128,1536]{1,0:T(8,128)(2,1)} %get-tuple-element.444.refs_0_), channel_id=1, source_target_pairs={{0,8},{4,12},{8,0},{12,4},{1,9},{5,13},{9,1},{13,5},{2,10},{6,14},... | collective-permute-start | bytes 1179656 | tf_op jit(solution)/shard_map/ppermute | solution.py:67
  317.2 35.2 %collective-permute-start.52 = (bf16[256,768]{1,0:T(8,128)(2,1)S(1)}, bf16[256,768]{1,0:T(8,128)(2,1)}, u32[]{:S(2)}, u32[]{:S(2)}) collective-permute-start(bf16[256,768]{1,0:T(8,128)(2,1)S(1)} %get-tuple-element.462), channel_id=1, source_target_pairs={{0,4},{4,0},{8,12},{12,8},{1,5},{5,1},{9,13},{13,9},{2,6},{6,2},{1... | collective-permute-start | bytes 1179656 | tf_op jit(solution)/shard_map/ppermute | solution.py:67
  318.2 34.2 %collective-permute-start.55 = (bf16[256,768]{1,0:T(8,128)(2,1)S(1)}, bf16[256,768]{1,0:T(8,128)(2,1)}, u32[]{:S(2)}, u32[]{:S(2)}) collective-permute-start(bf16[256,768]{1,0:T(8,128)(2,1)S(1)} %get-tuple-element.467), channel_id=1, source_target_pairs={{0,8},{4,12},{8,0},{12,4},{1,9},{5,13},{9,1},{13,5},{2,10},{6,14},... | collective-permute-start | bytes 1179656 | tf_op jit(solution)/shard_map/ppermute | solution.py:67
  329.1 23.3 %collective-permute-start.53 = (bf16[256,768]{1,0:T(8,128)(2,1)S(1)}, bf16[256,768]{1,0:T(8,128)(2,1)S(1)}, u32[]{:S(2)}, u32[]{:S(2)}) collective-permute-start(bf16[256,768]{1,0:T(8,128)(2,1)S(1)} %add_convert_fusion.3), channel_id=1, source_target_pairs={{0,8},{4,12},{8,0},{12,4},{1,9},{5,13},{9,1},{13,5},{2,10},{6,14},... | collective-permute-start | bytes 1179656 | tf_op jit(solution)/shard_map/ppermute | solution.py:67
  330.7 21.7 %collective-permute-start.54 = (bf16[256,768]{1,0:T(8,128)(2,1)S(1)}, bf16[256,768]{1,0:T(8,128)(2,1)S(1)}, u32[]{:S(2)}, u32[]{:S(2)}) collective-permute-start(bf16[256,768]{1,0:T(8,128)(2,1)S(1)} %add_convert_fusion.2), channel_id=1, source_target_pairs={{0,4},{4,0},{8,12},{12,8},{1,5},{5,1},{9,13},{13,9},{2,6},{6,2},{1... | collective-permute-start | bytes 1179656 | tf_op jit(solution)/shard_map/ppermute | solution.py:67
  358.3 26.0 %collective-permute-start.56 = (bf16[256,384]{1,0:T(8,128)(2,1)}, bf16[256,384]{1,0:T(8,128)(2,1)S(1)}, u32[]{:S(2)}, u32[]{:S(2)}) collective-permute-start(bf16[256,384]{1,0:T(8,128)(2,1)} %get-tuple-element.482), channel_id=1, source_target_pairs={{0,1},{1,0},{2,3},{3,2},{4,5},{5,4},{6,7},{7,6},{8,9},{9,8},{10,11... | collective-permute-start | bytes 589832 | tf_op jit(solution)/shard_map/ppermute | solution.py:67
  402.9 26.7 %collective-permute-start.59 = (bf16[256,768]{1,0:T(8,128)(2,1)S(1)}, bf16[256,768]{1,0:T(8,128)(2,1)S(1)}, u32[]{:S(2)}, u32[]{:S(2)}) collective-permute-start(bf16[256,768]{1,0:T(8,128)(2,1)S(1)} %get-tuple-element.494), channel_id=1, source_target_pairs={{0,4},{4,0},{8,12},{12,8},{1,5},{5,1},{9,13},{13,9},{2,6},{6,2},{1... | collective-permute-start | bytes 1179656 | tf_op jit(solution)/shard_map/ppermute | solution.py:67
  411.2 18.4 %collective-permute-start.61 = (bf16[256,768]{1,0:T(8,128)(2,1)S(1)}, bf16[256,768]{1,0:T(8,128)(2,1)S(1)}, u32[]{:S(2)}, u32[]{:S(2)}) collective-permute-start(bf16[256,768]{1,0:T(8,128)(2,1)S(1)} %add_convert_fusion.1), channel_id=1, source_target_pairs={{0,8},{4,12},{8,0},{12,4},{1,9},{5,13},{9,1},{13,5},{2,10},{6,14},... | collective-permute-start | bytes 1179656 | tf_op jit(solution)/shard_map/ppermute | solution.py:67
  413.0 18.2 %collective-permute-start.64 = (bf16[256,768]{1,0:T(8,128)(2,1)S(1)}, bf16[256,768]{1,0:T(8,128)(2,1)S(1)}, u32[]{:S(2)}, u32[]{:S(2)}) collective-permute-start(bf16[256,768]{1,0:T(8,128)(2,1)S(1)} %get-tuple-element.504), channel_id=1, source_target_pairs={{0,8},{4,12},{8,0},{12,4},{1,9},{5,13},{9,1},{13,5},{2,10},{6,14},... | collective-permute-start | bytes 1179656 | tf_op jit(solution)/shard_map/ppermute | solution.py:67
  413.1 18.1 %collective-permute-start.63 = (bf16[256,768]{1,0:T(8,128)(2,1)S(1)}, bf16[256,768]{1,0:T(8,128)(2,1)S(1)}, u32[]{:S(2)}, u32[]{:S(2)}) collective-permute-start(bf16[256,768]{1,0:T(8,128)(2,1)S(1)} %add_convert_fusion), channel_id=1, source_target_pairs={{0,4},{4,0},{8,12},{12,8},{1,5},{5,1},{9,13},{13,9},{2,6},{6,2},{1... | collective-permute-start | bytes 1179656 | tf_op jit(solution)/shard_map/ppermute | solution.py:67
  431.2 48.7 %collective-permute-start.76 = (bf16[192,2048]{1,0:T(8,128)(2,1)}, bf16[192,2048]{1,0:T(8,128)(2,1)S(1)}, u32[]{:S(2)}, u32[]{:S(2)}) collective-permute-start(bf16[192,2048]{1,0:T(8,128)(2,1)} %reduce-scatter.6.cloned.1.call-done), channel_id=1, source_target_pairs={{0,16},{16,0},{1,17},{17,1},{2,18},{18,2},{3,19},{19,3},{4,20},{20... | collective-permute-start | bytes 2359304 | tf_op jit(solution)/shard_map/ppermute | solution.py:67
  440.8 16.8 %collective-permute-start.69 = (bf16[256,384]{1,0:T(8,128)(2,1)}, bf16[256,384]{1,0:T(8,128)(2,1)S(1)}, u32[]{:S(2)}, u32[]{:S(2)}) collective-permute-start(bf16[256,384]{1,0:T(8,128)(2,1)} %get-tuple-element.518), channel_id=1, source_target_pairs={{0,1},{1,0},{2,3},{3,2},{4,5},{5,4},{6,7},{7,6},{8,9},{9,8},{10,11... | collective-permute-start | bytes 589832 | tf_op jit(solution)/shard_map/ppermute | solution.py:67
  443.7 18.5 %collective-permute-start.70 = (bf16[256,384]{1,0:T(8,128)(2,1)}, bf16[256,384]{1,0:T(8,128)(2,1)S(1)}, u32[]{:S(2)}, u32[]{:S(2)}) collective-permute-start(bf16[256,384]{1,0:T(8,128)(2,1)} %get-tuple-element.519), channel_id=1, source_target_pairs={{0,2},{1,3},{2,0},{3,1},{4,6},{5,7},{6,4},{7,5},{8,10},{9,11},{10,... | collective-permute-start | bytes 589832 | tf_op jit(solution)/shard_map/ppermute | solution.py:67
  444.0 29.8 %collective-permute-start.71 = (bf16[256,384]{1,0:T(8,128)(2,1)}, bf16[256,384]{1,0:T(8,128)(2,1)S(1)}, u32[]{:S(2)}, u32[]{:S(2)}) collective-permute-start(bf16[256,384]{1,0:T(8,128)(2,1)} %get-tuple-element.520), channel_id=1, source_target_pairs={{0,3},{1,2},{2,1},{3,0},{4,7},{5,6},{6,5},{7,4},{8,11},{9,10},{10,... | collective-permute-start | bytes 589832 | tf_op jit(solution)/shard_map/ppermute | solution.py:67
  477.3 14.5 %collective-permute-start.72 = (bf16[512,384]{1,0:T(8,128)(2,1)}, bf16[512,384]{1,0:T(8,128)(2,1)}, u32[]{:S(2)}, u32[]{:S(2)}) collective-permute-start(bf16[512,384]{1,0:T(8,128)(2,1)} %get-tuple-element.530), channel_id=1, source_target_pairs={{0,4},{4,0},{8,12},{12,8},{1,5},{5,1},{9,13},{13,9},{2,6},{6,2},{1... | collective-permute-start | bytes 1179656 | tf_op jit(solution)/shard_map/ppermute | solution.py:67
  478.3 13.9 %collective-permute-start.73 = (bf16[512,384]{1,0:T(8,128)(2,1)}, bf16[512,384]{1,0:T(8,128)(2,1)}, u32[]{:S(2)}, u32[]{:S(2)}) collective-permute-start(bf16[512,384]{1,0:T(8,128)(2,1)} %get-tuple-element.531), channel_id=1, source_target_pairs={{0,8},{4,12},{8,0},{12,4},{1,9},{5,13},{9,1},{13,5},{2,10},{6,14},... | collective-permute-start | bytes 1179656 | tf_op jit(solution)/shard_map/ppermute | solution.py:67
  479.5 16.7 %collective-permute-start.74 = (bf16[512,384]{1,0:T(8,128)(2,1)}, bf16[512,384]{1,0:T(8,128)(2,1)}, u32[]{:S(2)}, u32[]{:S(2)}) collective-permute-start(bf16[512,384]{1,0:T(8,128)(2,1)} %get-tuple-element.532), channel_id=1, source_target_pairs={{0,12},{4,8},{8,4},{12,0},{1,13},{5,9},{9,5},{13,1},{2,14},{6,10},... | collective-permute-start | bytes 1179656 | tf_op jit(solution)/shard_map/ppermute | solution.py:67
  (137 other events, 1094.1 us)
Sparse Core Ops, SparseCore 0:
  13.1 54.8 all-gather.4
  107.1 31.0 all-gather.6
  139.9 62.1 all-gather.8
  203.6 38.1 all-gather.10
  243.9 39.9 reduce-scatter.3
  289.0 76.9 reduce-scatter.5
  384.5 92.6 reduce-scatter.7

commit v3 on v2

--- a/solution.py
+++ b/solution.py
@@ -83,21 +83,24 @@
     return lax.optimization_barrier(groups)
 
 
+UPPER, LOWER = (0, 2, 5, 6), (1, 4, 3, 7)
+
+
 def gather_rows(top, low, beside=None, ahead=None):
     top_x, low_y = swap(top, "tx", 1), swap(low, "tx", 2)
     low_x, top_y = swap(low, "tx", 1), swap(top, "tx", 2)
     top_x, low_y, ahead = tie(top_x, low_y, ahead)
     top_d, low_d = swap(top_x, "tx", 2), swap(low_y, "tx", 1)
-    done = None if beside is None else beside((top_x, ahead))
-    return [top, low, top_x, low_x, top_y, low_y, top_d, low_d], done
+    done = None if beside is None else beside([top, low, top_x, low_y], ahead)
+    return [top, low, top_x, low_y, low_x, top_y, top_d, low_d], done
 
 
 def scatter_products(lefts, weights, beside=None):
-    a3, a1, a2, a0 = half_products(0, (3, 1, 2, 0), lefts, weights)
+    a3, a1, a2, a0 = part_products(0, (3, 1, 2, 0), lefts, weights)
     arrays, a3, a1 = tie([array for array, unused in lefts], a3, a1)
     lefts = [(array, lead) for array, (unused, lead) in zip(arrays, lefts)]
     a3, a1 = swap(a3, "tx", 1), swap(a1, "tx", 1)
-    b3, b2, b1, b0 = half_products(1, (3, 2, 1, 0), lefts, weights)
+    b3, b2, b1, b0 = part_products(1, (3, 2, 1, 0), lefts, weights)
     a3, b3, b2 = tie(a3, b3, b2)
     b3, b2 = swap(b3, "tx", 2), swap(b2, "tx", 2)
     send_a2 = (a2 + a3.astype(F32)).astype(BF)
@@ -136,23 +139,28 @@
     for left, right in zip(lefts, rights):
         rows = left[...]
         total += dot(rows.reshape(rows.shape[-2:]), right[...], NT)
-    piece = outs[0].shape[0]
+    half = outs[0].shape[0] // 2
     for at, out in zip(order, outs):
-        out[...] = total[at * piece : (at + 1) * piece].astype(out.dtype)
-
-
-def half_products(half_at, order, lefts, weights):
+        for n, place in enumerate((UPPER[at], LOWER[at])):
+            out[n * half : (n + 1) * half, :] = total[place * half : (place + 1) * half].astype(
+                out.dtype
+            )
+
+
+def part_products(half_at, order, lefts, weights):
     row_total, feature = lefts[0][0].shape[-2], weights[0][0].shape[0]
-    piece, half, block = row_total // 4, feature // 2, 256
-    first = half_at * half // block
+    piece, block = row_total // 4, 256
+    half = feature if half_at is None else feature // 2
+    first = (half_at or 0) * half // block
+    sent = 3 if half_at is None else 2
     left_specs, right_specs = [], []
     flops = 0
-    for (array, lead), (weight, width, at) in zip(lefts, weights):
-        if lead is None:
-            left_specs.append(pl.BlockSpec((row_total, width), lambda i: (0, 0)))
+    for (array, place), (weight, width, at) in zip(lefts, weights):
+        if array.ndim == 2:
+            left_specs.append(pl.BlockSpec((row_total, width), lambda i, place=place: (0, place)))
         else:
             left_specs.append(
-                pl.BlockSpec((1, row_total, width), lambda i, lead=lead: (lead, 0, 0))
+                pl.BlockSpec((1, row_total, width), lambda i, place=place: (place, 0, 0))
             )
         right_specs.append(pl.BlockSpec((block, width), lambda i, at=at: (first + i, at)))
         flops += 2 * row_total * half * width
@@ -161,8 +169,8 @@
         grid=(half // block,),
         in_specs=left_specs + right_specs,
         out_specs=[pl.BlockSpec((piece, block), lambda i: (0, i))] * 4,
-        out_shape=[jax.ShapeDtypeStruct((piece, half), BF)] * 2
-        + [jax.ShapeDtypeStruct((piece, half), F32)] * 2,
+        out_shape=[jax.ShapeDtypeStruct((piece, half), BF)] * sent
+        + [jax.ShapeDtypeStruct((piece, half), F32)] * (4 - sent),
         compiler_params=LIMIT,
         cost_estimate=cost(flops, flops // 500),
     )(*[a for a, unused in lefts], *[w for w, *unused in weights])
@@ -192,47 +200,37 @@
     )(left, right)
 
 
-def join_kernel(*refs):
-    join(refs[:8], refs[8])
-
-
-def joined(pieces):
-    rows, feature = pieces[0].shape
-    block = feature // 4
-    return pl.pallas_call(
-        join_kernel,
-        grid=(4,),
-        in_specs=[pl.BlockSpec((rows, block), lambda i: (0, i))] * 8,
-        out_specs=pl.BlockSpec((8 * rows, block), lambda i: (0, i)),
-        out_shape=jax.ShapeDtypeStruct((8 * rows, feature), BF),
-        compiler_params=ALONE,
-        cost_estimate=cost(1, 6 * 2**20),
-    )(*pieces)
-
-
-def turned_kernel(left, right, out):
+def turned_kernel(left, *refs):
+    out, right = refs[8:]
+    join(refs[:8], right)
     out[...] = dot(left[...], right[...], TN).astype(BF)
 
 
-def turned_products(left, right):
-    row_total, feature = right.shape
+def turned_products(left, pieces):
+    row_total, feature = left.shape[0], pieces[0].shape[1]
     width, block = left.shape[1], feature // 4
     flops = 2 * row_total * feature * width
     return pl.pallas_call(
         turned_kernel,
         grid=(4,),
-        in_specs=[
-            pl.BlockSpec((row_total, width), lambda i: (0, 0)),
+        in_specs=[pl.BlockSpec((row_total, width), lambda i: (0, 0))]
+        + [pl.BlockSpec((p.shape[0], block), lambda i: (0, i)) for p in pieces],
+        out_specs=[
+            pl.BlockSpec((width, block), lambda i: (i, 0)),
             pl.BlockSpec((row_total, block), lambda i: (0, i)),
         ],
-        out_specs=pl.BlockSpec((width, block), lambda i: (i, 0)),
-        out_shape=jax.ShapeDtypeStruct((4 * width, block), BF),
+        out_shape=[
+            jax.ShapeDtypeStruct((4 * width, block), BF),
+            jax.ShapeDtypeStruct((row_total, feature), BF),
+        ],
         compiler_params=LIMIT,
         cost_estimate=cost(flops, flops // 500),
-    )(left, right)
-
-
-def attn_kernel(h_ref, z_ref, d_ref, g_ref, y_ref, out):
+    )(left, *pieces)
+
+
+def attn_kernel(h_ref, d_ref, g_ref, y_ref, *refs):
+    out, z_ref = refs[8:]
+    join(refs[:8], z_ref)
     total, width = d_ref.shape[1], y_ref.shape[1]
     normed = h_ref[...]
     out[:, :total] = dot(normed, d_ref[...], TN).astype(BF)
@@ -240,11 +238,13 @@
     out[:, total + width :] = dot(y_ref[...], z_ref[...], TN).astype(BF)
 
 
-def attn_products(first_normed, grad_first, grad_gate, grad_z, gated):
+def attn_products(first_normed, grad_first, grad_gate, pieces, gated):
     row_total, feature = first_normed.shape
     total, width = grad_first.shape[1], gated.shape[1]
     block = feature // 4
-    column = pl.BlockSpec((row_total, block), lambda i: (0, i))
+
+    def column(rows):
+        return pl.BlockSpec((rows, block), lambda i: (0, i))
 
     def whole(columns):
         return pl.BlockSpec((row_total, columns), lambda i: (0, 0))
@@ -252,12 +252,14 @@
     return pl.pallas_call(
         attn_kernel,
         grid=(4,),
-        in_specs=[column, column, whole(total), whole(width), whole(width)],
+        in_specs=[column(row_total), whole(total), whole(width), whole(width)]
+        + [column(p.shape[0]) for p in pieces],
         out_specs=pl.BlockSpec((block, total + 2 * width), lambda i: (i, 0)),
         out_shape=jax.ShapeDtypeStruct((feature, total + 2 * width), BF),
+        scratch_shapes=[pltpu.VMEM((row_total, block), BF)],
         compiler_params=LIMIT,
         cost_estimate=cost(2 * row_total * feature * (total + 2 * width), 16 * 2**20),
-    )(first_normed, grad_z, grad_first, grad_gate, gated)
+    )(first_normed, grad_first, grad_gate, gated, *pieces)
 
 
 def place_kernel(at, *refs):
@@ -287,28 +289,28 @@
 
 def reorder_kernel(at, *refs):
     count = len(refs) // 4 - 1
-    rows = refs[0].shape[0]
+    width = refs[0].shape[1]
     for k in range(4):
         for n in range(4):
 
             @pl.when((at[0] ^ k) == n)
             def copy(k=k, n=n):
                 for m in range(count):
-                    refs[4 * count + k][m * rows : (m + 1) * rows, :] = refs[4 * m + n][...]
+                    refs[4 * count + k][:, m * width : (m + 1) * width] = refs[4 * m + n][...]
 
 
 def reordered(sets, start):
     rows, width = sets[0][0].shape
-    total = rows * len(sets)
+    total = width * len(sets)
     return pl.pallas_call(
         reorder_kernel,
         grid_spec=pltpu.PrefetchScalarGridSpec(
             num_scalar_prefetch=1,
             grid=(1,),
             in_specs=[pl.BlockSpec((rows, width), lambda i, at: (0, 0))] * (4 * len(sets)),
-            out_specs=[pl.BlockSpec((total, width), lambda i, at: (0, 0))] * 4,
+            out_specs=[pl.BlockSpec((rows, total), lambda i, at: (0, 0))] * 4,
         ),
-        out_shape=[jax.ShapeDtypeStruct((total, width), BF)] * 4,
+        out_shape=[jax.ShapeDtypeStruct((rows, total), BF)] * 4,
         compiler_params=ALONE,
         cost_estimate=cost(1, 4 * 2**20),
     )(start.astype(jnp.int32)[None], *[p for pieces in sets for p in pieces])
@@ -334,11 +336,11 @@
 def put_halves(value, top, low):
     step = pl.program_id(0)
 
-    @pl.when(step < 2)
+    @pl.when(step == 0)
     def first():
         top[...] = value
 
-    @pl.when(step >= 2)
+    @pl.when(step == 1)
     def second():
         low[...] = value
 
@@ -351,7 +353,7 @@
 
 
 def either(top, low):
-    return jnp.where(pl.program_id(0) < 2, top[...].astype(F32), low[...].astype(F32))
+    return jnp.where(pl.program_id(0) == 0, top[...].astype(F32), low[...].astype(F32))
 
 
 def up_norm_kernel(where, x_top, x_low, gain_ref, *refs):
@@ -368,9 +370,11 @@
     put_halves(grad.astype(BF), refs[7], refs[8])
 
 
-def result_kernel(where, second_ref, *refs):
-    result = second_ref[...] + half_sums(refs[:6])
-    put_quarters(where[2], result.astype(BF), refs[6:10], refs[10])
+def result_kernel(where, second_ref, own_ref, one, two, three, *refs):
+    result = second_ref[...] + own_ref[...]
+    for part in (one, two, three):
+        result += part[...].astype(F32)
+    put_quarters(where[2], result.astype(BF), refs[:4], refs[4])
 
 
 def input_norm_kernel(where, x_top, x_low, grad_ref, gain_ref, *refs):
@@ -381,15 +385,14 @@
 
 
 def on_rows(kernel, where, rows, gains, parts, quarters):
-    feature = gains.shape[1] if gains is not None else rows[0].shape[1]
-    row_total = parts[0].shape[0]
-    block = row_total // 4
+    feature = 2 * parts[0].shape[1] if parts else rows[0].shape[1]
+    row_total = rows[-1].shape[0] if not parts else parts[0].shape[0]
+    block = row_total // 2
 
     def spec(width):
         return pl.BlockSpec((block, width), lambda i, *_: (i, 0))
 
-    top = pl.BlockSpec((block, feature), lambda i, *_: (jnp.minimum(i, 1), 0))
-    low = pl.BlockSpec((block, feature), lambda i, *_: (jnp.maximum(i - 2, 0), 0))
+    top = low = pl.BlockSpec((block, feature), lambda i, *_: (0, 0))
     ins, args = [], []
     for r in rows:
         if isinstance(r, (list, tuple)):
@@ -400,7 +403,7 @@
             args.append(r)
     if gains is not None:
         ins.append(pl.BlockSpec(gains.shape, lambda i, *_: (0, 0)))
-    ins += [spec(feature // 2)] * 6
+    ins += [spec(feature // 2)] * len(parts)
     if quarters:
         outs = [spec(feature // 4)] * 4
         shapes = [jax.ShapeDtypeStruct((row_total, feature // 4), BF)] * 4
@@ -408,13 +411,13 @@
     else:
         outs = [spec(feature), top, low]
         shapes = [jax.ShapeDtypeStruct((row_total, feature), F32)]
-        shapes += [jax.ShapeDtypeStruct((2 * block, feature), BF)] * 2
+        shapes += [jax.ShapeDtypeStruct((block, feature), BF)] * 2
         scratch = []
     return pl.pallas_call(
         kernel,
         grid_spec=pltpu.PrefetchScalarGridSpec(
             num_scalar_prefetch=1,
-            grid=(4,),
+            grid=(2,),
             in_specs=ins,
             out_specs=outs,
             scratch_shapes=scratch,
@@ -425,7 +428,7 @@
     )(where, *args, *([] if gains is None else [gains]), *parts)
 
 
-def first_kernel(heads, pieces, w_ref, wf_ref, b_ref, h_ref, qkv_ref, keep_ref, slope_ref, gain_ref):
+def first_kernel(heads, pieces, w_ref, v_ref, wf_ref, b_ref, h_ref, qkv_ref, keep_ref, slope_ref, gain_ref):
     step = pl.program_id(0)
 
     @pl.when(step == 0)
@@ -437,22 +440,28 @@
                 turned[first : first + 1] + turned[first + 1 : first + 2] + turned[first + 2 : first + 3]
             )
         block = pieces[0].shape[0]
-        for at in range(8):
-            x = pieces[at][...].astype(F32)
+        for at, piece in enumerate(pieces):
+            x = piece[...].astype(F32)
             h_ref[pl.ds(at * block, block), :] = (x * mean_scale(x) * gain_ref[0:1, :]).astype(BF)
 
-    pre = dot(h_ref[...], w_ref[...])
-    qkv_ref[...] = pre.astype(BF)
-
-    @pl.when(step == 4)
-    def forget():
-        real = lanes_of(pre.shape[0]) < heads
-        forget_pre = jnp.where(real, pre[:, LANES:] + b_ref[...], 0.0)
-        less = jnp.exp(-jnp.abs(forget_pre))
-        keep_ref[...] = jnp.minimum(forget_pre, 0.0) - jnp.log1p(less)
-        slope_ref[...] = jnp.where(
-            real, jnp.where(forget_pre >= 0, less, 1.0) / (1.0 + less), 0.0
-        )
+    @pl.when(step < 3)
+    def query_key():
+        qkv_ref[...] = dot(h_ref[...], w_ref[...]).astype(BF)
+
+    @pl.when(step >= 3)
+    def value_forget():
+        pre = dot(h_ref[...], v_ref[...])
+        qkv_ref[...] = pre.astype(BF)
+
+        @pl.when(step == 4)
+        def forget():
+            real = lanes_of(pre.shape[0]) < heads
+            forget_pre = jnp.where(real, pre[:, LANES:] + b_ref[...], 0.0)
+            less = jnp.exp(-jnp.abs(forget_pre))
+            keep_ref[...] = jnp.minimum(forget_pre, 0.0) - jnp.log1p(less)
+            slope_ref[...] = jnp.where(
+                real, jnp.where(forget_pre >= 0, less, 1.0) / (1.0 + less), 0.0
+            )
 
 
 def first_products(heads, pieces, weights, bias):
@@ -461,9 +470,6 @@
 
     def whole_block(shape):
         return pl.BlockSpec(shape, lambda i: (0, 0))
-
-    def spec(shape, at):
-        return pl.BlockSpec(shape, at)
 
     def kernel(*refs):
         first_kernel(heads, refs[:8], *refs[8:])
@@ -473,13 +479,14 @@
         grid=(5,),
         in_specs=[whole_block(p.shape) for p in pieces]
         + [
-            spec((feature, block), lambda i: (0, i)),
-            spec((feature, LANES), lambda i: (0, 9)),
+            pl.BlockSpec((feature, block), lambda i: (0, jnp.minimum(i, 2))),
+            pl.BlockSpec((feature, block), lambda i: (0, jnp.maximum(i - 3, 0))),
+            pl.BlockSpec((feature, LANES), lambda i: (0, 3)),
             whole_block((1, LANES)),
         ],
         out_specs=[
             whole_block((row_total, feature)),
-            spec((row_total, block), lambda i: (0, i)),
+            pl.BlockSpec((row_total, block), lambda i: (0, i)),
             whole_block((row_total, LANES)),
             whole_block((row_total, LANES)),
             whole_block((8, feature)),
@@ -492,8 +499,8 @@
             jax.ShapeDtypeStruct((8, feature), F32),
         ],
         compiler_params=ALONE,
-        cost_estimate=cost(14 * row_total * feature * block, 16 * 2**20),
-    )(*pieces, weights, weights, bias)
+        cost_estimate=cost(10 * row_total * feature * block, 12 * 2**20),
+    )(*pieces, weights[0], weights[1], weights[1], bias)
 
 
 def gate_kernel(h_ref, w_ref, att_ref, gate_ref, y_ref):
@@ -529,12 +536,13 @@
 
 def join(pieces, whole):
     block = pieces[0].shape[0]
-    for at in range(8):
-        whole[pl.ds(at * block, block), :] = pieces[at][...]
+    for at, piece in enumerate(pieces):
+        whole[pl.ds(at * block, block), :] = piece[...]
 
 
 def up_kernel(*refs):
-    pieces, (g_ref, u_ref, h_ref, m_ref, to_gate_ref, to_up_ref) = refs[:8], refs[8:]
+    pieces, g_ref, u_ref = refs[:4], refs[4], refs[5]
+    h_ref, m_ref, to_gate_ref, to_up_ref = refs[-4:]
 
     @pl.when(pl.program_id(0) == 0)
     def first():
@@ -549,11 +557,10 @@
     to_up_ref[...] = silu.astype(to_up_ref.dtype)
 
 
-def up_products(pieces, weights):
-    row_total, feature = 8 * pieces[0].shape[0], pieces[0].shape[1]
+def up_products(half, held, pieces, weights):
+    rows, feature = 4 * pieces[0].shape[0], pieces[0].shape[1]
     hidden, block = weights.shape[1] // 2, 256
     steps = hidden // block
-    out = pl.BlockSpec((row_total, block), lambda i: (0, i))
     return pl.pallas_call(
         up_kernel,
         grid=(steps,),
@@ -561,17 +568,16 @@
         + [
             pl.BlockSpec((feature, block), lambda i: (0, i)),
             pl.BlockSpec((feature, block), lambda i: (0, steps + i)),
-        ],
-        out_specs=[pl.BlockSpec((row_total, feature), lambda i: (0, 0))] + [out] * 3,
-        out_shape=[
-            jax.ShapeDtypeStruct((row_total, feature), BF),
-            jax.ShapeDtypeStruct((row_total, hidden), BF),
-            jax.ShapeDtypeStruct((row_total, hidden), BF),
-            jax.ShapeDtypeStruct((row_total, hidden), BF),
-        ],
+        ]
+        + [pl.BlockSpec(memory_space=pl.ANY)] * len(held),
+        out_specs=[pl.BlockSpec((rows, feature), lambda i: (half, 0))]
+        + [pl.BlockSpec((rows, block), lambda i: (half, i))] * 3,
+        out_shape=[jax.ShapeDtypeStruct((2 * rows, feature), BF)]
+        + [jax.ShapeDtypeStruct((2 * rows, hidden), BF)] * 3,
+        input_output_aliases={6 + n: n for n in range(len(held))},
         compiler_params=ALONE,
-        cost_estimate=cost(4 * row_total * feature * hidden, 20 * 2**20),
-    )(*pieces, weights, weights)
+        cost_estimate=cost(4 * rows * feature * hidden, 16 * 2**20),
+    )(*pieces, weights, weights, *held)
 
 
 def down_kernel(g_ref, w_ref, to_gate_ref, to_up_ref, out_ref):
@@ -601,7 +607,7 @@
 
 
 def back_kernel(*refs):
-    pieces, (w_ref, gate_ref, att_ref, z_ref, datt_ref, dgate_ref) = refs[:8], refs[8:]
+    pieces, (w_ref, gate_ref, att_ref, datt_ref, dgate_ref, z_ref) = refs[:8], refs[8:]
     block = pieces[0].shape[0]
     for at in range(4):
 
@@ -631,12 +637,9 @@
         grid=(4,),
         in_specs=[spec(p.shape) for p in pieces]
         + [spec((feature, width), 1), by_rows(width), by_rows(width)],
-        out_specs=[by_rows(feature), by_rows(width), by_rows(width)],
-        out_shape=[
-            jax.ShapeDtypeStruct((row_total, feature), BF),
-            jax.ShapeDtypeStruct((row_total, width), BF),
-            jax.ShapeDtypeStruct((row_total, width), BF),
-        ],
+        out_specs=[by_rows(width)] * 2,
+        out_shape=[jax.ShapeDtypeStruct((row_total, width), BF)] * 2,
+        scratch_shapes=[pltpu.VMEM((row_total // 4, feature), BF)],
         compiler_params=ALONE,
         cost_estimate=cost(2 * row_total * feature * width, 10 * 2**20),
     )(*pieces, weights, gate, attended)
@@ -663,10 +666,9 @@
 
 
 def pick_kernel(backward, where, lengths, dealing, *refs):
-    count = 2
     column, row = where[0], where[1]
-    row_total = refs[0].shape[0] // (2 if backward else 1)
-    block = row_total // 4
+    block = refs[0].shape[0] // (1 if backward else 4)
+    row_total = 4 * block
     step = pl.program_id(0)
     given, slot_of, dealt, given_at = slot_tables(lengths, dealing, column)
     within = lax.broadcasted_iota(jnp.int32, (block, 1), 0)
@@ -693,33 +695,30 @@
         near = other + local + (jnp.bitwise_xor(part, column) - part) * block
     across = lax.broadcasted_iota(jnp.int32, (block, 2 * row_total), 1)
     chosen = jnp.where(across == near, 1.0, 0.0).astype(BF)
-    for at in range(count):
-        if backward:
-            picked = 0.0
-            for n in range(2):
-                for k in range(4):
-                    first = (4 * n + k) * block
-                    picked += dot(
-                        chosen[:, first : first + block],
-                        refs[n][(2 * k + at) * block : (2 * k + at + 1) * block, :],
-                    )
-            refs[2 + at][...] = picked.astype(BF)
-        else:
-            own, other = refs[2 * at][...], refs[2 * at + 1][...]
-            picked = dot(chosen[:, :row_total], own) + dot(chosen[:, row_total:], other)
-            picked = picked.astype(BF)
-            for k in range(4):
-
-                @pl.when(step == k)
-                def put(k=k, at=at, picked=picked):
-                    refs[2 * count + 4 * at + k][...] = picked
+    if backward:
+        picked = 0.0
+        for k in range(8):
+            picked += dot(chosen[:, k * block : (k + 1) * block], refs[k][...])
+        refs[8][...] = picked.astype(BF)
+        return
+    for at in range(2):
+        own, other = refs[2 * at][...], refs[2 * at + 1][...]
+        picked = dot(chosen[:, :row_total], own) + dot(chosen[:, row_total:], other)
+        picked = picked.astype(BF)
+        for k in range(4):
+
+            @pl.when(step == k)
+            def put(k=k, at=at, picked=picked):
+                refs[4 + 4 * at + k][...] = picked
 
 
 def moved_rows(backward, where, lengths, dealing, arrays):
-    row_total, width = arrays[0].shape
     if backward:
-        row_total = row_total // 2
-    block = row_total // 4
+        block, width = arrays[0].shape
+        row_total = 4 * block
+    else:
+        row_total, width = arrays[0].shape
+        block = row_total // 4
     if lax.axis_size("dp") != 2:
         column, row = where[0], where[1]
         local = jnp.arange(row_total, dtype=jnp.int32)
@@ -729,8 +728,7 @@
             to = given_targets(own_lengths, own_dealing, row * row_total + local)
             at = to % row_total
             to = to - at + ((at // block) ^ column) * block + at % block
-            both = arrays[0].reshape(4, 2, block, width).transpose(1, 0, 2, 3)
-            arrays = [half.reshape(row_total, width) for half in both]
+            arrays = [jnp.concatenate(arrays, axis=0)]
         else:
             swapped = (((local // block) ^ column) * block) + local % block
             to = dealt_sources(own_lengths, own_dealing, row * row_total + swapped)
@@ -738,24 +736,47 @@
         if backward:
             return moved
         return [m[k * block : (k + 1) * block] for m in moved for k in range(4)]
+    others = [swap(a, "dp", 1) for a in arrays]
     if backward:
-        outs = [pl.BlockSpec((block, width), lambda i, *_: (i, 0))] * 2
-        shapes = [jax.ShapeDtypeStruct((row_total, width), BF)] * 2
+        outs = [pl.BlockSpec((block, width), lambda i, *_: (i, 0))]
+        shapes = [jax.ShapeDtypeStruct((row_total, width), BF)]
+        ins = [*arrays, *others]
     else:
         outs = [pl.BlockSpec((block, width), lambda i, *_: (0, 0))] * 8
         shapes = [jax.ShapeDtypeStruct((block, width), BF)] * 8
+        ins = [arrays[0], others[0], arrays[1], others[1]]
     return pl.pallas_call(
         lambda *refs: pick_kernel(backward, *refs),
         grid_spec=pltpu.PrefetchScalarGridSpec(
             num_scalar_prefetch=3,
             grid=(4,),
-            in_specs=[pl.BlockSpec(arrays[0].shape, lambda i, *_: (0, 0))] * (2 * len(arrays)),
+            in_specs=[pl.BlockSpec(a.shape, lambda i, *_: (0, 0)) for a in ins],
             out_specs=outs,
         ),
         out_shape=shapes,
         compiler_params=pltpu.CompilerParams(vmem_limit_bytes=40 * 2**20),
-        cost_estimate=cost(8 * row_total * row_total * width * 2, 8 * 2**20),
-    )(where, lengths, dealing, *[half for a in arrays for half in (a, swap(a, "dp", 1))])
+        cost_estimate=cost(16 * row_total * row_total * width, 8 * 2**20),
+    )(where, lengths, dealing, *ins)
+
+
+def piece_rows(piece, half):
+    rows = []
+    for places in (UPPER, LOWER):
+        place = jnp.int32(places[0])
+        for k in (1, 2, 3):
+            place = jnp.where(piece == k, places[k], place)
+        rows.append(pl.ds(pl.multiple_of(place * half, half), half))
+    return rows
+
+
+def get_rows(ref, rows):
+    return jnp.concatenate([ref[part, :] for part in rows], axis=0)
+
+
+def put_rows(ref, rows, columns, value):
+    half = value.shape[0] // 2
+    for n, part in enumerate(rows):
+        ref[part, columns] = value[n * half : (n + 1) * half]
 
 
 def lanes_of(rows):
@@ -798,7 +819,7 @@
     lanes = lanes_of(block)
 
     def rows_of(at):
-        return pl.ds(pl.multiple_of((column ^ at) * block, block), block)
+        return piece_rows(column ^ at, block // 2)
 
     @pl.when(pair == 0)
     def sum_keeps():
@@ -809,7 +830,7 @@
         for at in range(4):
             sums = running + lax.dot_general(
                 ones,
-                keep_ref[rows_of(at), :],
+                get_rows(keep_ref, rows_of(at)),
                 (((1,), (0,)), ((), ())),
                 precision=lax.Precision.HIGHEST,
                 preferred_element_type=F32,
@@ -833,10 +854,10 @@
                 lanes, base, (-one, -two, -three, (second - 1.0) * FAR, 1.0, 1.0, 1.0), 0.0
             )
             qa_ref[head, own, :] = jnp.where(
-                mine, q_ref[rows, :].astype(F32) * 0.125, q_side
+                mine, get_rows(q_ref, rows).astype(F32) * 0.125, q_side
             ).astype(BF)
-            ka_ref[head, own, :] = jnp.where(mine, k_ref[rows, :].astype(F32), k_side).astype(BF)
-            va_ref[head, own, :] = jnp.where(mine, v_ref[rows, :].astype(F32), 1.0).astype(BF)
+            ka_ref[head, own, :] = jnp.where(mine, get_rows(k_ref, rows).astype(F32), k_side).astype(BF)
+            va_ref[head, own, :] = jnp.where(mine, get_rows(v_ref, rows).astype(F32), 1.0).astype(BF)
 
     below = lax.broadcasted_iota(jnp.int32, (block, block), 0)
     across = lax.broadcasted_iota(jnp.int32, (block, block), 1)
@@ -865,7 +886,7 @@
                 lanes, base + 4, (-one, -two, -three), queries.astype(F32)
             ).astype(BF)
         attended = jnp.where(lanes < 64, results[0], results[1])
-        att_ref[rows_of(at), :] = attended
+        put_rows(att_ref, rows_of(at), slice(None), attended)
 
 
 def attend_forward(where, lengths, dealing, qkv, keep):
@@ -930,7 +951,7 @@
     width = att_ref.shape[1] * pairs
 
     def rows_of(at):
-        return pl.ds(pl.multiple_of((column ^ at) * block, block), block)
+        return piece_rows(column ^ at, block // 2)
 
     def lanes_at(group):
         return pl.ds(pl.multiple_of((group * pairs + pair) * LANES, LANES), LANES)
@@ -941,9 +962,9 @@
 
     for at in range(4):
         rows, own = rows_of(at), pl.ds(at * block, block)
-        grad_att = datt_ref[rows, :].astype(F32)
-        inner = grad_att * att_ref[rows, :]
-        values = v_ref[rows, :].astype(F32)
+        grad_att = get_rows(datt_ref, rows).astype(F32)
+        inner = grad_att * get_rows(att_ref, rows)
+        values = get_rows(v_ref, rows).astype(F32)
         for head in range(2):
             mine = (lanes < 64) if head == 0 else (lanes >= 64)
             base = 64 if head == 0 else 0
@@ -994,7 +1015,7 @@
         left = lanes < 64
         for group, ref, scale in ((0, dq_ref, 0.125), (1, dk_ref, 1.0), (2, dv_ref, 1.0)):
             both = jnp.where(left, ref[0, own, :], ref[1, own, :])
-            out_ref[rows, lanes_at(group)] = (both * scale).astype(BF)
+            put_rows(out_ref, rows, lanes_at(group), (both * scale).astype(BF))
 
     @pl.when(pair == pairs - 1)
     def finish():
@@ -1010,7 +1031,12 @@
             )
             running = sums[:1, :]
             rows = rows_of(at)
-            out_ref[rows, 3 * width :] = (sums * slope_ref[rows, :]).astype(BF)
+            put_rows(
+                out_ref,
+                rows,
+                slice(3 * width, None),
+                (sums * get_rows(slope_ref, rows)).astype(BF),
+            )
 
 
 def attend_backward(where, qa, ka, qkv, grad_att, attended, slope):
@@ -1090,11 +1116,10 @@
     spare = jnp.zeros((w_query.shape[0], LANES - heads - 6), BF)
     side = 3 * width
     last = side + LANES
-    w_first = whole(
-        jnp.concatenate(
-            [own_share(w) for w in (w_query, w_key, w_value, w_forget, gains, spare)], axis=1
-        )
-    )
+    def side_by_side(*weights):
+        return jnp.concatenate([own_share(w) for w in weights], axis=1)
+
+    w_first = [whole(side_by_side(w_query, w_key))]
 
     where = jnp.stack([column, row, lane]).astype(jnp.int32)
     paired = lax.axis_size("dp") == 2
@@ -1105,34 +1130,39 @@
         spread_line(reordered([x_parts], column ^ lane)), spread_plane(grad_parts)
     )
     grad_parts, x_parts = tie(reordered([grad_parts], column ^ lane), x_parts)
+    w_first.append(whole(side_by_side(w_value, w_forget, gains, spare)))
+    later = [side_by_side(w_ogate, w_out.T), side_by_side(w_gate, w_up)]
+    x_parts, later, w_first[0] = tie(x_parts, later, w_first[0])
+    w_second, w_gate_up = [whole(w) for w in later]
     grad_parts = spread_line(grad_parts)
-    x_full, unused = gather_rows(*placed(x_parts, lane), ahead=grad_parts[1])
-    w_second = jnp.concatenate([own_share(w_ogate), own_share(w_out.T)], axis=1)
-    w_gate_up = jnp.concatenate([own_share(w_gate), own_share(w_up)], axis=1)
-    x_full, grad_parts, w_second, w_gate_up = tie(x_full, grad_parts, w_second, w_gate_up)
-    w_second, w_gate_up = whole(w_second), whole(w_gate_up)
-    grad_rows = placed(grad_parts, lane)
+    x_full, unused = gather_rows(*placed(x_parts, lane), ahead=(grad_parts[1], w_first[1]))
 
     bias = jnp.pad(b_forget, (0, LANES - heads))[None]
     first_normed, qkv, keep, slope, gains = first_products(heads, x_full, w_first, bias)
-    grad_full, (attended, qa, ka) = gather_rows(
-        *grad_rows,
-        lambda ready: attend_forward(where, seq_lengths, seq_deal, ready[1], keep),
-        qkv,
-    )
-    grad_full, attended = tie(grad_full, attended)
+    grad_parts, qkv = tie(grad_parts, qkv)
+    top, low = placed(grad_parts, lane)
+    grad_rows = [top, low]
+    qkv, top, low = tie(qkv, top, low)
+    top_x, low_y = swap(top, "tx", 1), swap(low, "tx", 2)
+    low_x, top_y = swap(low, "tx", 1), swap(top, "tx", 2)
+    attended, qa, ka = attend_forward(where, seq_lengths, seq_deal, qkv, keep)
+    attended, top_x, low_y, low_x, top_y = tie(attended, top_x, low_y, low_x, top_y)
+    top_d, low_d = swap(top_x, "tx", 2), swap(low_y, "tx", 1)
+    grad_full = [top, low, top_x, low_y, low_x, top_y, top_d, low_d]
     w_down_t, attended = tie(own_share(w_down.T), attended)
     w_down_t = whole(w_down_t)
     out_gate, gated = gate_products(first_normed, w_second, attended)
-    parts, unused = scatter_products([(gated, None)], [(w_second, width, 1)])
+    gated, grad_full[6:] = tie(gated, grad_full[6:])
+    parts, unused = scatter_products([(gated, 0)], [(w_second, width, 1)])
     second, top, low = on_rows(up_norm_kernel, where, [x_full[:2]], gains, parts, False)
 
-    h2_parts, grad_full = gather_rows(
-        top, low, lambda ready: joined(tie(grad_full, ready)[0])
-    )
-    h2_parts, w_gate_up = tie(h2_parts, w_gate_up)
-    h2_full, mid, to_gate, to_up = up_products(h2_parts, w_gate_up)
-    part, grad_full = tie(turned_products(mid, grad_full), grad_full)
+    def up_half(pieces, ahead):
+        return up_products(0, [], pieces, w_gate_up)
+
+    h2_parts, held = gather_rows(top, low, up_half)
+    h2_full, mid, to_gate, to_up = up_products(1, held, h2_parts[4:], w_gate_up)
+    part, grad_full = turned_products(mid, grad_full)
+    part, grad_full = tie(part, grad_full)
     grads_down = summed(part)
     grad_gate_up = down_products(grad_full, w_down_t, to_gate, to_up)
 
@@ -1151,53 +1181,56 @@
         down_norm_kernel, where, [second, grad_rows], gains, parts, False
     )
 
-    def result_products(ready):
-        left, unused = tie(mid, ready)
-        return [
-            half_products(at, order, [(left, None)], [(w_down_t, hidden, 0)])
-            for at, order in ((0, (3, 1, 2, 0)), (1, (3, 2, 1, 0)))
-        ]
-
-    z_parts, ((a3, a1, a2, a0), (b3, b2, b1, b0)) = gather_rows(top, low, result_products)
-
-    z_parts, a3, a1, b3, b2 = tie(z_parts, a3, a1, b3, b2)
-    a3, a1 = swap(a3, "tx", 1), swap(a1, "tx", 1)
-    b3, b2 = swap(b3, "tx", 2), swap(b2, "tx", 2)
-    z_full, grad_att, grad_ogate = back_products(z_parts, w_second, out_gate, attended)
-    a3, b3, grad_att = tie(a3, b3, grad_att)
-    a2 = swap((a2 + a3.astype(F32)).astype(BF), "tx", 2)
-    b1 = swap((b1 + b3.astype(F32)).astype(BF), "tx", 1)
+    def result_products(pieces, ahead):
+        left, unused = tie(mid, pieces)
+        return part_products(None, (1, 2, 3, 0), [(left, 0)], [(w_down_t, hidden, 0)])
+
+    z_parts, (*sent, own) = gather_rows(top, low, result_products)
+
+    sent = [swap(piece, "tx", k + 1) for k, piece in enumerate(sent)]
+    grad_att, grad_ogate = back_products(z_parts, w_second, out_gate, attended)
     grad_first = attend_backward(where, qa, ka, qkv, grad_att, attended, slope)
-    grad_first, a1, a2, b1, b2, grads_down = tie(grad_first, a1, a2, b1, b2, grads_down)
-    output = on_rows(result_kernel, where, [second], None, [a0, a1, a2, b0, b1, b2], True)
+    grad_first, sent, grads_down = tie(grad_first, sent, grads_down)
+    output = on_rows(result_kernel, where, [second, own, *sent], None, [], True)
     output, grad_first = tie(output, grad_first)
     output = spread_line(output)
-    part = attn_products(first_normed, grad_first, grad_ogate, z_full, gated)
+    part = attn_products(first_normed, grad_first, grad_ogate, z_parts, gated)
     part, grad_first, output = tie(part, grad_first, output)
     grads_attn = summed(part)
-    parts, unused = scatter_products(
-        [(grad_first, None), (grad_ogate, None)],
-        [(w_first, last, 0), (w_second, width, 0)],
-    )
-    bias_grad = jnp.sum(grad_first[:, side:].astype(F32), axis=0, keepdims=True)
-    if paired:
-        bias_grad = bias_grad + swap(bias_grad, "dp", 1)
-        bias_grad = pairs_sum(spread_line([bias_grad] * 4))
-    else:
-        bias_grad = lax.psum(bias_grad, ("dp", "ty"))
-    parts, grads_gate_up, bias_grad = tie(parts, grads_gate_up, bias_grad)
-    grad_x = on_rows(input_norm_kernel, where, [x_full[:2], grad_second], gains, parts, True)
-
-    output, grad_x = tie(output, spread_line(grad_x))
-    back = spread_plane(reordered([output, grad_x], column ^ lane))
-
-    grad_down = reduce_end(grads_down)
-    grad_gate_up = reduce_end(grads_gate_up)
-    grad_attn = reduce_end(grads_attn)
 
     def row_dots(*sides):
         return sum(jnp.sum(w.astype(F32) * g, axis=1) for w, g in sides)
 
+    def finish(ready):
+        down, gate_up, bias, unused = tie(
+            grads_down, grads_gate_up, grad_first[:, side:], ready
+        )
+        bias = jnp.sum(bias.astype(F32), axis=0, keepdims=True)
+        bias = bias + swap(bias, "dp", 1) if paired else lax.psum(bias, ("dp", "ty"))
+        down, gate_up = reduce_end(down), reduce_end(gate_up)
+        mlp = [gate_up[:, :hidden], gate_up[:, hidden:], down]
+        return mlp, row_dots((w_gate, mlp[0]), (w_up, mlp[1])) / mlp_gain, bias
+
+    parts, (grads_mlp, own_mlp_gain, bias_grad) = scatter_products(
+        [(grad_first, 0), (grad_first, 3), (grad_first, 4), (grad_ogate, 0)],
+        [(w_first[0], 2 * width, 0), (w_first[1], 256, 0), (w_first[1], 256, 1), (w_second, width, 0)],
+        finish,
+    )
+    grad_x = on_rows(input_norm_kernel, where, [x_full[:2], grad_second], gains, parts, True)
+
+    def given(pieces):
+        return moved_rows(True, where, seq_lengths, seq_deal, pieces)[0]
+
+    output, grad_x = tie(output, grad_x)
+    grad_x = spread_line(grad_x)
+    output = spread_plane(reordered([output], column ^ lane))
+    if paired:
+        bias_grad = pairs_sum(spread_line([bias_grad] * 4))
+    output, grad_x[1] = tie(output, grad_x[1])
+    output, grad_x, bias_grad = tie(given(output), grad_x, bias_grad)
+    grad_x = spread_plane(reordered([grad_x], column ^ lane))
+
+    grad_attn = reduce_end(grads_attn)
     grads = [
         grad_attn[:, :width],
         grad_attn[:, width : 2 * width],
@@ -1205,19 +1238,11 @@
         grad_attn[:, last : last + width],
         grad_attn[:, side : side + heads],
     ]
-    own_gains = jnp.stack(
-        [
-            row_dots(*zip((w_query, w_key, w_value, w_ogate, w_forget), grads)) / attn_gain,
-            row_dots((w_gate, grad_gate_up[:, :hidden]), (w_up, grad_gate_up[:, hidden:]))
-            / mlp_gain,
-        ]
-    )
-    grad_gains = spread_plane([own_gains] * 4)
-    back, grad_gains, grads = tie(back, grad_gains, grads)
+    own_gain = row_dots(*zip((w_query, w_key, w_value, w_ogate, w_forget), grads)) / attn_gain
+    grad_gains = spread_plane([jnp.stack([own_gain, own_mlp_gain])] * 4)
+    grad_x, output, grad_gains, grads = tie(grad_x, output, grad_gains, grads)
     grad_gains = pairs_sum(grad_gains)
-    output, grad_input = moved_rows(
-        True, where, seq_lengths, seq_deal, [jnp.concatenate(back, axis=0)]
-    )
+    grad_input = given(grad_x)
     return (
         output[None],
         grad_input[None],
@@ -1226,9 +1251,7 @@
         bias_grad[0, :heads],
         grad_attn[:, last + width :],
         grad_gains[1],
-        grad_gate_up[:, :hidden],
-        grad_gate_up[:, hidden:],
-        grad_down,
+        *grads_mlp,
     )
 
 

time: 531 us -> 499 us (0.940)
  starting transfers between devices: 101 us -> 84.5 us
  waiting for transfers between devices: 154 us -> 141 us
    ppermute x82 -> x89, starting transfers between devices: 100 us -> 83.2 us  [swap(): lax.ppermute(values, axis, [(at, at ^ step) for at in range(lax.axis_size...]
    ppermute x82 -> x89, waiting for transfers between devices: 152 us -> 141 us  [swap(): lax.ppermute(values, axis, [(at, at ^ step) for at in range(lax.axis_size...]
    pallas_call x10 -> x8, Pallas kernels: 56.8 us -> 51.2 us  [the longest x7 39.4 us: part_products(): pl.pallas_call(lambda *refs: part_kernel(order, len(lefts), *refs), grid=...]
    pallas_call x1 -> x2, Pallas kernels: 11.8 us -> 16 us  [up_products(): pl.pallas_call(up_kernel, grid=(steps,), in_specs=[pl.BlockSpec(p.shape,...]
    unnamed x200 -> x189, local copies, waits for them, and re-layouts: 26.3 us -> 23.2 us
    pallas_call x2 -> x3, Pallas kernels: 16.9 us -> 17.6 us  [moved_rows(): pl.pallas_call(lambda *refs: pick_kernel(backward, *refs), grid_spec=pltp...]
  transfers between devices with their start and end apart: 89 -> 97, of which waited for: 41 -> 38; matrix products, arithmetic and copies ran while one was open for 3% -> 5% of each run, Pallas kernels for 38% -> 41%
where the time goes in v3:
time: 499 us; the launch traced here: 494 us
  Pallas kernels  206 us (41%)
  waiting for transfers between devices  141 us (28%)
  starting transfers between devices  84.5 us (17%)
  local copies, waits for them, and re-layouts  29.4 us (6%)
  other arithmetic  16.5 us (3%)
  between operations  15.4 us (3%)
    ppermute x89, waiting for transfers between devices, swap(): lax.ppermute(values, axis, [(at, at ^ step) for at in range(lax.axis_size...  141 us
    ppermute x89, starting transfers between devices, swap(): lax.ppermute(values, axis, [(at, at ^ step) for at in range(lax.axis_size...  83.2 us
    pallas_call x7, Pallas kernels, part_products(): pl.pallas_call(lambda *refs: part_kernel(order, len(lefts), *refs), grid=...  39.4 us
    unnamed x189, local copies, waits for them, and re-layouts  23.2 us
    pallas_call x1, Pallas kernels, attend_backward(): pl.pallas_call(backward_kernel, grid_spec=pltpu.PrefetchScalarGridSpec(nu...  20.7 us
    pallas_call x4, Pallas kernels, on_rows(): pl.pallas_call(kernel, grid_spec=pltpu.PrefetchScalarGridSpec(num_scalar_...  20 us
    pallas_call x3, Pallas kernels, moved_rows(): pl.pallas_call(lambda *refs: pick_kernel(backward, *refs), grid_spec=pltp...  17.6 us
    pallas_call x1, Pallas kernels, attend_forward(): pl.pallas_call(forward_kernel, grid_spec=pltpu.PrefetchScalarGridSpec(num...  16.7 us
  transfers between devices with their start and end apart: 97, of which 38 were waited for; matrix products, arithmetic and copies ran while one was open for 5% of the time, Pallas kernels for 41%

profile of v3, /device:TPU:9, one launch (start us, length us, event | category | flops | bytes accessed | tf_op | source)
XLA Modules:
  0.0 493.5 jit_solution(11658027188820417834)
XLA Ops:
  17.6 8.7 %shard_map.263 = (bf16[256,384]{1,0:T(8,128)(2,1)S(1)}, bf16[256,384]{1,0:T(8,128)(2,1)}, bf16[256,384]{1,0:T(8,128)(2,1)}, bf16[256,384]{1,0:T(8,128)(2,1)}, bf...) custom-call(s32[3]{0:T(128)S(1)} %pad_add_fusion.refs_0_.where, ...), custom_call_target="tpu_custom_call" | custom-call | flops 6442450944 | bytes 8388608 | tf_op jit(solution)/shard_map/pallas_call | solution.py:748
  35.6 4.3 collective-permute-done.4.refs_3_
  49.4 5.3 %collective-permute-done.6.refs_2_ = bf16[256,384]{1,0:T(8,128)(2,1)S(1)} collective-permute-done((bf16[256,384]{1,0:T(8,128)(2,1)}, bf16[256,384]{1,0:T(8,128)(2,1)S(1)}, u32[]{:S(2)}, u32[]{:S(2)}) %collective-permute-start.6) | collective-permute-done | bytes 196640 | tf_op jit(solution)/shard_map/ppermute | solution.py:67
  54.7 16.5 %collective-permute-done.7.refs_3_ = bf16[256,384]{1,0:T(8,128)(2,1)S(1)} collective-permute-done((bf16[256,384]{1,0:T(8,128)(2,1)}, bf16[256,384]{1,0:T(8,128)(2,1)S(1)}, u32[]{:S(2)}, u32[]{:S(2)}) %collective-permute-start.7) | collective-permute-done | bytes 196640 | tf_op jit(solution)/shard_map/ppermute | solution.py:67
  80.4 3.0 collective-permute-done.13.refs_1_
  90.8 3.8 collective-permute-start.19
  94.7 5.5 %collective-permute-done.16.refs_6_ = bf16[128,1536]{1,0:T(8,128)(2,1)S(1)} collective-permute-done((bf16[128,1536]{1,0:T(8,128)(2,1)S(1)}, bf16[128,1536]{1,0:T(8,128)(2,1)S(1)}, u32[]{:S(2)}, u32[]{:S(2)}) %collective-permute-start.16) | collective-permute-done | bytes 393248 | tf_op jit(solution)/shard_map/ppermute | solution.py:67
  100.9 12.0 %shard_map.267 = (bf16[1024,1536]{1,0:T(8,128)(2,1)}, bf16[1024,1280]{1,0:T(8,128)(2,1)}, f32[1024,128]{1,0:T(8,128)}, f32[1024,128]{1,0:T(8,128)}, f32[8,1536]{1,0:T(8,128)}) custom-call(bf16[128,1536]{1,0:T(8,128)(2,1)} %get-tuple-element.302.refs_0_.x_top, bf16[128,1536]{1,0:T(8,128)(2,1)} %get-tuple-element.303.refs_1_.x_low, ...), custom_call_target="tpu_custom_call" | custom-call | flops 4026531840 | bytes 12582912 | tf_op jit(solution)/shard_map/pallas_call | solution.py:477
  112.9 11.2 %collective-permute-done.19.refs_3_ = bf16[256,384]{1,0:T(8,128)(2,1)S(1)} collective-permute-done((bf16[256,384]{1,0:T(8,128)(2,1)}, bf16[256,384]{1,0:T(8,128)(2,1)S(1)}, u32[]{:S(2)}, u32[]{:S(2)}) %collective-permute-start.19) | collective-permute-done | bytes 196640 | tf_op jit(solution)/shard_map/ppermute | solution.py:67
  129.9 16.7 %shard_map.269 = (f32[1024,384]{1,0:T(8,128)}, bf16[6,1024,128]{2,1,0:T(8,128)(2,1)}, bf16[6,1024,128]{2,1,0:T(8,128)(2,1)}) custom-call(s32[3]{0:T(128)} %copy-done.33, s32[4,4]{1,0:T(4,128)} %refs_1_.5, s32[4,4]{1,0:T(4,128)} %refs_2_.5, bf16[1024,1280]{1,0:T(8,128)(2,1)} %get-tuple-element.322.q_ref.k_ref.v_ref, ...), custom_call_target="tpu_custom_call" | custom-call | flops 10000000000 | bytes 8388608 | tf_op jit(solution)/shard_map/pallas_call | solution.py:901
  151.2 4.5 shard_map.270
  156.9 3.2 shard_map.271
  164.0 4.1 collective-permute-done.27
  170.1 4.7 collective-permute-done.29
  176.0 5.7 %collective-permute-done.28.refs_2_ = bf16[256,768]{1,0:T(8,128)(2,1)S(1)} collective-permute-done((bf16[256,768]{1,0:T(8,128)(2,1)S(1)}, bf16[256,768]{1,0:T(8,128)(2,1)S(1)}, u32[]{:S(2)}, u32[]{:S(2)}) %collective-permute-start.28) | collective-permute-done | bytes 393248 | tf_op jit(solution)/shard_map/ppermute | solution.py:67
  181.7 8.4 %collective-permute-done.31.refs_5_ = bf16[256,768]{1,0:T(8,128)(2,1)S(1)} collective-permute-done((bf16[256,768]{1,0:T(8,128)(2,1)S(1)}, bf16[256,768]{1,0:T(8,128)(2,1)S(1)}, u32[]{:S(2)}, u32[]{:S(2)}) %collective-permute-start.31) | collective-permute-done | bytes 393248 | tf_op jit(solution)/shard_map/ppermute | solution.py:67
  190.9 4.7 shard_map.273
  198.6 4.3 collective-permute-done.34.refs_2_
  204.4 8.0 %shard_map.274 = (bf16[1024,1536]{1,0:T(8,128)(2,1)}, bf16[1024,1024]{1,0:T(8,128)(2,1)}, bf16[1024,1024]{1,0:T(8,128)(2,1)}, bf16[1024,1024]{1,0:T(8,128)(2,1)}) custom-call(bf16[128,1536]{1,0:T(8,128)(2,1)} %get-tuple-element.353.refs_0_, bf16[128,1536]{1,0:T(8,128)(2,1)} %get-tuple-element.352.refs_1_, bf16[128,1536]{1,0:T(8,128)(2,1)} %copy-done.55, ...), custom_call_target="tpu_custom_call" | custom-call | flops 3221225472 | bytes 16777216 | tf_op jit(solution)/shard_map/pallas_call | solution.py:564
  212.4 4.6 collective-permute-done.36.refs_2_
  217.0 8.1 %shard_map.275 = (bf16[1024,1536]{1,0:T(8,128)(2,1)}, bf16[1024,1024]{1,0:T(8,128)(2,1)}, bf16[1024,1024]{1,0:T(8,128)(2,1)}, bf16[1024,1024]{1,0:T(8,128)(2,1)}) custom-call(bf16[128,1536]{1,0:T(8,128)(2,1)} %collective-permute-done.32.refs_0_, ...), custom_call_target="tpu_custom_call", output_to_operand_aliasing={{0}: (6, {}), {1}: (7, {}), {2}: (8, {}), {3}: (9, {})} | custom-call | flops 3221225472 | bytes 16777216 | tf_op jit(solution)/shard_map/pallas_call | solution.py:564
  225.1 8.1 %shard_map.276 = (bf16[4096,384]{1,0:T(8,128)(2,1)}, bf16[1024,1536]{1,0:T(8,128)(2,1)}) custom-call(bf16[1024,1024]{1,0:T(8,128)(2,1)} %get-tuple-element.402.left.refs_0_, bf16[128,1536]{1,0:T(8,128)(2,1)S(1)} %copy-done.29, bf16[128,1536]{1,0:T(8,128)(2,1)S(1)} %copy-done.30, bf16[128,1536]{1,0:T(8,128)(2,1)S(1)} %collective-permute-done.20.refs_2_, ...), custom_call_target="tpu_custom_call" | custom-call | flops 3221225472 | bytes 6442450 | tf_op jit(solution)/shard_map/pallas_call | solution.py:213
  234.8 8.2 %shard_map.277.refs_0_.refs_1_.right = bf16[2,1024,1024]{2,1,0:T(8,128)(2,1)} custom-call(bf16[1024,1536]{1,0:T(8,128)(2,1)} %get-tuple-element.366.g_ref, bf16[1536,1024]{1,0:T(8,128)(2,1)} %all-gather.14.cloned.1.call-done.w_ref.refs_1_, bf16[1024,1024]{1,0:T(8,128)(2,1)S(1)} %copy-done.2, bf16[1024,1024]{1,0:T(8,128)(2,1)} %get-tuple-element.369.to_up_ref), custom_call_target="tpu_custom_call" | custom-call | flops 3221225472 | bytes 16777216 | tf_op jit(solution)/shard_map/pallas_call | solution.py:593
  243.0 6.7 %shard_map.278 = (bf16[256,768]{1,0:T(8,128)(2,1)S(1)}, bf16[256,768]{1,0:T(8,128)(2,1)S(1)}, f32[256,768]{1,0:T(8,128)S(1)}, f32[256,768]{1,0:T(8,128)S(1)}) custom-call(bf16[2,1024,1024]{2,1,0:T(8,128)(2,1)} %shard_map.277.refs_0_.refs_1_.right, bf16[2,1024,1024]{2,1,0:T(8,128)(2,1)} %shard_map.277.refs_0_.refs_1_.right, ...), custom_call_target="tpu_custom_call" | custom-call | flops 3221225472 | bytes 6442450 | tf_op jit(solution)/shard_map/pallas_call | solution.py:167
  251.7 6.8 %shard_map.279 = (bf16[256,768]{1,0:T(8,128)(2,1)S(1)}, bf16[256,768]{1,0:T(8,128)(2,1)S(1)}, f32[256,768]{1,0:T(8,128)S(1)}, f32[256,768]{1,0:T(8,128)S(1)}) custom-call(bf16[2,1024,1024]{2,1,0:T(8,128)(2,1)} %shard_map.277.refs_0_.refs_1_.right, bf16[2,1024,1024]{2,1,0:T(8,128)(2,1)} %shard_map.277.refs_0_.refs_1_.right, ...), custom_call_target="tpu_custom_call" | custom-call | flops 3221225472 | bytes 6442450 | tf_op jit(solution)/shard_map/pallas_call | solution.py:167
  262.2 4.2 collective-permute-done.41
  266.8 11.3 %shard_map.280 = bf16[1536,2048]{1,0:T(8,128)(2,1)} custom-call(bf16[1024,1536]{1,0:T(8,128)(2,1)S(1)} %copy-done.6, bf16[2,1024,1024]{2,1,0:T(8,128)(2,1)} %shard_map.277.refs_0_.refs_1_.right), custom_call_target="tpu_custom_call" | custom-call | flops 6442450944 | bytes 12884901 | tf_op jit(solution)/shard_map/pallas_call | solution.py:189
  279.4 5.4 %shard_map.281 = (f32[256,1536]{1,0:T(8,128)}, bf16[128,1536]{1,0:T(8,128)(2,1)}, bf16[128,1536]{1,0:T(8,128)(2,1)}) custom-call(s32[3]{0:T(128)} %copy-done.33, f32[256,1536]{1,0:T(8,128)} %get-tuple-element.351.second_ref, bf16[128,1536]{1,0:T(8,128)(2,1)} %get-tuple-element.325.refs_0_.grad_top, bf16[128,1536]{1,0:T(8,128)(2,1)} %get-tuple-element.326.refs_1_.grad_low, ...), custom_call_target="tpu_custom_call" | custom-call | flops 1 | bytes 6291456 | tf_op jit(solution)/shard_map/pallas_call | solution.py:416
  287.8 3.9 collective-permute-done.44.refs_2_
  294.1 7.6 %shard_map.282 = (bf16[256,1536]{1,0:T(8,128)(2,1)}, bf16[256,1536]{1,0:T(8,128)(2,1)S(1)}, bf16[256,1536]{1,0:T(8,128)(2,1)S(1)}, f32[256,1536]{1,0:T(8,128)S(1)}) custom-call(bf16[1024,1024]{1,0:T(8,128)(2,1)} %get-tuple-element.402.left.refs_0_, bf16[1536,1024]{1,0:T(8,128)(2,1)} %all-gather.14.cloned.1.call-done.w_ref.refs_1_), custom_call_target="tpu_custom_call" | custom-call | flops 3221225472 | bytes 6442450 | tf_op jit(solution)/shard_map/pallas_call | solution.py:167
  306.4 6.6 %shard_map.283 = (bf16[1024,384]{1,0:T(8,128)(2,1)}, bf16[1024,384]{1,0:T(8,128)(2,1)}) custom-call(bf16[128,1536]{1,0:T(8,128)(2,1)} %get-tuple-element.398.refs_0_, bf16[128,1536]{1,0:T(8,128)(2,1)} %get-tuple-element.399.refs_1_, bf16[128,1536]{1,0:T(8,128)(2,1)} %copy-done.17, bf16[128,1536]{1,0:T(8,128)(2,1)} %copy-done.19, ...), custom_call_target="tpu_custom_call" | custom-call | flops 1207959552 | bytes 10485760 | tf_op jit(solution)/shard_map/pallas_call | solution.py:635
  313.0 20.7 %shard_map.284.d_ref.refs_0_.refs_1_.refs_2_ = bf16[1024,1280]{1,0:T(8,128)(2,1)} custom-call(s32[3]{0:T(128)} %copy-done.33, bf16[6,1024,128]{2,1,0:T(8,128)(2,1)} %get-tuple-element.404.qa_ref, bf16[6,1024,128]{2,1,0:T(8,128)(2,1)} %get-tuple-element.405.ka_ref, bf16[1024,1280]{1,0:T(8,128)(2,1)} %get-tuple-element.322.q_ref.k_ref.v_ref, ...), custom_call_target="tpu_custom_call" | custom-call | flops 12000000000 | bytes 8388608 | tf_op jit(solution)/shard_map/pallas_call | solution.py:1053
  333.8 5.9 %collective-permute-done.52.three = bf16[256,1536]{1,0:T(8,128)(2,1)} collective-permute-done((bf16[256,1536]{1,0:T(8,128)(2,1)S(1)}, bf16[256,1536]{1,0:T(8,128)(2,1)}, u32[]{:S(2)}, u32[]{:S(2)}) %collective-permute-start.52) | collective-permute-done | bytes 786464 | tf_op jit(solution)/shard_map/ppermute | solution.py:67
  339.7 4.9 shard_map.285
  347.3 11.9 %shard_map.286 = bf16[1536,2048]{1,0:T(8,128)(2,1)} custom-call(bf16[1024,1536]{1,0:T(8,128)(2,1)} %get-tuple-element.308.h_ref, bf16[1024,1280]{1,0:T(8,128)(2,1)} %shard_map.284.d_ref.refs_0_.refs_1_.refs_2_, bf16[1024,384]{1,0:T(8,128)(2,1)S(1)} %copy-done.4, bf16[1024,384]{1,0:T(8,128)(2,1)} %copy-done.5, bf16[128,1536]{1,0:T(8,128)(2,1)S(1)} %copy-done.15, ...), custom_call_target="tpu_custom_call" | custom-call | flops 6442450944 | bytes 16777216 | tf_op jit(solution)/shard_map/pallas_call | solution.py:252
  359.2 11.3 %collective-permute-done.55.refs_3_ = bf16[256,384]{1,0:T(8,128)(2,1)} collective-permute-done((bf16[256,384]{1,0:T(8,128)(2,1)}, bf16[256,384]{1,0:T(8,128)(2,1)}, u32[]{:S(2)}, u32[]{:S(2)}) %collective-permute-start.55) | collective-permute-done | bytes 196640 | tf_op jit(solution)/shard_map/ppermute | solution.py:67
  370.5 6.0 %shard_map.287 = (bf16[256,768]{1,0:T(8,128)(2,1)S(1)}, bf16[256,768]{1,0:T(8,128)(2,1)S(1)}, f32[256,768]{1,0:T(8,128)S(1)}, f32[256,768]{1,0:T(8,128)S(1)}) custom-call(bf16[1024,1280]{1,0:T(8,128)(2,1)} %shard_map.284.d_ref.refs_0_.refs_1_.refs_2_, bf16[1024,1280]{1,0:T(8,128)(2,1)} %shard_map.284.d_ref.refs_0_.refs_1_.refs_2_, ...), custom_call_target="tpu_custom_call" | custom-call | flops 2617245696 | bytes 5234491 | tf_op jit(solution)/shard_map/pallas_call | solution.py:167
  378.0 6.2 %shard_map.288 = (bf16[256,768]{1,0:T(8,128)(2,1)S(1)}, bf16[256,768]{1,0:T(8,128)(2,1)S(1)}, f32[256,768]{1,0:T(8,128)S(1)}, f32[256,768]{1,0:T(8,128)S(1)}) custom-call(bf16[1024,1280]{1,0:T(8,128)(2,1)} %shard_map.284.d_ref.refs_0_.refs_1_.refs_2_, bf16[1024,1280]{1,0:T(8,128)(2,1)} %shard_map.284.d_ref.refs_0_.refs_1_.refs_2_, ...), custom_call_target="tpu_custom_call" | custom-call | flops 2617245696 | bytes 5234491 | tf_op jit(solution)/shard_map/pallas_call | solution.py:167
  387.5 5.8 %collective-permute-done.59 = bf16[256,768]{1,0:T(8,128)(2,1)} collective-permute-done((bf16[256,768]{1,0:T(8,128)(2,1)S(1)}, bf16[256,768]{1,0:T(8,128)(2,1)}, u32[]{:S(2)}, u32[]{:S(2)}) %collective-permute-start.59) | collective-permute-done | bytes 393248 | tf_op jit(solution)/shard_map/ppermute | solution.py:67
  394.3 4.5 collective-permute-start.62
  411.4 8.4 %collective-permute-done.61.refs_5_ = bf16[256,768]{1,0:T(8,128)(2,1)S(1)} collective-permute-done((bf16[256,768]{1,0:T(8,128)(2,1)S(1)}, bf16[256,768]{1,0:T(8,128)(2,1)S(1)}, u32[]{:S(2)}, u32[]{:S(2)}) %collective-permute-start.61) | collective-permute-done | bytes 393248 | tf_op jit(solution)/shard_map/ppermute | solution.py:67
  420.8 5.0 %shard_map.289 = (bf16[256,384]{1,0:T(8,128)(2,1)}, bf16[256,384]{1,0:T(8,128)(2,1)}, bf16[256,384]{1,0:T(8,128)(2,1)}, bf16[256,384]{1,0:T(8,128)(2,1)}) custom-call(s32[3]{0:T(128)} %copy-done.33, bf16[128,1536]{1,0:T(8,128)(2,1)} %get-tuple-element.302.refs_0_.x_top, bf16[128,1536]{1,0:T(8,128)(2,1)} %get-tuple-element.303.refs_1_.x_low, ...), custom_call_target="tpu_custom_call" | custom-call | flops 1 | bytes 6291456 | tf_op jit(solution)/shard_map/pallas_call | solution.py:416
  435.1 3.7 collective-permute-start.75
  439.4 3.1 collective-permute-start.73
  449.1 4.5 shard_map.291
  454.0 6.7 %collective-permute-done.74.refs_3_ = bf16[256,384]{1,0:T(8,128)(2,1)S(1)} collective-permute-done((bf16[256,384]{1,0:T(8,128)(2,1)}, bf16[256,384]{1,0:T(8,128)(2,1)S(1)}, u32[]{:S(2)}, u32[]{:S(2)}) %collective-permute-start.74) | collective-permute-done | bytes 196640 | tf_op jit(solution)/shard_map/ppermute | solution.py:67
  475.6 4.3 collective-permute-start.85
  482.0 4.5 shard_map.293
  (428 shorter events, 145.1 us)
Async XLA Ops:
  7.2 67.1 %all-gather.6.cloned.1.call-start = ((), (), s32[]{:S(2)}) async-start(), calls=%async_computation.3 | async-start | bytes 2654208 | tf_op jit(solution)/shard_map/all_gather | solution.py:1113
  9.2 74.1 %all-gather.8.cloned.1.call-start = ((), (), s32[]{:S(2)}) async-start(), calls=%async_computation.4 | async-start | bytes 1769472 | tf_op jit(solution)/shard_map/all_gather | solution.py:1113
  13.6 136.1 %all-gather.10.cloned.1.call-start = ((), (), s32[]{:S(2)}) async-start(), calls=%async_computation.5 | async-start | bytes 2654208 | tf_op jit(solution)/shard_map/all_gather | solution.py:1113
  45.6 25.6 %collective-permute-start.7 = (bf16[256,384]{1,0:T(8,128)(2,1)}, bf16[256,384]{1,0:T(8,128)(2,1)S(1)}, u32[]{:S(2)}, u32[]{:S(2)}) collective-permute-start(bf16[256,384]{1,0:T(8,128)(2,1)} %get-tuple-element.277), channel_id=1, source_target_pairs={{0,3},{1,2},{2,1},{3,0},{4,7},{5,6},{6,5},{7,4},{8,11},{9,10},{10,... | collective-permute-start | bytes 589832 | tf_op jit(solution)/shard_map/ppermute | solution.py:67
  45.8 25.4 %collective-permute-start.8 = (bf16[256,384]{1,0:T(8,128)(2,1)S(1)}, bf16[256,384]{1,0:T(8,128)(2,1)S(1)}, u32[]{:S(2)}, u32[]{:S(2)}) collective-permute-start(bf16[256,384]{1,0:T(8,128)(2,1)S(1)} %copy-done.40), channel_id=1, source_target_pairs={{0,4},{4,0},{8,12},{12,8},{1,5},{5,1},{9,13},{13,9},{2,6},{6,2},{1... | collective-permute-start | bytes 589832 | tf_op jit(solution)/shard_map/ppermute | solution.py:67
  46.9 24.2 %collective-permute-start.9 = (bf16[256,384]{1,0:T(8,128)(2,1)S(1)}, bf16[256,384]{1,0:T(8,128)(2,1)S(1)}, u32[]{:S(2)}, u32[]{:S(2)}) collective-permute-start(bf16[256,384]{1,0:T(8,128)(2,1)S(1)} %get-tuple-element.280), channel_id=1, source_target_pairs={{0,8},{4,12},{8,0},{12,4},{1,9},{5,13},{9,1},{13,5},{2,10},{6,14},... | collective-permute-start | bytes 589832 | tf_op jit(solution)/shard_map/ppermute | solution.py:67
  47.4 23.8 %collective-permute-start.10 = (bf16[256,384]{1,0:T(8,128)(2,1)S(1)}, bf16[256,384]{1,0:T(8,128)(2,1)S(1)}, u32[]{:S(2)}, u32[]{:S(2)}) collective-permute-start(bf16[256,384]{1,0:T(8,128)(2,1)S(1)} %get-tuple-element.281), channel_id=1, source_target_pairs={{0,12},{4,8},{8,4},{12,0},{1,13},{5,9},{9,5},{13,1},{2,14},{6,10},... | collective-permute-start | bytes 589832 | tf_op jit(solution)/shard_map/ppermute | solution.py:67
  74.3 130.0 %all-gather.12.cloned.1.call-start = ((), (), s32[]{:S(2)}) async-start(), calls=%async_computation.6 | async-start | bytes 7077888 | tf_op jit(solution)/shard_map/all_gather | solution.py:1113
  74.9 158.4 %all-gather.14.cloned.1.call-start = ((), (), s32[]{:S(2)}) async-start(), calls=%async_computation.7 | async-start | bytes 3538944 | tf_op jit(solution)/shard_map/all_gather | solution.py:1113
  78.6 12.2 %collective-permute-start.14 = (bf16[128,1536]{1,0:T(8,128)(2,1)}, bf16[128,1536]{1,0:T(8,128)(2,1)S(1)}, u32[]{:S(2)}, u32[]{:S(2)}) collective-permute-start(bf16[128,1536]{1,0:T(8,128)(2,1)} %get-tuple-element.303.refs_1_.x_low), channel_id=1, source_target_pairs={{0,4},{4,0},{8,12},{12,8},{1,5},{5,1},{9,13},{13,9},{2,6},{6,2},{1... | collective-permute-start | bytes 1179656 | tf_op jit(solution)/shard_map/ppermute | solution.py:67
  79.7 14.9 %collective-permute-start.15 = (bf16[128,1536]{1,0:T(8,128)(2,1)}, bf16[128,1536]{1,0:T(8,128)(2,1)S(1)}, u32[]{:S(2)}, u32[]{:S(2)}) collective-permute-start(bf16[128,1536]{1,0:T(8,128)(2,1)} %get-tuple-element.302.refs_0_.x_top), channel_id=1, source_target_pairs={{0,8},{4,12},{8,0},{12,4},{1,9},{5,13},{9,1},{13,5},{2,10},{6,14},... | collective-permute-start | bytes 1179656 | tf_op jit(solution)/shard_map/ppermute | solution.py:67
  85.5 14.7 %collective-permute-start.16 = (bf16[128,1536]{1,0:T(8,128)(2,1)S(1)}, bf16[128,1536]{1,0:T(8,128)(2,1)S(1)}, u32[]{:S(2)}, u32[]{:S(2)}) collective-permute-start(bf16[128,1536]{1,0:T(8,128)(2,1)S(1)} %collective-permute-done.11.refs_2_), channel_id=1, source_target_pairs={{0,8},{4,12},{8,0},{12,4},{1,9},{5,13},{9,1},{13,5},{2,10},{6,14},... | collective-permute-start | bytes 1179656 | tf_op jit(solution)/shard_map/ppermute | solution.py:67
  85.5 14.7 %collective-permute-start.17 = (bf16[128,1536]{1,0:T(8,128)(2,1)S(1)}, bf16[128,1536]{1,0:T(8,128)(2,1)}, u32[]{:S(2)}, u32[]{:S(2)}) collective-permute-start(bf16[128,1536]{1,0:T(8,128)(2,1)S(1)} %collective-permute-done.12.refs_3_), channel_id=1, source_target_pairs={{0,4},{4,0},{8,12},{12,8},{1,5},{5,1},{9,13},{13,9},{2,6},{6,2},{1... | collective-permute-start | bytes 1179656 | tf_op jit(solution)/shard_map/ppermute | solution.py:67
  88.3 24.5 %collective-permute-start.18 = (bf16[256,384]{1,0:T(8,128)(2,1)}, bf16[256,384]{1,0:T(8,128)(2,1)S(1)}, u32[]{:S(2)}, u32[]{:S(2)}) collective-permute-start(bf16[256,384]{1,0:T(8,128)(2,1)} %get-tuple-element.312), channel_id=1, source_target_pairs={{0,2},{1,3},{2,0},{3,1},{4,6},{5,7},{6,4},{7,5},{8,10},{9,11},{10,... | collective-permute-start | bytes 589832 | tf_op jit(solution)/shard_map/ppermute | solution.py:67
  90.8 33.2 %collective-permute-start.19 = (bf16[256,384]{1,0:T(8,128)(2,1)}, bf16[256,384]{1,0:T(8,128)(2,1)S(1)}, u32[]{:S(2)}, u32[]{:S(2)}) collective-permute-start(bf16[256,384]{1,0:T(8,128)(2,1)} %get-tuple-element.313), channel_id=1, source_target_pairs={{0,3},{1,2},{2,1},{3,0},{4,7},{5,6},{6,5},{7,4},{8,11},{9,10},{10,... | collective-permute-start | bytes 589832 | tf_op jit(solution)/shard_map/ppermute | solution.py:67
  127.0 19.6 %collective-permute-start.21 = (bf16[128,1536]{1,0:T(8,128)(2,1)}, bf16[128,1536]{1,0:T(8,128)(2,1)S(1)}, u32[]{:S(2)}, u32[]{:S(2)}) collective-permute-start(bf16[128,1536]{1,0:T(8,128)(2,1)} %get-tuple-element.326.refs_1_.grad_low), channel_id=1, source_target_pairs={{0,8},{4,12},{8,0},{12,4},{1,9},{5,13},{9,1},{13,5},{2,10},{6,14},... | collective-permute-start | bytes 1179656 | tf_op jit(solution)/shard_map/ppermute | solution.py:67
  128.0 18.6 %collective-permute-start.22 = (bf16[128,1536]{1,0:T(8,128)(2,1)}, bf16[128,1536]{1,0:T(8,128)(2,1)S(1)}, u32[]{:S(2)}, u32[]{:S(2)}) collective-permute-start(bf16[128,1536]{1,0:T(8,128)(2,1)} %get-tuple-element.326.refs_1_.grad_low), channel_id=1, source_target_pairs={{0,4},{4,0},{8,12},{12,8},{1,5},{5,1},{9,13},{13,9},{2,6},{6,2},{1... | collective-permute-start | bytes 1179656 | tf_op jit(solution)/shard_map/ppermute | solution.py:67
  129.4 17.2 %collective-permute-start.20 = (bf16[128,1536]{1,0:T(8,128)(2,1)}, bf16[128,1536]{1,0:T(8,128)(2,1)S(1)}, u32[]{:S(2)}, u32[]{:S(2)}) collective-permute-start(bf16[128,1536]{1,0:T(8,128)(2,1)} %get-tuple-element.325.refs_0_.grad_top), channel_id=1, source_target_pairs={{0,4},{4,0},{8,12},{12,8},{1,5},{5,1},{9,13},{13,9},{2,6},{6,2},{1... | collective-permute-start | bytes 1179656 | tf_op jit(solution)/shard_map/ppermute | solution.py:67
  129.5 17.2 %collective-permute-start.23 = (bf16[128,1536]{1,0:T(8,128)(2,1)}, bf16[128,1536]{1,0:T(8,128)(2,1)S(1)}, u32[]{:S(2)}, u32[]{:S(2)}) collective-permute-start(bf16[128,1536]{1,0:T(8,128)(2,1)} %get-tuple-element.325.refs_0_.grad_top), channel_id=1, source_target_pairs={{0,8},{4,12},{8,0},{12,4},{1,9},{5,13},{9,1},{13,5},{2,10},{6,14},... | collective-permute-start | bytes 1179656 | tf_op jit(solution)/shard_map/ppermute | solution.py:67
  146.6 193.0 %reduce-scatter.4.cloned.1.call-start = ((), (), s32[]{:S(2)}) async-start(), calls=%async_computation.8 | async-start | bytes 3538944 | tf_op jit(solution)/shard_map/reduce_scatter | solution.py:115
  168.6 13.1 %collective-permute-start.28 = (bf16[256,768]{1,0:T(8,128)(2,1)S(1)}, bf16[256,768]{1,0:T(8,128)(2,1)S(1)}, u32[]{:S(2)}, u32[]{:S(2)}) collective-permute-start(bf16[256,768]{1,0:T(8,128)(2,1)S(1)} %add_convert_fusion.5), channel_id=1, source_target_pairs={{0,8},{4,12},{8,0},{12,4},{1,9},{5,13},{9,1},{13,5},{2,10},{6,14},... | collective-permute-start | bytes 1179656 | tf_op jit(solution)/shard_map/ppermute | solution.py:67
  169.7 20.4 %collective-permute-start.31 = (bf16[256,768]{1,0:T(8,128)(2,1)S(1)}, bf16[256,768]{1,0:T(8,128)(2,1)S(1)}, u32[]{:S(2)}, u32[]{:S(2)}) collective-permute-start(bf16[256,768]{1,0:T(8,128)(2,1)S(1)} %get-tuple-element.345), channel_id=1, source_target_pairs={{0,8},{4,12},{8,0},{12,4},{1,9},{5,13},{9,1},{13,5},{2,10},{6,14},... | collective-permute-start | bytes 1179656 | tf_op jit(solution)/shard_map/ppermute | solution.py:67
  174.9 15.2 %collective-permute-start.30 = (bf16[256,768]{1,0:T(8,128)(2,1)S(1)}, bf16[256,768]{1,0:T(8,128)(2,1)}, u32[]{:S(2)}, u32[]{:S(2)}) collective-permute-start(bf16[256,768]{1,0:T(8,128)(2,1)S(1)} %add_convert_fusion.4), channel_id=1, source_target_pairs={{0,4},{4,0},{8,12},{12,8},{1,5},{5,1},{9,13},{13,9},{2,6},{6,2},{1... | collective-permute-start | bytes 1179656 | tf_op jit(solution)/shard_map/ppermute | solution.py:67
  196.4 16.0 %collective-permute-start.32 = (bf16[128,1536]{1,0:T(8,128)(2,1)}, bf16[128,1536]{1,0:T(8,128)(2,1)}, u32[]{:S(2)}, u32[]{:S(2)}) collective-permute-start(bf16[128,1536]{1,0:T(8,128)(2,1)} %get-tuple-element.352.refs_1_), channel_id=1, source_target_pairs={{0,4},{4,0},{8,12},{12,8},{1,5},{5,1},{9,13},{13,9},{2,6},{6,2},{1... | collective-permute-start | bytes 1179656 | tf_op jit(solution)/shard_map/ppermute | solution.py:67
  197.4 15.0 %collective-permute-start.33 = (bf16[128,1536]{1,0:T(8,128)(2,1)}, bf16[128,1536]{1,0:T(8,128)(2,1)}, u32[]{:S(2)}, u32[]{:S(2)}) collective-permute-start(bf16[128,1536]{1,0:T(8,128)(2,1)} %get-tuple-element.353.refs_0_), channel_id=1, source_target_pairs={{0,8},{4,12},{8,0},{12,4},{1,9},{5,13},{9,1},{13,5},{2,10},{6,14},... | collective-permute-start | bytes 1179656 | tf_op jit(solution)/shard_map/ppermute | solution.py:67
  203.0 14.0 %collective-permute-start.36 = (bf16[128,1536]{1,0:T(8,128)(2,1)S(1)}, bf16[128,1536]{1,0:T(8,128)(2,1)}, u32[]{:S(2)}, u32[]{:S(2)}) collective-permute-start(bf16[128,1536]{1,0:T(8,128)(2,1)S(1)} %collective-permute-done.34.refs_2_), channel_id=1, source_target_pairs={{0,8},{4,12},{8,0},{12,4},{1,9},{5,13},{9,1},{13,5},{2,10},{6,14},... | collective-permute-start | bytes 1179656 | tf_op jit(solution)/shard_map/ppermute | solution.py:67
  203.6 13.4 %collective-permute-start.37 = (bf16[128,1536]{1,0:T(8,128)(2,1)S(1)}, bf16[128,1536]{1,0:T(8,128)(2,1)}, u32[]{:S(2)}, u32[]{:S(2)}) collective-permute-start(bf16[128,1536]{1,0:T(8,128)(2,1)S(1)} %collective-permute-done.35.refs_3_), channel_id=1, source_target_pairs={{0,4},{4,0},{8,12},{12,8},{1,5},{5,1},{9,13},{13,9},{2,6},{6,2},{1... | collective-permute-start | bytes 1179656 | tf_op jit(solution)/shard_map/ppermute | solution.py:67
  233.2 161.1 %reduce-scatter.6.cloned.1.call-start = ((), (), s32[]{:S(2)}) async-start(), calls=%async_computation.9 | async-start | bytes 7077888 | tf_op jit(solution)/shard_map/reduce_scatter | solution.py:115
  260.1 18.0 %collective-permute-start.38 = (bf16[256,768]{1,0:T(8,128)(2,1)S(1)}, bf16[256,768]{1,0:T(8,128)(2,1)S(1)}, u32[]{:S(2)}, u32[]{:S(2)}) collective-permute-start(bf16[256,768]{1,0:T(8,128)(2,1)S(1)} %get-tuple-element.372), channel_id=1, source_target_pairs={{0,4},{4,0},{8,12},{12,8},{1,5},{5,1},{9,13},{13,9},{2,6},{6,2},{1... | collective-permute-start | bytes 1179656 | tf_op jit(solution)/shard_map/ppermute | solution.py:67
  260.6 17.5 %collective-permute-start.40 = (bf16[256,768]{1,0:T(8,128)(2,1)S(1)}, bf16[256,768]{1,0:T(8,128)(2,1)S(1)}, u32[]{:S(2)}, u32[]{:S(2)}) collective-permute-start(bf16[256,768]{1,0:T(8,128)(2,1)S(1)} %add_convert_fusion.3), channel_id=1, source_target_pairs={{0,8},{4,12},{8,0},{12,4},{1,9},{5,13},{9,1},{13,5},{2,10},{6,14},... | collective-permute-start | bytes 1179656 | tf_op jit(solution)/shard_map/ppermute | solution.py:67
  261.3 16.9 %collective-permute-start.43 = (bf16[256,768]{1,0:T(8,128)(2,1)S(1)}, bf16[256,768]{1,0:T(8,128)(2,1)S(1)}, u32[]{:S(2)}, u32[]{:S(2)}) collective-permute-start(bf16[256,768]{1,0:T(8,128)(2,1)S(1)} %get-tuple-element.382), channel_id=1, source_target_pairs={{0,8},{4,12},{8,0},{12,4},{1,9},{5,13},{9,1},{13,5},{2,10},{6,14},... | collective-permute-start | bytes 1179656 | tf_op jit(solution)/shard_map/ppermute | solution.py:67
  279.2 168.2 %reduce-scatter.8.cloned.1.call-start = ((), (), s32[]{:S(2)}) async-start(), calls=%async_computation.10 | async-start | bytes 7077888 | tf_op jit(solution)/shard_map/reduce_scatter | solution.py:115
  286.8 17.1 %collective-permute-start.46 = (bf16[128,1536]{1,0:T(8,128)(2,1)}, bf16[128,1536]{1,0:T(8,128)(2,1)S(1)}, u32[]{:S(2)}, u32[]{:S(2)}) collective-permute-start(bf16[128,1536]{1,0:T(8,128)(2,1)} %get-tuple-element.399.refs_1_), channel_id=1, source_target_pairs={{0,4},{4,0},{8,12},{12,8},{1,5},{5,1},{9,13},{13,9},{2,6},{6,2},{1... | collective-permute-start | bytes 1179656 | tf_op jit(solution)/shard_map/ppermute | solution.py:67
  287.3 17.3 %collective-permute-start.47 = (bf16[128,1536]{1,0:T(8,128)(2,1)}, bf16[128,1536]{1,0:T(8,128)(2,1)S(1)}, u32[]{:S(2)}, u32[]{:S(2)}) collective-permute-start(bf16[128,1536]{1,0:T(8,128)(2,1)} %get-tuple-element.398.refs_0_), channel_id=1, source_target_pairs={{0,8},{4,12},{8,0},{12,4},{1,9},{5,13},{9,1},{13,5},{2,10},{6,14},... | collective-permute-start | bytes 1179656 | tf_op jit(solution)/shard_map/ppermute | solution.py:67
  292.8 12.7 %collective-permute-start.48 = (bf16[128,1536]{1,0:T(8,128)(2,1)S(1)}, bf16[128,1536]{1,0:T(8,128)(2,1)S(1)}, u32[]{:S(2)}, u32[]{:S(2)}) collective-permute-start(bf16[128,1536]{1,0:T(8,128)(2,1)S(1)} %collective-permute-done.44.refs_2_), channel_id=1, source_target_pairs={{0,8},{4,12},{8,0},{12,4},{1,9},{5,13},{9,1},{13,5},{2,10},{6,14},... | collective-permute-start | bytes 1179656 | tf_op jit(solution)/shard_map/ppermute | solution.py:67
  302.9 30.9 %collective-permute-start.50 = (bf16[256,1536]{1,0:T(8,128)(2,1)}, bf16[256,1536]{1,0:T(8,128)(2,1)}, u32[]{:S(2)}, u32[]{:S(2)}) collective-permute-start(bf16[256,1536]{1,0:T(8,128)(2,1)} %get-tuple-element.409), channel_id=1, source_target_pairs={{0,4},{4,0},{8,12},{12,8},{1,5},{5,1},{9,13},{13,9},{2,6},{6,2},{1... | collective-permute-start | bytes 2359304 | tf_op jit(solution)/shard_map/ppermute | solution.py:67
  303.9 29.9 %collective-permute-start.51 = (bf16[256,1536]{1,0:T(8,128)(2,1)S(1)}, bf16[256,1536]{1,0:T(8,128)(2,1)}, u32[]{:S(2)}, u32[]{:S(2)}) collective-permute-start(bf16[256,1536]{1,0:T(8,128)(2,1)S(1)} %get-tuple-element.410), channel_id=1, source_target_pairs={{0,8},{4,12},{8,0},{12,4},{1,9},{5,13},{9,1},{13,5},{2,10},{6,14},... | collective-permute-start | bytes 2359304 | tf_op jit(solution)/shard_map/ppermute | solution.py:67
  304.6 35.1 %collective-permute-start.52 = (bf16[256,1536]{1,0:T(8,128)(2,1)S(1)}, bf16[256,1536]{1,0:T(8,128)(2,1)}, u32[]{:S(2)}, u32[]{:S(2)}) collective-permute-start(bf16[256,1536]{1,0:T(8,128)(2,1)S(1)} %get-tuple-element.411), channel_id=1, source_target_pairs={{0,12},{4,8},{8,4},{12,0},{1,13},{5,9},{9,5},{13,1},{2,14},{6,10},... | collective-permute-start | bytes 2359304 | tf_op jit(solution)/shard_map/ppermute | solution.py:67
  344.6 14.6 %collective-permute-start.53 = (bf16[256,384]{1,0:T(8,128)(2,1)}, bf16[256,384]{1,0:T(8,128)(2,1)}, u32[]{:S(2)}, u32[]{:S(2)}) collective-permute-start(bf16[256,384]{1,0:T(8,128)(2,1)} %get-tuple-element.424), channel_id=1, source_target_pairs={{0,1},{1,0},{2,3},{3,2},{4,5},{5,4},{6,7},{7,6},{8,9},{9,8},{10,11... | collective-permute-start | bytes 589832 | tf_op jit(solution)/shard_map/ppermute | solution.py:67
  344.6 14.6 %collective-permute-start.54 = (bf16[256,384]{1,0:T(8,128)(2,1)}, bf16[256,384]{1,0:T(8,128)(2,1)}, u32[]{:S(2)}, u32[]{:S(2)}) collective-permute-start(bf16[256,384]{1,0:T(8,128)(2,1)} %get-tuple-element.425), channel_id=1, source_target_pairs={{0,2},{1,3},{2,0},{3,1},{4,6},{5,7},{6,4},{7,5},{8,10},{9,11},{10,... | collective-permute-start | bytes 589832 | tf_op jit(solution)/shard_map/ppermute | solution.py:67
  345.0 25.4 %collective-permute-start.55 = (bf16[256,384]{1,0:T(8,128)(2,1)}, bf16[256,384]{1,0:T(8,128)(2,1)}, u32[]{:S(2)}, u32[]{:S(2)}) collective-permute-start(bf16[256,384]{1,0:T(8,128)(2,1)} %get-tuple-element.426), channel_id=1, source_target_pairs={{0,3},{1,2},{2,1},{3,0},{4,7},{5,6},{6,5},{7,4},{8,11},{9,10},{10,... | collective-permute-start | bytes 589832 | tf_op jit(solution)/shard_map/ppermute | solution.py:67
  387.5 21.6 %collective-permute-start.56 = (bf16[256,768]{1,0:T(8,128)(2,1)S(1)}, bf16[256,768]{1,0:T(8,128)(2,1)S(1)}, u32[]{:S(2)}, u32[]{:S(2)}) collective-permute-start(bf16[256,768]{1,0:T(8,128)(2,1)S(1)} %get-tuple-element.436), channel_id=1, source_target_pairs={{0,4},{4,0},{8,12},{12,8},{1,5},{5,1},{9,13},{13,9},{2,6},{6,2},{1... | collective-permute-start | bytes 1179656 | tf_op jit(solution)/shard_map/ppermute | solution.py:67
  402.1 17.7 %collective-permute-start.61 = (bf16[256,768]{1,0:T(8,128)(2,1)S(1)}, bf16[256,768]{1,0:T(8,128)(2,1)S(1)}, u32[]{:S(2)}, u32[]{:S(2)}) collective-permute-start(bf16[256,768]{1,0:T(8,128)(2,1)S(1)} %get-tuple-element.448), channel_id=1, source_target_pairs={{0,8},{4,12},{8,0},{12,4},{1,9},{5,13},{9,1},{13,5},{2,10},{6,14},... | collective-permute-start | bytes 1179656 | tf_op jit(solution)/shard_map/ppermute | solution.py:67
  402.2 17.6 %collective-permute-start.60 = (bf16[256,768]{1,0:T(8,128)(2,1)S(1)}, bf16[256,768]{1,0:T(8,128)(2,1)S(1)}, u32[]{:S(2)}, u32[]{:S(2)}) collective-permute-start(bf16[256,768]{1,0:T(8,128)(2,1)S(1)} %add_convert_fusion), channel_id=1, source_target_pairs={{0,4},{4,0},{8,12},{12,8},{1,5},{5,1},{9,13},{13,9},{2,6},{6,2},{1... | collective-permute-start | bytes 1179656 | tf_op jit(solution)/shard_map/ppermute | solution.py:67
  430.7 12.0 %collective-permute-start.68 = (bf16[256,384]{1,0:T(8,128)(2,1)}, bf16[256,384]{1,0:T(8,128)(2,1)S(1)}, u32[]{:S(2)}, u32[]{:S(2)}) collective-permute-start(bf16[256,384]{1,0:T(8,128)(2,1)} %get-tuple-element.471), channel_id=1, source_target_pairs={{0,1},{1,0},{2,3},{3,2},{4,5},{5,4},{6,7},{7,6},{8,9},{9,8},{10,11... | collective-permute-start | bytes 589832 | tf_op jit(solution)/shard_map/ppermute | solution.py:67
  439.4 14.6 %collective-permute-start.73 = (bf16[256,384]{1,0:T(8,128)(2,1)}, bf16[256,384]{1,0:T(8,128)(2,1)S(1)}, u32[]{:S(2)}, u32[]{:S(2)}) collective-permute-start(bf16[256,384]{1,0:T(8,128)(2,1)} %get-tuple-element.478), channel_id=1, source_target_pairs={{0,2},{1,3},{2,0},{3,1},{4,6},{5,7},{6,4},{7,5},{8,10},{9,11},{10,... | collective-permute-start | bytes 589832 | tf_op jit(solution)/shard_map/ppermute | solution.py:67
  446.4 14.2 %collective-permute-start.74 = (bf16[256,384]{1,0:T(8,128)(2,1)}, bf16[256,384]{1,0:T(8,128)(2,1)S(1)}, u32[]{:S(2)}, u32[]{:S(2)}) collective-permute-start(bf16[256,384]{1,0:T(8,128)(2,1)} %get-tuple-element.479), channel_id=1, source_target_pairs={{0,3},{1,2},{2,1},{3,0},{4,7},{5,6},{6,5},{7,4},{8,11},{9,10},{10,... | collective-permute-start | bytes 589832 | tf_op jit(solution)/shard_map/ppermute | solution.py:67
  447.4 19.3 %collective-permute-start.81 = (bf16[192,2048]{1,0:T(8,128)(2,1)}, bf16[192,2048]{1,0:T(8,128)(2,1)}, u32[]{:S(2)}, u32[]{:S(2)}) collective-permute-start(bf16[192,2048]{1,0:T(8,128)(2,1)} %reduce-scatter.8.cloned.1.call-done), channel_id=1, source_target_pairs={{0,16},{16,0},{1,17},{17,1},{2,18},{18,2},{3,19},{19,3},{4,20},{20... | collective-permute-start | bytes 2359304 | tf_op jit(solution)/shard_map/ppermute | solution.py:67
  (142 other events, 1054.7 us)
Sparse Core Ops, SparseCore 0:
  10.3 32.7 all-gather.5
  45.3 32.7 all-gather.7
  79.7 40.8 all-gather.9
  122.1 67.1 all-gather.11
  190.8 38.1 all-gather.13
  233.3 44.0 reduce-scatter.3
  279.8 90.0 reduce-scatter.5
  372.2 67.9 reduce-scatter.7

commit v4 on v3

--- a/solution.py
+++ b/solution.py
@@ -95,17 +95,17 @@
     return [top, low, top_x, low_y, low_x, top_y, top_d, low_d], done
 
 
-def scatter_products(lefts, weights, beside=None):
-    a3, a1, a2, a0 = part_products(0, (3, 1, 2, 0), lefts, weights)
-    arrays, a3, a1 = tie([array for array, unused in lefts], a3, a1)
-    lefts = [(array, lead) for array, (unused, lead) in zip(arrays, lefts)]
-    a3, a1 = swap(a3, "tx", 1), swap(a1, "tx", 1)
-    b3, b2, b1, b0 = part_products(1, (3, 2, 1, 0), lefts, weights)
-    a3, b3, b2 = tie(a3, b3, b2)
-    b3, b2 = swap(b3, "tx", 2), swap(b2, "tx", 2)
+def scatter_products(lefts, weights, beside=None, ahead=None):
+    a3, b3 = part_products((3,), [BF, BF], True, lefts, weights)
+    arrays, a3, b3, ahead = tie([array for array, unused in lefts], a3, b3, ahead)
+    lefts = [(array, place) for array, (unused, place) in zip(arrays, lefts)]
+    a3, b3 = swap(a3, "tx", 1), swap(b3, "tx", 2)
+    rest = part_products((1, 2, 0), [BF, F32, F32, F32, BF, F32], True, lefts, weights)
+    a3, b3, (a1, a2, a0, b1, b2, b0) = tie(a3, b3, rest)
+    a1, b2 = swap(a1, "tx", 1), swap(b2, "tx", 2)
     send_a2 = (a2 + a3.astype(F32)).astype(BF)
     send_b1 = (b1 + b3.astype(F32)).astype(BF)
-    done = None if beside is None else beside(send_b1)
+    done = None if beside is None else beside((send_b1, ahead))
     a2, b1 = swap(send_a2, "tx", 2), swap(send_b1, "tx", 1)
     a1, a2, b1, b2, done = tie(a1, a2, b1, b2, done)
     return [a0, a1, a2, b0, b1, b2], done
@@ -133,44 +133,66 @@
 ALONE = pltpu.CompilerParams(vmem_limit_bytes=60 * 2**20)
 
 
-def part_kernel(order, count, *refs):
+def part_kernel(order, split, count, *refs):
     lefts, rights, outs = refs[:count], refs[count : 2 * count], refs[2 * count :]
     total = 0.0
     for left, right in zip(lefts, rights):
         rows = left[...]
         total += dot(rows.reshape(rows.shape[-2:]), right[...], NT)
     half = outs[0].shape[0] // 2
-    for at, out in zip(order, outs):
-        for n, place in enumerate((UPPER[at], LOWER[at])):
-            out[n * half : (n + 1) * half, :] = total[place * half : (place + 1) * half].astype(
-                out.dtype
-            )
-
-
-def part_products(half_at, order, lefts, weights):
+    low = min(min(UPPER[at], LOWER[at]) for at in order)
+
+    def put(outs):
+        for at, out in zip(order, outs):
+            for n, place in enumerate((UPPER[at] - low, LOWER[at] - low)):
+                out[n * half : (n + 1) * half, :] = total[
+                    place * half : (place + 1) * half
+                ].astype(out.dtype)
+
+    if not split:
+        put(outs)
+        return
+    step, steps = pl.program_id(0), pl.num_programs(0)
+
+    @pl.when(step < steps // 2)
+    def first():
+        put(outs[: len(order)])
+
+    @pl.when(step >= steps // 2)
+    def second():
+        put(outs[len(order) :])
+
+
+def part_products(order, dtypes, split, lefts, weights):
     row_total, feature = lefts[0][0].shape[-2], weights[0][0].shape[0]
     piece, block = row_total // 4, 256
-    half = feature if half_at is None else feature // 2
-    first = (half_at or 0) * half // block
-    sent = 3 if half_at is None else 2
+    steps = feature // block
+    rows, first_rows = (piece, 3) if order == (3,) else (len(order) * piece, 0)
     left_specs, right_specs = [], []
     flops = 0
     for (array, place), (weight, width, at) in zip(lefts, weights):
         if array.ndim == 2:
-            left_specs.append(pl.BlockSpec((row_total, width), lambda i, place=place: (0, place)))
+            left_specs.append(pl.BlockSpec((rows, width), lambda i, place=place: (first_rows, place)))
         else:
             left_specs.append(
-                pl.BlockSpec((1, row_total, width), lambda i, place=place: (place, 0, 0))
+                pl.BlockSpec((1, rows, width), lambda i, place=place: (place, first_rows, 0))
             )
-        right_specs.append(pl.BlockSpec((block, width), lambda i, at=at: (first + i, at)))
-        flops += 2 * row_total * half * width
-    return pl.pallas_call(
-        lambda *refs: part_kernel(order, len(lefts), *refs),
-        grid=(half // block,),
+        right_specs.append(pl.BlockSpec((block, width), lambda i, at=at: (i, at)))
+        flops += 2 * rows * feature * width
+    if split:
+        outs = [pl.BlockSpec((piece, block), lambda i: (0, jnp.minimum(i, steps // 2 - 1)))] * len(order)
+        outs += [pl.BlockSpec((piece, block), lambda i: (0, jnp.maximum(i - steps // 2, 0)))] * len(order)
+    else:
+        outs = [pl.BlockSpec((piece, block), lambda i: (0, i))] * len(order)
+    return pl.pallas_call(
+        lambda *refs: part_kernel(order, split, len(lefts), *refs),
+        grid=(steps,),
         in_specs=left_specs + right_specs,
-        out_specs=[pl.BlockSpec((piece, block), lambda i: (0, i))] * 4,
-        out_shape=[jax.ShapeDtypeStruct((piece, half), BF)] * sent
-        + [jax.ShapeDtypeStruct((piece, half), F32)] * (4 - sent),
+        out_specs=outs,
+        out_shape=[
+            jax.ShapeDtypeStruct((piece, feature // 2 if split else feature), dtype)
+            for dtype in dtypes
+        ],
         compiler_params=LIMIT,
         cost_estimate=cost(flops, flops // 500),
     )(*[a for a, unused in lefts], *[w for w, *unused in weights])
@@ -693,23 +715,47 @@
         local = near - other
         part = sum(jnp.where(local >= k * block, 1, 0) for k in (1, 2, 3))
         near = other + local + (jnp.bitwise_xor(part, column) - part) * block
-    across = lax.broadcasted_iota(jnp.int32, (block, 2 * row_total), 1)
-    chosen = jnp.where(across == near, 1.0, 0.0).astype(BF)
+    start = row * row_total + (step if backward else step ^ column) * block
+    held = refs[-1]
+    held[...] = jnp.zeros_like(held)
+    across = lax.broadcasted_iota(jnp.int32, (block, block), 1)
+    for part in range(8):
+        if backward:
+            place = 4 * ((part // 4) ^ row) + ((part % 4) ^ column)
+        else:
+            place = (part + 4 * row) & 7
+        met = jnp.bool_(False)
+        for n, (first, by) in enumerate(moves):
+            low = jnp.maximum(start, first) + by
+            high = start + block
+            if n + 1 < len(moves):
+                high = jnp.minimum(high, moves[n + 1][0])
+            high = high + by
+            met |= (low < high) & (low < (place + 1) * block) & (high > place * block)
+
+        @pl.when(met)
+        def add(part=part):
+            chosen = jnp.where(across == near - part * block, 1.0, 0.0).astype(BF)
+            if backward:
+                held[...] += dot(chosen, refs[part][...])
+            else:
+                rows = pl.ds(part % 4 * block, block)
+                width = refs[0].shape[1]
+                for at in range(2):
+                    held[:, at * width : (at + 1) * width] += dot(
+                        chosen, refs[2 * at + part // 4][rows, :]
+                    )
+
     if backward:
-        picked = 0.0
-        for k in range(8):
-            picked += dot(chosen[:, k * block : (k + 1) * block], refs[k][...])
-        refs[8][...] = picked.astype(BF)
+        refs[8][...] = held[...].astype(BF)
         return
+    width = refs[0].shape[1]
     for at in range(2):
-        own, other = refs[2 * at][...], refs[2 * at + 1][...]
-        picked = dot(chosen[:, :row_total], own) + dot(chosen[:, row_total:], other)
-        picked = picked.astype(BF)
         for k in range(4):
 
             @pl.when(step == k)
-            def put(k=k, at=at, picked=picked):
-                refs[4 + 4 * at + k][...] = picked
+            def put(k=k, at=at):
+                refs[4 + 4 * at + k][...] = held[:, at * width : (at + 1) * width].astype(BF)
 
 
 def moved_rows(backward, where, lengths, dealing, arrays):
@@ -752,6 +798,7 @@
             grid=(4,),
             in_specs=[pl.BlockSpec(a.shape, lambda i, *_: (0, 0)) for a in ins],
             out_specs=outs,
+            scratch_shapes=[pltpu.VMEM((block, width if backward else 2 * width), F32)],
         ),
         out_shape=shapes,
         compiler_params=pltpu.CompilerParams(vmem_limit_bytes=40 * 2**20),
@@ -1167,7 +1214,7 @@
     grad_gate_up = down_products(grad_full, w_down_t, to_gate, to_up)
 
     def gate_up_products(ready):
-        left, unused = tie(h2_full, ready)
+        left, unused = tie(h2_full, ready[0])
         return row_products(left, grad_gate_up)
 
     parts, part = scatter_products(
@@ -1183,7 +1230,9 @@
 
     def result_products(pieces, ahead):
         left, unused = tie(mid, pieces)
-        return part_products(None, (1, 2, 3, 0), [(left, 0)], [(w_down_t, hidden, 0)])
+        return part_products(
+            (1, 2, 3, 0), [BF, BF, BF, F32], False, [(left, 0)], [(w_down_t, hidden, 0)]
+        )
 
     z_parts, (*sent, own) = gather_rows(top, low, result_products)
 
@@ -1198,36 +1247,36 @@
     part, grad_first, output = tie(part, grad_first, output)
     grads_attn = summed(part)
 
+    def given(pieces):
+        return moved_rows(True, where, seq_lengths, seq_deal, pieces)[0]
+
     def row_dots(*sides):
         return sum(jnp.sum(w.astype(F32) * g, axis=1) for w, g in sides)
 
     def finish(ready):
-        down, gate_up, bias, unused = tie(
+        down, gate_up, bias, (unused, rows) = tie(
             grads_down, grads_gate_up, grad_first[:, side:], ready
         )
         bias = jnp.sum(bias.astype(F32), axis=0, keepdims=True)
-        bias = bias + swap(bias, "dp", 1) if paired else lax.psum(bias, ("dp", "ty"))
+        if paired:
+            bias = bias + swap(bias, "dp", 1)
+            bias = pairs_sum(spread_line([bias] * 4))
+        else:
+            bias = lax.psum(bias, ("dp", "ty"))
         down, gate_up = reduce_end(down), reduce_end(gate_up)
         mlp = [gate_up[:, :hidden], gate_up[:, hidden:], down]
-        return mlp, row_dots((w_gate, mlp[0]), (w_up, mlp[1])) / mlp_gain, bias
-
-    parts, (grads_mlp, own_mlp_gain, bias_grad) = scatter_products(
+        return mlp, row_dots((w_gate, mlp[0]), (w_up, mlp[1])) / mlp_gain, bias, given(rows)
+
+    parts, (grads_mlp, own_mlp_gain, bias_grad, output) = scatter_products(
         [(grad_first, 0), (grad_first, 3), (grad_first, 4), (grad_ogate, 0)],
         [(w_first[0], 2 * width, 0), (w_first[1], 256, 0), (w_first[1], 256, 1), (w_second, width, 0)],
         finish,
+        spread_plane(reordered([output], column ^ lane)),
     )
     grad_x = on_rows(input_norm_kernel, where, [x_full[:2], grad_second], gains, parts, True)
 
-    def given(pieces):
-        return moved_rows(True, where, seq_lengths, seq_deal, pieces)[0]
-
-    output, grad_x = tie(output, grad_x)
     grad_x = spread_line(grad_x)
-    output = spread_plane(reordered([output], column ^ lane))
-    if paired:
-        bias_grad = pairs_sum(spread_line([bias_grad] * 4))
-    output, grad_x[1] = tie(output, grad_x[1])
-    output, grad_x, bias_grad = tie(given(output), grad_x, bias_grad)
+    grad_x, grads_attn = tie(grad_x, grads_attn)
     grad_x = spread_plane(reordered([grad_x], column ^ lane))
 
     grad_attn = reduce_end(grads_attn)
@@ -1240,7 +1289,7 @@
     ]
     own_gain = row_dots(*zip((w_query, w_key, w_value, w_ogate, w_forget), grads)) / attn_gain
     grad_gains = spread_plane([jnp.stack([own_gain, own_mlp_gain])] * 4)
-    grad_x, output, grad_gains, grads = tie(grad_x, output, grad_gains, grads)
+    grad_x, grad_gains, grads = tie(grad_x, grad_gains, grads)
     grad_gains = pairs_sum(grad_gains)
     grad_input = given(grad_x)
     return (

time: 499 us -> 483 us (0.968)
  waiting for transfers between devices: 141 us -> 124 us
    ppermute x89, waiting for transfers between devices: 141 us -> 123 us  [swap(): lax.ppermute(values, axis, [(at, at ^ step) for at in range(lax.axis_size...]
    pallas_call x7, Pallas kernels: 39.4 us -> 44.5 us  [part_products(): pl.pallas_call(lambda *refs: part_kernel(order, split, len(lefts), *refs)...]
    unnamed x189 -> x213, local copies, waits for them, and re-layouts: 23.2 us -> 23.1 us
  transfers between devices with their start and end apart: 97 -> 97, of which waited for: 38 -> 33; matrix products, arithmetic and copies ran while one was open for 5% -> 4% of each run, Pallas kernels for 41% -> 43%
where the time goes in v4:
time: 483 us; the launch traced here: 477 us
  Pallas kernels  208 us (43%)
  waiting for transfers between devices  124 us (26%)
  starting transfers between devices  85.7 us (18%)
  local copies, waits for them, and re-layouts  29.2 us (6%)
  between operations  15.6 us (3%)
  other arithmetic  15 us (3%)
    ppermute x89, waiting for transfers between devices, swap(): lax.ppermute(values, axis, [(at, at ^ step) for at in range(lax.axis_size...  123 us
    ppermute x89, starting transfers between devices, swap(): lax.ppermute(values, axis, [(at, at ^ step) for at in range(lax.axis_size...  84.6 us
    pallas_call x7, Pallas kernels, part_products(): pl.pallas_call(lambda *refs: part_kernel(order, split, len(lefts), *refs)...  44.5 us
    unnamed x213, local copies, waits for them, and re-layouts  23.1 us
    pallas_call x1, Pallas kernels, attend_backward(): pl.pallas_call(backward_kernel, grid_spec=pltpu.PrefetchScalarGridSpec(nu...  20.8 us
    pallas_call x4, Pallas kernels, on_rows(): pl.pallas_call(kernel, grid_spec=pltpu.PrefetchScalarGridSpec(num_scalar_...  19.9 us
    pallas_call x1, Pallas kernels, attend_forward(): pl.pallas_call(forward_kernel, grid_spec=pltpu.PrefetchScalarGridSpec(num...  16.7 us
    pallas_call x2, Pallas kernels, up_products(): pl.pallas_call(up_kernel, grid=(steps,), in_specs=[pl.BlockSpec(p.shape,...  16.2 us
  transfers between devices with their start and end apart: 97, of which 33 were waited for; matrix products, arithmetic and copies ran while one was open for 4% of the time, Pallas kernels for 43%

profile of v4, /device:TPU:9, one launch (start us, length us, event | category | flops | bytes accessed | tf_op | source)
XLA Modules:
  0.0 477.4 jit_solution(13904531416777685886)
XLA Ops:
  17.6 6.0 %shard_map.263 = (bf16[256,384]{1,0:T(8,128)(2,1)S(1)}, bf16[256,384]{1,0:T(8,128)(2,1)}, bf16[256,384]{1,0:T(8,128)(2,1)}, bf16[256,384]{1,0:T(8,128)(2,1)}, bf...) custom-call(s32[3]{0:T(128)S(1)} %pad_add_fusion.refs_0_.where, ...), custom_call_target="tpu_custom_call" | custom-call | flops 6442450944 | bytes 8388608 | tf_op jit(solution)/shard_map/pallas_call | solution.py:794
  29.6 3.0 collective-permute-done.2.refs_1_
  32.6 4.7 collective-permute-done.3.refs_2_
  47.9 6.1 %collective-permute-done.6.refs_2_ = bf16[256,384]{1,0:T(8,128)(2,1)S(1)} collective-permute-done((bf16[256,384]{1,0:T(8,128)(2,1)}, bf16[256,384]{1,0:T(8,128)(2,1)S(1)}, u32[]{:S(2)}, u32[]{:S(2)}) %collective-permute-start.6) | collective-permute-done | bytes 196640 | tf_op jit(solution)/shard_map/ppermute | solution.py:67
  54.0 14.5 %collective-permute-done.7.refs_3_ = bf16[256,384]{1,0:T(8,128)(2,1)S(1)} collective-permute-done((bf16[256,384]{1,0:T(8,128)(2,1)}, bf16[256,384]{1,0:T(8,128)(2,1)S(1)}, u32[]{:S(2)}, u32[]{:S(2)}) %collective-permute-start.7) | collective-permute-done | bytes 196640 | tf_op jit(solution)/shard_map/ppermute | solution.py:67
  75.0 3.6 collective-permute-start.11
  80.1 3.3 collective-permute-done.13.refs_1_
  88.6 3.7 collective-permute-done.14.refs_4_
  92.3 3.3 collective-permute-start.19
  95.6 6.1 %collective-permute-done.16.refs_6_ = bf16[128,1536]{1,0:T(8,128)(2,1)S(1)} collective-permute-done((bf16[128,1536]{1,0:T(8,128)(2,1)S(1)}, bf16[128,1536]{1,0:T(8,128)(2,1)S(1)}, u32[]{:S(2)}, u32[]{:S(2)}) %collective-permute-start.16) | collective-permute-done | bytes 393248 | tf_op jit(solution)/shard_map/ppermute | solution.py:67
  102.4 12.0 %shard_map.267 = (bf16[1024,1536]{1,0:T(8,128)(2,1)}, bf16[1024,1280]{1,0:T(8,128)(2,1)}, f32[1024,128]{1,0:T(8,128)}, f32[1024,128]{1,0:T(8,128)}, f32[8,1536]{1,0:T(8,128)}) custom-call(bf16[128,1536]{1,0:T(8,128)(2,1)} %get-tuple-element.311.refs_0_.x_top, bf16[128,1536]{1,0:T(8,128)(2,1)} %get-tuple-element.312.refs_1_.x_low, ...), custom_call_target="tpu_custom_call" | custom-call | flops 4026531840 | bytes 12582912 | tf_op jit(solution)/shard_map/pallas_call | solution.py:499
  114.5 8.5 %collective-permute-done.19.refs_3_ = bf16[256,384]{1,0:T(8,128)(2,1)S(1)} collective-permute-done((bf16[256,384]{1,0:T(8,128)(2,1)}, bf16[256,384]{1,0:T(8,128)(2,1)S(1)}, u32[]{:S(2)}, u32[]{:S(2)}) %collective-permute-start.19) | collective-permute-done | bytes 196640 | tf_op jit(solution)/shard_map/ppermute | solution.py:67
  128.8 16.7 %shard_map.269 = (f32[1024,384]{1,0:T(8,128)}, bf16[6,1024,128]{2,1,0:T(8,128)(2,1)}, bf16[6,1024,128]{2,1,0:T(8,128)(2,1)}) custom-call(s32[3]{0:T(128)} %copy-done.35, s32[4,4]{1,0:T(4,128)} %refs_1_.5, s32[4,4]{1,0:T(4,128)} %refs_2_.5, bf16[1024,1280]{1,0:T(8,128)(2,1)} %get-tuple-element.331.q_ref.k_ref.v_ref, ...), custom_call_target="tpu_custom_call" | custom-call | flops 10000000000 | bytes 8388608 | tf_op jit(solution)/shard_map/pallas_call | solution.py:948
  151.1 4.6 shard_map.270
  159.9 5.2 %shard_map.272 = (bf16[256,768]{1,0:T(8,128)(2,1)S(1)}, f32[256,768]{1,0:T(8,128)S(1)}, f32[256,768]{1,0:T(8,128)S(1)}, f32[256,768]{1,0:T(8,128)S(1)}, bf16[256...) custom-call(bf16[1024,384]{1,0:T(8,128)(2,1)} %copy-done.10, ...), custom_call_target="tpu_custom_call" | custom-call | flops 905969664 | bytes 1811939 | tf_op jit(solution)/shard_map/pallas_call | solution.py:187
  169.6 4.5 collective-permute-done.28.refs_1_
  175.0 6.9 %collective-permute-done.30.refs_4_ = bf16[256,768]{1,0:T(8,128)(2,1)S(1)} collective-permute-done((bf16[256,768]{1,0:T(8,128)(2,1)S(1)}, bf16[256,768]{1,0:T(8,128)(2,1)S(1)}, u32[]{:S(2)}, u32[]{:S(2)}) %collective-permute-start.30) | collective-permute-done | bytes 393248 | tf_op jit(solution)/shard_map/ppermute | solution.py:67
  183.1 4.6 shard_map.273
  190.7 3.9 collective-permute-done.34.refs_2_
  196.7 8.1 %shard_map.274 = (bf16[1024,1536]{1,0:T(8,128)(2,1)}, bf16[1024,1024]{1,0:T(8,128)(2,1)}, bf16[1024,1024]{1,0:T(8,128)(2,1)}, bf16[1024,1024]{1,0:T(8,128)(2,1)}) custom-call(bf16[128,1536]{1,0:T(8,128)(2,1)} %get-tuple-element.367.refs_0_, bf16[128,1536]{1,0:T(8,128)(2,1)} %get-tuple-element.366.refs_1_, bf16[128,1536]{1,0:T(8,128)(2,1)} %copy-done.61, ...), custom_call_target="tpu_custom_call" | custom-call | flops 3221225472 | bytes 16777216 | tf_op jit(solution)/shard_map/pallas_call | solution.py:586
  204.9 5.3 %collective-permute-done.36.refs_2_ = bf16[128,1536]{1,0:T(8,128)(2,1)S(1)} collective-permute-done((bf16[128,1536]{1,0:T(8,128)(2,1)S(1)}, bf16[128,1536]{1,0:T(8,128)(2,1)S(1)}, u32[]{:S(2)}, u32[]{:S(2)}) %collective-permute-start.36) | collective-permute-done | bytes 393248 | tf_op jit(solution)/shard_map/ppermute | solution.py:67
  211.1 8.1 %shard_map.275 = (bf16[1024,1536]{1,0:T(8,128)(2,1)}, bf16[1024,1024]{1,0:T(8,128)(2,1)}, bf16[1024,1024]{1,0:T(8,128)(2,1)}, bf16[1024,1024]{1,0:T(8,128)(2,1)}) custom-call(bf16[128,1536]{1,0:T(8,128)(2,1)} %copy-done.77, bf16[128,1536]{1,0:T(8,128)(2,1)} %copy-done.78, ...), custom_call_target="tpu_custom_call", output_to_operand_aliasing={{0}: (6, {}), {1}: (7, {}), {2}: (8, {}), {3}: (9, {})} | custom-call | flops 3221225472 | bytes 16777216 | tf_op jit(solution)/shard_map/pallas_call | solution.py:586
  219.2 8.3 %shard_map.276 = (bf16[4096,384]{1,0:T(8,128)(2,1)}, bf16[1024,1536]{1,0:T(8,128)(2,1)}) custom-call(bf16[1024,1024]{1,0:T(8,128)(2,1)} %get-tuple-element.421.left.refs_0_, bf16[128,1536]{1,0:T(8,128)(2,1)S(1)} %copy-done.31, bf16[128,1536]{1,0:T(8,128)(2,1)S(1)} %copy-done.32, bf16[128,1536]{1,0:T(8,128)(2,1)} %collective-permute-done.20.refs_2_, ...), custom_call_target="tpu_custom_call" | custom-call | flops 3221225472 | bytes 6442450 | tf_op jit(solution)/shard_map/pallas_call | solution.py:235
  229.1 8.2 %shard_map.277.refs_0_.refs_1_.right = bf16[2,1024,1024]{2,1,0:T(8,128)(2,1)} custom-call(bf16[1024,1536]{1,0:T(8,128)(2,1)} %get-tuple-element.380.g_ref, bf16[1536,1024]{1,0:T(8,128)(2,1)} %all-gather.14.cloned.1.call-done.w_ref.refs_1_, bf16[1024,1024]{1,0:T(8,128)(2,1)S(1)} %copy-done.4, bf16[1024,1024]{1,0:T(8,128)(2,1)} %get-tuple-element.383.to_up_ref), custom_call_target="tpu_custom_call" | custom-call | flops 3221225472 | bytes 16777216 | tf_op jit(solution)/shard_map/pallas_call | solution.py:615
  237.3 6.2 %shard_map.278 = (bf16[256,768]{1,0:T(8,128)(2,1)S(1)}, bf16[256,768]{1,0:T(8,128)(2,1)S(1)}) custom-call(bf16[2,1024,1024]{2,1,0:T(8,128)(2,1)} %shard_map.277.refs_0_.refs_1_.right, bf16[2,1024,1024]{2,1,0:T(8,128)(2,1)} %shard_map.277.refs_0_.refs_1_.right, bf16[1536,2048]{1,0:T(8,128)(2,1)} %all-gather.12.cloned.1.call-done.refs_4_.refs_5_.refs_2_.refs_3_, ...), custom_call_target="tpu_custom_call" | custom-call | flops 1610612736 | bytes 3221225 | tf_op jit(solution)/shard_map/pallas_call | solution.py:187
  245.2 9.3 %shard_map.279 = (bf16[256,768]{1,0:T(8,128)(2,1)S(1)}, f32[256,768]{1,0:T(8,128)S(1)}, f32[256,768]{1,0:T(8,128)S(1)}, f32[256,768]{1,0:T(8,128)S(1)}, bf16[256...) custom-call(bf16[2,1024,1024]{2,1,0:T(8,128)(2,1)} %shard_map.277.refs_0_.refs_1_.right, ...), custom_call_target="tpu_custom_call" | custom-call | flops 4831838208 | bytes 9663676 | tf_op jit(solution)/shard_map/pallas_call | solution.py:187
  258.7 11.3 %shard_map.280 = bf16[1536,2048]{1,0:T(8,128)(2,1)} custom-call(bf16[1024,1536]{1,0:T(8,128)(2,1)S(1)} %copy-done.7, bf16[2,1024,1024]{2,1,0:T(8,128)(2,1)} %shard_map.277.refs_0_.refs_1_.right), custom_call_target="tpu_custom_call" | custom-call | flops 6442450944 | bytes 12884901 | tf_op jit(solution)/shard_map/pallas_call | solution.py:211
  271.3 5.4 %shard_map.281 = (f32[256,1536]{1,0:T(8,128)}, bf16[128,1536]{1,0:T(8,128)(2,1)}, bf16[128,1536]{1,0:T(8,128)(2,1)}) custom-call(s32[3]{0:T(128)} %copy-done.35, f32[256,1536]{1,0:T(8,128)} %get-tuple-element.365.second_ref, bf16[128,1536]{1,0:T(8,128)(2,1)} %get-tuple-element.334.refs_0_.grad_top, bf16[128,1536]{1,0:T(8,128)(2,1)} %get-tuple-element.335.refs_1_.grad_low, ...), custom_call_target="tpu_custom_call" | custom-call | flops 1 | bytes 6291456 | tf_op jit(solution)/shard_map/pallas_call | solution.py:438
  279.7 4.3 collective-permute-done.44.refs_2_
  285.7 7.6 %shard_map.282 = (bf16[256,1536]{1,0:T(8,128)(2,1)}, bf16[256,1536]{1,0:T(8,128)(2,1)S(1)}, bf16[256,1536]{1,0:T(8,128)(2,1)S(1)}, f32[256,1536]{1,0:T(8,128)S(1)}) custom-call(bf16[1024,1024]{1,0:T(8,128)(2,1)} %get-tuple-element.421.left.refs_0_, bf16[1536,1024]{1,0:T(8,128)(2,1)} %all-gather.14.cloned.1.call-done.w_ref.refs_1_), custom_call_target="tpu_custom_call" | custom-call | flops 3221225472 | bytes 6442450 | tf_op jit(solution)/shard_map/pallas_call | solution.py:187
  297.9 6.6 %shard_map.283 = (bf16[1024,384]{1,0:T(8,128)(2,1)}, bf16[1024,384]{1,0:T(8,128)(2,1)}) custom-call(bf16[128,1536]{1,0:T(8,128)(2,1)} %get-tuple-element.417.refs_0_, bf16[128,1536]{1,0:T(8,128)(2,1)} %get-tuple-element.418.refs_1_, bf16[128,1536]{1,0:T(8,128)(2,1)} %copy-done.19, bf16[128,1536]{1,0:T(8,128)(2,1)} %copy-done.21, ...), custom_call_target="tpu_custom_call" | custom-call | flops 1207959552 | bytes 10485760 | tf_op jit(solution)/shard_map/pallas_call | solution.py:657
  304.5 20.8 %shard_map.284.d_ref.refs_0_.refs_1_.refs_2_ = bf16[1024,1280]{1,0:T(8,128)(2,1)} custom-call(s32[3]{0:T(128)} %copy-done.35, bf16[6,1024,128]{2,1,0:T(8,128)(2,1)} %get-tuple-element.423.qa_ref, bf16[6,1024,128]{2,1,0:T(8,128)(2,1)} %get-tuple-element.424.ka_ref, bf16[1024,1280]{1,0:T(8,128)(2,1)} %get-tuple-element.331.q_ref.k_ref.v_ref, ...), custom_call_target="tpu_custom_call" | custom-call | flops 12000000000 | bytes 8388608 | tf_op jit(solution)/shard_map/pallas_call | solution.py:1100
  325.3 6.6 %collective-permute-done.52.three = bf16[256,1536]{1,0:T(8,128)(2,1)} collective-permute-done((bf16[256,1536]{1,0:T(8,128)(2,1)S(1)}, bf16[256,1536]{1,0:T(8,128)(2,1)}, u32[]{:S(2)}, u32[]{:S(2)}) %collective-permute-start.52) | collective-permute-done | bytes 786464 | tf_op jit(solution)/shard_map/ppermute | solution.py:67
  332.0 4.9 %shard_map.285 = (bf16[256,384]{1,0:T(8,128)(2,1)}, bf16[256,384]{1,0:T(8,128)(2,1)}, bf16[256,384]{1,0:T(8,128)(2,1)}, bf16[256,384]{1,0:T(8,128)(2,1)}) custom-call(s32[3]{0:T(128)} %copy-done.35, f32[256,1536]{1,0:T(8,128)} %get-tuple-element.365.second_ref, f32[256,1536]{1,0:T(8,128)} %copy-done.8, bf16[256,1536]{1,0:T(8,128)(2,1)} %collective-permute-done.50.one, ...), custom_call_target="tpu_custom_call" | custom-call | flops 1 | bytes 6291456 | tf_op jit(solution)/shard_map/pallas_call | solution.py:438
  339.9 11.9 %shard_map.286 = bf16[1536,2048]{1,0:T(8,128)(2,1)} custom-call(bf16[1024,1536]{1,0:T(8,128)(2,1)} %get-tuple-element.317.h_ref, bf16[1024,1280]{1,0:T(8,128)(2,1)} %shard_map.284.d_ref.refs_0_.refs_1_.refs_2_, bf16[1024,384]{1,0:T(8,128)(2,1)S(1)} %copy-done.6, bf16[1024,384]{1,0:T(8,128)(2,1)} %copy-done.10, bf16[128,1536]{1,0:T(8,128)(2,1)S(1)} %copy-done.17, ...), custom_call_target="tpu_custom_call" | custom-call | flops 6442450944 | bytes 16777216 | tf_op jit(solution)/shard_map/pallas_call | solution.py:274
  351.8 5.5 %collective-permute-done.55.refs_3_ = bf16[256,384]{1,0:T(8,128)(2,1)} collective-permute-done((bf16[256,384]{1,0:T(8,128)(2,1)}, bf16[256,384]{1,0:T(8,128)(2,1)}, u32[]{:S(2)}, u32[]{:S(2)}) %collective-permute-start.55) | collective-permute-done | bytes 196640 | tf_op jit(solution)/shard_map/ppermute | solution.py:67
  357.4 2.5 shard_map.288
  362.5 5.5 %shard_map.287 = (bf16[256,768]{1,0:T(8,128)(2,1)S(1)}, bf16[256,768]{1,0:T(8,128)(2,1)S(1)}) custom-call(bf16[1024,1280]{1,0:T(8,128)(2,1)} %shard_map.284.d_ref.refs_0_.refs_1_.refs_2_, bf16[1024,1280]{1,0:T(8,128)(2,1)} %shard_map.284.d_ref.refs_0_.refs_1_.refs_2_, bf16[1024,1280]{1,0:T(8,128)(2,1)} %shard_map.284.d_ref.refs_0_.refs_1_.refs_2_, ...), custom_call_target="tpu_custom_call" | custom-call | flops 1308622848 | bytes 2617245 | tf_op jit(solution)/shard_map/pallas_call | solution.py:187
  370.3 8.6 %shard_map.289 = (bf16[256,768]{1,0:T(8,128)(2,1)S(1)}, f32[256,768]{1,0:T(8,128)S(1)}, f32[256,768]{1,0:T(8,128)S(1)}, f32[256,768]{1,0:T(8,128)S(1)}, bf16[256...) custom-call(bf16[1024,1280]{1,0:T(8,128)(2,1)} %shard_map.284.d_ref.refs_0_.refs_1_.refs_2_, ...), custom_call_target="tpu_custom_call" | custom-call | flops 3925868544 | bytes 7851737 | tf_op jit(solution)/shard_map/pallas_call | solution.py:187
  382.5 7.4 %collective-permute-start.67 = (f32[1,128]{1,0:T(1,128)S(1)}, f32[1,128]{1,0:T(1,128)S(1)}, u32[]{:S(2)}, u32[]{:S(2)}) collective-permute-start(f32[1,128]{1,0:T(1,128)S(1)} %bitcast.22), channel_id=1, source_target_pairs={{0,16},{16,0},{1,17},{17,1},{2,18},{18,2},{3,19},{19,3},{4,20},{20... | collective-permute-start | bytes 1544 | tf_op jit(solution)/shard_map/ppermute | solution.py:67
  401.1 3.8 shard_map.290
  410.8 7.6 %collective-permute-done.64.refs_5_ = bf16[256,768]{1,0:T(8,128)(2,1)S(1)} collective-permute-done((bf16[256,768]{1,0:T(8,128)(2,1)S(1)}, bf16[256,768]{1,0:T(8,128)(2,1)S(1)}, u32[]{:S(2)}, u32[]{:S(2)}) %collective-permute-start.64) | collective-permute-done | bytes 393248 | tf_op jit(solution)/shard_map/ppermute | solution.py:67
  419.2 5.0 %shard_map.291 = (bf16[256,384]{1,0:T(8,128)(2,1)}, bf16[256,384]{1,0:T(8,128)(2,1)}, bf16[256,384]{1,0:T(8,128)(2,1)}, bf16[256,384]{1,0:T(8,128)(2,1)}) custom-call(s32[3]{0:T(128)} %copy-done.35, bf16[128,1536]{1,0:T(8,128)(2,1)} %get-tuple-element.311.refs_0_.x_top, bf16[128,1536]{1,0:T(8,128)(2,1)} %get-tuple-element.312.refs_1_.x_low, ...), custom_call_target="tpu_custom_call" | custom-call | flops 1 | bytes 6291456 | tf_op jit(solution)/shard_map/pallas_call | solution.py:438
  426.8 6.7 %collective-permute-done.75.refs_1_ = bf16[256,384]{1,0:T(8,128)(2,1)S(1)} collective-permute-done((bf16[256,384]{1,0:T(8,128)(2,1)}, bf16[256,384]{1,0:T(8,128)(2,1)S(1)}, u32[]{:S(2)}, u32[]{:S(2)}) %collective-permute-start.75) | collective-permute-done | bytes 196640 | tf_op jit(solution)/shard_map/ppermute | solution.py:67
  433.6 3.4 collective-permute-done.76.refs_2_
  437.0 7.3 %collective-permute-done.77.refs_3_ = bf16[256,384]{1,0:T(8,128)(2,1)S(1)} collective-permute-done((bf16[256,384]{1,0:T(8,128)(2,1)}, bf16[256,384]{1,0:T(8,128)(2,1)S(1)}, u32[]{:S(2)}, u32[]{:S(2)}) %collective-permute-start.77) | collective-permute-done | bytes 196640 | tf_op jit(solution)/shard_map/ppermute | solution.py:67
  461.8 2.6 collective-permute-start.85
  466.4 3.8 shard_map.293
  (452 shorter events, 137.8 us)
Async XLA Ops:
  7.2 64.5 %all-gather.6.cloned.1.call-start = ((), (), s32[]{:S(2)}) async-start(), calls=%async_computation.3 | async-start | bytes 2654208 | tf_op jit(solution)/shard_map/all_gather | solution.py:1160
  9.2 74.1 %all-gather.8.cloned.1.call-start = ((), (), s32[]{:S(2)}) async-start(), calls=%async_computation.4 | async-start | bytes 1769472 | tf_op jit(solution)/shard_map/all_gather | solution.py:1160
  13.6 136.1 %all-gather.10.cloned.1.call-start = ((), (), s32[]{:S(2)}) async-start(), calls=%async_computation.5 | async-start | bytes 2654208 | tf_op jit(solution)/shard_map/all_gather | solution.py:1160
  40.6 13.5 %collective-permute-start.6 = (bf16[256,384]{1,0:T(8,128)(2,1)}, bf16[256,384]{1,0:T(8,128)(2,1)S(1)}, u32[]{:S(2)}, u32[]{:S(2)}) collective-permute-start(bf16[256,384]{1,0:T(8,128)(2,1)} %get-tuple-element.285), channel_id=1, source_target_pairs={{0,2},{1,3},{2,0},{3,1},{4,6},{5,7},{6,4},{7,5},{8,10},{9,11},{10,... | collective-permute-start | bytes 589832 | tf_op jit(solution)/shard_map/ppermute | solution.py:67
  42.9 25.6 %collective-permute-start.7 = (bf16[256,384]{1,0:T(8,128)(2,1)}, bf16[256,384]{1,0:T(8,128)(2,1)S(1)}, u32[]{:S(2)}, u32[]{:S(2)}) collective-permute-start(bf16[256,384]{1,0:T(8,128)(2,1)} %get-tuple-element.286), channel_id=1, source_target_pairs={{0,3},{1,2},{2,1},{3,0},{4,7},{5,6},{6,5},{7,4},{8,11},{9,10},{10,... | collective-permute-start | bytes 589832 | tf_op jit(solution)/shard_map/ppermute | solution.py:67
  43.1 25.5 %collective-permute-start.8 = (bf16[256,384]{1,0:T(8,128)(2,1)S(1)}, bf16[256,384]{1,0:T(8,128)(2,1)S(1)}, u32[]{:S(2)}, u32[]{:S(2)}) collective-permute-start(bf16[256,384]{1,0:T(8,128)(2,1)S(1)} %copy-done.47), channel_id=1, source_target_pairs={{0,4},{4,0},{8,12},{12,8},{1,5},{5,1},{9,13},{13,9},{2,6},{6,2},{1... | collective-permute-start | bytes 589832 | tf_op jit(solution)/shard_map/ppermute | solution.py:67
  45.3 23.3 %collective-permute-start.9 = (bf16[256,384]{1,0:T(8,128)(2,1)S(1)}, bf16[256,384]{1,0:T(8,128)(2,1)S(1)}, u32[]{:S(2)}, u32[]{:S(2)}) collective-permute-start(bf16[256,384]{1,0:T(8,128)(2,1)S(1)} %get-tuple-element.289), channel_id=1, source_target_pairs={{0,8},{4,12},{8,0},{12,4},{1,9},{5,13},{9,1},{13,5},{2,10},{6,14},... | collective-permute-start | bytes 589832 | tf_op jit(solution)/shard_map/ppermute | solution.py:67
  45.3 23.2 %collective-permute-start.10 = (bf16[256,384]{1,0:T(8,128)(2,1)S(1)}, bf16[256,384]{1,0:T(8,128)(2,1)S(1)}, u32[]{:S(2)}, u32[]{:S(2)}) collective-permute-start(bf16[256,384]{1,0:T(8,128)(2,1)S(1)} %get-tuple-element.290), channel_id=1, source_target_pairs={{0,12},{4,8},{8,4},{12,0},{1,13},{5,9},{9,5},{13,1},{2,14},{6,10},... | collective-permute-start | bytes 589832 | tf_op jit(solution)/shard_map/ppermute | solution.py:67
  71.7 125.0 %all-gather.12.cloned.1.call-start = ((), (), s32[]{:S(2)}) async-start(), calls=%async_computation.6 | async-start | bytes 7077888 | tf_op jit(solution)/shard_map/all_gather | solution.py:1160
  72.3 155.3 %all-gather.14.cloned.1.call-start = ((), (), s32[]{:S(2)}) async-start(), calls=%async_computation.7 | async-start | bytes 3538944 | tf_op jit(solution)/shard_map/all_gather | solution.py:1160
  78.6 13.7 %collective-permute-start.14 = (bf16[128,1536]{1,0:T(8,128)(2,1)}, bf16[128,1536]{1,0:T(8,128)(2,1)S(1)}, u32[]{:S(2)}, u32[]{:S(2)}) collective-permute-start(bf16[128,1536]{1,0:T(8,128)(2,1)} %get-tuple-element.312.refs_1_.x_low), channel_id=1, source_target_pairs={{0,4},{4,0},{8,12},{12,8},{1,5},{5,1},{9,13},{13,9},{2,6},{6,2},{1... | collective-permute-start | bytes 1179656 | tf_op jit(solution)/shard_map/ppermute | solution.py:67
  79.3 16.3 %collective-permute-start.15 = (bf16[128,1536]{1,0:T(8,128)(2,1)}, bf16[128,1536]{1,0:T(8,128)(2,1)S(1)}, u32[]{:S(2)}, u32[]{:S(2)}) collective-permute-start(bf16[128,1536]{1,0:T(8,128)(2,1)} %get-tuple-element.311.refs_0_.x_top), channel_id=1, source_target_pairs={{0,8},{4,12},{8,0},{12,4},{1,9},{5,13},{9,1},{13,5},{2,10},{6,14},... | collective-permute-start | bytes 1179656 | tf_op jit(solution)/shard_map/ppermute | solution.py:67
  85.8 15.9 %collective-permute-start.16 = (bf16[128,1536]{1,0:T(8,128)(2,1)S(1)}, bf16[128,1536]{1,0:T(8,128)(2,1)S(1)}, u32[]{:S(2)}, u32[]{:S(2)}) collective-permute-start(bf16[128,1536]{1,0:T(8,128)(2,1)S(1)} %collective-permute-done.11.refs_2_), channel_id=1, source_target_pairs={{0,8},{4,12},{8,0},{12,4},{1,9},{5,13},{9,1},{13,5},{2,10},{6,14},... | collective-permute-start | bytes 1179656 | tf_op jit(solution)/shard_map/ppermute | solution.py:67
  85.8 15.9 %collective-permute-start.17 = (bf16[128,1536]{1,0:T(8,128)(2,1)S(1)}, bf16[128,1536]{1,0:T(8,128)(2,1)}, u32[]{:S(2)}, u32[]{:S(2)}) collective-permute-start(bf16[128,1536]{1,0:T(8,128)(2,1)S(1)} %collective-permute-done.12.refs_3_), channel_id=1, source_target_pairs={{0,4},{4,0},{8,12},{12,8},{1,5},{5,1},{9,13},{13,9},{2,6},{6,2},{1... | collective-permute-start | bytes 1179656 | tf_op jit(solution)/shard_map/ppermute | solution.py:67
  87.8 26.7 %collective-permute-start.18 = (bf16[256,384]{1,0:T(8,128)(2,1)}, bf16[256,384]{1,0:T(8,128)(2,1)S(1)}, u32[]{:S(2)}, u32[]{:S(2)}) collective-permute-start(bf16[256,384]{1,0:T(8,128)(2,1)} %get-tuple-element.321), channel_id=1, source_target_pairs={{0,2},{1,3},{2,0},{3,1},{4,6},{5,7},{6,4},{7,5},{8,10},{9,11},{10,... | collective-permute-start | bytes 589832 | tf_op jit(solution)/shard_map/ppermute | solution.py:67
  92.3 30.6 %collective-permute-start.19 = (bf16[256,384]{1,0:T(8,128)(2,1)}, bf16[256,384]{1,0:T(8,128)(2,1)S(1)}, u32[]{:S(2)}, u32[]{:S(2)}) collective-permute-start(bf16[256,384]{1,0:T(8,128)(2,1)} %get-tuple-element.322), channel_id=1, source_target_pairs={{0,3},{1,2},{2,1},{3,0},{4,7},{5,6},{6,5},{7,4},{8,11},{9,10},{10,... | collective-permute-start | bytes 589832 | tf_op jit(solution)/shard_map/ppermute | solution.py:67
  125.8 19.6 %collective-permute-start.21 = (bf16[128,1536]{1,0:T(8,128)(2,1)}, bf16[128,1536]{1,0:T(8,128)(2,1)S(1)}, u32[]{:S(2)}, u32[]{:S(2)}) collective-permute-start(bf16[128,1536]{1,0:T(8,128)(2,1)} %get-tuple-element.335.refs_1_.grad_low), channel_id=1, source_target_pairs={{0,8},{4,12},{8,0},{12,4},{1,9},{5,13},{9,1},{13,5},{2,10},{6,14},... | collective-permute-start | bytes 1179656 | tf_op jit(solution)/shard_map/ppermute | solution.py:67
  127.0 18.4 %collective-permute-start.22 = (bf16[128,1536]{1,0:T(8,128)(2,1)}, bf16[128,1536]{1,0:T(8,128)(2,1)S(1)}, u32[]{:S(2)}, u32[]{:S(2)}) collective-permute-start(bf16[128,1536]{1,0:T(8,128)(2,1)} %get-tuple-element.335.refs_1_.grad_low), channel_id=1, source_target_pairs={{0,4},{4,0},{8,12},{12,8},{1,5},{5,1},{9,13},{13,9},{2,6},{6,2},{1... | collective-permute-start | bytes 1179656 | tf_op jit(solution)/shard_map/ppermute | solution.py:67
  128.2 17.2 %collective-permute-start.20 = (bf16[128,1536]{1,0:T(8,128)(2,1)}, bf16[128,1536]{1,0:T(8,128)(2,1)}, u32[]{:S(2)}, u32[]{:S(2)}) collective-permute-start(bf16[128,1536]{1,0:T(8,128)(2,1)} %get-tuple-element.334.refs_0_.grad_top), channel_id=1, source_target_pairs={{0,4},{4,0},{8,12},{12,8},{1,5},{5,1},{9,13},{13,9},{2,6},{6,2},{1... | collective-permute-start | bytes 1179656 | tf_op jit(solution)/shard_map/ppermute | solution.py:67
  128.5 17.8 %collective-permute-start.23 = (bf16[128,1536]{1,0:T(8,128)(2,1)}, bf16[128,1536]{1,0:T(8,128)(2,1)S(1)}, u32[]{:S(2)}, u32[]{:S(2)}) collective-permute-start(bf16[128,1536]{1,0:T(8,128)(2,1)} %get-tuple-element.334.refs_0_.grad_top), channel_id=1, source_target_pairs={{0,8},{4,12},{8,0},{12,4},{1,9},{5,13},{9,1},{13,5},{2,10},{6,14},... | collective-permute-start | bytes 1179656 | tf_op jit(solution)/shard_map/ppermute | solution.py:67
  147.0 184.9 %reduce-scatter.4.cloned.1.call-start = ((), (), s32[]{:S(2)}) async-start(), calls=%async_computation.8 | async-start | bytes 3538944 | tf_op jit(solution)/shard_map/reduce_scatter | solution.py:115
  167.9 14.0 %collective-permute-start.30 = (bf16[256,768]{1,0:T(8,128)(2,1)S(1)}, bf16[256,768]{1,0:T(8,128)(2,1)S(1)}, u32[]{:S(2)}, u32[]{:S(2)}) collective-permute-start(bf16[256,768]{1,0:T(8,128)(2,1)S(1)} %add_convert_fusion.4), channel_id=1, source_target_pairs={{0,4},{4,0},{8,12},{12,8},{1,5},{5,1},{9,13},{13,9},{2,6},{6,2},{1... | collective-permute-start | bytes 1179656 | tf_op jit(solution)/shard_map/ppermute | solution.py:67
  168.6 13.7 %collective-permute-start.31 = (bf16[256,768]{1,0:T(8,128)(2,1)S(1)}, bf16[256,768]{1,0:T(8,128)(2,1)S(1)}, u32[]{:S(2)}, u32[]{:S(2)}) collective-permute-start(bf16[256,768]{1,0:T(8,128)(2,1)S(1)} %get-tuple-element.359), channel_id=1, source_target_pairs={{0,8},{4,12},{8,0},{12,4},{1,9},{5,13},{9,1},{13,5},{2,10},{6,14},... | collective-permute-start | bytes 1179656 | tf_op jit(solution)/shard_map/ppermute | solution.py:67
  188.8 16.0 %collective-permute-start.32 = (bf16[128,1536]{1,0:T(8,128)(2,1)}, bf16[128,1536]{1,0:T(8,128)(2,1)S(1)}, u32[]{:S(2)}, u32[]{:S(2)}) collective-permute-start(bf16[128,1536]{1,0:T(8,128)(2,1)} %get-tuple-element.366.refs_1_), channel_id=1, source_target_pairs={{0,4},{4,0},{8,12},{12,8},{1,5},{5,1},{9,13},{13,9},{2,6},{6,2},{1... | collective-permute-start | bytes 1179656 | tf_op jit(solution)/shard_map/ppermute | solution.py:67
  189.9 15.0 %collective-permute-start.33 = (bf16[128,1536]{1,0:T(8,128)(2,1)}, bf16[128,1536]{1,0:T(8,128)(2,1)S(1)}, u32[]{:S(2)}, u32[]{:S(2)}) collective-permute-start(bf16[128,1536]{1,0:T(8,128)(2,1)} %get-tuple-element.367.refs_0_), channel_id=1, source_target_pairs={{0,8},{4,12},{8,0},{12,4},{1,9},{5,13},{9,1},{13,5},{2,10},{6,14},... | collective-permute-start | bytes 1179656 | tf_op jit(solution)/shard_map/ppermute | solution.py:67
  195.4 14.8 %collective-permute-start.36 = (bf16[128,1536]{1,0:T(8,128)(2,1)S(1)}, bf16[128,1536]{1,0:T(8,128)(2,1)S(1)}, u32[]{:S(2)}, u32[]{:S(2)}) collective-permute-start(bf16[128,1536]{1,0:T(8,128)(2,1)S(1)} %collective-permute-done.34.refs_2_), channel_id=1, source_target_pairs={{0,8},{4,12},{8,0},{12,4},{1,9},{5,13},{9,1},{13,5},{2,10},{6,14},... | collective-permute-start | bytes 1179656 | tf_op jit(solution)/shard_map/ppermute | solution.py:67
  195.6 14.6 %collective-permute-start.37 = (bf16[128,1536]{1,0:T(8,128)(2,1)S(1)}, bf16[128,1536]{1,0:T(8,128)(2,1)S(1)}, u32[]{:S(2)}, u32[]{:S(2)}) collective-permute-start(bf16[128,1536]{1,0:T(8,128)(2,1)S(1)} %collective-permute-done.35.refs_3_), channel_id=1, source_target_pairs={{0,4},{4,0},{8,12},{12,8},{1,5},{5,1},{9,13},{13,9},{2,6},{6,2},{1... | collective-permute-start | bytes 1179656 | tf_op jit(solution)/shard_map/ppermute | solution.py:67
  227.5 154.8 %reduce-scatter.6.cloned.1.call-start = ((), (), s32[]{:S(2)}) async-start(), calls=%async_computation.9 | async-start | bytes 7077888 | tf_op jit(solution)/shard_map/reduce_scatter | solution.py:115
  255.4 14.6 %collective-permute-start.40 = (bf16[256,768]{1,0:T(8,128)(2,1)S(1)}, bf16[256,768]{1,0:T(8,128)(2,1)S(1)}, u32[]{:S(2)}, u32[]{:S(2)}) collective-permute-start(bf16[256,768]{1,0:T(8,128)(2,1)S(1)} %get-tuple-element.396), channel_id=1, source_target_pairs={{0,4},{4,0},{8,12},{12,8},{1,5},{5,1},{9,13},{13,9},{2,6},{6,2},{1... | collective-permute-start | bytes 1179656 | tf_op jit(solution)/shard_map/ppermute | solution.py:67
  255.7 14.2 %collective-permute-start.41 = (bf16[256,768]{1,0:T(8,128)(2,1)S(1)}, bf16[256,768]{1,0:T(8,128)(2,1)S(1)}, u32[]{:S(2)}, u32[]{:S(2)}) collective-permute-start(bf16[256,768]{1,0:T(8,128)(2,1)S(1)} %add_convert_fusion.3), channel_id=1, source_target_pairs={{0,8},{4,12},{8,0},{12,4},{1,9},{5,13},{9,1},{13,5},{2,10},{6,14},... | collective-permute-start | bytes 1179656 | tf_op jit(solution)/shard_map/ppermute | solution.py:67
  257.0 13.0 %collective-permute-start.42 = (bf16[256,768]{1,0:T(8,128)(2,1)S(1)}, bf16[256,768]{1,0:T(8,128)(2,1)S(1)}, u32[]{:S(2)}, u32[]{:S(2)}) collective-permute-start(bf16[256,768]{1,0:T(8,128)(2,1)S(1)} %add_convert_fusion.2), channel_id=1, source_target_pairs={{0,4},{4,0},{8,12},{12,8},{1,5},{5,1},{9,13},{13,9},{2,6},{6,2},{1... | collective-permute-start | bytes 1179656 | tf_op jit(solution)/shard_map/ppermute | solution.py:67
  257.8 12.2 %collective-permute-start.43 = (bf16[256,768]{1,0:T(8,128)(2,1)S(1)}, bf16[256,768]{1,0:T(8,128)(2,1)S(1)}, u32[]{:S(2)}, u32[]{:S(2)}) collective-permute-start(bf16[256,768]{1,0:T(8,128)(2,1)S(1)} %get-tuple-element.401), channel_id=1, source_target_pairs={{0,8},{4,12},{8,0},{12,4},{1,9},{5,13},{9,1},{13,5},{2,10},{6,14},... | collective-permute-start | bytes 1179656 | tf_op jit(solution)/shard_map/ppermute | solution.py:67
  271.1 173.2 %reduce-scatter.8.cloned.1.call-start = ((), (), s32[]{:S(2)}) async-start(), calls=%async_computation.10 | async-start | bytes 7077888 | tf_op jit(solution)/shard_map/reduce_scatter | solution.py:115
  278.1 17.4 %collective-permute-start.46 = (bf16[128,1536]{1,0:T(8,128)(2,1)}, bf16[128,1536]{1,0:T(8,128)(2,1)S(1)}, u32[]{:S(2)}, u32[]{:S(2)}) collective-permute-start(bf16[128,1536]{1,0:T(8,128)(2,1)} %get-tuple-element.418.refs_1_), channel_id=1, source_target_pairs={{0,4},{4,0},{8,12},{12,8},{1,5},{5,1},{9,13},{13,9},{2,6},{6,2},{1... | collective-permute-start | bytes 1179656 | tf_op jit(solution)/shard_map/ppermute | solution.py:67
  278.8 17.1 %collective-permute-start.47 = (bf16[128,1536]{1,0:T(8,128)(2,1)}, bf16[128,1536]{1,0:T(8,128)(2,1)S(1)}, u32[]{:S(2)}, u32[]{:S(2)}) collective-permute-start(bf16[128,1536]{1,0:T(8,128)(2,1)} %get-tuple-element.417.refs_0_), channel_id=1, source_target_pairs={{0,8},{4,12},{8,0},{12,4},{1,9},{5,13},{9,1},{13,5},{2,10},{6,14},... | collective-permute-start | bytes 1179656 | tf_op jit(solution)/shard_map/ppermute | solution.py:67
  284.2 12.8 %collective-permute-start.48 = (bf16[128,1536]{1,0:T(8,128)(2,1)S(1)}, bf16[128,1536]{1,0:T(8,128)(2,1)S(1)}, u32[]{:S(2)}, u32[]{:S(2)}) collective-permute-start(bf16[128,1536]{1,0:T(8,128)(2,1)S(1)} %collective-permute-done.44.refs_2_), channel_id=1, source_target_pairs={{0,8},{4,12},{8,0},{12,4},{1,9},{5,13},{9,1},{13,5},{2,10},{6,14},... | collective-permute-start | bytes 1179656 | tf_op jit(solution)/shard_map/ppermute | solution.py:67
  294.4 30.9 %collective-permute-start.50 = (bf16[256,1536]{1,0:T(8,128)(2,1)}, bf16[256,1536]{1,0:T(8,128)(2,1)}, u32[]{:S(2)}, u32[]{:S(2)}) collective-permute-start(bf16[256,1536]{1,0:T(8,128)(2,1)} %get-tuple-element.428), channel_id=1, source_target_pairs={{0,4},{4,0},{8,12},{12,8},{1,5},{5,1},{9,13},{13,9},{2,6},{6,2},{1... | collective-permute-start | bytes 2359304 | tf_op jit(solution)/shard_map/ppermute | solution.py:67
  295.6 29.7 %collective-permute-start.51 = (bf16[256,1536]{1,0:T(8,128)(2,1)S(1)}, bf16[256,1536]{1,0:T(8,128)(2,1)}, u32[]{:S(2)}, u32[]{:S(2)}) collective-permute-start(bf16[256,1536]{1,0:T(8,128)(2,1)S(1)} %get-tuple-element.429), channel_id=1, source_target_pairs={{0,8},{4,12},{8,0},{12,4},{1,9},{5,13},{9,1},{13,5},{2,10},{6,14},... | collective-permute-start | bytes 2359304 | tf_op jit(solution)/shard_map/ppermute | solution.py:67
  295.9 36.0 %collective-permute-start.52 = (bf16[256,1536]{1,0:T(8,128)(2,1)S(1)}, bf16[256,1536]{1,0:T(8,128)(2,1)}, u32[]{:S(2)}, u32[]{:S(2)}) collective-permute-start(bf16[256,1536]{1,0:T(8,128)(2,1)S(1)} %get-tuple-element.430), channel_id=1, source_target_pairs={{0,12},{4,8},{8,4},{12,0},{1,13},{5,9},{9,5},{13,1},{2,14},{6,10},... | collective-permute-start | bytes 2359304 | tf_op jit(solution)/shard_map/ppermute | solution.py:67
  336.9 14.9 %collective-permute-start.53 = (bf16[256,384]{1,0:T(8,128)(2,1)}, bf16[256,384]{1,0:T(8,128)(2,1)}, u32[]{:S(2)}, u32[]{:S(2)}) collective-permute-start(bf16[256,384]{1,0:T(8,128)(2,1)} %get-tuple-element.443), channel_id=1, source_target_pairs={{0,1},{1,0},{2,3},{3,2},{4,5},{5,4},{6,7},{7,6},{8,9},{9,8},{10,11... | collective-permute-start | bytes 589832 | tf_op jit(solution)/shard_map/ppermute | solution.py:67
  338.5 13.3 %collective-permute-start.54 = (bf16[256,384]{1,0:T(8,128)(2,1)}, bf16[256,384]{1,0:T(8,128)(2,1)}, u32[]{:S(2)}, u32[]{:S(2)}) collective-permute-start(bf16[256,384]{1,0:T(8,128)(2,1)} %get-tuple-element.444), channel_id=1, source_target_pairs={{0,2},{1,3},{2,0},{3,1},{4,6},{5,7},{6,4},{7,5},{8,10},{9,11},{10,... | collective-permute-start | bytes 589832 | tf_op jit(solution)/shard_map/ppermute | solution.py:67
  338.5 18.8 %collective-permute-start.55 = (bf16[256,384]{1,0:T(8,128)(2,1)}, bf16[256,384]{1,0:T(8,128)(2,1)}, u32[]{:S(2)}, u32[]{:S(2)}) collective-permute-start(bf16[256,384]{1,0:T(8,128)(2,1)} %get-tuple-element.445), channel_id=1, source_target_pairs={{0,3},{1,2},{2,1},{3,0},{4,7},{5,6},{6,5},{7,4},{8,11},{9,10},{10,... | collective-permute-start | bytes 589832 | tf_op jit(solution)/shard_map/ppermute | solution.py:67
  368.1 12.7 %collective-permute-start.59 = (bf16[256,768]{1,0:T(8,128)(2,1)S(1)}, bf16[256,768]{1,0:T(8,128)(2,1)S(1)}, u32[]{:S(2)}, u32[]{:S(2)}) collective-permute-start(bf16[256,768]{1,0:T(8,128)(2,1)S(1)} %get-tuple-element.457), channel_id=1, source_target_pairs={{0,4},{4,0},{8,12},{12,8},{1,5},{5,1},{9,13},{13,9},{2,6},{6,2},{1... | collective-permute-start | bytes 1179656 | tf_op jit(solution)/shard_map/ppermute | solution.py:67
  389.9 20.9 %collective-permute-start.63 = (bf16[256,768]{1,0:T(8,128)(2,1)}, bf16[256,768]{1,0:T(8,128)(2,1)S(1)}, u32[]{:S(2)}, u32[]{:S(2)}) collective-permute-start(bf16[256,768]{1,0:T(8,128)(2,1)} %add_convert_fusion), channel_id=1, source_target_pairs={{0,4},{4,0},{8,12},{12,8},{1,5},{5,1},{9,13},{13,9},{2,6},{6,2},{1... | collective-permute-start | bytes 1179656 | tf_op jit(solution)/shard_map/ppermute | solution.py:67
  398.7 12.1 %collective-permute-start.61 = (bf16[256,768]{1,0:T(8,128)(2,1)S(1)}, bf16[256,768]{1,0:T(8,128)(2,1)S(1)}, u32[]{:S(2)}, u32[]{:S(2)}) collective-permute-start(bf16[256,768]{1,0:T(8,128)(2,1)S(1)} %get-tuple-element.469), channel_id=1, source_target_pairs={{0,4},{4,0},{8,12},{12,8},{1,5},{5,1},{9,13},{13,9},{2,6},{6,2},{1... | collective-permute-start | bytes 1179656 | tf_op jit(solution)/shard_map/ppermute | solution.py:67
  404.8 13.6 %collective-permute-start.64 = (bf16[256,768]{1,0:T(8,128)(2,1)S(1)}, bf16[256,768]{1,0:T(8,128)(2,1)S(1)}, u32[]{:S(2)}, u32[]{:S(2)}) collective-permute-start(bf16[256,768]{1,0:T(8,128)(2,1)S(1)} %get-tuple-element.474), channel_id=1, source_target_pairs={{0,8},{4,12},{8,0},{12,4},{1,9},{5,13},{9,1},{13,5},{2,10},{6,14},... | collective-permute-start | bytes 1179656 | tf_op jit(solution)/shard_map/ppermute | solution.py:67
  425.0 12.0 %collective-permute-start.76 = (bf16[256,384]{1,0:T(8,128)(2,1)}, bf16[256,384]{1,0:T(8,128)(2,1)S(1)}, u32[]{:S(2)}, u32[]{:S(2)}) collective-permute-start(bf16[256,384]{1,0:T(8,128)(2,1)} %get-tuple-element.498), channel_id=1, source_target_pairs={{0,2},{1,3},{2,0},{3,1},{4,6},{5,7},{6,4},{7,5},{8,10},{9,11},{10,... | collective-permute-start | bytes 589832 | tf_op jit(solution)/shard_map/ppermute | solution.py:67
  425.0 19.3 %collective-permute-start.77 = (bf16[256,384]{1,0:T(8,128)(2,1)}, bf16[256,384]{1,0:T(8,128)(2,1)S(1)}, u32[]{:S(2)}, u32[]{:S(2)}) collective-permute-start(bf16[256,384]{1,0:T(8,128)(2,1)} %get-tuple-element.499), channel_id=1, source_target_pairs={{0,3},{1,2},{2,1},{3,0},{4,7},{5,6},{6,5},{7,4},{8,11},{9,10},{10,... | collective-permute-start | bytes 589832 | tf_op jit(solution)/shard_map/ppermute | solution.py:67
  (154 other events, 1097.5 us)
Sparse Core Ops, SparseCore 0:
  10.3 32.7 all-gather.5
  45.3 30.0 all-gather.7
  77.0 42.5 all-gather.9
  121.1 66.6 all-gather.11
  189.3 38.1 all-gather.13
  229.7 40.7 reduce-scatter.3
  272.8 71.8 reduce-scatter.5
  357.5 71.3 reduce-scatter.7

commit v5 on v4

--- a/solution.py
+++ b/solution.py
@@ -6,7 +6,7 @@
 from jax.sharding import PartitionSpec as P
 
 EPSILON = 1e-06
-FAR = 1e30
+FAR = 2.0**100
 LANES = 128
 BF = jnp.bfloat16
 F32 = jnp.float32
@@ -830,15 +830,28 @@
     return lax.broadcasted_iota(jnp.int32, (rows, LANES), 1)
 
 
-def split_column(column):
-    one = column.astype(BF).astype(F32)
-    two = (column - one).astype(BF).astype(F32)
-    return one, two, column - one - two
-
-
-def fill(lanes, base, columns, rest):
-    for at, column in reversed(list(enumerate(columns))):
-        rest = jnp.where(lanes == base + at, column, rest)
+COLUMN_SUM, ROW_SUM, SECOND = 16, 32, 24
+
+
+def parts_of(values):
+    one = values.astype(BF).astype(F32)
+    two = (values - one).astype(BF).astype(F32)
+    return one, two, values - one - two
+
+
+def packed(values):
+    one, two, three = parts_of(values)
+    return one + pltpu.roll(two, 8, 1) + pltpu.roll(three, 16, 1)
+
+
+def ordered_sums(ones, values):
+    sums = dot(ones, jnp.concatenate(parts_of(values), axis=1).astype(BF))
+    return sums[:, :LANES] + sums[:, LANES : 2 * LANES] + sums[:, 2 * LANES :]
+
+
+def at_lane(lanes, base, offsets, value, rest):
+    for offset in offsets:
+        rest = jnp.where(lanes == base + offset, value, rest)
     return rest
 
 
@@ -853,6 +866,7 @@
     att_ref,
     qa_ref,
     ka_ref,
+    log_ref,
     c_ref,
     va_ref,
 ):
@@ -872,38 +886,46 @@
     def sum_keeps():
         below = lax.broadcasted_iota(jnp.int32, (block, block), 0)
         across = lax.broadcasted_iota(jnp.int32, (block, block), 1)
-        ones = jnp.where(below >= across, 1.0, 0.0)
+        ones = jnp.where(below >= across, 1.0, 0.0).astype(BF)
         running = jnp.zeros((1, LANES), F32)
+        log_ref[...] = jnp.zeros_like(log_ref)
         for at in range(4):
-            sums = running + lax.dot_general(
-                ones,
-                get_rows(keep_ref, rows_of(at)),
-                (((1,), (0,)), ((), ())),
-                precision=lax.Precision.HIGHEST,
-                preferred_element_type=F32,
+            own = pl.ds(at * block, block)
+            keeps = jnp.where(
+                lanes < 2 * pl.num_programs(0), get_rows(keep_ref, rows_of(at)), 0.0
             )
-            c_ref[pl.ds(at * block, block), :] = sums
+            sums = running + ordered_sums(ones, keeps)
             running = sums[block - 1 :, :]
-
+            places = at * block + lax.broadcasted_iota(jnp.int32, (block, LANES), 0)
+            second = jnp.where((places >= first_length) & (lanes == SECOND), 1.0, 0.0)
+            c_ref[own, :] = (packed(sums) + second).astype(BF)
+
+    source = lax.broadcasted_iota(jnp.int32, (LANES, 2 * LANES), 0)
+    target = lax.broadcasted_iota(jnp.int32, (LANES, 2 * LANES), 1)
+    one_row = lax.broadcasted_iota(jnp.int32, (1, LANES), 1)
     for head in range(2):
+        number = 2 * pair + head
         mine = (lanes < 64) if head == 0 else (lanes >= 64)
         base = 64 if head == 0 else 0
+        moves = jnp.zeros((LANES, 2 * LANES), F32)
+        for part in range(3):
+            moves = jnp.where(
+                (source == 8 * part + number) & (target == base + part), -1.0, moves
+            )
+        moves = jnp.where((source == SECOND) & (target == base + 3), FAR, moves)
+        moves = jnp.where((source == SECOND) & (target == LANES + base + 3), 1.0, moves).astype(BF)
+        k_ones = at_lane(one_row, base, (4, 5, 6, ROW_SUM + number), 1.0, 0.0)
+        k_ones = at_lane(one_row, base, (3,), -FAR, k_ones)
+        q_ones = at_lane(one_row, base, (0, 1, 2, COLUMN_SUM + number), 1.0, 0.0)
         for at in range(4):
             rows, own = rows_of(at), pl.ds(at * block, block)
-            decay = jnp.sum(
-                jnp.where(lanes == 2 * pair + head, c_ref[own, :], 0.0), axis=1, keepdims=True
-            )
-            one, two, three = split_column(decay)
-            places = at * block + lax.broadcasted_iota(jnp.int32, (block, 1), 0)
-            second = jnp.where(places >= first_length, 1.0, 0.0)
-            q_side = fill(lanes, base, (1.0, 1.0, 1.0, second), 0.0)
-            k_side = fill(
-                lanes, base, (-one, -two, -three, (second - 1.0) * FAR, 1.0, 1.0, 1.0), 0.0
-            )
+            sides = dot(c_ref[own, :], moves)
             qa_ref[head, own, :] = jnp.where(
-                mine, get_rows(q_ref, rows).astype(F32) * 0.125, q_side
+                mine, get_rows(q_ref, rows).astype(F32) * 0.125, sides[:, LANES:] + q_ones
             ).astype(BF)
-            ka_ref[head, own, :] = jnp.where(mine, get_rows(k_ref, rows).astype(F32), k_side).astype(BF)
+            ka_ref[head, own, :] = jnp.where(
+                mine, get_rows(k_ref, rows).astype(F32), sides[:, :LANES] + k_ones
+            ).astype(BF)
             va_ref[head, own, :] = jnp.where(mine, get_rows(v_ref, rows).astype(F32), 1.0).astype(BF)
 
     below = lax.broadcasted_iota(jnp.int32, (block, block), 0)
@@ -912,8 +934,8 @@
         own = pl.ds(at * block, block)
         width = (at + 1) * block
         results = []
+        logs = log_ref[own, :]
         for head in range(2):
-            base = 64 if head == 0 else 0
             queries = qa_ref[head, own, :]
             last = jnp.where(
                 below >= across, dot(queries, ka_ref[head, at * block : width, :], NT), -FAR
@@ -925,13 +947,10 @@
             total = dot(jnp.exp(last - top).astype(BF), va_ref[head, at * block : width, :])
             if at > 0:
                 total += dot(jnp.exp(early - top).astype(BF), va_ref[head, : at * block, :])
-            weight = pltpu.roll(total, 64, 1)
-            results.append(total / weight)
-            log_total = top + jnp.log(total[:, base : base + 1])
-            one, two, three = split_column(log_total)
-            qa_ref[head, own, :] = fill(
-                lanes, base + 4, (-one, -two, -three), queries.astype(F32)
-            ).astype(BF)
+            results.append(total / pltpu.roll(total, 64, 1))
+            kept = 64 * (1 - head) + 2 * pair + head
+            logs = jnp.where(lanes == kept, top + jnp.log(total), logs)
+        log_ref[own, :] = logs
         attended = jnp.where(lanes < 64, results[0], results[1])
         put_rows(att_ref, rows_of(at), slice(None), attended)
 
@@ -956,9 +975,14 @@
                 columns(2 * pairs),
                 pl.BlockSpec((row_total, LANES), lambda p, *_: (0, 0)),
             ],
-            out_specs=[columns(0), sided, sided],
+            out_specs=[
+                columns(0),
+                sided,
+                sided,
+                pl.BlockSpec((row_total, LANES), lambda p, *_: (0, 0)),
+            ],
             scratch_shapes=[
-                pltpu.VMEM((row_total, LANES), F32),
+                pltpu.VMEM((row_total, LANES), BF),
                 pltpu.VMEM((2, row_total, LANES), BF),
             ],
         ),
@@ -966,6 +990,7 @@
             jax.ShapeDtypeStruct((row_total, width), F32),
             jax.ShapeDtypeStruct((heads, row_total, LANES), BF),
             jax.ShapeDtypeStruct((heads, row_total, LANES), BF),
+            jax.ShapeDtypeStruct((row_total, LANES), F32),
         ],
         compiler_params=pltpu.CompilerParams(vmem_limit_bytes=60 * 2**20),
         cost_estimate=cost(10 * 10**9, 8 * 2**20),
@@ -976,18 +1001,22 @@
     where,
     qa_ref,
     ka_ref,
+    log_ref,
     v_ref,
     datt_ref,
     att_ref,
     slope_ref,
     out_ref,
+    l_ref,
+    qf_ref,
     va_ref,
     da_ref,
     kt_ref,
     dk_ref,
     dv_ref,
     dq_ref,
-    dc_ref,
+    row_ref,
+    column_ref,
 ):
     pair = pl.program_id(0)
     pairs = pl.num_programs(0)
@@ -1004,24 +1033,48 @@
         return pl.ds(pl.multiple_of((group * pairs + pair) * LANES, LANES), LANES)
 
     @pl.when(pair == 0)
-    def clear():
-        dc_ref[...] = jnp.zeros_like(dc_ref)
+    def start():
+        row_ref[...] = jnp.zeros_like(row_ref)
+        column_ref[...] = jnp.zeros_like(column_ref)
+        for at in range(4):
+            own = pl.ds(at * block, block)
+            l_ref[own, :] = packed(log_ref[own, :]).astype(BF)
+
+    source = lax.broadcasted_iota(jnp.int32, (LANES, LANES), 0)
+    target = lax.broadcasted_iota(jnp.int32, (LANES, LANES), 1)
+    halves_at = lax.broadcasted_iota(jnp.int32, (2 * LANES, 2 * LANES), 0) & (LANES - 1)
+    sums_at = lax.broadcasted_iota(jnp.int32, (2 * LANES, 2 * LANES), 1)
+    halves = jnp.where((halves_at < 64) == (sums_at < LANES), 1.0, 0.0).astype(BF)
+    moves = []
+    for head in range(2):
+        kept = 64 * (1 - head) + 2 * pair + head
+        base = 64 if head == 0 else 0
+        move = jnp.zeros((LANES, LANES), F32)
+        for part in range(3):
+            move = jnp.where((source == kept + 8 * part) & (target == base + 4 + part), -1.0, move)
+        moves.append(move.astype(BF))
 
     for at in range(4):
         rows, own = rows_of(at), pl.ds(at * block, block)
         grad_att = get_rows(datt_ref, rows).astype(F32)
         inner = grad_att * get_rows(att_ref, rows)
+        high = inner.astype(BF)
+        rest = (inner - high.astype(F32)).astype(BF)
+        deltas = dot(jnp.concatenate([high, rest], axis=1), halves)
         values = get_rows(v_ref, rows).astype(F32)
         for head in range(2):
             mine = (lanes < 64) if head == 0 else (lanes >= 64)
             base = 64 if head == 0 else 0
-            delta = jnp.sum(jnp.where(mine, inner, 0.0), axis=1, keepdims=True)
-            one, two, three = split_column(delta)
-            da_ref[head, own, :] = jnp.where(
-                mine, grad_att, fill(lanes, base, (-one, -two, -three), 0.0)
+            one, two, three = parts_of(deltas[:, head * LANES : (head + 1) * LANES])
+            side = jnp.where(lanes == base, -one, 0.0)
+            side = jnp.where(lanes == base + 1, -two, side)
+            side = jnp.where(lanes == base + 2, -three, side)
+            da_ref[head, own, :] = jnp.where(mine, grad_att, side).astype(BF)
+            va_ref[head, own, :] = jnp.where(
+                mine, values, jnp.where((lanes >= base) & (lanes < base + 3), 1.0, 0.0)
             ).astype(BF)
-            va_ref[head, own, :] = jnp.where(
-                mine, values, fill(lanes, base, (1.0, 1.0, 1.0), 0.0)
+            qf_ref[head, own, :] = (
+                qa_ref[head, own, :].astype(F32) + dot(l_ref[own, :], moves[head])
             ).astype(BF)
 
     below = lax.broadcasted_iota(jnp.int32, (block, block), 0)
@@ -1030,20 +1083,22 @@
         for at in range(4):
             own = pl.ds(at * block, block)
             kt_ref[:, own] = ka_ref[head, own, :].astype(F32).T.astype(BF)
-        for at in range(4):
+        for at in reversed(range(4)):
             own = pl.ds(at * block, block)
-            queries, grads = qa_ref[head, own, :], da_ref[head, own, :]
+            queries, grads = qf_ref[head, own, :], da_ref[head, own, :]
             dq_t = jnp.zeros((LANES, block), F32)
-            for past in range(at + 1):
-                keys = pl.ds(past * block, block)
+            spans = [pl.ds(at * block, block)]
+            if at > 0:
+                spans.append(pl.ds(0, at * block))
+            for n, keys in enumerate(spans):
                 probs = jnp.exp(dot(ka_ref[head, keys, :], queries, NT))
-                if past == at:
+                if n == 0:
                     probs = jnp.where(below <= across, probs, 0.0)
                 grad_scores = (probs * dot(va_ref[head, keys, :], grads, NT)).astype(BF)
                 dv = dot(probs.astype(BF), grads)
                 dk = dot(grad_scores, queries)
                 dq_t += dot(kt_ref[:, keys], grad_scores)
-                if past == at:
+                if at == 3:
                     dv_ref[head, keys, :] = dv
                     dk_ref[head, keys, :] = dk
                 else:
@@ -1054,11 +1109,9 @@
     for at in range(4):
         rows, own = rows_of(at), pl.ds(at * block, block)
         for head in range(2):
-            base = 64 if head == 0 else 0
-            change = (
-                dq_ref[head, own, base + 4 : base + 5] - dk_ref[head, own, base : base + 1]
-            )
-            dc_ref[own, :] += jnp.where(lanes == 2 * pair + head, change, 0.0)
+            lane = 64 * (1 - head) + 2 * pair + head
+            row_ref[own, :] += jnp.where(lanes == lane + ROW_SUM, dq_ref[head, own, :], 0.0)
+            column_ref[own, :] += jnp.where(lanes == lane + COLUMN_SUM, dk_ref[head, own, :], 0.0)
         left = lanes < 64
         for group, ref, scale in ((0, dq_ref, 0.125), (1, dk_ref, 1.0), (2, dv_ref, 1.0)):
             both = jnp.where(left, ref[0, own, :], ref[1, own, :])
@@ -1066,16 +1119,14 @@
 
     @pl.when(pair == pairs - 1)
     def finish():
-        ones = jnp.where(below <= across, 1.0, 0.0)
+        ones = jnp.where(below <= across, 1.0, 0.0).astype(BF)
         running = jnp.zeros((1, LANES), F32)
         for at in reversed(range(4)):
-            sums = running + lax.dot_general(
-                ones,
-                dc_ref[pl.ds(at * block, block), :],
-                (((1,), (0,)), ((), ())),
-                precision=lax.Precision.HIGHEST,
-                preferred_element_type=F32,
-            )
+            own = pl.ds(at * block, block)
+            change = pltpu.roll(row_ref[own, :], LANES - ROW_SUM, 1)
+            change = change - pltpu.roll(column_ref[own, :], LANES - COLUMN_SUM, 1)
+            change = jnp.where(lanes < 2 * pairs, change + pltpu.roll(change, 64, 1), 0.0)
+            sums = running + ordered_sums(ones, change)
             running = sums[:1, :]
             rows = rows_of(at)
             put_rows(
@@ -1086,7 +1137,7 @@
             )
 
 
-def attend_backward(where, qa, ka, qkv, grad_att, attended, slope):
+def attend_backward(where, qa, ka, logs, qkv, grad_att, attended, slope):
     row_total, width = attended.shape
     pairs = width // LANES
     heads = 2 * pairs
@@ -1105,6 +1156,7 @@
             in_specs=[
                 sided,
                 sided,
+                pl.BlockSpec((row_total, LANES), lambda p, *_: (0, 0)),
                 columns(2 * pairs),
                 columns(0),
                 columns(0),
@@ -1112,6 +1164,8 @@
             ],
             out_specs=pl.BlockSpec((row_total, total), lambda p, *_: (0, 0)),
             scratch_shapes=[
+                pltpu.VMEM((row_total, LANES), BF),
+                pltpu.VMEM(both, BF),
                 pltpu.VMEM(both, BF),
                 pltpu.VMEM(both, BF),
                 pltpu.VMEM((LANES, row_total), BF),
@@ -1119,12 +1173,13 @@
                 pltpu.VMEM(both, F32),
                 pltpu.VMEM(both, F32),
                 pltpu.VMEM((row_total, LANES), F32),
+                pltpu.VMEM((row_total, LANES), F32),
             ],
         ),
         out_shape=jax.ShapeDtypeStruct((row_total, total), BF),
         compiler_params=pltpu.CompilerParams(vmem_limit_bytes=60 * 2**20),
         cost_estimate=cost(12 * 10**9, 8 * 2**20),
-    )(where, qa, ka, qkv, grad_att, attended, slope)
+    )(where, qa, ka, logs, qkv, grad_att, attended, slope)
 
 
 def on_device(
@@ -1192,7 +1247,7 @@
     qkv, top, low = tie(qkv, top, low)
     top_x, low_y = swap(top, "tx", 1), swap(low, "tx", 2)
     low_x, top_y = swap(low, "tx", 1), swap(top, "tx", 2)
-    attended, qa, ka = attend_forward(where, seq_lengths, seq_deal, qkv, keep)
+    attended, qa, ka, logs = attend_forward(where, seq_lengths, seq_deal, qkv, keep)
     attended, top_x, low_y, low_x, top_y = tie(attended, top_x, low_y, low_x, top_y)
     top_d, low_d = swap(top_x, "tx", 2), swap(low_y, "tx", 1)
     grad_full = [top, low, top_x, low_y, low_x, top_y, top_d, low_d]
@@ -1238,7 +1293,7 @@
 
     sent = [swap(piece, "tx", k + 1) for k, piece in enumerate(sent)]
     grad_att, grad_ogate = back_products(z_parts, w_second, out_gate, attended)
-    grad_first = attend_backward(where, qa, ka, qkv, grad_att, attended, slope)
+    grad_first = attend_backward(where, qa, ka, logs, qkv, grad_att, attended, slope)
     grad_first, sent, grads_down = tie(grad_first, sent, grads_down)
     output = on_rows(result_kernel, where, [second, own, *sent], None, [], True)
     output, grad_first = tie(output, grad_first)

time: 483 us -> 485 us (level)
  Pallas kernels: 208 us -> 203 us
  waiting for transfers between devices: 124 us -> 129 us
    ppermute x89, waiting for transfers between devices: 123 us -> 128 us  [swap(): lax.ppermute(values, axis, [(at, at ^ step) for at in range(lax.axis_size...]
  transfers between devices with their start and end apart: 97 -> 97, of which waited for: 33 -> 36; matrix products, arithmetic and copies ran while one was open for 4% -> 4% of each run, Pallas kernels for 43% -> 41%
where the time goes in v5:
time: 485 us; the launch traced here: 481 us
  Pallas kernels  203 us (42%)
  waiting for transfers between devices  129 us (27%)
  starting transfers between devices  89.2 us (18%)
  local copies, waits for them, and re-layouts  29.3 us (6%)
  between operations  15.4 us (3%)
  other arithmetic  15 us (3%)
    ppermute x89, waiting for transfers between devices, swap(): lax.ppermute(values, axis, [(at, at ^ step) for at in range(lax.axis_size...  128 us
    ppermute x89, starting transfers between devices, swap(): lax.ppermute(values, axis, [(at, at ^ step) for at in range(lax.axis_size...  88.1 us
    pallas_call x7, Pallas kernels, part_products(): pl.pallas_call(lambda *refs: part_kernel(order, split, len(lefts), *refs)...  44.7 us
    unnamed x213, local copies, waits for them, and re-layouts  23.2 us
    pallas_call x1, Pallas kernels, attend_backward(): pl.pallas_call(backward_kernel, grid_spec=pltpu.PrefetchScalarGridSpec(nu...  20.2 us
    pallas_call x4, Pallas kernels, on_rows(): pl.pallas_call(kernel, grid_spec=pltpu.PrefetchScalarGridSpec(num_scalar_...  19.9 us
    pallas_call x2, Pallas kernels, up_products(): pl.pallas_call(up_kernel, grid=(steps,), in_specs=[pl.BlockSpec(p.shape,...  16.2 us
    pallas_call x1, Pallas kernels, attend_forward(): pl.pallas_call(forward_kernel, grid_spec=pltpu.PrefetchScalarGridSpec(num...  13.6 us
  transfers between devices with their start and end apart: 97, of which 36 were waited for; matrix products, arithmetic and copies ran while one was open for 4% of the time, Pallas kernels for 41%

profile of v5, /device:TPU:9, one launch (start us, length us, event | category | flops | bytes accessed | tf_op | source)
XLA Modules:
  0.0 480.8 jit_solution(6313195640529307749)
XLA Ops:
  17.6 4.9 %shard_map.263 = (bf16[256,384]{1,0:T(8,128)(2,1)S(1)}, bf16[256,384]{1,0:T(8,128)(2,1)}, bf16[256,384]{1,0:T(8,128)(2,1)}, bf16[256,384]{1,0:T(8,128)(2,1)}, bf...) custom-call(s32[3]{0:T(128)S(1)} %pad_add_fusion.refs_0_.where, ...), custom_call_target="tpu_custom_call" | custom-call | flops 6442450944 | bytes 8388608 | tf_op jit(solution)/shard_map/pallas_call | solution.py:794
  30.2 7.1 %collective-permute-done.3.refs_2_ = bf16[256,384]{1,0:T(8,128)(2,1)} collective-permute-done((bf16[256,384]{1,0:T(8,128)(2,1)}, bf16[256,384]{1,0:T(8,128)(2,1)}, u32[]{:S(2)}, u32[]{:S(2)}) %collective-permute-start.3) | collective-permute-done | bytes 196640 | tf_op jit(solution)/shard_map/ppermute | solution.py:67
  47.5 8.6 %collective-permute-done.6.refs_2_ = bf16[256,384]{1,0:T(8,128)(2,1)S(1)} collective-permute-done((bf16[256,384]{1,0:T(8,128)(2,1)}, bf16[256,384]{1,0:T(8,128)(2,1)S(1)}, u32[]{:S(2)}, u32[]{:S(2)}) %collective-permute-start.6) | collective-permute-done | bytes 196640 | tf_op jit(solution)/shard_map/ppermute | solution.py:67
  56.1 12.1 %collective-permute-done.7.refs_3_ = bf16[256,384]{1,0:T(8,128)(2,1)S(1)} collective-permute-done((bf16[256,384]{1,0:T(8,128)(2,1)}, bf16[256,384]{1,0:T(8,128)(2,1)S(1)}, u32[]{:S(2)}, u32[]{:S(2)}) %collective-permute-start.7) | collective-permute-done | bytes 196640 | tf_op jit(solution)/shard_map/ppermute | solution.py:67
  74.4 4.2 collective-permute-start.11
  80.1 3.3 collective-permute-done.13.refs_1_
  88.8 4.2 collective-permute-done.14.refs_4_
  93.0 3.5 collective-permute-start.19
  96.6 6.3 %collective-permute-done.16.refs_6_ = bf16[128,1536]{1,0:T(8,128)(2,1)S(1)} collective-permute-done((bf16[128,1536]{1,0:T(8,128)(2,1)S(1)}, bf16[128,1536]{1,0:T(8,128)(2,1)S(1)}, u32[]{:S(2)}, u32[]{:S(2)}) %collective-permute-start.16) | collective-permute-done | bytes 393248 | tf_op jit(solution)/shard_map/ppermute | solution.py:67
  103.6 12.0 %shard_map.267 = (bf16[1024,1536]{1,0:T(8,128)(2,1)}, bf16[1024,1280]{1,0:T(8,128)(2,1)}, f32[1024,128]{1,0:T(8,128)}, f32[1024,128]{1,0:T(8,128)}, f32[8,1536]{1,0:T(8,128)}) custom-call(bf16[128,1536]{1,0:T(8,128)(2,1)} %get-tuple-element.312.refs_0_.x_top, bf16[128,1536]{1,0:T(8,128)(2,1)} %get-tuple-element.313.refs_1_.x_low, ...), custom_call_target="tpu_custom_call" | custom-call | flops 4026531840 | bytes 12582912 | tf_op jit(solution)/shard_map/pallas_call | solution.py:499
  115.6 7.5 %collective-permute-done.19.refs_3_ = bf16[256,384]{1,0:T(8,128)(2,1)S(1)} collective-permute-done((bf16[256,384]{1,0:T(8,128)(2,1)}, bf16[256,384]{1,0:T(8,128)(2,1)S(1)}, u32[]{:S(2)}, u32[]{:S(2)}) %collective-permute-start.19) | collective-permute-done | bytes 196640 | tf_op jit(solution)/shard_map/ppermute | solution.py:67
  128.8 13.6 %shard_map.269 = (f32[1024,384]{1,0:T(8,128)}, bf16[6,1024,128]{2,1,0:T(8,128)(2,1)}, bf16[6,1024,128]{2,1,0:T(8,128)(2,1)}, f32[1024,128]{1,0:T(8,128)}) custom-call(s32[3]{0:T(128)} %copy-done.35, s32[4,4]{1,0:T(4,128)} %refs_1_.5, s32[4,4]{1,0:T(4,128)} %refs_2_.5, bf16[1024,1280]{1,0:T(8,128)(2,1)} %get-tuple-element.332.q_ref.k_ref.v_ref, ...), custom_call_target="tpu_custom_call" | custom-call | flops 10000000000 | bytes 8388608 | tf_op jit(solution)/shard_map/pallas_call | solution.py:967
  142.5 2.6 collective-permute-done.20.refs_2_
  149.8 4.7 shard_map.270
  159.8 5.2 %shard_map.272 = (bf16[256,768]{1,0:T(8,128)(2,1)S(1)}, f32[256,768]{1,0:T(8,128)S(1)}, f32[256,768]{1,0:T(8,128)S(1)}, f32[256,768]{1,0:T(8,128)S(1)}, bf16[256...) custom-call(bf16[1024,384]{1,0:T(8,128)(2,1)} %copy-done.10, ...), custom_call_target="tpu_custom_call" | custom-call | flops 905969664 | bytes 1811939 | tf_op jit(solution)/shard_map/pallas_call | solution.py:187
  169.0 4.2 collective-permute-done.28.refs_1_
  174.1 6.4 %collective-permute-done.30.refs_4_ = bf16[256,768]{1,0:T(8,128)(2,1)S(1)} collective-permute-done((bf16[256,768]{1,0:T(8,128)(2,1)S(1)}, bf16[256,768]{1,0:T(8,128)(2,1)S(1)}, u32[]{:S(2)}, u32[]{:S(2)}) %collective-permute-start.30) | collective-permute-done | bytes 393248 | tf_op jit(solution)/shard_map/ppermute | solution.py:67
  182.9 4.6 shard_map.273
  190.5 3.9 collective-permute-done.34.refs_2_
  196.5 8.1 %shard_map.274 = (bf16[1024,1536]{1,0:T(8,128)(2,1)}, bf16[1024,1024]{1,0:T(8,128)(2,1)}, bf16[1024,1024]{1,0:T(8,128)(2,1)}, bf16[1024,1024]{1,0:T(8,128)(2,1)}) custom-call(bf16[128,1536]{1,0:T(8,128)(2,1)} %get-tuple-element.368.refs_0_, bf16[128,1536]{1,0:T(8,128)(2,1)} %get-tuple-element.367.refs_1_, bf16[128,1536]{1,0:T(8,128)(2,1)} %copy-done.61, ...), custom_call_target="tpu_custom_call" | custom-call | flops 3221225472 | bytes 16777216 | tf_op jit(solution)/shard_map/pallas_call | solution.py:586
  204.7 6.0 %collective-permute-done.36.refs_2_ = bf16[128,1536]{1,0:T(8,128)(2,1)S(1)} collective-permute-done((bf16[128,1536]{1,0:T(8,128)(2,1)S(1)}, bf16[128,1536]{1,0:T(8,128)(2,1)S(1)}, u32[]{:S(2)}, u32[]{:S(2)}) %collective-permute-start.36) | collective-permute-done | bytes 393248 | tf_op jit(solution)/shard_map/ppermute | solution.py:67
  211.6 8.1 %shard_map.275 = (bf16[1024,1536]{1,0:T(8,128)(2,1)}, bf16[1024,1024]{1,0:T(8,128)(2,1)}, bf16[1024,1024]{1,0:T(8,128)(2,1)}, bf16[1024,1024]{1,0:T(8,128)(2,1)}) custom-call(bf16[128,1536]{1,0:T(8,128)(2,1)} %copy-done.77, bf16[128,1536]{1,0:T(8,128)(2,1)} %copy-done.78, ...), custom_call_target="tpu_custom_call", output_to_operand_aliasing={{0}: (6, {}), {1}: (7, {}), {2}: (8, {}), {3}: (9, {})} | custom-call | flops 3221225472 | bytes 16777216 | tf_op jit(solution)/shard_map/pallas_call | solution.py:586
  219.8 8.3 %shard_map.276 = (bf16[4096,384]{1,0:T(8,128)(2,1)}, bf16[1024,1536]{1,0:T(8,128)(2,1)}) custom-call(bf16[1024,1024]{1,0:T(8,128)(2,1)} %get-tuple-element.422.left.refs_0_, bf16[128,1536]{1,0:T(8,128)(2,1)S(1)} %copy-done.31, bf16[128,1536]{1,0:T(8,128)(2,1)S(1)} %copy-done.32, bf16[128,1536]{1,0:T(8,128)(2,1)} %collective-permute-done.20.refs_2_, ...), custom_call_target="tpu_custom_call" | custom-call | flops 3221225472 | bytes 6442450 | tf_op jit(solution)/shard_map/pallas_call | solution.py:235
  229.6 8.2 %shard_map.277.refs_0_.refs_1_.right = bf16[2,1024,1024]{2,1,0:T(8,128)(2,1)} custom-call(bf16[1024,1536]{1,0:T(8,128)(2,1)} %get-tuple-element.381.g_ref, bf16[1536,1024]{1,0:T(8,128)(2,1)} %all-gather.14.cloned.1.call-done.w_ref.refs_1_, bf16[1024,1024]{1,0:T(8,128)(2,1)S(1)} %copy-done.4, bf16[1024,1024]{1,0:T(8,128)(2,1)} %get-tuple-element.384.to_up_ref), custom_call_target="tpu_custom_call" | custom-call | flops 3221225472 | bytes 16777216 | tf_op jit(solution)/shard_map/pallas_call | solution.py:615
  237.8 6.3 %shard_map.278 = (bf16[256,768]{1,0:T(8,128)(2,1)S(1)}, bf16[256,768]{1,0:T(8,128)(2,1)S(1)}) custom-call(bf16[2,1024,1024]{2,1,0:T(8,128)(2,1)} %shard_map.277.refs_0_.refs_1_.right, bf16[2,1024,1024]{2,1,0:T(8,128)(2,1)} %shard_map.277.refs_0_.refs_1_.right, bf16[1536,2048]{1,0:T(8,128)(2,1)} %all-gather.12.cloned.1.call-done.refs_4_.refs_5_.refs_2_.refs_3_, ...), custom_call_target="tpu_custom_call" | custom-call | flops 1610612736 | bytes 3221225 | tf_op jit(solution)/shard_map/pallas_call | solution.py:187
  245.2 9.4 %shard_map.279 = (bf16[256,768]{1,0:T(8,128)(2,1)S(1)}, f32[256,768]{1,0:T(8,128)S(1)}, f32[256,768]{1,0:T(8,128)S(1)}, f32[256,768]{1,0:T(8,128)S(1)}, bf16[256...) custom-call(bf16[2,1024,1024]{2,1,0:T(8,128)(2,1)} %shard_map.277.refs_0_.refs_1_.right, ...), custom_call_target="tpu_custom_call" | custom-call | flops 4831838208 | bytes 9663676 | tf_op jit(solution)/shard_map/pallas_call | solution.py:187
  258.7 11.3 %shard_map.280 = bf16[1536,2048]{1,0:T(8,128)(2,1)} custom-call(bf16[1024,1536]{1,0:T(8,128)(2,1)S(1)} %copy-done.7, bf16[2,1024,1024]{2,1,0:T(8,128)(2,1)} %shard_map.277.refs_0_.refs_1_.right), custom_call_target="tpu_custom_call" | custom-call | flops 6442450944 | bytes 12884901 | tf_op jit(solution)/shard_map/pallas_call | solution.py:211
  271.6 5.4 %shard_map.281 = (f32[256,1536]{1,0:T(8,128)}, bf16[128,1536]{1,0:T(8,128)(2,1)}, bf16[128,1536]{1,0:T(8,128)(2,1)}) custom-call(s32[3]{0:T(128)} %copy-done.35, f32[256,1536]{1,0:T(8,128)} %get-tuple-element.366.second_ref, bf16[128,1536]{1,0:T(8,128)(2,1)} %get-tuple-element.335.refs_0_.grad_top, bf16[128,1536]{1,0:T(8,128)(2,1)} %get-tuple-element.336.refs_1_.grad_low, ...), custom_call_target="tpu_custom_call" | custom-call | flops 1 | bytes 6291456 | tf_op jit(solution)/shard_map/pallas_call | solution.py:438
  280.0 4.3 collective-permute-done.44.refs_2_
  287.2 7.6 %shard_map.282 = (bf16[256,1536]{1,0:T(8,128)(2,1)}, bf16[256,1536]{1,0:T(8,128)(2,1)S(1)}, bf16[256,1536]{1,0:T(8,128)(2,1)S(1)}, f32[256,1536]{1,0:T(8,128)S(1)}) custom-call(bf16[1024,1024]{1,0:T(8,128)(2,1)} %get-tuple-element.422.left.refs_0_, bf16[1536,1024]{1,0:T(8,128)(2,1)} %all-gather.14.cloned.1.call-done.w_ref.refs_1_), custom_call_target="tpu_custom_call" | custom-call | flops 3221225472 | bytes 6442450 | tf_op jit(solution)/shard_map/pallas_call | solution.py:187
  299.5 6.6 %shard_map.283 = (bf16[1024,384]{1,0:T(8,128)(2,1)}, bf16[1024,384]{1,0:T(8,128)(2,1)}) custom-call(bf16[128,1536]{1,0:T(8,128)(2,1)} %get-tuple-element.418.refs_0_, bf16[128,1536]{1,0:T(8,128)(2,1)} %get-tuple-element.419.refs_1_, bf16[128,1536]{1,0:T(8,128)(2,1)} %copy-done.19, bf16[128,1536]{1,0:T(8,128)(2,1)} %copy-done.21, ...), custom_call_target="tpu_custom_call" | custom-call | flops 1207959552 | bytes 10485760 | tf_op jit(solution)/shard_map/pallas_call | solution.py:657
  306.1 20.2 %shard_map.284.d_ref.refs_0_.refs_1_.refs_2_ = bf16[1024,1280]{1,0:T(8,128)(2,1)} custom-call(s32[3]{0:T(128)} %copy-done.35, bf16[6,1024,128]{2,1,0:T(8,128)(2,1)} %get-tuple-element.424.qa_ref, bf16[6,1024,128]{2,1,0:T(8,128)(2,1)} %get-tuple-element.425.ka_ref, f32[1024,128]{1,0:T(8,128)} %get-tuple-element.426.log_ref, ...), custom_call_target="tpu_custom_call" | custom-call | flops 12000000000 | bytes 8388608 | tf_op jit(solution)/shard_map/pallas_call | solution.py:1151
  326.4 6.1 %collective-permute-done.52.three = bf16[256,1536]{1,0:T(8,128)(2,1)} collective-permute-done((bf16[256,1536]{1,0:T(8,128)(2,1)S(1)}, bf16[256,1536]{1,0:T(8,128)(2,1)}, u32[]{:S(2)}, u32[]{:S(2)}) %collective-permute-start.52) | collective-permute-done | bytes 786464 | tf_op jit(solution)/shard_map/ppermute | solution.py:67
  332.6 4.8 %shard_map.285 = (bf16[256,384]{1,0:T(8,128)(2,1)}, bf16[256,384]{1,0:T(8,128)(2,1)}, bf16[256,384]{1,0:T(8,128)(2,1)}, bf16[256,384]{1,0:T(8,128)(2,1)}) custom-call(s32[3]{0:T(128)} %copy-done.35, f32[256,1536]{1,0:T(8,128)} %get-tuple-element.366.second_ref, f32[256,1536]{1,0:T(8,128)} %copy-done.8, bf16[256,1536]{1,0:T(8,128)(2,1)} %collective-permute-done.50.one, ...), custom_call_target="tpu_custom_call" | custom-call | flops 1 | bytes 6291456 | tf_op jit(solution)/shard_map/pallas_call | solution.py:438
  337.4 8.5 %collective-permute-start.53 = (bf16[256,384]{1,0:T(8,128)(2,1)}, bf16[256,384]{1,0:T(8,128)(2,1)}, u32[]{:S(2)}, u32[]{:S(2)}) collective-permute-start(bf16[256,384]{1,0:T(8,128)(2,1)} %get-tuple-element.445), channel_id=1, source_target_pairs={{0,1},{1,0},{2,3},{3,2},{4,5},{5,4},{6,7},{7,6},{8,9},{9,8},{10,11... | collective-permute-start | bytes 589832 | tf_op jit(solution)/shard_map/ppermute | solution.py:67
  347.3 11.9 %shard_map.286 = bf16[1536,2048]{1,0:T(8,128)(2,1)} custom-call(bf16[1024,1536]{1,0:T(8,128)(2,1)} %get-tuple-element.318.h_ref, bf16[1024,1280]{1,0:T(8,128)(2,1)} %shard_map.284.d_ref.refs_0_.refs_1_.refs_2_, bf16[1024,384]{1,0:T(8,128)(2,1)S(1)} %copy-done.6, bf16[1024,384]{1,0:T(8,128)(2,1)} %copy-done.10, bf16[128,1536]{1,0:T(8,128)(2,1)S(1)} %copy-done.17, ...), custom_call_target="tpu_custom_call" | custom-call | flops 6442450944 | bytes 16777216 | tf_op jit(solution)/shard_map/pallas_call | solution.py:274
  359.2 3.5 collective-permute-done.55.refs_3_
  368.2 5.6 %shard_map.287 = (bf16[256,768]{1,0:T(8,128)(2,1)S(1)}, bf16[256,768]{1,0:T(8,128)(2,1)S(1)}) custom-call(bf16[1024,1280]{1,0:T(8,128)(2,1)} %shard_map.284.d_ref.refs_0_.refs_1_.refs_2_, bf16[1024,1280]{1,0:T(8,128)(2,1)} %shard_map.284.d_ref.refs_0_.refs_1_.refs_2_, bf16[1024,1280]{1,0:T(8,128)(2,1)} %shard_map.284.d_ref.refs_0_.refs_1_.refs_2_, ...), custom_call_target="tpu_custom_call" | custom-call | flops 1308622848 | bytes 2617245 | tf_op jit(solution)/shard_map/pallas_call | solution.py:187
  376.5 8.6 %shard_map.289 = (bf16[256,768]{1,0:T(8,128)(2,1)S(1)}, f32[256,768]{1,0:T(8,128)S(1)}, f32[256,768]{1,0:T(8,128)S(1)}, f32[256,768]{1,0:T(8,128)S(1)}, bf16[256...) custom-call(bf16[1024,1280]{1,0:T(8,128)(2,1)} %shard_map.284.d_ref.refs_0_.refs_1_.refs_2_, ...), custom_call_target="tpu_custom_call" | custom-call | flops 3925868544 | bytes 7851737 | tf_op jit(solution)/shard_map/pallas_call | solution.py:187
  388.7 4.4 collective-permute-start.67
  403.4 3.5 shard_map.290
  413.0 7.6 %collective-permute-done.64.refs_5_ = bf16[256,768]{1,0:T(8,128)(2,1)S(1)} collective-permute-done((bf16[256,768]{1,0:T(8,128)(2,1)S(1)}, bf16[256,768]{1,0:T(8,128)(2,1)S(1)}, u32[]{:S(2)}, u32[]{:S(2)}) %collective-permute-start.64) | collective-permute-done | bytes 393248 | tf_op jit(solution)/shard_map/ppermute | solution.py:67
  421.3 5.0 %shard_map.291 = (bf16[256,384]{1,0:T(8,128)(2,1)}, bf16[256,384]{1,0:T(8,128)(2,1)}, bf16[256,384]{1,0:T(8,128)(2,1)}, bf16[256,384]{1,0:T(8,128)(2,1)}) custom-call(s32[3]{0:T(128)} %copy-done.35, bf16[128,1536]{1,0:T(8,128)(2,1)} %get-tuple-element.312.refs_0_.x_top, bf16[128,1536]{1,0:T(8,128)(2,1)} %get-tuple-element.313.refs_1_.x_low, ...), custom_call_target="tpu_custom_call" | custom-call | flops 1 | bytes 6291456 | tf_op jit(solution)/shard_map/pallas_call | solution.py:438
  429.3 9.0 %collective-permute-done.75.refs_1_ = bf16[256,384]{1,0:T(8,128)(2,1)S(1)} collective-permute-done((bf16[256,384]{1,0:T(8,128)(2,1)}, bf16[256,384]{1,0:T(8,128)(2,1)S(1)}, u32[]{:S(2)}, u32[]{:S(2)}) %collective-permute-start.75) | collective-permute-done | bytes 196640 | tf_op jit(solution)/shard_map/ppermute | solution.py:67
  438.2 2.6 collective-permute-done.76.refs_2_
  440.8 7.6 %collective-permute-done.77.refs_3_ = bf16[256,384]{1,0:T(8,128)(2,1)S(1)} collective-permute-done((bf16[256,384]{1,0:T(8,128)(2,1)}, bf16[256,384]{1,0:T(8,128)(2,1)S(1)}, u32[]{:S(2)}, u32[]{:S(2)}) %collective-permute-start.77) | collective-permute-done | bytes 196640 | tf_op jit(solution)/shard_map/ppermute | solution.py:67
  465.6 2.6 collective-permute-start.85
  470.2 3.5 shard_map.293
  (452 shorter events, 141.7 us)
Async XLA Ops:
  7.2 64.2 %all-gather.6.cloned.1.call-start = ((), (), s32[]{:S(2)}) async-start(), calls=%async_computation.3 | async-start | bytes 2654208 | tf_op jit(solution)/shard_map/all_gather | solution.py:1215
  9.2 74.1 %all-gather.8.cloned.1.call-start = ((), (), s32[]{:S(2)}) async-start(), calls=%async_computation.4 | async-start | bytes 1769472 | tf_op jit(solution)/shard_map/all_gather | solution.py:1215
  13.6 134.7 %all-gather.10.cloned.1.call-start = ((), (), s32[]{:S(2)}) async-start(), calls=%async_computation.5 | async-start | bytes 2654208 | tf_op jit(solution)/shard_map/all_gather | solution.py:1215
  40.6 15.5 %collective-permute-start.6 = (bf16[256,384]{1,0:T(8,128)(2,1)}, bf16[256,384]{1,0:T(8,128)(2,1)S(1)}, u32[]{:S(2)}, u32[]{:S(2)}) collective-permute-start(bf16[256,384]{1,0:T(8,128)(2,1)} %get-tuple-element.286), channel_id=1, source_target_pairs={{0,2},{1,3},{2,0},{3,1},{4,6},{5,7},{6,4},{7,5},{8,10},{9,11},{10,... | collective-permute-start | bytes 589832 | tf_op jit(solution)/shard_map/ppermute | solution.py:67
  42.9 25.3 %collective-permute-start.7 = (bf16[256,384]{1,0:T(8,128)(2,1)}, bf16[256,384]{1,0:T(8,128)(2,1)S(1)}, u32[]{:S(2)}, u32[]{:S(2)}) collective-permute-start(bf16[256,384]{1,0:T(8,128)(2,1)} %get-tuple-element.287), channel_id=1, source_target_pairs={{0,3},{1,2},{2,1},{3,0},{4,7},{5,6},{6,5},{7,4},{8,11},{9,10},{10,... | collective-permute-start | bytes 589832 | tf_op jit(solution)/shard_map/ppermute | solution.py:67
  43.1 25.1 %collective-permute-start.8 = (bf16[256,384]{1,0:T(8,128)(2,1)S(1)}, bf16[256,384]{1,0:T(8,128)(2,1)S(1)}, u32[]{:S(2)}, u32[]{:S(2)}) collective-permute-start(bf16[256,384]{1,0:T(8,128)(2,1)S(1)} %copy-done.47), channel_id=1, source_target_pairs={{0,4},{4,0},{8,12},{12,8},{1,5},{5,1},{9,13},{13,9},{2,6},{6,2},{1... | collective-permute-start | bytes 589832 | tf_op jit(solution)/shard_map/ppermute | solution.py:67
  44.8 23.4 %collective-permute-start.9 = (bf16[256,384]{1,0:T(8,128)(2,1)S(1)}, bf16[256,384]{1,0:T(8,128)(2,1)S(1)}, u32[]{:S(2)}, u32[]{:S(2)}) collective-permute-start(bf16[256,384]{1,0:T(8,128)(2,1)S(1)} %get-tuple-element.290), channel_id=1, source_target_pairs={{0,8},{4,12},{8,0},{12,4},{1,9},{5,13},{9,1},{13,5},{2,10},{6,14},... | collective-permute-start | bytes 589832 | tf_op jit(solution)/shard_map/ppermute | solution.py:67
  45.3 22.9 %collective-permute-start.10 = (bf16[256,384]{1,0:T(8,128)(2,1)S(1)}, bf16[256,384]{1,0:T(8,128)(2,1)S(1)}, u32[]{:S(2)}, u32[]{:S(2)}) collective-permute-start(bf16[256,384]{1,0:T(8,128)(2,1)S(1)} %get-tuple-element.291), channel_id=1, source_target_pairs={{0,12},{4,8},{8,4},{12,0},{1,13},{5,9},{9,5},{13,1},{2,14},{6,10},... | collective-permute-start | bytes 589832 | tf_op jit(solution)/shard_map/ppermute | solution.py:67
  71.4 125.1 %all-gather.12.cloned.1.call-start = ((), (), s32[]{:S(2)}) async-start(), calls=%async_computation.6 | async-start | bytes 7077888 | tf_op jit(solution)/shard_map/all_gather | solution.py:1215
  72.0 156.1 %all-gather.14.cloned.1.call-start = ((), (), s32[]{:S(2)}) async-start(), calls=%async_computation.7 | async-start | bytes 3538944 | tf_op jit(solution)/shard_map/all_gather | solution.py:1215
  78.6 14.4 %collective-permute-start.14 = (bf16[128,1536]{1,0:T(8,128)(2,1)}, bf16[128,1536]{1,0:T(8,128)(2,1)S(1)}, u32[]{:S(2)}, u32[]{:S(2)}) collective-permute-start(bf16[128,1536]{1,0:T(8,128)(2,1)} %get-tuple-element.313.refs_1_.x_low), channel_id=1, source_target_pairs={{0,4},{4,0},{8,12},{12,8},{1,5},{5,1},{9,13},{13,9},{2,6},{6,2},{1... | collective-permute-start | bytes 1179656 | tf_op jit(solution)/shard_map/ppermute | solution.py:67
  79.7 16.8 %collective-permute-start.15 = (bf16[128,1536]{1,0:T(8,128)(2,1)}, bf16[128,1536]{1,0:T(8,128)(2,1)S(1)}, u32[]{:S(2)}, u32[]{:S(2)}) collective-permute-start(bf16[128,1536]{1,0:T(8,128)(2,1)} %get-tuple-element.312.refs_0_.x_top), channel_id=1, source_target_pairs={{0,8},{4,12},{8,0},{12,4},{1,9},{5,13},{9,1},{13,5},{2,10},{6,14},... | collective-permute-start | bytes 1179656 | tf_op jit(solution)/shard_map/ppermute | solution.py:67
  85.9 17.0 %collective-permute-start.16 = (bf16[128,1536]{1,0:T(8,128)(2,1)S(1)}, bf16[128,1536]{1,0:T(8,128)(2,1)S(1)}, u32[]{:S(2)}, u32[]{:S(2)}) collective-permute-start(bf16[128,1536]{1,0:T(8,128)(2,1)S(1)} %collective-permute-done.11.refs_2_), channel_id=1, source_target_pairs={{0,8},{4,12},{8,0},{12,4},{1,9},{5,13},{9,1},{13,5},{2,10},{6,14},... | collective-permute-start | bytes 1179656 | tf_op jit(solution)/shard_map/ppermute | solution.py:67
  85.9 17.0 %collective-permute-start.17 = (bf16[128,1536]{1,0:T(8,128)(2,1)S(1)}, bf16[128,1536]{1,0:T(8,128)(2,1)}, u32[]{:S(2)}, u32[]{:S(2)}) collective-permute-start(bf16[128,1536]{1,0:T(8,128)(2,1)S(1)} %collective-permute-done.12.refs_3_), channel_id=1, source_target_pairs={{0,4},{4,0},{8,12},{12,8},{1,5},{5,1},{9,13},{13,9},{2,6},{6,2},{1... | collective-permute-start | bytes 1179656 | tf_op jit(solution)/shard_map/ppermute | solution.py:67
  88.6 27.0 %collective-permute-start.18 = (bf16[256,384]{1,0:T(8,128)(2,1)}, bf16[256,384]{1,0:T(8,128)(2,1)S(1)}, u32[]{:S(2)}, u32[]{:S(2)}) collective-permute-start(bf16[256,384]{1,0:T(8,128)(2,1)} %get-tuple-element.322), channel_id=1, source_target_pairs={{0,2},{1,3},{2,0},{3,1},{4,6},{5,7},{6,4},{7,5},{8,10},{9,11},{10,... | collective-permute-start | bytes 589832 | tf_op jit(solution)/shard_map/ppermute | solution.py:67
  93.0 30.0 %collective-permute-start.19 = (bf16[256,384]{1,0:T(8,128)(2,1)}, bf16[256,384]{1,0:T(8,128)(2,1)S(1)}, u32[]{:S(2)}, u32[]{:S(2)}) collective-permute-start(bf16[256,384]{1,0:T(8,128)(2,1)} %get-tuple-element.323), channel_id=1, source_target_pairs={{0,3},{1,2},{2,1},{3,0},{4,7},{5,6},{6,5},{7,4},{8,11},{9,10},{10,... | collective-permute-start | bytes 589832 | tf_op jit(solution)/shard_map/ppermute | solution.py:67
  125.9 19.2 %collective-permute-start.21 = (bf16[128,1536]{1,0:T(8,128)(2,1)}, bf16[128,1536]{1,0:T(8,128)(2,1)S(1)}, u32[]{:S(2)}, u32[]{:S(2)}) collective-permute-start(bf16[128,1536]{1,0:T(8,128)(2,1)} %get-tuple-element.336.refs_1_.grad_low), channel_id=1, source_target_pairs={{0,8},{4,12},{8,0},{12,4},{1,9},{5,13},{9,1},{13,5},{2,10},{6,14},... | collective-permute-start | bytes 1179656 | tf_op jit(solution)/shard_map/ppermute | solution.py:67
  127.3 17.8 %collective-permute-start.22 = (bf16[128,1536]{1,0:T(8,128)(2,1)}, bf16[128,1536]{1,0:T(8,128)(2,1)S(1)}, u32[]{:S(2)}, u32[]{:S(2)}) collective-permute-start(bf16[128,1536]{1,0:T(8,128)(2,1)} %get-tuple-element.336.refs_1_.grad_low), channel_id=1, source_target_pairs={{0,4},{4,0},{8,12},{12,8},{1,5},{5,1},{9,13},{13,9},{2,6},{6,2},{1... | collective-permute-start | bytes 1179656 | tf_op jit(solution)/shard_map/ppermute | solution.py:67
  128.5 16.6 %collective-permute-start.20 = (bf16[128,1536]{1,0:T(8,128)(2,1)}, bf16[128,1536]{1,0:T(8,128)(2,1)}, u32[]{:S(2)}, u32[]{:S(2)}) collective-permute-start(bf16[128,1536]{1,0:T(8,128)(2,1)} %get-tuple-element.335.refs_0_.grad_top), channel_id=1, source_target_pairs={{0,4},{4,0},{8,12},{12,8},{1,5},{5,1},{9,13},{13,9},{2,6},{6,2},{1... | collective-permute-start | bytes 1179656 | tf_op jit(solution)/shard_map/ppermute | solution.py:67
  128.8 17.2 %collective-permute-start.23 = (bf16[128,1536]{1,0:T(8,128)(2,1)}, bf16[128,1536]{1,0:T(8,128)(2,1)S(1)}, u32[]{:S(2)}, u32[]{:S(2)}) collective-permute-start(bf16[128,1536]{1,0:T(8,128)(2,1)} %get-tuple-element.335.refs_0_.grad_top), channel_id=1, source_target_pairs={{0,8},{4,12},{8,0},{12,4},{1,9},{5,13},{9,1},{13,5},{2,10},{6,14},... | collective-permute-start | bytes 1179656 | tf_op jit(solution)/shard_map/ppermute | solution.py:67
  146.7 185.8 %reduce-scatter.4.cloned.1.call-start = ((), (), s32[]{:S(2)}) async-start(), calls=%async_computation.8 | async-start | bytes 3538944 | tf_op jit(solution)/shard_map/reduce_scatter | solution.py:115
  168.1 12.4 %collective-permute-start.30 = (bf16[256,768]{1,0:T(8,128)(2,1)S(1)}, bf16[256,768]{1,0:T(8,128)(2,1)S(1)}, u32[]{:S(2)}, u32[]{:S(2)}) collective-permute-start(bf16[256,768]{1,0:T(8,128)(2,1)S(1)} %add_convert_fusion.4), channel_id=1, source_target_pairs={{0,4},{4,0},{8,12},{12,8},{1,5},{5,1},{9,13},{13,9},{2,6},{6,2},{1... | collective-permute-start | bytes 1179656 | tf_op jit(solution)/shard_map/ppermute | solution.py:67
  168.5 13.6 %collective-permute-start.31 = (bf16[256,768]{1,0:T(8,128)(2,1)S(1)}, bf16[256,768]{1,0:T(8,128)(2,1)S(1)}, u32[]{:S(2)}, u32[]{:S(2)}) collective-permute-start(bf16[256,768]{1,0:T(8,128)(2,1)S(1)} %get-tuple-element.360), channel_id=1, source_target_pairs={{0,8},{4,12},{8,0},{12,4},{1,9},{5,13},{9,1},{13,5},{2,10},{6,14},... | collective-permute-start | bytes 1179656 | tf_op jit(solution)/shard_map/ppermute | solution.py:67
  189.0 15.6 %collective-permute-start.32 = (bf16[128,1536]{1,0:T(8,128)(2,1)}, bf16[128,1536]{1,0:T(8,128)(2,1)S(1)}, u32[]{:S(2)}, u32[]{:S(2)}) collective-permute-start(bf16[128,1536]{1,0:T(8,128)(2,1)} %get-tuple-element.367.refs_1_), channel_id=1, source_target_pairs={{0,4},{4,0},{8,12},{12,8},{1,5},{5,1},{9,13},{13,9},{2,6},{6,2},{1... | collective-permute-start | bytes 1179656 | tf_op jit(solution)/shard_map/ppermute | solution.py:67
  189.7 15.0 %collective-permute-start.33 = (bf16[128,1536]{1,0:T(8,128)(2,1)}, bf16[128,1536]{1,0:T(8,128)(2,1)S(1)}, u32[]{:S(2)}, u32[]{:S(2)}) collective-permute-start(bf16[128,1536]{1,0:T(8,128)(2,1)} %get-tuple-element.368.refs_0_), channel_id=1, source_target_pairs={{0,8},{4,12},{8,0},{12,4},{1,9},{5,13},{9,1},{13,5},{2,10},{6,14},... | collective-permute-start | bytes 1179656 | tf_op jit(solution)/shard_map/ppermute | solution.py:67
  195.0 15.8 %collective-permute-start.36 = (bf16[128,1536]{1,0:T(8,128)(2,1)S(1)}, bf16[128,1536]{1,0:T(8,128)(2,1)S(1)}, u32[]{:S(2)}, u32[]{:S(2)}) collective-permute-start(bf16[128,1536]{1,0:T(8,128)(2,1)S(1)} %collective-permute-done.34.refs_2_), channel_id=1, source_target_pairs={{0,8},{4,12},{8,0},{12,4},{1,9},{5,13},{9,1},{13,5},{2,10},{6,14},... | collective-permute-start | bytes 1179656 | tf_op jit(solution)/shard_map/ppermute | solution.py:67
  195.9 14.8 %collective-permute-start.37 = (bf16[128,1536]{1,0:T(8,128)(2,1)S(1)}, bf16[128,1536]{1,0:T(8,128)(2,1)S(1)}, u32[]{:S(2)}, u32[]{:S(2)}) collective-permute-start(bf16[128,1536]{1,0:T(8,128)(2,1)S(1)} %collective-permute-done.35.refs_3_), channel_id=1, source_target_pairs={{0,4},{4,0},{8,12},{12,8},{1,5},{5,1},{9,13},{13,9},{2,6},{6,2},{1... | collective-permute-start | bytes 1179656 | tf_op jit(solution)/shard_map/ppermute | solution.py:67
  228.1 160.4 %reduce-scatter.6.cloned.1.call-start = ((), (), s32[]{:S(2)}) async-start(), calls=%async_computation.9 | async-start | bytes 7077888 | tf_op jit(solution)/shard_map/reduce_scatter | solution.py:115
  255.4 14.6 %collective-permute-start.40 = (bf16[256,768]{1,0:T(8,128)(2,1)S(1)}, bf16[256,768]{1,0:T(8,128)(2,1)S(1)}, u32[]{:S(2)}, u32[]{:S(2)}) collective-permute-start(bf16[256,768]{1,0:T(8,128)(2,1)S(1)} %get-tuple-element.397), channel_id=1, source_target_pairs={{0,4},{4,0},{8,12},{12,8},{1,5},{5,1},{9,13},{13,9},{2,6},{6,2},{1... | collective-permute-start | bytes 1179656 | tf_op jit(solution)/shard_map/ppermute | solution.py:67
  256.7 13.3 %collective-permute-start.41 = (bf16[256,768]{1,0:T(8,128)(2,1)S(1)}, bf16[256,768]{1,0:T(8,128)(2,1)S(1)}, u32[]{:S(2)}, u32[]{:S(2)}) collective-permute-start(bf16[256,768]{1,0:T(8,128)(2,1)S(1)} %add_convert_fusion.3), channel_id=1, source_target_pairs={{0,8},{4,12},{8,0},{12,4},{1,9},{5,13},{9,1},{13,5},{2,10},{6,14},... | collective-permute-start | bytes 1179656 | tf_op jit(solution)/shard_map/ppermute | solution.py:67
  257.7 12.4 %collective-permute-start.42 = (bf16[256,768]{1,0:T(8,128)(2,1)S(1)}, bf16[256,768]{1,0:T(8,128)(2,1)S(1)}, u32[]{:S(2)}, u32[]{:S(2)}) collective-permute-start(bf16[256,768]{1,0:T(8,128)(2,1)S(1)} %add_convert_fusion.2), channel_id=1, source_target_pairs={{0,4},{4,0},{8,12},{12,8},{1,5},{5,1},{9,13},{13,9},{2,6},{6,2},{1... | collective-permute-start | bytes 1179656 | tf_op jit(solution)/shard_map/ppermute | solution.py:67
  271.2 177.3 %reduce-scatter.8.cloned.1.call-start = ((), (), s32[]{:S(2)}) async-start(), calls=%async_computation.10 | async-start | bytes 7077888 | tf_op jit(solution)/shard_map/reduce_scatter | solution.py:115
  279.0 17.5 %collective-permute-start.46 = (bf16[128,1536]{1,0:T(8,128)(2,1)}, bf16[128,1536]{1,0:T(8,128)(2,1)S(1)}, u32[]{:S(2)}, u32[]{:S(2)}) collective-permute-start(bf16[128,1536]{1,0:T(8,128)(2,1)} %get-tuple-element.419.refs_1_), channel_id=1, source_target_pairs={{0,4},{4,0},{8,12},{12,8},{1,5},{5,1},{9,13},{13,9},{2,6},{6,2},{1... | collective-permute-start | bytes 1179656 | tf_op jit(solution)/shard_map/ppermute | solution.py:67
  280.0 17.2 %collective-permute-start.47 = (bf16[128,1536]{1,0:T(8,128)(2,1)}, bf16[128,1536]{1,0:T(8,128)(2,1)S(1)}, u32[]{:S(2)}, u32[]{:S(2)}) collective-permute-start(bf16[128,1536]{1,0:T(8,128)(2,1)} %get-tuple-element.418.refs_0_), channel_id=1, source_target_pairs={{0,8},{4,12},{8,0},{12,4},{1,9},{5,13},{9,1},{13,5},{2,10},{6,14},... | collective-permute-start | bytes 1179656 | tf_op jit(solution)/shard_map/ppermute | solution.py:67
  285.5 13.2 %collective-permute-start.48 = (bf16[128,1536]{1,0:T(8,128)(2,1)S(1)}, bf16[128,1536]{1,0:T(8,128)(2,1)S(1)}, u32[]{:S(2)}, u32[]{:S(2)}) collective-permute-start(bf16[128,1536]{1,0:T(8,128)(2,1)S(1)} %collective-permute-done.44.refs_2_), channel_id=1, source_target_pairs={{0,8},{4,12},{8,0},{12,4},{1,9},{5,13},{9,1},{13,5},{2,10},{6,14},... | collective-permute-start | bytes 1179656 | tf_op jit(solution)/shard_map/ppermute | solution.py:67
  286.2 12.4 %collective-permute-start.49 = (bf16[128,1536]{1,0:T(8,128)(2,1)S(1)}, bf16[128,1536]{1,0:T(8,128)(2,1)S(1)}, u32[]{:S(2)}, u32[]{:S(2)}) collective-permute-start(bf16[128,1536]{1,0:T(8,128)(2,1)S(1)} %collective-permute-done.45.refs_3_), channel_id=1, source_target_pairs={{0,4},{4,0},{8,12},{12,8},{1,5},{5,1},{9,13},{13,9},{2,6},{6,2},{1... | collective-permute-start | bytes 1179656 | tf_op jit(solution)/shard_map/ppermute | solution.py:67
  296.0 30.4 %collective-permute-start.50 = (bf16[256,1536]{1,0:T(8,128)(2,1)}, bf16[256,1536]{1,0:T(8,128)(2,1)}, u32[]{:S(2)}, u32[]{:S(2)}) collective-permute-start(bf16[256,1536]{1,0:T(8,128)(2,1)} %get-tuple-element.430), channel_id=1, source_target_pairs={{0,4},{4,0},{8,12},{12,8},{1,5},{5,1},{9,13},{13,9},{2,6},{6,2},{1... | collective-permute-start | bytes 2359304 | tf_op jit(solution)/shard_map/ppermute | solution.py:67
  296.5 29.9 %collective-permute-start.51 = (bf16[256,1536]{1,0:T(8,128)(2,1)S(1)}, bf16[256,1536]{1,0:T(8,128)(2,1)}, u32[]{:S(2)}, u32[]{:S(2)}) collective-permute-start(bf16[256,1536]{1,0:T(8,128)(2,1)S(1)} %get-tuple-element.431), channel_id=1, source_target_pairs={{0,8},{4,12},{8,0},{12,4},{1,9},{5,13},{9,1},{13,5},{2,10},{6,14},... | collective-permute-start | bytes 2359304 | tf_op jit(solution)/shard_map/ppermute | solution.py:67
  297.2 35.3 %collective-permute-start.52 = (bf16[256,1536]{1,0:T(8,128)(2,1)S(1)}, bf16[256,1536]{1,0:T(8,128)(2,1)}, u32[]{:S(2)}, u32[]{:S(2)}) collective-permute-start(bf16[256,1536]{1,0:T(8,128)(2,1)S(1)} %get-tuple-element.432), channel_id=1, source_target_pairs={{0,12},{4,8},{8,4},{12,0},{1,13},{5,9},{9,5},{13,1},{2,14},{6,10},... | collective-permute-start | bytes 2359304 | tf_op jit(solution)/shard_map/ppermute | solution.py:67
  337.4 21.8 %collective-permute-start.53 = (bf16[256,384]{1,0:T(8,128)(2,1)}, bf16[256,384]{1,0:T(8,128)(2,1)}, u32[]{:S(2)}, u32[]{:S(2)}) collective-permute-start(bf16[256,384]{1,0:T(8,128)(2,1)} %get-tuple-element.445), channel_id=1, source_target_pairs={{0,1},{1,0},{2,3},{3,2},{4,5},{5,4},{6,7},{7,6},{8,9},{9,8},{10,11... | collective-permute-start | bytes 589832 | tf_op jit(solution)/shard_map/ppermute | solution.py:67
  346.0 13.2 %collective-permute-start.54 = (bf16[256,384]{1,0:T(8,128)(2,1)}, bf16[256,384]{1,0:T(8,128)(2,1)}, u32[]{:S(2)}, u32[]{:S(2)}) collective-permute-start(bf16[256,384]{1,0:T(8,128)(2,1)} %get-tuple-element.446), channel_id=1, source_target_pairs={{0,2},{1,3},{2,0},{3,1},{4,6},{5,7},{6,4},{7,5},{8,10},{9,11},{10,... | collective-permute-start | bytes 589832 | tf_op jit(solution)/shard_map/ppermute | solution.py:67
  346.0 16.8 %collective-permute-start.55 = (bf16[256,384]{1,0:T(8,128)(2,1)}, bf16[256,384]{1,0:T(8,128)(2,1)}, u32[]{:S(2)}, u32[]{:S(2)}) collective-permute-start(bf16[256,384]{1,0:T(8,128)(2,1)} %get-tuple-element.447), channel_id=1, source_target_pairs={{0,3},{1,2},{2,1},{3,0},{4,7},{5,6},{6,5},{7,4},{8,11},{9,10},{10,... | collective-permute-start | bytes 589832 | tf_op jit(solution)/shard_map/ppermute | solution.py:67
  374.7 12.2 %collective-permute-start.59 = (bf16[256,768]{1,0:T(8,128)(2,1)S(1)}, bf16[256,768]{1,0:T(8,128)(2,1)S(1)}, u32[]{:S(2)}, u32[]{:S(2)}) collective-permute-start(bf16[256,768]{1,0:T(8,128)(2,1)S(1)} %get-tuple-element.459), channel_id=1, source_target_pairs={{0,4},{4,0},{8,12},{12,8},{1,5},{5,1},{9,13},{13,9},{2,6},{6,2},{1... | collective-permute-start | bytes 1179656 | tf_op jit(solution)/shard_map/ppermute | solution.py:67
  393.0 19.9 %collective-permute-start.63 = (bf16[256,768]{1,0:T(8,128)(2,1)}, bf16[256,768]{1,0:T(8,128)(2,1)S(1)}, u32[]{:S(2)}, u32[]{:S(2)}) collective-permute-start(bf16[256,768]{1,0:T(8,128)(2,1)} %add_convert_fusion), channel_id=1, source_target_pairs={{0,4},{4,0},{8,12},{12,8},{1,5},{5,1},{9,13},{13,9},{2,6},{6,2},{1... | collective-permute-start | bytes 1179656 | tf_op jit(solution)/shard_map/ppermute | solution.py:67
  407.0 13.6 %collective-permute-start.64 = (bf16[256,768]{1,0:T(8,128)(2,1)S(1)}, bf16[256,768]{1,0:T(8,128)(2,1)S(1)}, u32[]{:S(2)}, u32[]{:S(2)}) collective-permute-start(bf16[256,768]{1,0:T(8,128)(2,1)S(1)} %get-tuple-element.476), channel_id=1, source_target_pairs={{0,8},{4,12},{8,0},{12,4},{1,9},{5,13},{9,1},{13,5},{2,10},{6,14},... | collective-permute-start | bytes 1179656 | tf_op jit(solution)/shard_map/ppermute | solution.py:67
  426.3 11.9 %collective-permute-start.75 = (bf16[256,384]{1,0:T(8,128)(2,1)}, bf16[256,384]{1,0:T(8,128)(2,1)S(1)}, u32[]{:S(2)}, u32[]{:S(2)}) collective-permute-start(bf16[256,384]{1,0:T(8,128)(2,1)} %get-tuple-element.499), channel_id=1, source_target_pairs={{0,1},{1,0},{2,3},{3,2},{4,5},{5,4},{6,7},{7,6},{8,9},{9,8},{10,11... | collective-permute-start | bytes 589832 | tf_op jit(solution)/shard_map/ppermute | solution.py:67
  428.0 12.8 %collective-permute-start.76 = (bf16[256,384]{1,0:T(8,128)(2,1)}, bf16[256,384]{1,0:T(8,128)(2,1)S(1)}, u32[]{:S(2)}, u32[]{:S(2)}) collective-permute-start(bf16[256,384]{1,0:T(8,128)(2,1)} %get-tuple-element.500), channel_id=1, source_target_pairs={{0,2},{1,3},{2,0},{3,1},{4,6},{5,7},{6,4},{7,5},{8,10},{9,11},{10,... | collective-permute-start | bytes 589832 | tf_op jit(solution)/shard_map/ppermute | solution.py:67
  428.0 20.4 %collective-permute-start.77 = (bf16[256,384]{1,0:T(8,128)(2,1)}, bf16[256,384]{1,0:T(8,128)(2,1)S(1)}, u32[]{:S(2)}, u32[]{:S(2)}) collective-permute-start(bf16[256,384]{1,0:T(8,128)(2,1)} %get-tuple-element.501), channel_id=1, source_target_pairs={{0,3},{1,2},{2,1},{3,0},{4,7},{5,6},{6,5},{7,4},{8,11},{9,10},{10,... | collective-permute-start | bytes 589832 | tf_op jit(solution)/shard_map/ppermute | solution.py:67
  (154 other events, 1150.2 us)
Sparse Core Ops, SparseCore 0:
  10.3 32.7 all-gather.5
  45.3 30.1 all-gather.7
  77.1 42.5 all-gather.9
  121.2 67.0 all-gather.11
  189.8 38.1 all-gather.13
  230.2 39.8 reduce-scatter.3
  272.4 71.6 reduce-scatter.5
  362.9 70.3 reduce-scatter.7
